TPU v7x, 32 devices: a whole 2x2x4 slice. The times are simulated.
32 devices in a mesh: fsdp: 2 (over y), ctx: 4 (over z), tp: 4 (over x, core).
Axes of the slice: x: 2, y: 2, z: 4, core: 2. Of those that a mesh axis runs over, the one named last changes fastest.
Arguments:
- inputs: bfloat16 [4, 2048, 768], P('fsdp', 'ctx'), may hold values from -6 to 6
- positions: int32 [4, 2048], P('fsdp'), may hold values from 0 to 2047, as said below
- query_key_value_weight: bfloat16 [768, 3, 768], P('fsdp', None, 'tp'), may hold values from -0.21875 to 0.21875
- query_key_value_bias: float32 [3, 768], P(None, 'tp'), may hold values from -3 to 3
- attention_output_weight: bfloat16 [768, 768], P('tp', 'fsdp'), may hold values from -1.75 to 1.75
- attention_output_bias: float32 [768], replicated, may hold values from -3 to 3
- up_projection_weight: bfloat16 [768, 3072], P('fsdp', 'tp'), may hold values from -0.21875 to 0.21875
- up_projection_bias: float32 [3072], P('tp'), may hold values from -3 to 3
- down_projection_weight: bfloat16 [3072, 768], P('tp', 'fsdp'), may hold values from -0.109375 to 0.109375
- down_projection_bias: float32 [768], replicated, may hold values from -3 to 3
- first_scale: float32 [768], replicated, may hold values from 0.5 to 1.5
- first_shift: float32 [768], replicated, may hold values from -1.8 to 1.8
- second_scale: float32 [768], replicated, may hold values from 0.5 to 1.5
- second_shift: float32 [768], replicated, may hold values from -1.8 to 1.8
- cotangent: bfloat16 [4, 2048, 768], P('fsdp', 'ctx'), may hold values from -6 to 6
Outputs:
- block_out: float32 [4, 2048, 768], P('fsdp', 'ctx')
- inputs_grad: float32 [4, 2048, 768], P('fsdp', 'ctx')
- mix_weight_grad: float32 [768, 3, 768], P('fsdp', None, 'tp')
- mix_bias_grad: float32 [3, 768], P(None, 'tp')
- out_weight_grad: float32 [768, 768], P('tp', 'fsdp')
- out_bias_grad: float32 [768], replicated
- up_weight_grad: float32 [768, 3072], P('fsdp', 'tp')
- up_bias_grad: float32 [3072], P('tp')
- down_weight_grad: float32 [3072, 768], P('tp', 'fsdp')
- down_bias_grad: float32 [768], replicated
- first_scale_grad: float32 [768], replicated
- first_shift_grad: float32 [768], replicated
- second_scale_grad: float32 [768], replicated
- second_shift_grad: float32 [768], replicated
Inputs may be any that keep to these rules, and one draw needn't show every extreme that they name: `positions`: each row is a permutation of the ids 0 to 2047 made of runs of 64 ids that rise by one, each run starting at a multiple of 64.
All inputs are finite; a program needn't handle non-finite values.
Results may differ from a plain program's by a relative error of at most 0.0089.
Values may be sent and summed in bfloat16 or wider, within the bound.
No kernel may reach another device: no remote copies, remote signals or barrier semaphores. Data moves between devices by JAX's collectives and lax.ppermute only.
A program may use at most 128 MiB of HBM per device.

v0:
```python
import jax
import jax.numpy as jnp
from jax import lax
from jax.sharding import PartitionSpec as P

HEAD = 64
ROT = 16


def layer_norm(values, scales, offsets):
    average = jnp.mean(values, axis=-1, keepdims=True)
    centred = values - average
    spread = jnp.mean(centred * centred, axis=-1, keepdims=True)
    return centred * lax.rsqrt(spread + 1e-05) * scales + offsets


def rotate(values, places):
    halfway = ROT // 2
    inverse = 10000.0 ** (-2.0 * jnp.arange(halfway, dtype=jnp.float32) / ROT)
    angles = places.astype(jnp.float32)[..., None] * inverse
    cosine = jnp.cos(angles)[..., None, :]
    sine_part = jnp.sin(angles)[..., None, :]
    leading = values[..., :halfway]
    trailing = values[..., halfway:ROT]
    return jnp.concatenate(
        [
            leading * cosine - trailing * sine_part,
            trailing * cosine + leading * sine_part,
            values[..., ROT:],
        ],
        axis=-1,
    )


def exact_gelu(values):
    return jax.nn.gelu(values, approximate=False)


def score_block(query_part, key_part, query_ids, key_ids, factor):
    products = jnp.einsum("qhe,khe->hqk", query_part, key_part, preferred_element_type=jnp.float32)
    allowed = key_ids[None, :] <= query_ids[:, None]
    return jnp.where(allowed[None], products * factor, -1e30)


def shards(
    inputs,
    positions,
    query_key_value_weight,
    query_key_value_bias,
    attention_output_weight,
    attention_output_bias,
    up_projection_weight,
    up_projection_bias,
    down_projection_weight,
    down_projection_bias,
    first_scale,
    first_shift,
    second_scale,
    second_shift,
    cotangent,
):
    seq_count, block, width = inputs.shape
    length = positions.shape[1]
    local_width = query_key_value_weight.shape[2]
    heads_here = local_width // HEAD
    factor = HEAD ** (-0.5)
    row_count = seq_count * block
    start = lax.axis_index("ctx") * block
    query_places = lax.dynamic_slice_in_dim(positions, start, block, 1)
    flat = inputs.reshape(row_count, width).astype(jnp.float32)
    full_mix, full_out, full_up, full_down = (
        lax.all_gather(query_key_value_weight, "fsdp", axis=0, tiled=True),
        lax.all_gather(attention_output_weight, "fsdp", axis=1, tiled=True),
        lax.all_gather(up_projection_weight, "fsdp", axis=0, tiled=True),
        lax.all_gather(down_projection_weight, "fsdp", axis=1, tiled=True),
    )

    def norms(values, scale_one, shift_one, scale_two, shift_two):
        return (layer_norm(values, scale_one, shift_one), layer_norm(values, scale_two, shift_two))

    (first_norm, second_norm), norm_pull = jax.vjp(
        norms, flat, first_scale, first_shift, second_scale, second_shift
    )
    first_reduced = first_norm.astype(jnp.bfloat16)
    second_reduced = second_norm.astype(jnp.bfloat16)
    query_key_value_output = jnp.dot(
        first_reduced, full_mix.reshape(width, 3 * local_width), preferred_element_type=jnp.float32
    ) + query_key_value_bias.reshape(-1)
    pieces = query_key_value_output.reshape(seq_count, block, 3, heads_here, HEAD)

    def turn(query_pre, key_pre):
        return (rotate(query_pre, query_places), rotate(key_pre, query_places))

    (query_turned, key_turned), turn_pull = jax.vjp(turn, pieces[:, :, 0], pieces[:, :, 1])
    queries = query_turned.astype(jnp.bfloat16)
    own_keys = key_turned.astype(jnp.bfloat16).reshape(seq_count, block, local_width)
    own_values = pieces[:, :, 2].astype(jnp.bfloat16).reshape(seq_count, block, local_width)
    all_keys, all_values = (
        lax.all_gather(own_keys, "ctx", axis=1, tiled=True),
        lax.all_gather(own_values, "ctx", axis=1, tiled=True),
    )
    all_keys = all_keys.reshape(seq_count, length, heads_here, HEAD)
    all_values = all_values.reshape(seq_count, length, heads_here, HEAD)

    def attend(blocks_in):
        query_part, key_part, value_part, query_ids, key_ids = blocks_in
        scores = score_block(query_part, key_part, query_ids, key_ids, factor)
        highest_score = jnp.max(scores, axis=-1, keepdims=True)
        weights = jnp.exp(scores - highest_score)
        denominator = jnp.sum(weights, axis=-1, keepdims=True)
        probabilities = weights / denominator
        result = jnp.einsum(
            "hqk,khe->qhe",
            probabilities.astype(jnp.bfloat16),
            value_part,
            preferred_element_type=jnp.float32,
        )
        return (result, (highest_score + jnp.log(denominator))[..., 0])

    attention_result, log_totals = lax.map(
        attend, (queries, all_keys, all_values, query_places, positions)
    )
    attended_low = attention_result.astype(jnp.bfloat16).reshape(row_count, local_width)
    attention_branch = jnp.dot(attended_low, full_out, preferred_element_type=jnp.float32)
    up_preactivation = (
        jnp.dot(second_reduced, full_up, preferred_element_type=jnp.float32) + up_projection_bias
    )
    hidden_activation, gelu_pull = jax.vjp(exact_gelu, up_preactivation)
    act_low = hidden_activation.astype(jnp.bfloat16)
    feedforward_branch = jnp.dot(act_low, full_down, preferred_element_type=jnp.float32)
    branches = lax.psum(attention_branch + feedforward_branch, "tp")
    block_out = (flat + branches + attention_output_bias + down_projection_bias).reshape(
        seq_count, block, width
    )
    grad_rows = cotangent.reshape(row_count, width)
    bias_grad = jnp.sum(grad_rows, axis=0, dtype=jnp.float32)
    back_mix, back_out, back_up, back_down = (full_mix, full_out, full_up, full_down)
    act_grad = jnp.einsum("rd,fd->rf", grad_rows, back_down, preferred_element_type=jnp.float32)
    down_part = jnp.einsum("rf,rd->fd", act_low, grad_rows, preferred_element_type=jnp.float32)
    up_grad = gelu_pull(act_grad)[0].astype(jnp.bfloat16)
    up_bias_grad = jnp.sum(up_grad, axis=0, dtype=jnp.float32)
    up_part = jnp.einsum("rd,rf->df", second_reduced, up_grad, preferred_element_type=jnp.float32)
    second_grad = jnp.einsum("rf,df->rd", up_grad, back_up, preferred_element_type=jnp.float32)
    attended_grad = jnp.einsum(
        "rd,cd->rc", grad_rows, back_out, preferred_element_type=jnp.float32
    ).astype(jnp.bfloat16)
    out_part = jnp.einsum("rc,rd->cd", attended_low, grad_rows, preferred_element_type=jnp.float32)
    attended_grad = attended_grad.reshape(seq_count, block, heads_here, HEAD)

    def attend_back(blocks_in):
        query_part, key_part, value_part, query_ids, key_ids, log_total, out_grad = blocks_in
        scores = score_block(query_part, key_part, query_ids, key_ids, factor)
        probabilities = jnp.exp(scores - log_total[..., None])
        prob_grad = jnp.einsum(
            "qhe,khe->hqk", out_grad, value_part, preferred_element_type=jnp.float32
        )
        inner = jnp.sum(prob_grad * probabilities, axis=-1, keepdims=True)
        score_grad = (probabilities * (prob_grad - inner) * factor).astype(jnp.bfloat16)
        query_grad = jnp.einsum(
            "hqk,khe->qhe", score_grad, key_part, preferred_element_type=jnp.float32
        )
        key_grad = jnp.einsum(
            "hqk,qhe->khe", score_grad, query_part, preferred_element_type=jnp.float32
        )
        value_grad = jnp.einsum(
            "hqk,qhe->khe",
            probabilities.astype(jnp.bfloat16),
            out_grad,
            preferred_element_type=jnp.float32,
        )
        return (query_grad, key_grad, value_grad)

    query_grad, key_grads, value_grads = lax.map(
        attend_back,
        (queries, all_keys, all_values, query_places, positions, log_totals, attended_grad),
    )
    own_key_grad, own_value_grad = (
        lax.psum_scatter(
            key_grads.reshape(seq_count, length, local_width),
            "ctx",
            scatter_dimension=1,
            tiled=True,
        ),
        lax.psum_scatter(
            value_grads.reshape(seq_count, length, local_width),
            "ctx",
            scatter_dimension=1,
            tiled=True,
        ),
    )
    query_pre_grad, key_pre_grad = turn_pull(
        (query_grad, own_key_grad.reshape(seq_count, block, heads_here, HEAD))
    )
    mixed_grad = jnp.stack(
        [query_pre_grad, key_pre_grad, own_value_grad.reshape(seq_count, block, heads_here, HEAD)],
        axis=2,
    )
    mixed_grad = mixed_grad.reshape(row_count, 3 * local_width).astype(jnp.bfloat16)
    mix_bias_grad = jnp.sum(mixed_grad, axis=0, dtype=jnp.float32).reshape(3, local_width)
    mix_part = jnp.einsum(
        "rd,rc->dc", first_reduced, mixed_grad, preferred_element_type=jnp.float32
    ).reshape(width, 3, local_width)
    first_grad = jnp.einsum(
        "rc,dc->rd",
        mixed_grad,
        back_mix.reshape(width, 3 * local_width),
        preferred_element_type=jnp.float32,
    )
    first_grad, second_grad = lax.psum((first_grad, second_grad), "tp")
    flat_grad, scale_one_grad, shift_one_grad, scale_two_grad, shift_two_grad = norm_pull(
        (first_grad, second_grad)
    )
    inputs_grad = (grad_rows.astype(jnp.float32) + flat_grad).reshape(seq_count, block, width)
    owned = (
        lax.psum_scatter(mix_part, "fsdp", scatter_dimension=0, tiled=True),
        lax.psum_scatter(out_part, "fsdp", scatter_dimension=1, tiled=True),
        lax.psum_scatter(up_part, "fsdp", scatter_dimension=0, tiled=True),
        lax.psum_scatter(down_part, "fsdp", scatter_dimension=1, tiled=True),
    )
    mix_total, out_total, up_total, down_total = lax.psum(
        (owned[0], owned[1], owned[2], owned[3]), "ctx"
    )
    (
        mix_bias_total,
        up_bias_total,
        bias_total,
        scale_one_total,
        shift_one_total,
        scale_two_total,
        shift_two_total,
    ) = lax.psum(
        (
            mix_bias_grad,
            up_bias_grad,
            bias_grad,
            scale_one_grad,
            shift_one_grad,
            scale_two_grad,
            shift_two_grad,
        ),
        ("fsdp", "ctx"),
    )
    return (
        block_out,
        inputs_grad,
        mix_total,
        mix_bias_total,
        out_total,
        bias_total,
        up_total,
        up_bias_total,
        down_total,
        bias_total,
        scale_one_total,
        shift_one_total,
        scale_two_total,
        shift_two_total,
    )


def solution(mesh):
    in_specs = (
        P("fsdp", "ctx", None),
        P("fsdp", None),
        P("fsdp", None, "tp"),
        P(None, "tp"),
        P("tp", "fsdp"),
        P(),
        P("fsdp", "tp"),
        P("tp"),
        P("tp", "fsdp"),
        P(),
        P(),
        P(),
        P(),
        P(),
        P("fsdp", "ctx", None),
    )
    out_specs = (
        P("fsdp", "ctx", None),
        P("fsdp", "ctx", None),
        P("fsdp", None, "tp"),
        P(None, "tp"),
        P("tp", "fsdp"),
        P(),
        P("fsdp", "tp"),
        P("tp"),
        P("tp", "fsdp"),
        P(),
        P(),
        P(),
        P(),
        P(),
    )
    return jax.shard_map(shards, mesh=mesh, in_specs=in_specs, out_specs=out_specs, check_vma=False)
```

profile of v0, /device:TPU:0, one launch (start us, length us, event | category | flops | bytes accessed | tf_op | source)
XLA Modules:
  0.0 873.2 jit_solution(2727033944340339151)
XLA Ops:
  9.7 2.0 fusion.108
  12.3 13.8 %all_gather.18 = bf16[768,3,192]{0,2,1:T(8,128)(2,1)S(1)} all-gather(bf16[384,3,192]{0,2,1:T(8,128)(2,1)S(1)} %copy-done.27), channel_id=1, replica_groups=mesh['fsdp'=2,'ctx'=4,'tp'=4] {'fsdp'}, dimensions={0}, use_global_device_ids=true | all-gather | bytes 1327104 | tf_op jit(solution)/shard_map/all_gather | solution.py:72
  28.1 2.5 convolution_add_fusion.1
  30.6 3.3 reshape.301
  35.6 2.3 copy_bitcast_fusion
  46.7 5.8 all_gather.21
  54.2 25.6 %all-gather.7.cloned.1.call-done = bf16[2,2048,192]{1,2,0:T(8,128)(2,1)} async-done(((bf16[2,512,192]{1,2,0:T(8,128)(2,1)}), bf16[2,2048,192]{1,2,0:T(8,128)(2,1)}) %all-gather.7.cloned.1.call-update) | async-done | bytes 1572880 | tf_op jit(solution)/shard_map/all_gather | solution.py:99
  79.8 38.1 %all-gather.5.cloned.1.call-done = bf16[2,2048,192]{1,2,0:T(8,128)(2,1)} async-done(((bf16[2,512,192]{1,2,0:T(8,128)(2,1)}), bf16[2,2048,192]{1,2,0:T(8,128)(2,1)}) %all-gather.5.cloned.1.call-update) | async-done | bytes 1572880 | tf_op jit(solution)/shard_map/all_gather | solution.py:100
  118.0 45.0 %while.28 = (s32[]{:T(128)}, bf16[2,512,3,64]{1,3,2,0:T(8,128)(2,1)}, f32[2,3,512]{2,1,0:T(4,128)S(1)}, bf16[2,2048,3,64]{1,3,2,0:T(8,128)(2,1)}, s32[2,2048]{1,...) while((s32[]{:T(128)}, ...), condition=%wide.region_5.6_spmd.clone, body=%wide.region_2.5_spmd.sunk.clone | while | flops 844102144 | bytes 53635252 | solution.py:120
  118.7 7.3 fusion.206
  125.9 7.0 fusion.207
  133.0 6.7 fusion.208
  141.1 7.1 fusion.206
  148.3 7.2 fusion.207
  155.5 6.7 fusion.208
  163.0 140.2 %while.29 = (s32[]{:T(128)}, f32[2,512,3,64]{1,3,2,0:T(8,128)}, f32[2,2048,3,64]{1,3,2,0:T(8,128)}, f32[2,2048,3,64]{1,3,2,0:T(8,128)}, bf16[2,2048,3,64]{1,3,2,...) while((s32[]{:T(128)}, f32[2,512,3,64]{1,3,2,0:T(8,128)}, ...), condition=%wide.region_12.13_spmd.clone, body=%wide.region_10.12_spmd.sunk.clone | while | flops 2096110592 | bytes 164060336 | solution.py:173
  173.7 7.6 fusion.220
  181.3 6.4 fusion.219
  187.7 21.8 %fusion.222 = f32[2,2048,3,64]{1,3,2,0:T(8,128)} fusion(f32[2,2048,3,64]{1,3,2,0:T(8,128)} %get-tuple-element.443, s32[]{:T(128)} %get-tuple-element.441, f32[3,512,2048]{2,1,0:T(8,128)} %fusion.219, f32[3,512,2048]{2,1,0:T(8,128)} %fusion.220, f32[3,512]{1,0:T(4,128)S(1)} %dynamic-slice_bitcast_fusion.3, ...), kind=kOutput, calls=%fused_computation.44.clone.1.clone | convolution fusion | flops 437259776 | bytes 54215680 | tf_op jit(solution)/shard_map/while/body/eval_jaxpr/hqk,qhe->khe/dot_general | solution.py:162
  209.5 20.8 %fusion.221 = f32[2,512,3,64]{1,3,2,0:T(8,128)} fusion(f32[2,512,3,64]{1,3,2,0:T(8,128)} %get-tuple-element.442, s32[]{:T(128)} %get-tuple-element.441, f32[3,512,2048]{2,1,0:T(8,128)} %fusion.219, f32[3,512,2048]{2,1,0:T(8,128)} %fusion.220, f32[3,512]{1,0:T(4,128)S(1)} %dynamic-slice_bitcast_fusion.3, ...), kind=kOutput, calls=%fused_computation.47.clone.1.clone | convolution fusion | flops 437259776 | bytes 53625856 | tf_op jit(solution)/shard_map/while/body/eval_jaxpr/hqk,khe->qhe/dot_general | solution.py:159
  230.2 7.7 fusion.223
  238.6 7.6 fusion.220
  246.2 6.4 fusion.219
  252.6 21.8 %fusion.222 = f32[2,2048,3,64]{1,3,2,0:T(8,128)} fusion(f32[2,2048,3,64]{1,3,2,0:T(8,128)} %get-tuple-element.443, s32[]{:T(128)} %get-tuple-element.441, f32[3,512,2048]{2,1,0:T(8,128)} %fusion.219, f32[3,512,2048]{2,1,0:T(8,128)} %fusion.220, f32[3,512]{1,0:T(4,128)S(1)} %dynamic-slice_bitcast_fusion.3, ...), kind=kOutput, calls=%fused_computation.44.clone.1.clone | convolution fusion | flops 437259776 | bytes 54215680 | tf_op jit(solution)/shard_map/while/body/eval_jaxpr/hqk,qhe->khe/dot_general | solution.py:162
  274.4 20.8 %fusion.221 = f32[2,512,3,64]{1,3,2,0:T(8,128)} fusion(f32[2,512,3,64]{1,3,2,0:T(8,128)} %get-tuple-element.442, s32[]{:T(128)} %get-tuple-element.441, f32[3,512,2048]{2,1,0:T(8,128)} %fusion.219, f32[3,512,2048]{2,1,0:T(8,128)} %fusion.220, f32[3,512]{1,0:T(4,128)S(1)} %dynamic-slice_bitcast_fusion.3, ...), kind=kOutput, calls=%fused_computation.47.clone.1.clone | convolution fusion | flops 437259776 | bytes 53625856 | tf_op jit(solution)/shard_map/while/body/eval_jaxpr/hqk,khe->qhe/dot_general | solution.py:159
  295.2 7.6 fusion.223
  306.4 5.0 fusion.135
  313.4 12.2 %convert_reduce_fusion.1 = (f32[768]{0:T(1024)}, bf16[1024,768]{1,0:T(8,128)(2,1)}, f32[1024,768]{1,0:T(8,128)S(1)}) fusion(f32[1024,768]{1,0:T(8,128)} %fusion.135, f32[768]{0:T(1024)} %param.26, bf16[1024,768]{1,0:T(8,128)(2,1)S(1)} %bitcast.244, bf16[768,768]{1,0:T(8,128)(2,1)} %all-gather.11.cloned.1.call-done), kind=kOutput, calls=%fused_computation.110 | convolution fusion | flops 1266941184 | bytes 10622976 | tf_op jit(solution)/shard_map/rd,fd->rf/dot_general | solution.py:138
  327.2 2.8 fusion.142
  330.1 4.7 fusion.141
  337.0 25.6 %reduce-scatter.7.cloned.1.call-done = f32[2,512,192]{1,2,0:T(8,128)} async-done(((f32[2,2048,192]{1,2,0:T(8,128)}), f32[2,512,192]{1,2,0:T(8,128)}) %reduce-scatter.7.cloned.1.call-update) | async-done | bytes 786448 | tf_op jit(solution)/shard_map/reduce_scatter | solution.py:178
  367.5 57.6 %reduce-scatter.9.cloned.1.call-done = f32[2,512,192]{1,2,0:T(8,128)} async-done(((f32[2,2048,192]{1,2,0:T(8,128)}), f32[2,512,192]{1,2,0:T(8,128)}) %reduce-scatter.9.cloned.1.call-update) | async-done | bytes 786448 | tf_op jit(solution)/shard_map/reduce_scatter | solution.py:184
  425.0 2.3 convert_reduce_fusion.3
  429.9 2.4 fusion.139
  432.3 3.5 fusion.136
  435.8 3.1 fusion.137
  438.9 2.3 convolution_add_fusion
  441.2 3.1 fusion.138
  444.4 35.3 %reduce-scatter.17.cloned.1.call-done = f32[768,384]{1,0:T(8,128)} async-done(((f32[768,768]{1,0:T(8,128)}), f32[768,384]{1,0:T(8,128)}) %reduce-scatter.17.cloned.1.call-update) | async-done | bytes 1179664 | tf_op jit(solution)/shard_map/reduce_scatter | solution.py:218
  479.7 37.0 %reduce-scatter.15.cloned.1.call-done = f32[384,768]{1,0:T(8,128)} async-done(((f32[768,768]{1,0:T(8,128)}), f32[384,768]{1,0:T(8,128)}) %reduce-scatter.15.cloned.1.call-update) | async-done | bytes 1179664 | tf_op jit(solution)/shard_map/reduce_scatter | solution.py:217
  516.7 30.5 %reduce-scatter.11.cloned.1.call-done = f32[384,3,192]{0,2,1:T(8,128)} async-done(((f32[768,3,192]{0,2,1:T(8,128)}), f32[384,3,192]{0,2,1:T(8,128)}) %reduce-scatter.11.cloned.1.call-update) | async-done | bytes 884752 | tf_op jit(solution)/shard_map/reduce_scatter | solution.py:215
  547.6 173.5 %all-reduce.12.cloned.1.call-done = (f32[1024,768]{1,0:T(8,128)}, f32[1024,768]{1,0:T(8,128)}, f32[1024,768]{1,0:T(8,128)}) async-done(((f32[1024,768]{1,0:T(8,128)}, f32[1024,768]{1,0:T(8,128)}, f32[1024,768]{1,0:T(8,128)}), (f32[1024,768]{1,0:T(8,128)}, f32[1024,768]{1,0:T(8,128)}, f32[1024,768]{1,0:T(8,128)})) %all-reduce.12.cloned.1.call-update) | async-done | bytes 9437200 | tf_op jit(solution)/shard_map/psum | solution.py:131
  721.1 4.3 fusion.131
  725.8 2.7 fusion.115
  728.5 39.9 %all-reduce.6 = (f32[3,192]{1,0:T(4,128)}, f32[768]{0:T(1024)S(1)}, f32[768]{0:T(1024)}, f32[768]{0:T(1024)}, f32[768]{0:T(1024)}, /*index=5*/f32[768]{0:T(1024)}, f32[768]{0:T(1024)}) all-reduce(f32[3,192]{1,0:T(4,128)S(1)} %reshape.312, f32[768]{0:T(1024)S(1)} %convert_reduce_fusion.2, ...), channel_id=1, replica_groups=mesh['fsdp'=2,'ctx'=4,'tp'=4] {'fsdp','ctx'}, use_global_device_ids=true, to_apply=%region_21.22 | all-reduce | flops 5184 | bytes 41472 | tf_op jit(solution)/shard_map/psum | solution.py:231
  768.4 6.7 add_add_fusion.2
  775.1 84.5 %all-reduce.14.cloned.1.call-done = (f32[384,3,192]{0,2,1:T(8,128)}, f32[192,384]{1,0:T(8,128)}, f32[384,768]{1,0:T(8,128)}, f32[768,384]{1,0:T(8,128)}) async-done(((f32[384,3,192]{0,2,1:T(8,128)}, f32[192,384]{1,0:T(8,128)}, f32[384,768]{1,0:T(8,128)}, f32[768,384]{1,0:T(8,128)}), (f32[384,3,192]{0,2,1:T(8,128)}, f32[192,384]{1,0:T(8,128)}, f32[384,768]{1,0:T(8,128)}, ...) | async-done | bytes 3538960 | tf_op jit(solution)/shard_map/psum | solution.py:220
  860.2 2.2 copy.84
  (195 shorter events, 42.7 us)
Async XLA Ops:
  7.2 19.0 %copy-start = (bf16[2,512,768]{2,1,0:T(8,128)(2,1)S(1)}, bf16[2,512,768]{2,1,0:T(8,128)(2,1)}, u32[]{:S(2)}) copy-start(bf16[2,512,768]{2,1,0:T(8,128)(2,1)} %param.19) | copy-start | bytes 4718596
  7.2 5.1 copy-start.27
  7.2 18.9 %copy-start.43 = (f32[3,192]{1,0:T(4,128)S(1)}, f32[3,192]{1,0:T(4,128)}, u32[]{:S(2)}) copy-start(f32[3,192]{1,0:T(4,128)} %param.22) | copy-start | bytes 6916
  7.2 19.0 %copy-start.31 = (f32[768]{0:T(1024)S(1)}, f32[768]{0:T(1024)}, u32[]{:S(2)}) copy-start(f32[768]{0:T(1024)} %param.29) | copy-start | bytes 9220
  7.2 19.0 %copy-start.38 = (f32[768]{0:T(1024)S(1)}, f32[768]{0:T(1024)}, u32[]{:S(2)}) copy-start(f32[768]{0:T(1024)} %param.30) | copy-start | bytes 9220
  7.2 72.6 %all-gather.7.cloned.1.call-start = ((), (), s32[]{:S(2)}) async-start(), calls=%async_computation.7 | async-start | bytes 1966080 | tf_op jit(solution)/shard_map/all_gather | solution.py:99
  34.0 4.0 copy-start.9
  34.0 4.9 copy-start.26
  38.9 7.8 copy-start.30
  39.1 13.4 %copy-start.28 = (f32[2,512,8]{1,2,0:T(8,128)}, f32[2,512,8]{1,2,0:T(8,128)S(1)}, u32[]{:S(2)}) copy-start(f32[2,512,8]{1,2,0:T(8,128)S(1)} %get-tuple-element.232) | copy-start | bytes 98308
  39.1 13.4 %copy-start.29 = (f32[2,512,8]{1,2,0:T(8,128)}, f32[2,512,8]{1,2,0:T(8,128)S(1)}, u32[]{:S(2)}) copy-start(f32[2,512,8]{1,2,0:T(8,128)S(1)} %get-tuple-element.233) | copy-start | bytes 98308
  39.1 14.1 %copy-start.4 = (bf16[2,512,768]{2,1,0:T(8,128)(2,1)S(1)}, bf16[2,512,768]{2,1,0:T(8,128)(2,1)}, u32[]{:S(2)}) copy-start(bf16[2,512,768]{2,1,0:T(8,128)(2,1)} %param.33) | copy-start | bytes 4718596
  41.1 76.8 %all-gather.5.cloned.1.call-start = ((), (), s32[]{:S(2)}) async-start(), calls=%async_computation.6 | async-start | bytes 1966080 | tf_op jit(solution)/shard_map/all_gather | solution.py:100
  43.4 263.0 %all-gather.9.cloned.1.call-start = ((), (), s32[]{:S(2)}) async-start(), calls=%async_computation.8 | async-start | bytes 1769472 | tf_op jit(solution)/shard_map/all_gather | solution.py:74
  44.2 269.2 %all-gather.11.cloned.1.call-start = ((), (), s32[]{:S(2)}) async-start(), calls=%async_computation.9 | async-start | bytes 1769472 | tf_op jit(solution)/shard_map/all_gather | solution.py:75
  44.7 317.8 %reduce-scatter.7.cloned.1.call-start = ((), (), s32[]{:S(2)}) async-start(), calls=%async_computation.10 | async-start | bytes 3932160 | tf_op jit(solution)/shard_map/reduce_scatter | solution.py:178
  125.9 7.1 copy-start.7
  125.9 7.1 copy-start.15
  148.3 7.2 copy-start.7
  148.3 7.2 copy-start.15
  173.7 7.6 copy-start.8
  187.7 21.8 %copy-start.6 = (bf16[2,2048,3,64]{1,3,2,0:T(8,128)(2,1)S(1)}, bf16[2,2048,3,64]{1,3,2,0:T(8,128)(2,1)}, u32[]{:S(2)}) copy-start(bf16[2,2048,3,64]{1,3,2,0:T(8,128)(2,1)} %get-tuple-element.456) | copy-start | bytes 4718596 | tf_op jit(solution)/shard_map/while
  238.6 7.6 copy-start.8
  252.6 21.8 %copy-start.6 = (bf16[2,2048,3,64]{1,3,2,0:T(8,128)(2,1)S(1)}, bf16[2,2048,3,64]{1,3,2,0:T(8,128)(2,1)}, u32[]{:S(2)}) copy-start(bf16[2,2048,3,64]{1,3,2,0:T(8,128)(2,1)} %get-tuple-element.456) | copy-start | bytes 4718596 | tf_op jit(solution)/shard_map/while
  303.3 121.8 %reduce-scatter.9.cloned.1.call-start = ((), (), s32[]{:S(2)}) async-start(), calls=%async_computation.11 | async-start | bytes 3932160 | tf_op jit(solution)/shard_map/reduce_scatter | solution.py:184
  303.8 140.6 %reduce-scatter.13.cloned.1.call-start = ((), (), s32[]{:S(2)}) async-start(), calls=%async_computation.13 | async-start | bytes 884736 | tf_op jit(solution)/shard_map/reduce_scatter | solution.py:216
  306.4 5.0 copy-start.17
  306.4 5.5 copy-start.5
  313.3 166.4 %reduce-scatter.17.cloned.1.call-start = ((), (), s32[]{:S(2)}) async-start(), calls=%async_computation.15 | async-start | bytes 3538944 | tf_op jit(solution)/shard_map/reduce_scatter | solution.py:218
  313.3 12.3 %copy-start.10 = (f32[1024,768]{1,0:T(8,128)S(1)}, f32[1024,768]{1,0:T(8,128)}, u32[]{:S(2)}) copy-start(f32[1024,768]{1,0:T(8,128)} %fusion.135) | copy-start | bytes 9437188
  313.3 12.3 %copy-start.37 = (f32[768]{0:T(1024)S(1)}, f32[768]{0:T(1024)}, u32[]{:S(2)}) copy-start(f32[768]{0:T(1024)} %param.26) | copy-start | bytes 9220
  330.0 186.7 %reduce-scatter.15.cloned.1.call-start = ((), (), s32[]{:S(2)}) async-start(), calls=%async_computation.14 | async-start | bytes 3538944 | tf_op jit(solution)/shard_map/reduce_scatter | solution.py:217
  334.8 212.3 %reduce-scatter.11.cloned.1.call-start = ((), (), s32[]{:S(2)}) async-start(), calls=%async_computation.12 | async-start | bytes 2654208 | tf_op jit(solution)/shard_map/reduce_scatter | solution.py:215
  425.0 4.8 copy-start.14
  432.3 288.8 %all-reduce.12.cloned.1.call-start = ((), (), s32[]{:S(2)}) async-start(), calls=%async_computation.16 | async-start | bytes 18874368 | tf_op jit(solution)/shard_map/psum | solution.py:131
  432.3 3.5 copy-start.45
  432.3 3.5 copy-start.46
  435.8 3.1 copy-start.23
  444.3 103.1 %copy-start.34 = (f32[3,3,64]{2,1,0:T(4,128)S(1)}, f32[3,3,64]{2,1,0:T(4,128)}, u32[]{:S(2)}) copy-start(f32[3,3,64]{2,1,0:T(4,128)} %get-tuple-element.208) | copy-start | bytes 6916
  444.4 276.7 %copy-start.32 = (f32[768]{0:T(1024)S(1)}, f32[768]{0:T(1024)}, u32[]{:S(2)}) copy-start(f32[768]{0:T(1024)} %param.29) | copy-start | bytes 9220
  444.4 415.2 %all-reduce.14.cloned.1.call-start = ((), (), s32[]{:S(2)}) async-start(), calls=%async_computation.17 | async-start | bytes 7077888 | tf_op jit(solution)/shard_map/psum | solution.py:220
  721.1 4.3 copy-start.2
  721.1 4.7 copy-start.3
  725.8 42.7 %copy-start.40 = (f32[768]{0:T(1024)S(1)}, f32[768]{0:T(1024)}, u32[]{:S(2)}) copy-start(f32[768]{0:T(1024)} %param.28) | copy-start | bytes 9220
  725.8 42.7 %copy-start.41 = (f32[768]{0:T(1024)S(1)}, f32[768]{0:T(1024)}, u32[]{:S(2)}) copy-start(f32[768]{0:T(1024)} %param.24) | copy-start | bytes 9220
  768.4 91.2 %copy-start.44 = (f32[768]{0:T(1024)}, f32[768]{0:T(1024)S(1)}, u32[]{:S(2)}) copy-start(f32[768]{0:T(1024)S(1)} %get-tuple-element.496) | copy-start | bytes 9220
  859.6 4.5 copy-start.19
  859.6 5.6 copy-start.18
  (16 other events, 20.4 us)
Sparse Core Ops, SparseCore 0:
  41.3 38.5 all-gather.6
  82.0 35.9 all-gather.4
  119.5 21.6 all-gather.8
  142.6 22.7 all-gather.10
  303.4 59.1 reduce-scatter.6
  364.7 60.2 reduce-scatter.8
  427.3 15.2 reduce-scatter.12
  445.0 34.6 reduce-scatter.16
  482.0 34.7 reduce-scatter.14
  518.9 28.2 reduce-scatter.10
  550.5 170.5 all-reduce.11
  723.5 136.0 all-reduce.13
where the time goes:
time: 877 us; the launch traced here: 873 us
  waiting for transfers between devices  509 us (58%)
  matrix products  200 us (23%)
  blocking collectives  59.5 us (7%)
  other arithmetic  47.8 us (5%)
  local copies, waits for them, and re-layouts  30.4 us (3%)
  between operations  14.9 us (2%)
  loops' own time  10.6 us (1%)
    psum x1, waiting for transfers between devices, shards(): branches = lax.psum(attention_branch + feedforward_branch, 'tp')  173 us
    psum x1, waiting for transfers between devices, shards(): lax.psum((owned[0], owned[1], owned[2], owned[3]), 'ctx')  84.5 us
    reduce_scatter x1, waiting for transfers between devices, shards(): lax.psum_scatter(value_grads.reshape(seq_count, length, local_width), 'ct...  57.6 us
    dot_general x2, matrix products, attend_back(): jnp.einsum('hqk,qhe->khe', score_grad, query_part, preferred_element_type...  43.7 us
    dot_general x2, matrix products, attend_back(): jnp.einsum('hqk,khe->qhe', score_grad, key_part, preferred_element_type=j...  41.5 us
    psum x1, blocking collectives, shards(): lax.psum((mix_bias_grad, up_bias_grad, bias_grad, scale_one_grad, shift_o...  39.9 us
    all_gather x1, waiting for transfers between devices, shards(): lax.all_gather(own_values, 'ctx', axis=1, tiled=True)  38.1 us
    reduce_scatter x1, waiting for transfers between devices, shards(): lax.psum_scatter(up_part, 'fsdp', scatter_dimension=0, tiled=True)  37 us
  transfers between devices with their start and end apart: 12, of which 9 were waited for; matrix products, arithmetic and copies ran while one was open for 28% of the time, Pallas kernels for 0%

commit v1 on v0

v1 whole, which is shorter than its diff:
```python
import functools

import jax
import jax.numpy as jnp
from jax import lax
from jax.experimental import pallas as pl
from jax.experimental.pallas import tpu as pltpu
from jax.sharding import PartitionSpec as P

HEAD = 64
ROT = 16
HALF = ROT // 2
EPS = 1e-5
NEG = -1e30
F32 = jnp.float32
BF16 = jnp.bfloat16
MIB = 1024 * 1024


def mm(a, b, ca=1, cb=0):
    return lax.dot_general(a, b, (((ca,), (cb,)), ((), ())), preferred_element_type=F32)


def params(mib):
    return pltpu.CompilerParams(vmem_limit_bytes=mib * MIB)


def xhat_of(x):
    width = x.shape[-1]
    centred = x - jnp.sum(x, axis=-1, keepdims=True) * (1.0 / width)
    spread = jnp.sum(centred * centred, axis=-1, keepdims=True) * (1.0 / width)
    inv = lax.rsqrt(spread + EPS)
    return centred * inv, inv


def prep_kernel(own, *refs):
    if own:
        (x_ref, cos_ref, sin_ref, w_ref, b_ref, s1_ref, b1_ref, s2_ref, b2_ref,
         n1_ref, k_ref, v_ref, q_ref, n2_ref) = refs
    else:
        x_ref, cos_ref, sin_ref, w_ref, b_ref, s1_ref, b1_ref, n1_ref, k_ref, v_ref = refs
    xhat, _ = xhat_of(x_ref[...].astype(F32))
    n1 = (xhat * s1_ref[...] + b1_ref[...]).astype(BF16)
    n1_ref[...] = n1
    if own:
        n2_ref[...] = (xhat * s2_ref[...] + b2_ref[...]).astype(BF16)
    mixed = mm(w_ref[...], n1, 1, 1) + b_ref[...]
    cosine, sine = cos_ref[...], sin_ref[...]
    wide = k_ref.shape[0]

    def rotated(ref, base, factor):
        for h in range(0, wide, HEAD):
            a = mixed[base + h : base + h + HALF]
            b = mixed[base + h + HALF : base + h + ROT]
            turned = jnp.concatenate([a * cosine - b * sine, b * cosine + a * sine], axis=0)
            ref[h : h + ROT, :] = turned.astype(BF16) * factor
            ref[h + ROT : h + HEAD, :] = (
                mixed[base + h + ROT : base + h + HEAD].astype(BF16) * factor
            )

    at = 0
    if own:
        rotated(q_ref, 0, BF16(HEAD**-0.5))
        at = wide
    rotated(k_ref, at, BF16(1.0))
    v_ref[...] = mixed[at + wide : at + 2 * wide].astype(BF16)


def prep(own, x, cosine, sine, wt, bias, norm_params):
    rows, width = x.shape
    tall = wt.shape[0]
    wide = tall // 3 if own else tall // 2
    step = 256
    row = pl.BlockSpec((step, width), lambda i: (i, 0))
    trig = pl.BlockSpec((HALF, step), lambda i: (0, i))
    col = pl.BlockSpec((wide, step), lambda i: (0, i))
    vec = pl.BlockSpec((1, width), lambda i: (0, 0))
    out_specs = [row, col, col] + ([col, row] if own else [])
    low_rows = jax.ShapeDtypeStruct((rows, width), BF16)
    low_cols = jax.ShapeDtypeStruct((wide, rows), BF16)
    out_shape = [low_rows, low_cols, low_cols] + ([low_cols, low_rows] if own else [])
    return pl.pallas_call(
        functools.partial(prep_kernel, own),
        grid=(rows // step,),
        in_specs=[row, trig, trig, pl.BlockSpec((tall, width), lambda i: (0, 0)),
                  pl.BlockSpec((tall, 1), lambda i: (0, 0))] + [vec] * len(norm_params),
        out_specs=out_specs,
        out_shape=out_shape,
        compiler_params=params(24),
        cost_estimate=pl.CostEstimate(
            flops=2 * rows * width * tall, bytes_accessed=rows * width * 8, transcendentals=0
        ),
    )(x, cosine, sine, wt, bias, *norm_params)


def attention_kernel(chunk, q_ref, do_ref, ko_ref, kx_ref, vo_ref, vx_ref, kpos_ref, qpos_ref,
                     qcos_ref, qsin_ref, kcos_ref, ksin_ref, o_ref, dq_ref, dk_ref, dv_ref,
                     kn, vn, kt, vt, dk, dv, es, dps):
    i = pl.program_id(1)
    half = ko_ref.shape[1]
    length = 2 * half
    steps = length // chunk

    @pl.when(i == 0)
    def _():
        kt[:, :half] = ko_ref[...]
        kt[:, half:] = kx_ref[...]
        vt[:, :half] = vo_ref[...]
        vt[:, half:] = vx_ref[...]
        kn[:half, :] = ko_ref[...].T
        kn[half:, :] = kx_ref[...].T
        vn[:half, :] = vo_ref[...].T
        vn[half:, :] = vx_ref[...].T
        dk[...] = jnp.zeros_like(dk)
        dv[...] = jnp.zeros_like(dv)

    qt = q_ref[...]
    dot = do_ref[...]
    qn = qt.T
    don = dot.T
    qpos = qpos_ref[...]
    lanes = qt.shape[1]
    fold = (chunk // 8, 8, lanes)

    top = jnp.full((8, lanes), NEG, F32)
    for j in range(steps):
        here = slice(j * chunk, (j + 1) * chunk)
        s = mm(kn[here, :], qt)
        s = jnp.where(kpos_ref[here, :] <= qpos, s, NEG)
        es[here, :] = s
        top = jnp.maximum(top, jnp.max(s.reshape(fold), axis=0))
    top = jnp.max(top, axis=0, keepdims=True)

    total = jnp.zeros((8, lanes), F32)
    inner = jnp.zeros((8, lanes), F32)
    for j in range(steps):
        here = slice(j * chunk, (j + 1) * chunk)
        e = jnp.exp(es[here, :] - top)
        dp = mm(vn[here, :], dot)
        es[here, :] = e
        dps[here, :] = dp
        total = total + jnp.sum(e.reshape(fold), axis=0)
        inner = inner + jnp.sum((e * dp).reshape(fold), axis=0)
    share = 1.0 / jnp.sum(total, axis=0, keepdims=True)
    inner = jnp.sum(inner, axis=0, keepdims=True) * share

    ot = jnp.zeros((HEAD, lanes), F32)
    dqt = jnp.zeros((HEAD, lanes), F32)
    for j in range(steps):
        here = slice(j * chunk, (j + 1) * chunk)
        p = es[here, :] * share
        ds = (p * (dps[here, :] - inner)).astype(BF16)
        p = p.astype(BF16)
        dv[here, :] += mm(p, don)
        dk[here, :] += mm(ds, qn)
        ot = ot + mm(vt[:, here], p)
        dqt = dqt + mm(kt[:, here], ds)
    o_ref[...] = ot.astype(BF16)

    def unrotated(ref, grad, cosine, sine):
        a, b = grad[:HALF], grad[HALF:ROT]
        ref[:ROT, :] = jnp.concatenate(
            [a * cosine + b * sine, b * cosine - a * sine], axis=0
        ).astype(BF16)
        ref[ROT:, :] = grad[ROT:].astype(BF16)

    unrotated(dq_ref, dqt * (HEAD**-0.5), qcos_ref[...], qsin_ref[...])

    @pl.when(i == pl.num_programs(1) - 1)
    def _():
        unrotated(dk_ref, dk[...].T, kcos_ref[...], ksin_ref[...])
        dv_ref[...] = dv[...].T.astype(BF16)


def attention(qt, dot, ko, kx, vo, vx, kpos, qpos, qcos, qsin, kcos, ksin):
    wide, rows = qt.shape
    half = ko.shape[1]
    length = 2 * half
    lanes, chunk = 256, 256
    heads = wide // HEAD
    q_spec = pl.BlockSpec((HEAD, lanes), lambda h, i: (h, i))
    k_spec = pl.BlockSpec((HEAD, half), lambda h, i: (h, 0))
    whole = pl.BlockSpec((HEAD, length), lambda h, i: (h, 0))
    trig_q = pl.BlockSpec((HALF, lanes), lambda h, i: (0, i))
    trig_k = pl.BlockSpec((HALF, length), lambda h, i: (0, 0))
    return pl.pallas_call(
        functools.partial(attention_kernel, chunk),
        grid=(heads, rows // lanes),
        in_specs=[q_spec, q_spec, k_spec, k_spec, k_spec, k_spec,
                  pl.BlockSpec((length, 1), lambda h, i: (0, 0)),
                  pl.BlockSpec((1, lanes), lambda h, i: (0, i)),
                  trig_q, trig_q, trig_k, trig_k],
        out_specs=[q_spec, q_spec, whole, whole],
        out_shape=[jax.ShapeDtypeStruct((wide, rows), BF16)] * 2
        + [jax.ShapeDtypeStruct((wide, length), BF16)] * 2,
        scratch_shapes=[
            pltpu.VMEM((length, HEAD), BF16),
            pltpu.VMEM((length, HEAD), BF16),
            pltpu.VMEM((HEAD, length), BF16),
            pltpu.VMEM((HEAD, length), BF16),
            pltpu.VMEM((length, HEAD), F32),
            pltpu.VMEM((length, HEAD), F32),
            pltpu.VMEM((length, lanes), F32),
            pltpu.VMEM((length, lanes), F32),
        ],
        compiler_params=params(32),
        cost_estimate=pl.CostEstimate(
            flops=40 * rows * length * wide, bytes_accessed=16 * wide * length,
            transcendentals=heads * rows * length,
        ),
    )(qt, dot, ko, kx, vo, vx, kpos, qpos, qcos, qsin, kcos, ksin)


def forward_kernel(n2_ref, g_ref, x_ref, up_ref, bias_ref, down_ref, s2_ref,
                   ff_ref, a_ref, up_part, down_part, small_ref):
    i = pl.program_id(0)

    @pl.when(i == 0)
    def _():
        up_part[...] = jnp.zeros_like(up_part)
        down_part[...] = jnp.zeros_like(down_part)
        small_ref[...] = jnp.zeros_like(small_ref)

    n2, g = n2_ref[...], g_ref[...]
    up = mm(n2, up_ref[...]) + bias_ref[...]
    cdf = 0.5 + 0.5 * lax.erf(up * (0.5**0.5))
    act = (up * cdf).astype(BF16)
    slope = cdf + up * (jnp.exp(up * up * -0.5) * 0.3989422804014327)
    up_grad_f = mm(g, down_ref[...], 1, 1) * slope
    up_grad = up_grad_f.astype(BF16)
    ff_ref[...] = mm(act, down_ref[...])
    second = mm(up_grad, up_ref[...], 1, 1)
    up_part[...] += mm(n2, up_grad, 0, 0)
    down_part[...] += mm(act, g, 0, 0)
    xhat, _ = xhat_of(x_ref[...].astype(F32))
    a_ref[...] = second * s2_ref[...]
    small_ref[0:1, :] += jnp.sum(up_grad.astype(F32), axis=0, keepdims=True)
    small_ref[1:2, :] += jnp.sum(g.astype(F32), axis=0, keepdims=True)
    small_ref[2:3, :] += jnp.sum(second * xhat, axis=0, keepdims=True)
    small_ref[3:4, :] += jnp.sum(second, axis=0, keepdims=True)


def feed_forward(n2, g, x, up, bias, down, scale):
    rows, width = x.shape
    hidden = up.shape[1]
    step = 256
    row = pl.BlockSpec((step, width), lambda i: (i, 0))

    def fixed(*shape):
        return pl.BlockSpec(shape, lambda i: (0, 0))

    return pl.pallas_call(
        forward_kernel,
        grid=(rows // step,),
        in_specs=[row, row, row, fixed(width, hidden), fixed(1, hidden), fixed(hidden, width),
                  fixed(1, width)],
        out_specs=[row, row, fixed(width, hidden), fixed(hidden, width), fixed(8, width)],
        out_shape=[jax.ShapeDtypeStruct((rows, width), F32)] * 2
        + [jax.ShapeDtypeStruct((width, hidden), F32), jax.ShapeDtypeStruct((hidden, width), F32),
           jax.ShapeDtypeStruct((8, width), F32)],
        compiler_params=params(40),
        cost_estimate=pl.CostEstimate(
            flops=12 * rows * width * hidden, bytes_accessed=16 * MIB, transcendentals=0
        ),
    )(n2, g, x, up, bias, down, scale)


def back_kernel(own, *refs):
    if own:
        (dq_ref, dk_ref, dv_ref, n1_ref, x_ref, w_ref, s1_ref, a2_ref,
         a_ref, part_ref, small_ref, bias_ref) = refs
        grads = [dq_ref[...], dk_ref[...], dv_ref[...]]
    else:
        (dk_ref, dv_ref, n1_ref, x_ref, w_ref, s1_ref, a_ref, part_ref, small_ref, bias_ref) = refs
        grads = [dk_ref[...], dv_ref[...]]

    @pl.when(pl.program_id(0) == 0)
    def _():
        part_ref[...] = jnp.zeros_like(part_ref)
        small_ref[...] = jnp.zeros_like(small_ref)
        bias_ref[...] = jnp.zeros_like(bias_ref)

    grad = jnp.concatenate(grads, axis=0)
    part_ref[...] += mm(grad, n1_ref[...])
    bias_ref[...] += jnp.sum(grad.astype(F32), axis=1, keepdims=True)
    first = mm(grad, w_ref[...], 0, 0)
    xhat, _ = xhat_of(x_ref[...].astype(F32))
    a = first * s1_ref[...]
    if own:
        a = a + a2_ref[...]
    a_ref[...] = a.astype(BF16)
    small_ref[0:1, :] += jnp.sum(first * xhat, axis=0, keepdims=True)
    small_ref[1:2, :] += jnp.sum(first, axis=0, keepdims=True)


def back(own, grads, offset, n1, x, wt, scale, extra):
    rows, width = x.shape
    tall = wt.shape[0]
    step = 256
    wide = tall // len(grads)
    row = pl.BlockSpec((step, width), lambda i: (i, 0))
    shift = offset // step
    cols = [pl.BlockSpec((wide, step), lambda i: (0, i))] * (len(grads) - 2)
    cols += [pl.BlockSpec((wide, step), lambda i: (0, i + shift))] * 2

    def fixed(*shape):
        return pl.BlockSpec(shape, lambda i: (0, 0))

    return pl.pallas_call(
        functools.partial(back_kernel, own),
        grid=(rows // step,),
        in_specs=cols + [row, row, fixed(tall, width), fixed(1, width)] + [row] * len(extra),
        out_specs=[row, fixed(tall, width), fixed(8, width), fixed(tall, 1)],
        out_shape=[jax.ShapeDtypeStruct((rows, width), BF16),
                   jax.ShapeDtypeStruct((tall, width), F32),
                   jax.ShapeDtypeStruct((8, width), F32),
                   jax.ShapeDtypeStruct((tall, 1), F32)],
        compiler_params=params(24),
        cost_estimate=pl.CostEstimate(
            flops=4 * rows * width * tall, bytes_accessed=8 * MIB, transcendentals=0
        ),
    )(*grads, n1, x, wt, scale, *extra)


def swap(v, axis, size, distance):
    return lax.ppermute(v, axis, [(i, i ^ distance) for i in range(size)])


def by_xor(pieces, index):
    low, high = (index & 1) == 1, (index & 2) == 2
    a, b, c, d = pieces
    a, b, c, d = (jnp.where(low, b, a), jnp.where(low, a, b),
                  jnp.where(low, d, c), jnp.where(low, c, d))
    return (jnp.where(high, c, a), jnp.where(high, d, b),
            jnp.where(high, a, c), jnp.where(high, b, d))


def gather_rows(shard, axis_name, size, mine, dim):
    if size != 2:
        return lax.all_gather(shard, axis_name, axis=dim, tiled=True)
    other = swap(shard, axis_name, 2, 1)
    first = mine == 0
    return jnp.concatenate(
        [jnp.where(first, shard, other), jnp.where(first, other, shard)], axis=dim
    )


def scatter_rows(part, axis_name, size, mine, dim):
    if size != 2:
        return lax.psum_scatter(
            part.astype(BF16), axis_name, scatter_dimension=dim, tiled=True
        ).astype(F32)
    width = part.shape[dim] // 2
    send = lax.dynamic_slice_in_dim(part, (1 - mine) * width, width, dim).astype(BF16)
    keep = lax.dynamic_slice_in_dim(part, mine * width, width, dim)
    return keep + swap(send, axis_name, 2, 1).astype(F32)


def sum_over_four(v, axis_name, mine):
    rows = v.shape[0] // 4
    low = v.astype(BF16)

    def part(j):
        return lax.dynamic_slice_in_dim(low, (mine ^ j) * rows, rows, 0)

    total = lax.dynamic_slice_in_dim(v, mine * rows, rows, 0)
    for j in (3, 2, 1):
        total = total + swap(part(j), axis_name, 4, j).astype(F32)
    total = total.astype(BF16)
    pieces = [total] + [swap(total, axis_name, 4, j) for j in (1, 2, 3)]
    return jnp.concatenate(by_xor(pieces, mine), axis=0).astype(F32)


def butterfly(v, axis_name, size):
    distance = 1
    while distance < size:
        v = v + swap(v, axis_name, size, distance)
        distance *= 2
    return v


def shards(
    sizes,
    inputs,
    positions,
    query_key_value_weight,
    query_key_value_bias,
    attention_output_weight,
    attention_output_bias,
    up_projection_weight,
    up_projection_bias,
    down_projection_weight,
    down_projection_bias,
    first_scale,
    first_shift,
    second_scale,
    second_shift,
    cotangent,
):
    fsdp = sizes["fsdp"]
    seq_count, block, width = inputs.shape
    assert seq_count == 2 and sizes["ctx"] == 4 and sizes["tp"] == 4
    length = positions.shape[1]
    local = query_key_value_weight.shape[2]
    quarter = block // 4
    f = lax.axis_index("fsdp")
    c = lax.axis_index("ctx")
    t = lax.axis_index("tp")
    s = c // 2

    mix_shard = query_key_value_weight.transpose(1, 2, 0).reshape(3 * local, -1)
    wt = gather_rows(mix_shard, "fsdp", fsdp, f, 1)
    wo = gather_rows(attention_output_weight, "fsdp", fsdp, f, 1)
    wup = gather_rows(up_projection_weight, "fsdp", fsdp, f, 0)
    wdown = gather_rows(down_projection_weight, "fsdp", fsdp, f, 1)

    def quarters(v, seq):
        one = lax.dynamic_index_in_dim(v, seq, 0, keepdims=False)
        return [
            lax.dynamic_slice_in_dim(one, (t ^ j) * quarter, quarter, 0) for j in (0, 2, 1, 3)
        ]

    def over_tp(v):
        v = jnp.concatenate([v, swap(v, "tp", 4, 2)], axis=-2)
        return jnp.concatenate([v, swap(v, "tp", 4, 1)], axis=-2)

    x_mine = quarters(inputs, s)
    x_theirs = quarters(inputs, 1 - s)[0]
    g_mine = quarters(cotangent, s)
    g_theirs = quarters(cotangent, 1 - s)[0]
    x_far = over_tp(swap(x_theirs, "ctx", 4, 2))
    x_near = over_tp(swap(x_mine[0], "ctx", 4, 1))
    x_cross = over_tp(swap(x_theirs, "ctx", 4, 3))
    g_far = over_tp(swap(g_theirs, "ctx", 4, 2))
    x_own = jnp.concatenate(x_mine + [x_far], axis=0)
    x_other = jnp.concatenate([x_near, x_cross], axis=0)
    g_own = jnp.concatenate(g_mine + [g_far], axis=0)

    places = lax.dynamic_index_in_dim(positions, s, 0, keepdims=False)
    places = places.reshape(2, 2, 2, 2, quarter)
    for axis, bit in ((0, c >> 1), (1, c & 1), (2, t >> 1), (3, t & 1)):
        places = jnp.where(bit == 1, jnp.flip(places, axis), places)
    places = places.transpose(1, 0, 3, 2, 4).reshape(length)
    inverse = 10000.0 ** (-2.0 * jnp.arange(HALF, dtype=F32) / ROT)
    angles = inverse[:, None] * places.astype(F32)[None, :]
    cosine, sine = jnp.cos(angles), jnp.sin(angles)
    own_rows = 2 * block

    s1, b1 = first_scale.reshape(1, width), first_shift.reshape(1, width)
    s2, b2 = second_scale.reshape(1, width), second_shift.reshape(1, width)
    mix_bias = query_key_value_bias.reshape(3 * local, 1)
    n1_own, k_own, v_own, qt, n2 = prep(
        True, x_own, cosine[:, :own_rows], sine[:, :own_rows], wt, mix_bias, (s1, b1, s2, b2)
    )
    n1_other, k_other, v_other = prep(
        False, x_other, cosine[:, own_rows:], sine[:, own_rows:], wt[local:], mix_bias[local:],
        (s1, b1),
    )
    dot = mm(wo, g_own, 1, 1).astype(BF16)

    ff, a2, up_part, down_part, small_ff = feed_forward(
        n2, g_own, x_own, wup, up_projection_bias.reshape(1, -1), wdown, s2
    )

    ot, dqt, dkt, dvt = attention(
        qt, dot, k_own, k_other, v_own, v_other, places.reshape(length, 1),
        places[:own_rows].reshape(1, own_rows), cosine[:, :own_rows], sine[:, :own_rows],
        cosine, sine,
    )
    branches = (mm(ot, wo, 0, 0) + ff).astype(BF16)
    out_part = mm(ot, g_own)

    a_other, part_other, small_other, bias_other = back(
        False, (dkt, dvt), own_rows, n1_other, x_other, wt[local:], s1, ()
    )
    a_own, part_own, small_own, bias_own = back(
        True, (dqt, dkt, dvt), 0, n1_own, x_own, wt, s1, (a2,)
    )

    def scatter_tp(v):
        v = v.reshape(-1, 2, 2 * quarter, width)
        kept = v[:, 0].astype(F32) + swap(v[:, 1], "tp", 4, 1).astype(F32)
        kept = kept.reshape(-1, 2, quarter, width)
        return kept[:, 0] + swap(kept[:, 1].astype(BF16), "tp", 4, 2).astype(F32)

    def gather_tp(v):
        v = v.astype(BF16)
        x_side = swap(v, "tp", 4, 2)
        pair = jnp.stack([v, x_side])
        core_side = swap(pair, "tp", 4, 1)
        pieces = (v, core_side[0], x_side, core_side[1])
        return jnp.concatenate(by_xor(pieces, t), axis=1)

    def by_sequence(mine, theirs):
        return jnp.stack([jnp.where(s == 0, mine, theirs), jnp.where(s == 0, theirs, mine)])

    branch_sums = scatter_tp(branches)
    theirs = swap(branch_sums[1].astype(BF16), "ctx", 4, 2).astype(F32)
    full = gather_tp(by_sequence(branch_sums[0], theirs))
    block_out = (
        inputs.astype(F32) + full.astype(F32) + (attention_output_bias + down_projection_bias)
    )

    other_sums = scatter_tp(a_other)
    own_sums = scatter_tp(a_own)
    crossed = swap(other_sums[1].astype(BF16), "ctx", 4, 3).astype(F32)
    far = swap(own_sums[1].astype(BF16), "ctx", 4, 2).astype(F32)
    near = swap(other_sums[0].astype(BF16), "ctx", 4, 1).astype(F32)
    a = by_sequence(own_sums[0] + near, far + crossed)
    x_quarter = by_sequence(x_mine[0], x_theirs).astype(F32)
    xhat, inv = xhat_of(x_quarter)
    norm_grad = inv * (
        a
        - jnp.mean(a, axis=-1, keepdims=True)
        - xhat * jnp.mean(a * xhat, axis=-1, keepdims=True)
    )
    inputs_grad = cotangent.astype(F32) + gather_tp(norm_grad).astype(F32)

    def owned(part, dim):
        return sum_over_four(scatter_rows(part, "fsdp", fsdp, f, dim), "ctx", c)

    up_total = owned(up_part, 0)
    down_total = owned(down_part, 1)
    out_total = owned(out_part, 1)
    mix_part = part_own + jnp.concatenate([jnp.zeros((local, width), F32), part_other], axis=0)
    mix_total = owned(mix_part, 1).reshape(3, local, -1).transpose(2, 0, 1)

    mix_bias_grad = bias_own + jnp.concatenate([jnp.zeros((local, 1), F32), bias_other], axis=0)
    mix_bias_grad = jnp.pad(mix_bias_grad.reshape(1, -1), ((0, 0), (0, width - 3 * local)))
    small = jnp.concatenate(
        [small_own[0:2] + small_other[0:2], small_ff[2:4], small_ff[0:2], mix_bias_grad,
         jnp.zeros((1, width), F32)], axis=0
    )
    small = butterfly(small, "fsdp", fsdp)
    small = butterfly(small, "ctx", 4)
    norm_small = butterfly(small[0:4], "tp", 4)
    bias_total = small[5]
    return (
        block_out,
        inputs_grad,
        mix_total,
        small[6, : 3 * local].reshape(3, local),
        out_total,
        bias_total,
        up_total,
        small[4],
        down_total,
        bias_total,
        norm_small[0],
        norm_small[1],
        norm_small[2],
        norm_small[3],
    )


def solution(mesh):
    in_specs = (
        P("fsdp", "ctx", None),
        P("fsdp", None),
        P("fsdp", None, "tp"),
        P(None, "tp"),
        P("tp", "fsdp"),
        P(),
        P("fsdp", "tp"),
        P("tp"),
        P("tp", "fsdp"),
        P(),
        P(),
        P(),
        P(),
        P(),
        P("fsdp", "ctx", None),
    )
    out_specs = (
        P("fsdp", "ctx", None),
        P("fsdp", "ctx", None),
        P("fsdp", None, "tp"),
        P(None, "tp"),
        P("tp", "fsdp"),
        P(),
        P("fsdp", "tp"),
        P("tp"),
        P("tp", "fsdp"),
        P(),
        P(),
        P(),
        P(),
        P(),
    )
    body = functools.partial(shards, dict(mesh.shape))
    return jax.shard_map(body, mesh=mesh, in_specs=in_specs, out_specs=out_specs, check_vma=False)
```

time: 877 us -> 300 us (0.34)
  waiting for transfers between devices: 509 us -> 92.3 us
  matrix products: 200 us -> 6.66 us
  starting transfers between devices: 0.66 us -> 77.5 us
  blocking collectives: 59.5 us -> 0 us
  Pallas kernels: 0 us -> 50.4 us
  other arithmetic: 47.8 us -> 27.2 us
  between operations: 14.9 us -> 1.91 us
  local copies, waits for them, and re-layouts: 30.4 us -> 42.4 us
  loops' own time: 10.6 us -> 0 us
    psum x2 -> x0, waiting for transfers between devices: 258 us -> none  [the longest x1 173 us: shards(): branches = lax.psum(attention_branch + feedforward_branch, 'tp')]
    dot_general x26 -> x3, matrix products: 200 us -> 6.66 us  [mm(): lax.dot_general(a, b, (((ca,), (cb,)), ((), ())), preferred_element_type=...]
    reduce_scatter x6 -> x0, waiting for transfers between devices: 186 us -> none  [the longest x1 57.6 us: shards(): lax.psum_scatter(value_grads.reshape(seq_count, length, local_width), 'ct...]
    ppermute x0 -> x63, waiting for transfers between devices: none -> 92.3 us  [swap(): return lax.ppermute(v, axis, [(i, i ^ distance) for i in range(size)])]
    ppermute x0 -> x63, starting transfers between devices: none -> 77.5 us  [swap(): return lax.ppermute(v, axis, [(i, i ^ distance) for i in range(size)])]
    all_gather x4 -> x0, waiting for transfers between devices: 63.8 us -> none  [the longest x1 38.1 us: shards(): lax.all_gather(own_values, 'ctx', axis=1, tiled=True)]
    pallas_call x0 -> x6, Pallas kernels: none -> 50.4 us  [the longest x1 28.6 us: attention(): pl.pallas_call(functools.partial(attention_kernel, chunk), grid=(heads, r...]
    psum x1 -> x0, blocking collectives: 39.9 us -> none  [shards(): lax.psum((mix_bias_grad, up_bias_grad, bias_grad, scale_one_grad, shift_o...]
  transfers between devices with their start and end apart: 12 -> 63, of which waited for: 9 -> 22; matrix products, arithmetic and copies ran while one was open for 28% -> 22% of each run, Pallas kernels for 0% -> 6%
where the time goes in v1:
time: 300 us; the launch traced here: 298 us
  waiting for transfers between devices  92.3 us (31%)
  starting transfers between devices  77.5 us (26%)
  Pallas kernels  50.4 us (17%)
  local copies, waits for them, and re-layouts  42.4 us (14%)
  other arithmetic  27.2 us (9%)
  matrix products  6.66 us (2%)
    ppermute x63, waiting for transfers between devices, swap(): return lax.ppermute(v, axis, [(i, i ^ distance) for i in range(size)])  92.3 us
    ppermute x63, starting transfers between devices, swap(): return lax.ppermute(v, axis, [(i, i ^ distance) for i in range(size)])  77.5 us
    pallas_call x1, Pallas kernels, attention(): pl.pallas_call(functools.partial(attention_kernel, chunk), grid=(heads, r...  28.6 us
    unnamed x104, local copies, waits for them, and re-layouts  18.7 us
    pallas_call x1, Pallas kernels, feed_forward(): pl.pallas_call(forward_kernel, grid=(rows // step,), in_specs=[row, row,...  9.18 us
    pallas_call x2, Pallas kernels, back(): pl.pallas_call(functools.partial(back_kernel, own), grid=(rows // step,),...  6.76 us
    dot_general x3, matrix products, mm(): lax.dot_general(a, b, (((ca,), (cb,)), ((), ())), preferred_element_type=...  6.66 us
  transfers between devices with their start and end apart: 63, of which 22 were waited for; matrix products, arithmetic and copies ran while one was open for 22% of the time, Pallas kernels for 6%

profile of v1, /device:TPU:0, one launch (start us, length us, event | category | flops | bytes accessed | tf_op | source)
XLA Modules:
  0.0 298.3 jit_solution(9404756821784210917)
XLA Ops:
  0.7 1.8 broadcast_select_fusion.23
  2.5 5.0 %collective-permute-start.11 = (bf16[128,768]{1,0:T(8,128)(2,1)}, bf16[128,768]{1,0:T(8,128)(2,1)}, u32[]{:S(2)}, u32[]{:S(2)}) collective-permute-start(bf16[128,768]{1,0:T(8,128)(2,1)} %get-tuple-element.89), channel_id=1, source_target_pairs={{0,12},{4,8},{8,4},{12,0},{1,13},{5,9},{9,5},{13,1},{2,14},{6,10},... | collective-permute-start | bytes 589832 | tf_op jit(solution)/shard_map/ppermute | solution.py:326
  9.1 1.7 dynamic-slice_bitcast_fusion
  10.8 2.9 collective-permute-start.5
  15.7 1.7 constant_dynamic-update-slice_fusion.3
  32.7 2.0 copy.53.kpos_ref
  43.3 2.4 collective-permute-done.8
  49.9 3.7 %collective-permute-done.1 = bf16[128,768]{1,0:T(8,128)(2,1)S(1)} collective-permute-done((bf16[128,768]{1,0:T(8,128)(2,1)}, bf16[128,768]{1,0:T(8,128)(2,1)S(1)}, u32[]{:S(2)}, u32[]{:S(2)}) %collective-permute-start.1) | collective-permute-done | bytes 196640 | tf_op jit(solution)/shard_map/ppermute | solution.py:326
  53.6 1.6 collective-permute-start.12
  56.2 3.3 %collective-permute-done.12 = bf16[128,768]{1,0:T(8,128)(2,1)S(1)} collective-permute-done((bf16[128,768]{1,0:T(8,128)(2,1)}, bf16[128,768]{1,0:T(8,128)(2,1)S(1)}, u32[]{:S(2)}, u32[]{:S(2)}) %collective-permute-start.12) | collective-permute-done | bytes 196640 | tf_op jit(solution)/shard_map/ppermute | solution.py:326
  65.8 2.8 shard_map.255
  69.6 3.0 %shard_map.254 = (bf16[1024,768]{1,0:T(8,128)(2,1)S(1)}, bf16[192,1024]{1,0:T(8,128)(2,1)S(1)}, bf16[192,1024]{1,0:T(8,128)(2,1)S(1)}, bf16[192,1024]{1,0:T(8,128)(2,1)S(1)}, bf16[1024,768]{1,0:T(8,128)(2,1)S(1)}) custom-call(bf16[1024,768]{1,0:T(8,128)(2,1)S(1)} %constant_dynamic-update-slice_fusion.refs_0_.x_ref.refs_4_, f32[8,1024]{1,0:T(8,128)S(1)} %copy-done.18, ...), custom_call_target="tpu_custom_call" | custom-call | flops 905969664 | bytes 6291456 | tf_op jit(solution)/shard_map/pallas_call | solution.py:82
  72.7 28.6 %shard_map.256 = (bf16[192,1024]{1,0:T(8,128)(2,1)S(1)}, bf16[192,1024]{1,0:T(8,128)(2,1)S(1)}, bf16[192,2048]{1,0:T(8,128)(2,1)S(1)}, bf16[192,2048]{1,0:T(8,128)(2,1)S(1)}) custom-call(bf16[192,1024]{1,0:T(8,128)(2,1)S(1)} %get-tuple-element.39.q_ref, bf16[192,1024]{1,0:T(8,128)(2,1)S(1)} %convolution_convert_fusion.do_ref, ...), custom_call_target="tpu_custom_call" | custom-call | flops 16106127360 | bytes 6291456 | tf_op jit(solution)/shard_map/pallas_call | solution.py:186
  101.9 1.6 collective-permute-start.40
  103.5 2.9 shard_map.259
  108.5 9.2 %shard_map.257 = (f32[1024,768]{1,0:T(8,128)}, f32[1024,768]{1,0:T(8,128)}, f32[768,768]{1,0:T(8,128)S(1)}, f32[768,768]{1,0:T(8,128)S(1)}, f32[8,768]{1,0:T(8,128)S(1)}) custom-call(bf16[1024,768]{1,0:T(8,128)(2,1)S(1)} %get-tuple-element.45.n2_ref, bf16[1024,768]{1,0:T(8,128)(2,1)S(1)} %constant_dynamic-update-slice_fusion.4.g_ref, ...), custom_call_target="tpu_custom_call" | custom-call | flops 7247757312 | bytes 16777216 | tf_op jit(solution)/shard_map/pallas_call | solution.py:252
  117.7 5.5 %add_convert_fusion = bf16[1024,768]{1,0:T(8,128)(2,1)} fusion(f32[1024,768]{1,0:T(8,128)} %get-tuple-element.46, bf16[192,1024]{1,0:T(8,128)(2,1)S(1)} %get-tuple-element.44, bf16[192,384]{1,0:T(8,128)(2,1)S(1)} %get-tuple-element.131, bf16[192,384]{1,0:T(8,128)(2,1)S(1)} %get-tuple-element.130), kind=kOutput, calls=%fused_computation.2 | convolution fusion | flops 304152576 | bytes 5406720 | tf_op jit(solution)/shard_map/dot_general | solution.py:21
  123.2 3.9 %shard_map.258 = (bf16[1024,768]{1,0:T(8,128)(2,1)S(1)}, f32[576,768]{1,0:T(8,128)S(1)}, f32[8,768]{1,0:T(8,128)S(1)}, f32[576,1]{1,0:T(8,128)S(1)}) custom-call(bf16[192,1024]{1,0:T(8,128)(2,1)S(1)} %get-tuple-element.47.refs_0_, bf16[192,2048]{1,0:T(8,128)(2,1)S(1)} %get-tuple-element.48.refs_1_.refs_0_, ...), custom_call_target="tpu_custom_call" | custom-call | flops 1811939328 | bytes 8388608 | tf_op jit(solution)/shard_map/pallas_call | solution.py:309
  131.6 2.8 dynamic-slice_convert_fusion.1
  135.8 2.1 dynamic-slice_convert_fusion
  139.4 3.6 %collective-permute-done.39 = f32[8,768]{1,0:T(8,128)S(1)} collective-permute-done((f32[8,768]{1,0:T(8,128)S(1)}, f32[8,768]{1,0:T(8,128)S(1)}, u32[]{:S(2)}, u32[]{:S(2)}) %collective-permute-start.39) | collective-permute-done | bytes 24608 | tf_op jit(solution)/shard_map/ppermute | solution.py:326
  148.8 3.0 collective-permute-start.42
  156.1 2.0 collective-permute-start.45
  158.1 2.3 collective-permute-start.44
  161.7 2.1 collective-permute-done.44
  163.9 2.4 collective-permute-done.30
  168.6 3.5 %collective-permute-start.32 = (bf16[144,384]{1,0:T(8,128)(2,1)S(1)}, bf16[144,384]{1,0:T(8,128)(2,1)S(1)}, u32[]{:S(2)}, u32[]{:S(2)}) collective-permute-start(bf16[144,384]{1,0:T(8,128)(2,1)S(1)} %get-tuple-element.127), channel_id=1, source_target_pairs={{0,8},{4,12},{8,0},{12,4},{1,9},{5,13},{9,1},{13,5},{2,10},{6,14},... | collective-permute-start | bytes 331784 | tf_op jit(solution)/shard_map/ppermute | solution.py:326
  175.8 1.6 collective-permute-start.36
  179.2 10.4 %collective-permute-done.47 = bf16[384,768]{1,0:T(8,128)(2,1)S(1)} collective-permute-done((bf16[384,768]{1,0:T(8,128)(2,1)S(1)}, bf16[384,768]{1,0:T(8,128)(2,1)S(1)}, u32[]{:S(2)}, u32[]{:S(2)}) %collective-permute-start.47) | collective-permute-done | bytes 589856 | tf_op jit(solution)/shard_map/ppermute | solution.py:326
  190.7 3.0 %collective-permute-start.55 = (bf16[192,384]{1,0:T(8,128)(2,1)S(1)}, bf16[192,384]{1,0:T(8,128)(2,1)S(1)}, u32[]{:S(2)}, u32[]{:S(2)}) collective-permute-start(bf16[192,384]{1,0:T(8,128)(2,1)S(1)} %get-tuple-element.109), channel_id=1, source_target_pairs={{0,12},{4,8},{8,4},{12,0},{1,13},{5,9},{9,5},{13,1},{2,14},{6,10},... | collective-permute-start | bytes 442376 | tf_op jit(solution)/shard_map/ppermute | solution.py:326
  193.7 3.7 %collective-permute-done.34 = bf16[144,384]{1,0:T(8,128)(2,1)S(1)} collective-permute-done((bf16[144,384]{1,0:T(8,128)(2,1)S(1)}, bf16[144,384]{1,0:T(8,128)(2,1)S(1)}, u32[]{:S(2)}, u32[]{:S(2)}) %collective-permute-start.34) | collective-permute-done | bytes 110624 | tf_op jit(solution)/shard_map/ppermute | solution.py:326
  197.4 4.0 %collective-permute-start.56 = (bf16[192,384]{1,0:T(8,128)(2,1)S(1)}, bf16[192,384]{1,0:T(8,128)(2,1)S(1)}, u32[]{:S(2)}, u32[]{:S(2)}) collective-permute-start(bf16[192,384]{1,0:T(8,128)(2,1)S(1)} %get-tuple-element.111), channel_id=1, source_target_pairs={{0,8},{4,12},{8,0},{12,4},{1,9},{5,13},{9,1},{13,5},{2,10},{6,14},... | collective-permute-start | bytes 442376 | tf_op jit(solution)/shard_map/ppermute | solution.py:326
  202.6 3.9 %collective-permute-start.48 = (bf16[96,768]{1,0:T(8,128)(2,1)S(1)}, bf16[96,768]{1,0:T(8,128)(2,1)S(1)}, u32[]{:S(2)}, u32[]{:S(2)}) collective-permute-start(bf16[96,768]{1,0:T(8,128)(2,1)S(1)} %get-tuple-element.116), channel_id=1, source_target_pairs={{0,12},{4,8},{8,4},{12,0},{1,13},{5,9},{9,5},{13,1},{2,14},{6,10},... | collective-permute-start | bytes 442376 | tf_op jit(solution)/shard_map/ppermute | solution.py:326
  207.6 6.8 %collective-permute-done.56 = bf16[192,384]{1,0:T(8,128)(2,1)S(1)} collective-permute-done((bf16[192,384]{1,0:T(8,128)(2,1)S(1)}, bf16[192,384]{1,0:T(8,128)(2,1)S(1)}, u32[]{:S(2)}, u32[]{:S(2)}) %collective-permute-start.56) | collective-permute-done | bytes 147488 | tf_op jit(solution)/shard_map/ppermute | solution.py:326
  214.6 4.7 %collective-permute-start.60 = (bf16[192,384]{1,0:T(8,128)(2,1)S(1)}, bf16[192,384]{1,0:T(8,128)(2,1)S(1)}, u32[]{:S(2)}, u32[]{:S(2)}) collective-permute-start(bf16[192,384]{1,0:T(8,128)(2,1)S(1)} %add_convert_fusion.1), channel_id=1, source_target_pairs={{0,4},{4,0},{8,12},{12,8},{1,5},{5,1},{9,13},{13,9},{2,6},{6,2},{1... | collective-permute-start | bytes 442376 | tf_op jit(solution)/shard_map/ppermute | solution.py:326
  225.4 8.8 %collective-permute-done.24 = bf16[2,128,768]{2,1,0:T(8,128)(2,1)S(1)} collective-permute-done((bf16[2,128,768]{2,1,0:T(8,128)(2,1)S(1)}, bf16[2,128,768]{2,1,0:T(8,128)(2,1)S(1)}, u32[]{:S(2)}, u32[]{:S(2)}) %collective-permute-start.24) | collective-permute-done | bytes 393248 | tf_op jit(solution)/shard_map/ppermute | solution.py:326
  234.4 2.6 collective-permute-start.27
  236.9 12.1 %collective-permute-done.22 = bf16[2,128,768]{2,1,0:T(8,128)(2,1)S(1)} collective-permute-done((bf16[2,128,768]{2,1,0:T(8,128)(2,1)S(1)}, bf16[2,128,768]{2,1,0:T(8,128)(2,1)S(1)}, u32[]{:S(2)}, u32[]{:S(2)}) %collective-permute-start.22) | collective-permute-done | bytes 393248 | tf_op jit(solution)/shard_map/ppermute | solution.py:326
  249.5 2.7 collective-permute-start.26
  253.8 2.6 collective-permute-done.25
  256.4 3.1 %collective-permute-start.18 = (bf16[128,768]{1,0:T(8,128)(2,1)S(1)}, bf16[128,768]{1,0:T(8,128)(2,1)S(1)}, u32[]{:S(2)}, u32[]{:S(2)}) collective-permute-start(bf16[128,768]{1,0:T(8,128)(2,1)S(1)} %fusion.26), channel_id=1, source_target_pairs={{0,8},{4,12},{8,0},{12,4},{1,9},{5,13},{9,1},{13,5},{2,10},{6,14},... | collective-permute-start | bytes 589832 | tf_op jit(solution)/shard_map/ppermute | solution.py:326
  259.6 10.0 %collective-permute-done.26 = bf16[128,768]{1,0:T(8,128)(2,1)S(1)} collective-permute-done((bf16[128,768]{1,0:T(8,128)(2,1)S(1)}, bf16[128,768]{1,0:T(8,128)(2,1)S(1)}, u32[]{:S(2)}, u32[]{:S(2)}) %collective-permute-start.26) | collective-permute-done | bytes 196640 | tf_op jit(solution)/shard_map/ppermute | solution.py:326
  271.1 3.4 %collective-permute-done.18 = bf16[128,768]{1,0:T(8,128)(2,1)S(1)} collective-permute-done((bf16[128,768]{1,0:T(8,128)(2,1)S(1)}, bf16[128,768]{1,0:T(8,128)(2,1)S(1)}, u32[]{:S(2)}, u32[]{:S(2)}) %collective-permute-start.18) | collective-permute-done | bytes 196640 | tf_op jit(solution)/shard_map/ppermute | solution.py:326
  274.8 3.4 %collective-permute-done.28 = bf16[2,128,768]{2,1,0:T(8,128)(2,1)S(1)} collective-permute-done((bf16[2,128,768]{2,1,0:T(8,128)(2,1)S(1)}, bf16[2,128,768]{2,1,0:T(8,128)(2,1)S(1)}, u32[]{:S(2)}, u32[]{:S(2)}) %collective-permute-start.28) | collective-permute-done | bytes 393248 | tf_op jit(solution)/shard_map/ppermute | solution.py:326
  278.3 2.3 collective-permute-start.51
  281.2 7.2 %collective-permute-done.52 = bf16[96,768]{1,0:T(8,128)(2,1)S(1)} collective-permute-done((bf16[96,768]{1,0:T(8,128)(2,1)S(1)}, bf16[96,768]{1,0:T(8,128)(2,1)S(1)}, u32[]{:S(2)}, u32[]{:S(2)}) %collective-permute-start.52) | collective-permute-done | bytes 147488 | tf_op jit(solution)/shard_map/ppermute | solution.py:326
  292.2 2.0 convert_add_fusion
  295.6 2.1 add_add_fusion
  (306 shorter events, 88.4 us)
Async XLA Ops:
  2.5 46.2 %collective-permute-start.11 = (bf16[128,768]{1,0:T(8,128)(2,1)}, bf16[128,768]{1,0:T(8,128)(2,1)}, u32[]{:S(2)}, u32[]{:S(2)}) collective-permute-start(bf16[128,768]{1,0:T(8,128)(2,1)} %get-tuple-element.89), channel_id=1, source_target_pairs={{0,12},{4,8},{8,4},{12,0},{1,13},{5,9},{9,5},{13,1},{2,14},{6,10},... | collective-permute-start | bytes 589832 | tf_op jit(solution)/shard_map/ppermute | solution.py:326
  7.6 33.2 %collective-permute-start = (bf16[128,768]{1,0:T(8,128)(2,1)}, bf16[128,768]{1,0:T(8,128)(2,1)}, u32[]{:S(2)}, u32[]{:S(2)}) collective-permute-start(bf16[128,768]{1,0:T(8,128)(2,1)} %get-tuple-element.89), channel_id=1, source_target_pairs={{0,8},{4,12},{8,0},{12,4},{1,9},{5,13},{9,1},{13,5},{2,10},{6,14},... | collective-permute-start | bytes 589832 | tf_op jit(solution)/shard_map/ppermute | solution.py:326
  7.6 29.5 %collective-permute-start.4 = (bf16[192,384]{1,0:T(8,128)(2,1)}, bf16[192,384]{1,0:T(8,128)(2,1)}, u32[]{:S(2)}, u32[]{:S(2)}) collective-permute-start(bf16[192,384]{1,0:T(8,128)(2,1)} %param.19), channel_id=1, source_target_pairs={{0,16},{16,0},{1,17},{17,1},{2,18},{18,2},{3,19},{19,3},{4,20},{20... | collective-permute-start | bytes 442376 | tf_op jit(solution)/shard_map/ppermute | solution.py:326
  10.8 29.0 %collective-permute-start.5 = (bf16[128,768]{1,0:T(8,128)(2,1)}, bf16[128,768]{1,0:T(8,128)(2,1)}, u32[]{:S(2)}, u32[]{:S(2)}) collective-permute-start(bf16[128,768]{1,0:T(8,128)(2,1)} %dynamic-slice_bitcast_fusion), channel_id=1, source_target_pairs={{0,8},{4,12},{8,0},{12,4},{1,9},{5,13},{9,1},{13,5},{2,10},{6,14},... | collective-permute-start | bytes 589832 | tf_op jit(solution)/shard_map/ppermute | solution.py:326
  13.7 47.4 %collective-permute-start.3 = (bf16[576,384]{1,0:T(8,128)(2,1)}, bf16[576,384]{1,0:T(8,128)(2,1)}, u32[]{:S(2)}, u32[]{:S(2)}) collective-permute-start(bf16[576,384]{1,0:T(8,128)(2,1)} %bitcast.228), channel_id=1, source_target_pairs={{0,16},{16,0},{1,17},{17,1},{2,18},{18,2},{3,19},{19,3},{4,20},{20... | collective-permute-start | bytes 1327112 | tf_op jit(solution)/shard_map/ppermute | solution.py:326
  37.1 25.3 %collective-permute-start.14 = (bf16[384,768]{1,0:T(8,128)(2,1)}, bf16[384,768]{1,0:T(8,128)(2,1)S(1)}, u32[]{:S(2)}, u32[]{:S(2)}) collective-permute-start(bf16[384,768]{1,0:T(8,128)(2,1)} %param.21), channel_id=1, source_target_pairs={{0,16},{16,0},{1,17},{17,1},{2,18},{18,2},{3,19},{19,3},{4,20},{20... | collective-permute-start | bytes 1769480 | tf_op jit(solution)/shard_map/ppermute | solution.py:326
  45.7 7.9 %collective-permute-start.1 = (bf16[128,768]{1,0:T(8,128)(2,1)}, bf16[128,768]{1,0:T(8,128)(2,1)S(1)}, u32[]{:S(2)}, u32[]{:S(2)}) collective-permute-start(bf16[128,768]{1,0:T(8,128)(2,1)} %collective-permute-done), channel_id=1, source_target_pairs={{0,2},{1,3},{2,0},{3,1},{4,6},{5,7},{6,4},{7,5},{8,10},{9,11},{10,... | collective-permute-start | bytes 589832 | tf_op jit(solution)/shard_map/ppermute | solution.py:326
  47.2 17.2 %collective-permute-start.15 = (bf16[768,384]{1,0:T(8,128)(2,1)S(1)}, bf16[768,384]{1,0:T(8,128)(2,1)S(1)}, u32[]{:S(2)}, u32[]{:S(2)}) collective-permute-start(bf16[768,384]{1,0:T(8,128)(2,1)S(1)} %copy-done.32), channel_id=1, source_target_pairs={{0,16},{16,0},{1,17},{17,1},{2,18},{18,2},{3,19},{19,3},{4,20},{20... | collective-permute-start | bytes 1769480 | tf_op jit(solution)/shard_map/ppermute | solution.py:326
  48.8 11.7 %collective-permute-start.9 = (bf16[128,768]{1,0:T(8,128)(2,1)S(1)}, bf16[128,768]{1,0:T(8,128)(2,1)S(1)}, u32[]{:S(2)}, u32[]{:S(2)}) collective-permute-start(bf16[128,768]{1,0:T(8,128)(2,1)S(1)} %collective-permute-done.8), channel_id=1, source_target_pairs={{0,2},{1,3},{2,0},{3,1},{4,6},{5,7},{6,4},{7,5},{8,10},{9,11},{10,... | collective-permute-start | bytes 589832 | tf_op jit(solution)/shard_map/ppermute | solution.py:326
  59.5 9.1 %collective-permute-start.7 = (bf16[256,768]{1,0:T(8,128)(2,1)S(1)}, bf16[256,768]{1,0:T(8,128)(2,1)S(1)}, u32[]{:S(2)}, u32[]{:S(2)}) collective-permute-start(bf16[256,768]{1,0:T(8,128)(2,1)S(1)} %pad_maximum_fusion.8), channel_id=1, source_target_pairs={{0,1},{1,0},{2,3},{3,2},{4,5},{5,4},{6,7},{7,6},{8,9},{9,8},{10,11... | collective-permute-start | bytes 1179656 | tf_op jit(solution)/shard_map/ppermute | solution.py:326
  61.1 8.2 %collective-permute-start.2 = (bf16[256,768]{1,0:T(8,128)(2,1)S(1)}, bf16[256,768]{1,0:T(8,128)(2,1)S(1)}, u32[]{:S(2)}, u32[]{:S(2)}) collective-permute-start(bf16[256,768]{1,0:T(8,128)(2,1)S(1)} %pad_maximum_fusion.7), channel_id=1, source_target_pairs={{0,1},{1,0},{2,3},{3,2},{4,5},{5,4},{6,7},{7,6},{8,9},{9,8},{10,11... | collective-permute-start | bytes 1179656 | tf_op jit(solution)/shard_map/ppermute | solution.py:326
  101.9 43.9 %collective-permute-start.40 = (bf16[192,384]{1,0:T(8,128)(2,1)S(1)}, bf16[192,384]{1,0:T(8,128)(2,1)}, u32[]{:S(2)}, u32[]{:S(2)}) collective-permute-start(bf16[192,384]{1,0:T(8,128)(2,1)S(1)} %dynamic-slice_convert_fusion.3), channel_id=1, source_target_pairs={{0,16},{16,0},{1,17},{17,1},{2,18},{18,2},{3,19},{19,3},{4,20},{20... | collective-permute-start | bytes 442376 | tf_op jit(solution)/shard_map/ppermute | solution.py:326
  108.5 112.2 %collective-permute-start.23 = (bf16[2,256,768]{2,1,0:T(8,128)(2,1)}, bf16[2,256,768]{2,1,0:T(8,128)(2,1)}, u32[]{:S(2)}, u32[]{:S(2)}) collective-permute-start(bf16[2,256,768]{2,1,0:T(8,128)(2,1)} %slice_bitcast_fusion), channel_id=1, source_target_pairs={{0,1},{1,0},{2,3},{3,2},{4,5},{5,4},{6,7},{7,6},{8,9},{9,8},{10,11... | collective-permute-start | bytes 2359304 | tf_op jit(solution)/shard_map/ppermute | solution.py:326
  144.3 8.1 %collective-permute-start.62 = (f32[4,768]{1,0:T(4,128)S(1)}, f32[4,768]{1,0:T(4,128)S(1)}, u32[]{:S(2)}, u32[]{:S(2)}) collective-permute-start(f32[4,768]{1,0:T(4,128)S(1)} %slice_add_fusion.1), channel_id=1, source_target_pairs={{0,2},{1,3},{2,0},{3,1},{4,6},{5,7},{6,4},{7,5},{8,10},{9,11},{10,... | collective-permute-start | bytes 36872 | tf_op jit(solution)/shard_map/ppermute | solution.py:326
  147.3 7.7 %collective-permute-start.41 = (bf16[48,384]{1,0:T(8,128)(2,1)}, bf16[48,384]{1,0:T(8,128)(2,1)S(1)}, u32[]{:S(2)}, u32[]{:S(2)}) collective-permute-start(bf16[48,384]{1,0:T(8,128)(2,1)} %get-tuple-element.136), channel_id=1, source_target_pairs={{0,12},{4,8},{8,4},{12,0},{1,13},{5,9},{9,5},{13,1},{2,14},{6,10},... | collective-permute-start | bytes 110600 | tf_op jit(solution)/shard_map/ppermute | solution.py:326
  148.2 6.9 %collective-permute-start.43 = (bf16[48,384]{1,0:T(8,128)(2,1)}, bf16[48,384]{1,0:T(8,128)(2,1)}, u32[]{:S(2)}, u32[]{:S(2)}) collective-permute-start(bf16[48,384]{1,0:T(8,128)(2,1)} %get-tuple-element.137), channel_id=1, source_target_pairs={{0,4},{4,0},{8,12},{12,8},{1,5},{5,1},{9,13},{13,9},{2,6},{6,2},{1... | collective-permute-start | bytes 110600 | tf_op jit(solution)/shard_map/ppermute | solution.py:326
  153.0 13.3 %collective-permute-start.30 = (bf16[576,384]{1,0:T(8,128)(2,1)}, bf16[576,384]{1,0:T(8,128)(2,1)S(1)}, u32[]{:S(2)}, u32[]{:S(2)}) collective-permute-start(bf16[576,384]{1,0:T(8,128)(2,1)} %dynamic-slice_convert_fusion.2), channel_id=1, source_target_pairs={{0,16},{16,0},{1,17},{17,1},{2,18},{18,2},{3,19},{19,3},{4,20},{20... | collective-permute-start | bytes 1327112 | tf_op jit(solution)/shard_map/ppermute | solution.py:326
  161.0 18.0 %collective-permute-start.54 = (bf16[768,384]{1,0:T(8,128)(2,1)}, bf16[768,384]{1,0:T(8,128)(2,1)S(1)}, u32[]{:S(2)}, u32[]{:S(2)}) collective-permute-start(bf16[768,384]{1,0:T(8,128)(2,1)} %dynamic-slice_convert_fusion), channel_id=1, source_target_pairs={{0,16},{16,0},{1,17},{17,1},{2,18},{18,2},{3,19},{19,3},{4,20},{20... | collective-permute-start | bytes 1769480 | tf_op jit(solution)/shard_map/ppermute | solution.py:326
  167.7 6.8 %collective-permute-start.31 = (bf16[144,384]{1,0:T(8,128)(2,1)S(1)}, bf16[144,384]{1,0:T(8,128)(2,1)S(1)}, u32[]{:S(2)}, u32[]{:S(2)}) collective-permute-start(bf16[144,384]{1,0:T(8,128)(2,1)S(1)} %get-tuple-element.125), channel_id=1, source_target_pairs={{0,12},{4,8},{8,4},{12,0},{1,13},{5,9},{9,5},{13,1},{2,14},{6,10},... | collective-permute-start | bytes 331784 | tf_op jit(solution)/shard_map/ppermute | solution.py:326
  168.6 7.1 %collective-permute-start.33 = (bf16[144,384]{1,0:T(8,128)(2,1)S(1)}, bf16[144,384]{1,0:T(8,128)(2,1)S(1)}, u32[]{:S(2)}, u32[]{:S(2)}) collective-permute-start(bf16[144,384]{1,0:T(8,128)(2,1)S(1)} %get-tuple-element.126), channel_id=1, source_target_pairs={{0,4},{4,0},{8,12},{12,8},{1,5},{5,1},{9,13},{13,9},{2,6},{6,2},{1... | collective-permute-start | bytes 331784 | tf_op jit(solution)/shard_map/ppermute | solution.py:326
  168.6 7.1 %collective-permute-start.32 = (bf16[144,384]{1,0:T(8,128)(2,1)S(1)}, bf16[144,384]{1,0:T(8,128)(2,1)S(1)}, u32[]{:S(2)}, u32[]{:S(2)}) collective-permute-start(bf16[144,384]{1,0:T(8,128)(2,1)S(1)} %get-tuple-element.127), channel_id=1, source_target_pairs={{0,8},{4,12},{8,0},{12,4},{1,9},{5,13},{9,1},{13,5},{2,10},{6,14},... | collective-permute-start | bytes 331784 | tf_op jit(solution)/shard_map/ppermute | solution.py:326
  174.5 15.2 %collective-permute-start.47 = (bf16[384,768]{1,0:T(8,128)(2,1)S(1)}, bf16[384,768]{1,0:T(8,128)(2,1)S(1)}, u32[]{:S(2)}, u32[]{:S(2)}) collective-permute-start(bf16[384,768]{1,0:T(8,128)(2,1)S(1)} %copy-done.33), channel_id=1, source_target_pairs={{0,16},{16,0},{1,17},{17,1},{2,18},{18,2},{3,19},{19,3},{4,20},{20... | collective-permute-start | bytes 1769480 | tf_op jit(solution)/shard_map/ppermute | solution.py:326
  175.7 47.0 %collective-permute-start.16 = (bf16[2,256,768]{2,1,0:T(8,128)(2,1)S(1)}, bf16[2,256,768]{2,1,0:T(8,128)(2,1)S(1)}, u32[]{:S(2)}, u32[]{:S(2)}) collective-permute-start(bf16[2,256,768]{2,1,0:T(8,128)(2,1)S(1)} %slice_bitcast_fusion.5), channel_id=1, source_target_pairs={{0,1},{1,0},{2,3},{3,2},{4,5},{5,4},{6,7},{7,6},{8,9},{9,8},{10,11... | collective-permute-start | bytes 2359304 | tf_op jit(solution)/shard_map/ppermute | solution.py:326
  175.8 14.9 %collective-permute-start.36 = (bf16[144,384]{1,0:T(8,128)(2,1)S(1)}, bf16[144,384]{1,0:T(8,128)(2,1)S(1)}, u32[]{:S(2)}, u32[]{:S(2)}) collective-permute-start(bf16[144,384]{1,0:T(8,128)(2,1)S(1)} %add_convert_fusion.3), channel_id=1, source_target_pairs={{0,4},{4,0},{8,12},{12,8},{1,5},{5,1},{9,13},{13,9},{2,6},{6,2},{1... | collective-permute-start | bytes 331784 | tf_op jit(solution)/shard_map/ppermute | solution.py:326
  179.0 14.7 %collective-permute-start.35 = (bf16[144,384]{1,0:T(8,128)(2,1)S(1)}, bf16[144,384]{1,0:T(8,128)(2,1)S(1)}, u32[]{:S(2)}, u32[]{:S(2)}) collective-permute-start(bf16[144,384]{1,0:T(8,128)(2,1)S(1)} %add_convert_fusion.3), channel_id=1, source_target_pairs={{0,8},{4,12},{8,0},{12,4},{1,9},{5,13},{9,1},{13,5},{2,10},{6,14},... | collective-permute-start | bytes 331784 | tf_op jit(solution)/shard_map/ppermute | solution.py:326
  189.6 7.8 %collective-permute-start.34 = (bf16[144,384]{1,0:T(8,128)(2,1)S(1)}, bf16[144,384]{1,0:T(8,128)(2,1)S(1)}, u32[]{:S(2)}, u32[]{:S(2)}) collective-permute-start(bf16[144,384]{1,0:T(8,128)(2,1)S(1)} %add_convert_fusion.3), channel_id=1, source_target_pairs={{0,12},{4,8},{8,4},{12,0},{1,13},{5,9},{9,5},{13,1},{2,14},{6,10},... | collective-permute-start | bytes 331784 | tf_op jit(solution)/shard_map/ppermute | solution.py:326
  190.7 11.9 %collective-permute-start.55 = (bf16[192,384]{1,0:T(8,128)(2,1)S(1)}, bf16[192,384]{1,0:T(8,128)(2,1)S(1)}, u32[]{:S(2)}, u32[]{:S(2)}) collective-permute-start(bf16[192,384]{1,0:T(8,128)(2,1)S(1)} %get-tuple-element.109), channel_id=1, source_target_pairs={{0,12},{4,8},{8,4},{12,0},{1,13},{5,9},{9,5},{13,1},{2,14},{6,10},... | collective-permute-start | bytes 442376 | tf_op jit(solution)/shard_map/ppermute | solution.py:326
  193.7 12.7 %collective-permute-start.57 = (bf16[192,384]{1,0:T(8,128)(2,1)S(1)}, bf16[192,384]{1,0:T(8,128)(2,1)S(1)}, u32[]{:S(2)}, u32[]{:S(2)}) collective-permute-start(bf16[192,384]{1,0:T(8,128)(2,1)S(1)} %get-tuple-element.110), channel_id=1, source_target_pairs={{0,4},{4,0},{8,12},{12,8},{1,5},{5,1},{9,13},{13,9},{2,6},{6,2},{1... | collective-permute-start | bytes 442376 | tf_op jit(solution)/shard_map/ppermute | solution.py:326
  197.4 17.0 %collective-permute-start.56 = (bf16[192,384]{1,0:T(8,128)(2,1)S(1)}, bf16[192,384]{1,0:T(8,128)(2,1)S(1)}, u32[]{:S(2)}, u32[]{:S(2)}) collective-permute-start(bf16[192,384]{1,0:T(8,128)(2,1)S(1)} %get-tuple-element.111), channel_id=1, source_target_pairs={{0,8},{4,12},{8,0},{12,4},{1,9},{5,13},{9,1},{13,5},{2,10},{6,14},... | collective-permute-start | bytes 442376 | tf_op jit(solution)/shard_map/ppermute | solution.py:326
  202.6 12.0 %collective-permute-start.48 = (bf16[96,768]{1,0:T(8,128)(2,1)S(1)}, bf16[96,768]{1,0:T(8,128)(2,1)S(1)}, u32[]{:S(2)}, u32[]{:S(2)}) collective-permute-start(bf16[96,768]{1,0:T(8,128)(2,1)S(1)} %get-tuple-element.116), channel_id=1, source_target_pairs={{0,12},{4,8},{8,4},{12,0},{1,13},{5,9},{9,5},{13,1},{2,14},{6,10},... | collective-permute-start | bytes 442376 | tf_op jit(solution)/shard_map/ppermute | solution.py:326
  206.4 8.2 %collective-permute-start.50 = (bf16[96,768]{1,0:T(8,128)(2,1)S(1)}, bf16[96,768]{1,0:T(8,128)(2,1)S(1)}, u32[]{:S(2)}, u32[]{:S(2)}) collective-permute-start(bf16[96,768]{1,0:T(8,128)(2,1)S(1)} %get-tuple-element.117), channel_id=1, source_target_pairs={{0,4},{4,0},{8,12},{12,8},{1,5},{5,1},{9,13},{13,9},{2,6},{6,2},{1... | collective-permute-start | bytes 442376 | tf_op jit(solution)/shard_map/ppermute | solution.py:326
  214.5 10.0 %collective-permute-start.21 = (bf16[2,256,768]{2,1,0:T(8,128)(2,1)S(1)}, bf16[2,256,768]{2,1,0:T(8,128)(2,1)S(1)}, u32[]{:S(2)}, u32[]{:S(2)}) collective-permute-start(bf16[2,256,768]{2,1,0:T(8,128)(2,1)S(1)} %slice_bitcast_fusion.2), channel_id=1, source_target_pairs={{0,1},{1,0},{2,3},{3,2},{4,5},{5,4},{6,7},{7,6},{8,9},{9,8},{10,11... | collective-permute-start | bytes 2359304 | tf_op jit(solution)/shard_map/ppermute | solution.py:326
  214.6 63.7 %collective-permute-start.60 = (bf16[192,384]{1,0:T(8,128)(2,1)S(1)}, bf16[192,384]{1,0:T(8,128)(2,1)S(1)}, u32[]{:S(2)}, u32[]{:S(2)}) collective-permute-start(bf16[192,384]{1,0:T(8,128)(2,1)S(1)} %add_convert_fusion.1), channel_id=1, source_target_pairs={{0,4},{4,0},{8,12},{12,8},{1,5},{5,1},{9,13},{13,9},{2,6},{6,2},{1... | collective-permute-start | bytes 442376 | tf_op jit(solution)/shard_map/ppermute | solution.py:326
  220.5 60.2 %collective-permute-start.59 = (bf16[192,384]{1,0:T(8,128)(2,1)S(1)}, bf16[192,384]{1,0:T(8,128)(2,1)S(1)}, u32[]{:S(2)}, u32[]{:S(2)}) collective-permute-start(bf16[192,384]{1,0:T(8,128)(2,1)S(1)} %add_convert_fusion.1), channel_id=1, source_target_pairs={{0,8},{4,12},{8,0},{12,4},{1,9},{5,13},{9,1},{13,5},{2,10},{6,14},... | collective-permute-start | bytes 442376 | tf_op jit(solution)/shard_map/ppermute | solution.py:326
  222.1 12.1 %collective-permute-start.24 = (bf16[2,128,768]{2,1,0:T(8,128)(2,1)S(1)}, bf16[2,128,768]{2,1,0:T(8,128)(2,1)S(1)}, u32[]{:S(2)}, u32[]{:S(2)}) collective-permute-start(bf16[2,128,768]{2,1,0:T(8,128)(2,1)S(1)} %fusion.22), channel_id=1, source_target_pairs={{0,2},{1,3},{2,0},{3,1},{4,6},{5,7},{6,4},{7,5},{8,10},{9,11},{10,... | collective-permute-start | bytes 1179656 | tf_op jit(solution)/shard_map/ppermute | solution.py:326
  223.0 26.5 %collective-permute-start.17 = (bf16[2,128,768]{2,1,0:T(8,128)(2,1)S(1)}, bf16[2,128,768]{2,1,0:T(8,128)(2,1)S(1)}, u32[]{:S(2)}, u32[]{:S(2)}) collective-permute-start(bf16[2,128,768]{2,1,0:T(8,128)(2,1)S(1)} %fusion.20), channel_id=1, source_target_pairs={{0,2},{1,3},{2,0},{3,1},{4,6},{5,7},{6,4},{7,5},{8,10},{9,11},{10,... | collective-permute-start | bytes 1179656 | tf_op jit(solution)/shard_map/ppermute | solution.py:326
  224.8 24.3 %collective-permute-start.22 = (bf16[2,128,768]{2,1,0:T(8,128)(2,1)S(1)}, bf16[2,128,768]{2,1,0:T(8,128)(2,1)S(1)}, u32[]{:S(2)}, u32[]{:S(2)}) collective-permute-start(bf16[2,128,768]{2,1,0:T(8,128)(2,1)S(1)} %fusion.21), channel_id=1, source_target_pairs={{0,2},{1,3},{2,0},{3,1},{4,6},{5,7},{6,4},{7,5},{8,10},{9,11},{10,... | collective-permute-start | bytes 1179656 | tf_op jit(solution)/shard_map/ppermute | solution.py:326
  234.4 18.0 %collective-permute-start.27 = (bf16[128,768]{1,0:T(8,128)(2,1)S(1)}, bf16[128,768]{1,0:T(8,128)(2,1)S(1)}, u32[]{:S(2)}, u32[]{:S(2)}) collective-permute-start(bf16[128,768]{1,0:T(8,128)(2,1)S(1)} %get-tuple-element.128), channel_id=1, source_target_pairs={{0,12},{4,8},{8,4},{12,0},{1,13},{5,9},{9,5},{13,1},{2,14},{6,10},... | collective-permute-start | bytes 589832 | tf_op jit(solution)/shard_map/ppermute | solution.py:326
  249.0 7.4 %collective-permute-start.25 = (bf16[128,768]{1,0:T(8,128)(2,1)S(1)}, bf16[128,768]{1,0:T(8,128)(2,1)S(1)}, u32[]{:S(2)}, u32[]{:S(2)}) collective-permute-start(bf16[128,768]{1,0:T(8,128)(2,1)S(1)} %get-tuple-element.129), channel_id=1, source_target_pairs={{0,4},{4,0},{8,12},{12,8},{1,5},{5,1},{9,13},{13,9},{2,6},{6,2},{1... | collective-permute-start | bytes 589832 | tf_op jit(solution)/shard_map/ppermute | solution.py:326
  249.5 20.0 %collective-permute-start.26 = (bf16[128,768]{1,0:T(8,128)(2,1)S(1)}, bf16[128,768]{1,0:T(8,128)(2,1)S(1)}, u32[]{:S(2)}, u32[]{:S(2)}) collective-permute-start(bf16[128,768]{1,0:T(8,128)(2,1)S(1)} %fusion.27), channel_id=1, source_target_pairs={{0,8},{4,12},{8,0},{12,4},{1,9},{5,13},{9,1},{13,5},{2,10},{6,14},... | collective-permute-start | bytes 589832 | tf_op jit(solution)/shard_map/ppermute | solution.py:326
  252.4 28.7 %collective-permute-start.58 = (bf16[192,384]{1,0:T(8,128)(2,1)S(1)}, bf16[192,384]{1,0:T(8,128)(2,1)S(1)}, u32[]{:S(2)}, u32[]{:S(2)}) collective-permute-start(bf16[192,384]{1,0:T(8,128)(2,1)S(1)} %add_convert_fusion.1), channel_id=1, source_target_pairs={{0,12},{4,8},{8,4},{12,0},{1,13},{5,9},{9,5},{13,1},{2,14},{6,10},... | collective-permute-start | bytes 442376 | tf_op jit(solution)/shard_map/ppermute | solution.py:326
  256.4 18.1 %collective-permute-start.18 = (bf16[128,768]{1,0:T(8,128)(2,1)S(1)}, bf16[128,768]{1,0:T(8,128)(2,1)S(1)}, u32[]{:S(2)}, u32[]{:S(2)}) collective-permute-start(bf16[128,768]{1,0:T(8,128)(2,1)S(1)} %fusion.26), channel_id=1, source_target_pairs={{0,8},{4,12},{8,0},{12,4},{1,9},{5,13},{9,1},{13,5},{2,10},{6,14},... | collective-permute-start | bytes 589832 | tf_op jit(solution)/shard_map/ppermute | solution.py:326
  270.3 7.8 %collective-permute-start.28 = (bf16[2,128,768]{2,1,0:T(8,128)(2,1)S(1)}, bf16[2,128,768]{2,1,0:T(8,128)(2,1)S(1)}, u32[]{:S(2)}, u32[]{:S(2)}) collective-permute-start(bf16[2,128,768]{2,1,0:T(8,128)(2,1)S(1)} %fusion.7), channel_id=1, source_target_pairs={{0,2},{1,3},{2,0},{3,1},{4,6},{5,7},{6,4},{7,5},{8,10},{9,11},{10,... | collective-permute-start | bytes 1179656 | tf_op jit(solution)/shard_map/ppermute | solution.py:326
  274.5 6.7 %collective-permute-start.53 = (bf16[96,768]{1,0:T(8,128)(2,1)S(1)}, bf16[96,768]{1,0:T(8,128)(2,1)S(1)}, u32[]{:S(2)}, u32[]{:S(2)}) collective-permute-start(bf16[96,768]{1,0:T(8,128)(2,1)S(1)} %add_convert_fusion.2), channel_id=1, source_target_pairs={{0,4},{4,0},{8,12},{12,8},{1,5},{5,1},{9,13},{13,9},{2,6},{6,2},{1... | collective-permute-start | bytes 442376 | tf_op jit(solution)/shard_map/ppermute | solution.py:326
  278.2 10.2 %collective-permute-start.52 = (bf16[96,768]{1,0:T(8,128)(2,1)S(1)}, bf16[96,768]{1,0:T(8,128)(2,1)S(1)}, u32[]{:S(2)}, u32[]{:S(2)}) collective-permute-start(bf16[96,768]{1,0:T(8,128)(2,1)S(1)} %add_convert_fusion.2), channel_id=1, source_target_pairs={{0,8},{4,12},{8,0},{12,4},{1,9},{5,13},{9,1},{13,5},{2,10},{6,14},... | collective-permute-start | bytes 442376 | tf_op jit(solution)/shard_map/ppermute | solution.py:326
  278.3 10.1 %collective-permute-start.51 = (bf16[96,768]{1,0:T(8,128)(2,1)S(1)}, bf16[96,768]{1,0:T(8,128)(2,1)S(1)}, u32[]{:S(2)}, u32[]{:S(2)}) collective-permute-start(bf16[96,768]{1,0:T(8,128)(2,1)S(1)} %add_convert_fusion.2), channel_id=1, source_target_pairs={{0,12},{4,8},{8,4},{12,0},{1,13},{5,9},{9,5},{13,1},{2,14},{6,10},... | collective-permute-start | bytes 442376 | tf_op jit(solution)/shard_map/ppermute | solution.py:326
  280.6 7.8 %collective-permute-start.19 = (bf16[2,128,768]{2,1,0:T(8,128)(2,1)S(1)}, bf16[2,128,768]{2,1,0:T(8,128)(2,1)S(1)}, u32[]{:S(2)}, u32[]{:S(2)}) collective-permute-start(bf16[2,128,768]{2,1,0:T(8,128)(2,1)S(1)} %pad_maximum_fusion.11), channel_id=1, source_target_pairs={{0,2},{1,3},{2,0},{3,1},{4,6},{5,7},{6,4},{7,5},{8,10},{9,11},{10,... | collective-permute-start | bytes 1179656 | tf_op jit(solution)/shard_map/ppermute | solution.py:326
  281.1 9.7 %collective-permute-start.29 = (bf16[2,2,128,768]{3,2,1,0:T(8,128)(2,1)S(1)}, bf16[2,2,128,768]{3,2,1,0:T(8,128)(2,1)S(1)}, u32[]{:S(2)}, u32[]{:S(2)}) collective-permute-start(bf16[2,2,128,768]{3,2,1,0:T(8,128)(2,1)S(1)} %pad_maximum_fusion.5), channel_id=1, source_target_pairs={{0,1},{1,0},{2,3},{3,2},{4,5},{5,4},{6,7},{7,6},{8,9},{9,8},{10,11... | collective-permute-start | bytes 2359304 | tf_op jit(solution)/shard_map/ppermute | solution.py:326
  (58 other events, 608.3 us)

commit v2 on v1

v2 whole, which is shorter than its diff:
```python
import functools

import jax
import jax.numpy as jnp
from jax import lax
from jax.experimental import pallas as pl
from jax.experimental.pallas import tpu as pltpu
from jax.sharding import PartitionSpec as P

HEAD = 64
ROT = 16
HALF = ROT // 2
EPS = 1e-5
NEG = -1e30
STEP = 256
F32 = jnp.float32
BF16 = jnp.bfloat16
MIB = 1024 * 1024


def mm(a, b, ca=1, cb=0):
    return lax.dot_general(a, b, (((ca,), (cb,)), ((), ())), preferred_element_type=F32)


def params(mib):
    return pltpu.CompilerParams(vmem_limit_bytes=mib * MIB)


def cost(flops, moved, exps=0):
    return pl.CostEstimate(flops=int(flops), bytes_accessed=int(moved), transcendentals=int(exps))


def xhat_of(x):
    width = x.shape[-1]
    centred = x - jnp.sum(x, axis=-1, keepdims=True) * (1.0 / width)
    spread = jnp.sum(centred * centred, axis=-1, keepdims=True) * (1.0 / width)
    inv = lax.rsqrt(spread + EPS)
    return centred * inv, inv


def row_of(ref):
    return ref[...].reshape(1, -1)


def shape(*dims):
    return jax.ShapeDtypeStruct(dims, F32)


def low_shape(*dims):
    return jax.ShapeDtypeStruct(dims, BF16)


def norm_own_kernel(at, xa, xb, ga, gb, fz, fx, fc, ta, tb, s1, b1, s2, b2,
                    n1_ref, n2_ref, xhat_ref, g_ref, trig_ref, x):
    i = pl.program_id(0)
    q = xa.shape[1]

    @pl.when(i < 2)
    def _():
        x[:q, :] = xa[0]
        x[q:, :] = xb[0]
        g_ref[:q, :] = ga[0]
        g_ref[q:, :] = gb[0]

    @pl.when(i == 2)
    def _():
        x[:q, :] = fz[0]
        x[q:, :] = fx[0]
        g_ref[:q, :] = fz[1]
        g_ref[q:, :] = fx[1]

    @pl.when(i == 3)
    def _():
        x[:q, :] = fc[0, 0]
        x[q:, :] = fc[1, 0]
        g_ref[:q, :] = fc[0, 1]
        g_ref[q:, :] = fc[1, 1]

    trig_ref[:, :q] = ta[0]
    trig_ref[:, q:] = tb[0]
    xhat, _ = xhat_of(x[...].astype(F32))
    xhat_ref[...] = xhat.astype(BF16)
    n1_ref[...] = (xhat * row_of(s1) + row_of(b1)).astype(BF16)
    n2_ref[...] = (xhat * row_of(s2) + row_of(b2)).astype(BF16)


def norm_other_kernel(at, nz, nx, nc, ta, tb, s1, b1, n1_ref, xhat_ref, trig_ref, x):
    i = pl.program_id(0)
    q = nz.shape[1]
    b = i // 2

    @pl.when(i % 2 == 0)
    def _():
        x[:q, :] = nz[b]
        x[q:, :] = nx[b]

    @pl.when(i % 2 == 1)
    def _():
        x[:q, :] = nc[0, b]
        x[q:, :] = nc[1, b]

    trig_ref[:, :q] = ta[0]
    trig_ref[:, q:] = tb[0]
    xhat, _ = xhat_of(x[...].astype(F32))
    xhat_ref[...] = xhat.astype(BF16)
    n1_ref[...] = (xhat * row_of(s1) + row_of(b1)).astype(BF16)


def norms(at, own, arrays, trig, vectors):
    width = vectors[0].shape[0]
    rows, q = 4 * STEP, STEP // 2
    tall = trig.shape[1]
    first = 0 if own else 1

    def pick(high):
        def place(i, at):
            block = at[1] ^ (first + 2 * (i // 2))
            return (at[0], 0, block * 4 + (at[2] ^ (i % 2 + high)))

        return pl.BlockSpec((1, tall, q), place)

    def piece(high):
        return pl.BlockSpec(
            (1, q, width), lambda i, at: (at[0], at[2] ^ (jnp.minimum(i, 1) + high), 0)
        )

    def whole(v):
        return pl.BlockSpec(v.shape, lambda i, at: (0,) * v.ndim)

    row = pl.BlockSpec((STEP, width), lambda i, at: (i, 0))
    out_trig = pl.BlockSpec((tall, STEP), lambda i, at: (0, i))
    if own:
        x, g, received = arrays[0], arrays[1], arrays[2:]
        specs = [piece(0), piece(2), piece(0), piece(2)]
        operands = [x, x, g, g]
        kernel, count = norm_own_kernel, 4
    else:
        received, specs, operands = arrays, [], []
        kernel, count = norm_other_kernel, 2
    specs += [whole(v) for v in received] + [pick(0), pick(2)] + [whole(v) for v in vectors]
    operands += [*received, trig, trig, *vectors]
    return pl.pallas_call(
        kernel,
        grid_spec=pltpu.PrefetchScalarGridSpec(
            num_scalar_prefetch=1,
            grid=(rows // STEP,),
            in_specs=specs,
            out_specs=[row] * count + [out_trig],
            scratch_shapes=[pltpu.VMEM((STEP, width), BF16)],
        ),
        out_shape=[low_shape(rows, width)] * count + [shape(tall, rows)],
        compiler_params=params(24),
        cost_estimate=cost(0, 6 * rows * width),
    )(at, *operands)


def project_kernel(n1o, n1x, to, tx, g_ref, w_ref, b_ref, k_ref, v_ref, q_ref, do_ref, bias):
    i = pl.program_id(0)
    wide = k_ref.shape[0]

    @pl.when(i == 0)
    def _():
        for j in range(3):
            line = jnp.broadcast_to(b_ref[j : j + 1, :], (8, wide))
            bias[j * wide : (j + 1) * wide, :] = line.T[:, 0:1]

    def rotated(ref, mixed, trig, factor):
        cosine, sine = trig[:HALF], trig[HALF:ROT]
        for h in range(0, wide, HEAD):
            a, b = mixed[h : h + HALF], mixed[h + HALF : h + ROT]
            turned = jnp.concatenate([a * cosine - b * sine, b * cosine + a * sine], axis=0)
            ref[h : h + ROT, :] = turned.astype(BF16) * factor
            ref[h + ROT : h + HEAD, :] = mixed[h + ROT : h + HEAD].astype(BF16) * factor

    def keys_values(mixed, trig):
        rotated(k_ref, mixed[:wide], trig, BF16(1.0))
        v_ref[...] = mixed[wide:].astype(BF16)

    @pl.when(i < 4)
    def _():
        trig = to[...]
        mixed = mm(w_ref[: 3 * wide, :], n1o[...], 1, 1) + bias[...]
        rotated(q_ref, mixed[:wide], trig, BF16(HEAD**-0.5))
        keys_values(mixed[wide:], trig)
        do_ref[...] = mm(w_ref[3 * wide :, :], g_ref[...], 1, 1).astype(BF16)

    @pl.when(i >= 4)
    def _():
        mixed = mm(w_ref[wide : 3 * wide, :], n1x[...], 1, 1) + bias[wide:, :]
        keys_values(mixed, tx[...])


def project(n1_own, n1_other, trig_own, trig_other, g, weights, bias):
    rows, width = n1_own.shape
    wide = bias.shape[1]
    tall = trig_own.shape[0]

    def own(i):
        return jnp.minimum(i, 3)

    def other(i):
        return jnp.maximum(i - 4, 0)

    col = pl.BlockSpec((wide, STEP), lambda i: (0, i))
    own_col = pl.BlockSpec((wide, STEP), lambda i: (0, own(i)))
    return pl.pallas_call(
        project_kernel,
        grid=(8,),
        in_specs=[
            pl.BlockSpec((STEP, width), lambda i: (own(i), 0)),
            pl.BlockSpec((STEP, width), lambda i: (other(i), 0)),
            pl.BlockSpec((tall, STEP), lambda i: (0, own(i))),
            pl.BlockSpec((tall, STEP), lambda i: (0, other(i))),
            pl.BlockSpec((STEP, width), lambda i: (own(i), 0)),
            pl.BlockSpec((4 * wide, width), lambda i: (0, 0)),
            pl.BlockSpec((3, wide), lambda i: (0, 0)),
        ],
        out_specs=[col, col, own_col, own_col],
        out_shape=[low_shape(wide, 2 * rows)] * 2 + [low_shape(wide, rows)] * 2,
        scratch_shapes=[pltpu.VMEM((3 * wide, 1), F32)],
        compiler_params=params(24),
        cost_estimate=cost(12 * rows * width * wide, 12 * rows * width),
    )(n1_own, n1_other, trig_own, trig_other, g, weights, bias)


def attention_kernel(after, q_ref, do_ref, k_ref, v_ref, tq_ref, to_ref, tx_ref,
                     o_ref, dq_ref, dk_ref, dv_ref, kn, vn, kp, dk, dv, es, dps):
    i = pl.program_id(0)
    length = k_ref.shape[1]
    half = length // 2
    chunk = STEP
    steps = length // chunk

    @pl.when(i == 0)
    def _():
        kn[...] = k_ref[...].T
        vn[...] = v_ref[...].T
        kp[:half, :] = to_ref[ROT:, :].T[:, 0:1]
        kp[half:, :] = tx_ref[ROT:, :].T[:, 0:1]
        dk[...] = jnp.zeros_like(dk)
        dv[...] = jnp.zeros_like(dv)

    qt = q_ref[...]
    dot = do_ref[...]
    qn = qt.T
    don = dot.T
    qpos = tq_ref[ROT : ROT + 1, :]
    lanes = qt.shape[1]
    fold = (chunk // 8, 8, lanes)

    top = jnp.full((8, lanes), NEG, F32)
    for j in range(steps):
        here = slice(j * chunk, (j + 1) * chunk)
        s = mm(kn[here, :], qt)
        s = jnp.where(kp[here, :] <= qpos, s, NEG)
        es[here, :] = s
        top = jnp.maximum(top, jnp.max(s.reshape(fold), axis=0))
    top = jnp.max(top, axis=0, keepdims=True)

    total = jnp.zeros((8, lanes), F32)
    inner = jnp.zeros((8, lanes), F32)
    for j in range(steps):
        here = slice(j * chunk, (j + 1) * chunk)
        e = jnp.exp(es[here, :] - top)
        dp = mm(vn[here, :], dot)
        es[here, :] = e
        dps[here, :] = dp
        total = total + jnp.sum(e.reshape(fold), axis=0)
        inner = inner + jnp.sum((e * dp).reshape(fold), axis=0)
    share = 1.0 / jnp.sum(total, axis=0, keepdims=True)
    inner = jnp.sum(inner, axis=0, keepdims=True) * share

    ot = jnp.zeros((HEAD, lanes), F32)
    dqt = jnp.zeros((HEAD, lanes), F32)
    for j in range(steps):
        here = slice(j * chunk, (j + 1) * chunk)
        p = es[here, :] * share
        ds = (p * (dps[here, :] - inner)).astype(BF16)
        p = p.astype(BF16)
        dv[here, :] += mm(p, don)
        dk[here, :] += mm(ds, qn)
        ot = ot + mm(v_ref[:, here], p)
        dqt = dqt + mm(k_ref[:, here], ds)
    o_ref[...] = ot.astype(BF16)

    def unrotated(grad, trig):
        cosine, sine = trig[:HALF], trig[HALF:ROT]
        a, b = grad[:HALF], grad[HALF:ROT]
        turned = jnp.concatenate([a * cosine + b * sine, b * cosine - a * sine], axis=0)
        return turned.astype(BF16), grad[ROT:].astype(BF16)

    dq_ref[:ROT, :], dq_ref[ROT:, :] = unrotated(dqt * (HEAD**-0.5), tq_ref[...])

    @pl.when(i == pl.num_programs(0) - 1)
    def _():
        grad = dk[...].T
        dk_ref[:ROT, :half], dk_ref[ROT:, :half] = unrotated(grad[:, :half], to_ref[...])
        dk_ref[:ROT, half:], dk_ref[ROT:, half:] = unrotated(grad[:, half:], tx_ref[...])
        dv_ref[...] = dv[...].T.astype(BF16)


def attention(h, after, qt, dot, kt, vt, trig_own, trig_other):
    rows, length = qt.shape[1], kt.shape[1]
    lanes = STEP
    tall = trig_own.shape[0]
    q_spec = pl.BlockSpec((HEAD, lanes), lambda i: (h, i))
    k_spec = pl.BlockSpec((HEAD, length), lambda i: (h, 0))
    trig_spec = pl.BlockSpec((tall, rows), lambda i: (0, 0))
    return pl.pallas_call(
        attention_kernel,
        grid=(rows // lanes,),
        in_specs=[pl.BlockSpec(memory_space=pl.ANY), q_spec, q_spec, k_spec, k_spec,
                  pl.BlockSpec((tall, lanes), lambda i: (0, i)), trig_spec, trig_spec],
        out_specs=[pl.BlockSpec((HEAD, lanes), lambda i: (0, i))] * 2
        + [pl.BlockSpec((HEAD, length), lambda i: (0, 0))] * 2,
        out_shape=[low_shape(HEAD, rows)] * 2 + [low_shape(HEAD, length)] * 2,
        scratch_shapes=[
            pltpu.VMEM((length, HEAD), BF16),
            pltpu.VMEM((length, HEAD), BF16),
            pltpu.VMEM((length, 1), F32),
            pltpu.VMEM((length, HEAD), F32),
            pltpu.VMEM((length, HEAD), F32),
            pltpu.VMEM((length, lanes), F32),
            pltpu.VMEM((length, lanes), F32),
        ],
        compiler_params=params(32),
        cost_estimate=cost(40 * rows * length * HEAD, 16 * HEAD * length, rows * length),
    )(after, qt, dot, kt, vt, trig_own, trig_own, trig_other)


def forward_kernel(split, at, n2_ref, g_ref, xhat_ref, up_ref, bias_ref, down_ref, s2_ref,
                   ff_ref, a_ref, small_ref, first_ref, second_ref, *scratch):
    i = pl.program_id(0)
    up_part, down_part = scratch if split else (first_ref, second_ref)

    @pl.when(i == 0)
    def _():
        up_part[...] = jnp.zeros_like(up_part)
        down_part[...] = jnp.zeros_like(down_part)
        small_ref[...] = jnp.zeros_like(small_ref)

    n2, g = n2_ref[...], g_ref[...]
    up = mm(n2, up_ref[...]) + row_of(bias_ref)
    cdf = 0.5 + 0.5 * lax.erf(up * (0.5**0.5))
    act = (up * cdf).astype(BF16)
    slope = cdf + up * (jnp.exp(up * up * -0.5) * 0.3989422804014327)
    up_grad = (mm(g, down_ref[...], 1, 1) * slope).astype(BF16)
    ff_ref[...] = mm(act, down_ref[...]).astype(BF16)
    second = mm(up_grad, up_ref[...], 1, 1)
    up_part[...] += mm(n2, up_grad, 0, 0)
    down_part[...] += mm(act, g, 0, 0)
    a_ref[...] = (second * row_of(s2_ref)).astype(BF16)
    small_ref[0:1, :] += jnp.sum(up_grad.astype(F32), axis=0, keepdims=True)
    small_ref[1:2, :] += jnp.sum(g.astype(F32), axis=0, keepdims=True)
    small_ref[2:3, :] += jnp.sum(second * xhat_ref[...].astype(F32), axis=0, keepdims=True)
    small_ref[3:4, :] += jnp.sum(second, axis=0, keepdims=True)

    if split:
        half = up_part.shape[0] // 2

        @pl.when(i == pl.num_programs(0) - 1)
        def _():
            for ref, f in ((first_ref, at[3]), (second_ref, 1 - at[3])):
                piece = pl.ds(pl.multiple_of(f * half, 128), half)
                ref[:half, :] = up_part[piece, :].astype(ref.dtype)
                ref[half:, :half] = down_part[:half, piece].astype(ref.dtype)
                ref[half:, half:] = down_part[half:, piece].astype(ref.dtype)


def feed_forward(split, at, n2, g, xhat, up, bias, down, scale):
    rows, width = n2.shape
    hidden = up.shape[1]
    row = pl.BlockSpec((STEP, width), lambda i, at: (i, 0))

    def whole(*dims):
        return pl.BlockSpec(dims, lambda i, at: (0,) * len(dims))

    if split:
        assert width == hidden
        parts = [shape(width, hidden), low_shape(width, hidden)]
    else:
        parts = [shape(width, hidden), shape(hidden, width)]
    return pl.pallas_call(
        functools.partial(forward_kernel, split),
        grid_spec=pltpu.PrefetchScalarGridSpec(
            num_scalar_prefetch=1,
            grid=(rows // STEP,),
            in_specs=[row, row, row, whole(width, hidden), whole(hidden), whole(hidden, width),
                      whole(width)],
            out_specs=[row, row, whole(8, width)] + [whole(*p.shape) for p in parts],
            scratch_shapes=[pltpu.VMEM((width, hidden), F32), pltpu.VMEM((hidden, width), F32)]
            if split
            else [],
        ),
        out_shape=[low_shape(rows, width)] * 2 + [shape(8, width)] + parts,
        compiler_params=params(40),
        cost_estimate=cost(12 * rows * width * hidden, 16 * MIB, 2 * rows * hidden),
    )(at, n2, g, xhat, up, bias, down, scale)


def back_kernel(split, heads, at, *refs):
    o, dq, dk, dv = (refs[j * heads : (j + 1) * heads] for j in range(4))
    (n1o, n1x, xho, xhx, g_ref, ff_ref, a2_ref, w_ref, s1_ref, small_ff,
     keep_ref, send_ref, first_ref, second_ref, mix, out, small) = refs[4 * heads :]
    i = pl.program_id(0)
    wide = heads * HEAD

    @pl.when(i == 0)
    def _():
        mix[...] = jnp.zeros_like(mix)
        out[...] = jnp.zeros_like(out)
        small[...] = jnp.zeros_like(small)

    def emit(v):
        @pl.when(i % 2 == 0)
        def _():
            keep_ref[0] = v.astype(BF16)

        @pl.when(i % 2 == 1)
        def _():
            send_ref[0] = v.astype(BF16)

    @pl.when(i < 4)
    def _():
        ot = jnp.concatenate([r[...] for r in o], axis=0)
        emit(mm(ot, w_ref[3 * wide :, :], 0, 0) + ff_ref[...].astype(F32))
        out[...] += mm(ot, g_ref[...])

    def through(grad, low, n1, xhat, extra):
        rows = slice(low, 3 * wide)
        first = mm(grad, w_ref[rows, :], 0, 0)
        a = first * row_of(s1_ref)
        emit(a if extra is None else a + extra)
        mix[rows, :] += mm(grad, n1)
        small[0:1, :] += jnp.sum(first * xhat.astype(F32), axis=0, keepdims=True)
        small[1:2, :] += jnp.sum(first, axis=0, keepdims=True)
        ones = jnp.ones((8, grad.shape[1]), BF16)
        small[6:7, low : 3 * wide] += mm(ones, grad, 1, 1)[0:1]

    @pl.when((i >= 4) & (i < 8))
    def _():
        grad = jnp.concatenate([r[...] for r in (*dq, *dk, *dv)], axis=0)
        through(grad, 0, n1o[...], xho[...], a2_ref[...].astype(F32))

    @pl.when(i >= 8)
    def _():
        grad = jnp.concatenate([r[...] for r in (*dk, *dv)], axis=0)
        through(grad, wide, n1x[...], xhx[...], None)

    @pl.when(i == 11)
    def _():
        small[2:4, :] = small_ff[2:4, :]
        small[4:6, :] = small_ff[0:2, :]
        if split:
            half = mix.shape[1] // 2
            vectors = small[...].astype(BF16)
            for ref, f in ((first_ref, at[3]), (second_ref, 1 - at[3])):
                piece = pl.ds(pl.multiple_of(f * half, 128), half)
                ref[: 3 * wide, :] = mix[:, piece].astype(ref.dtype)
                ref[3 * wide : 4 * wide, :] = out[:, piece].astype(ref.dtype)
                both = jnp.concatenate([vectors[:, :half], vectors[:, half:]], axis=0)
                ref[4 * wide : 4 * wide + 16, :] = both.astype(ref.dtype)
                ref[4 * wide + 16 :, :] = jnp.zeros((48, half), ref.dtype)
        else:
            first_ref[: 3 * wide, :] = mix[...]
            first_ref[3 * wide :, :] = out[...]
            second_ref[...] = small[...]


def back(split, at, o, dq, dk, dv, n1_own, n1_other, xhat_own, xhat_other, g, ff, a2, weights,
         scale, small_ff):
    rows, width = g.shape
    heads = len(o)
    wide = heads * HEAD

    def branch(i, at):
        return jnp.minimum(i, 3)

    def own(i, at):
        return jnp.clip(i - 4, 0, 3)

    def other(i, at):
        return jnp.maximum(i - 8, 0)

    def key(i, at):
        return jnp.maximum(i - 4, 0)

    def row(of):
        return pl.BlockSpec((STEP, width), lambda i, at: (of(i, at), 0))

    def col(of):
        return [pl.BlockSpec((HEAD, STEP), lambda i, at: (0, of(i, at)))] * heads

    def whole(*dims):
        return pl.BlockSpec(dims, lambda i, at: (0,) * len(dims))

    def slot(i, at):
        b = jnp.maximum(i - 4, 0) // 2
        return (jnp.where(i < 4, 4 * (1 - i // 2), jnp.where(b == 0, 5, b)), 0, 0)

    half = width // 2
    if split:
        parts = [shape(4 * wide + 64, half), low_shape(4 * wide + 64, half)]
    else:
        parts = [shape(4 * wide, width), shape(8, width)]
    slots = pl.BlockSpec((1, STEP, width), slot)
    return pl.pallas_call(
        functools.partial(back_kernel, split, heads),
        grid_spec=pltpu.PrefetchScalarGridSpec(
            num_scalar_prefetch=1,
            grid=(12,),
            in_specs=col(branch) + col(own) + col(key) + col(key)
            + [row(own), row(other), row(own), row(other), row(branch), row(branch), row(own),
               whole(4 * wide, width), whole(width), whole(8, width)],
            out_specs=[slots, slots] + [whole(*p.shape) for p in parts],
            scratch_shapes=[pltpu.VMEM((3 * wide, width), F32), pltpu.VMEM((wide, width), F32),
                            pltpu.VMEM((8, width), F32)],
        ),
        out_shape=[low_shape(6, STEP, width)] * 2 + parts,
        compiler_params=params(32),
        cost_estimate=cost(28 * rows * width * wide, 20 * MIB),
    )(at, *o, *dq, *dk, *dv, n1_own, n1_other, xhat_own, xhat_other, g, ff, a2, weights, scale,
      small_ff)


def finish_kernel(at, pair, core, x_ref, g_ref, bias_a, bias_b, out_ref, grad_ref):
    j = at[2] ^ pl.program_id(1)

    def write(part):
        bias = row_of(bias_a) + row_of(bias_b)
        out_ref[0] = x_ref[0].astype(F32) + part[0, 0, 0].astype(F32) + bias
        grad_ref[0] = g_ref[0].astype(F32) + part[0, 1, 0].astype(F32)

    @pl.when(j % 2 == 0)
    def _():
        write(pair)

    @pl.when(j % 2 == 1)
    def _():
        write(core)


def finish(at, pair, core, x, g, bias_a, bias_b):
    seqs, block, width = x.shape
    q = block // 4

    def place(i, j, at):
        return (i, j, 0)

    piece = pl.BlockSpec(
        (1, 2, 1, q, width), lambda i, j, at: ((at[2] ^ j) // 2, 0, at[0] ^ i, 0, 0)
    )
    rows = pl.BlockSpec((1, q, width), place)
    vec = pl.BlockSpec((width,), lambda i, j, at: (0,))
    return pl.pallas_call(
        finish_kernel,
        grid_spec=pltpu.PrefetchScalarGridSpec(
            num_scalar_prefetch=1,
            grid=(seqs, 4),
            in_specs=[piece, piece, rows, rows, vec, vec],
            out_specs=[rows, rows],
        ),
        out_shape=[shape(seqs, block, width)] * 2,
        compiler_params=params(24),
        cost_estimate=cost(0, 16 * seqs * block * width),
    )(at, pair, core, x, g, bias_a, bias_b)


def swap(v, axis, size, distance):
    return lax.ppermute(v, axis, [(i, i ^ distance) for i in range(size)])


def by_xor(pieces, index):
    low, high = (index & 1) == 1, (index & 2) == 2
    a, b, c, d = pieces
    a, b, c, d = (jnp.where(low, b, a), jnp.where(low, a, b),
                  jnp.where(low, d, c), jnp.where(low, c, d))
    return (jnp.where(high, c, a), jnp.where(high, d, b),
            jnp.where(high, a, c), jnp.where(high, b, d))


def gather_halves(shard, size, mine, dim):
    if size != 2:
        return lax.all_gather(shard, "fsdp", axis=dim, tiled=True)
    other = swap(shard, "fsdp", 2, 1)
    first = mine == 0
    return jnp.concatenate(
        [jnp.where(first, shard, other), jnp.where(first, other, shard)], axis=dim
    )


def scatter_any(part, dim):
    return lax.psum_scatter(
        part.astype(BF16), "fsdp", scatter_dimension=dim, tiled=True
    ).astype(F32)


def sum_over_ctx(v, c):
    low, high = c % 2, c // 2
    rows = v.shape[0] // 2
    keep = lax.dynamic_slice_in_dim(v, low * rows, rows, 0)
    send = lax.dynamic_slice_in_dim(v, (1 - low) * rows, rows, 0).astype(BF16)
    v = keep + swap(send, "ctx", 4, 1).astype(F32)
    rows = rows // 2
    keep = lax.dynamic_slice_in_dim(v, high * rows, rows, 0)
    send = lax.dynamic_slice_in_dim(v, (1 - high) * rows, rows, 0).astype(BF16)
    v = (keep + swap(send, "ctx", 4, 2).astype(F32)).astype(BF16)
    pair = jnp.stack([v, swap(v, "ctx", 4, 2)])
    others = swap(pair, "ctx", 4, 1)
    return by_xor([pair[0], pair[1], others[0], others[1]], 2 * low + high)


def butterfly(v, axis_name, size):
    distance = 1
    while distance < size:
        v = v + swap(v, axis_name, size, distance)
        distance *= 2
    return v


def shards(
    sizes,
    inputs,
    positions,
    query_key_value_weight,
    query_key_value_bias,
    attention_output_weight,
    attention_output_bias,
    up_projection_weight,
    up_projection_bias,
    down_projection_weight,
    down_projection_bias,
    first_scale,
    first_shift,
    second_scale,
    second_shift,
    cotangent,
):
    fsdp = sizes["fsdp"]
    split = fsdp == 2
    seq_count, block, width = inputs.shape
    assert seq_count == 2 and sizes["ctx"] == 4 and sizes["tp"] == 4 and block == 2 * STEP
    length = positions.shape[1]
    local = query_key_value_weight.shape[2]
    heads = local // HEAD
    hidden = up_projection_weight.shape[1]
    quarter = block // 4
    f = lax.axis_index("fsdp")
    c = lax.axis_index("ctx")
    t = lax.axis_index("tp")
    s = c // 2
    at = jnp.stack([s, c, t, f]).astype(jnp.int32)

    def my_quarter(v, seq):
        return lax.dynamic_slice(v, (seq, t * quarter, 0), (1, quarter, width))

    x_mine, x_theirs = my_quarter(inputs, s), my_quarter(inputs, 1 - s)
    g_theirs = my_quarter(cotangent, 1 - s)
    far_z = swap(jnp.concatenate([x_theirs, g_theirs], axis=0), "ctx", 4, 2)
    cross = swap(x_theirs, "ctx", 4, 3)
    near = swap(x_mine, "ctx", 4, 1)

    def over_tp(v):
        v_x = swap(v, "tp", 4, 2)
        return v, v_x, swap(jnp.stack([v, v_x]), "tp", 4, 1)

    far = over_tp(far_z)
    others = over_tp(jnp.concatenate([near, cross], axis=0))

    wup = gather_halves(up_projection_weight, fsdp, f, 0)
    wdown = gather_halves(down_projection_weight, fsdp, f, 1)
    mix_shard = query_key_value_weight.transpose(1, 2, 0).reshape(3 * local, -1)
    weights = gather_halves(
        jnp.concatenate([mix_shard, attention_output_weight], axis=0), fsdp, f, 1
    )

    inverse = 10000.0 ** (-2.0 * jnp.arange(HALF, dtype=F32) / ROT)
    places = positions.astype(F32)[:, None, :]
    angles = inverse[None, :, None] * places
    trig = jnp.concatenate(
        [jnp.cos(angles), jnp.sin(angles), jnp.broadcast_to(places, angles.shape)], axis=1
    )

    n1_own, n2, xhat_own, g, trig_own = norms(
        at, True, (inputs, cotangent, *far), trig,
        (first_scale, first_shift, second_scale, second_shift),
    )
    ff, a2, small_ff, ff_first, ff_second = feed_forward(
        split, at, n2, g, xhat_own, wup, up_projection_bias, wdown, second_scale
    )
    n1_other, xhat_other, trig_other = norms(
        at, False, others, trig, (first_scale, first_shift)
    )
    kt, vt, qt, dot = project(
        n1_own, n1_other, trig_own, trig_other, g, weights, query_key_value_bias
    )
    per_head = []
    after = small_ff
    for h in range(heads):
        per_head.append(attention(h, after, qt, dot, kt, vt, trig_own, trig_other))
        after = per_head[-1][0]
    o, dq, dk, dv = zip(*per_head)
    keep, send, late_first, late_second = back(
        split, at, o, dq, dk, dv, n1_own, n1_other, xhat_own, xhat_other, g, ff, a2, weights,
        first_scale, small_ff,
    )

    half_sums = keep.astype(F32) + swap(send, "tp", 4, 1).astype(F32)
    half_sums = half_sums.reshape(6, 2, quarter, width)

    def over_x(v):
        return v[:, 0] + swap(v[:, 1].astype(BF16), "tp", 4, 2).astype(F32)

    travel = over_x(half_sums[0:4]).astype(BF16)
    far_back = swap(travel[0:2], "ctx", 4, 2).astype(F32)
    near_back = swap(travel[2], "ctx", 4, 1).astype(F32)
    cross_back = swap(travel[3], "ctx", 4, 3).astype(F32)
    stay = over_x(half_sums[4:6])
    branches = jnp.stack([stay[0], far_back[0]])
    a = jnp.stack([stay[1] + near_back, far_back[1] + cross_back])
    xhat, inv = xhat_of(jnp.concatenate([x_mine, x_theirs], axis=0).astype(F32))
    norm_grad = inv * (
        a
        - jnp.mean(a, axis=-1, keepdims=True)
        - xhat * jnp.mean(a * xhat, axis=-1, keepdims=True)
    )
    ours = jnp.stack([branches, norm_grad]).astype(BF16)
    pair = jnp.stack([ours, swap(ours, "tp", 4, 2)])
    core = swap(pair, "tp", 4, 1)
    block_out, inputs_grad = finish(
        at, pair, core, inputs, cotangent, attention_output_bias, down_projection_bias
    )

    if split:
        q = sum_over_ctx(ff_first + swap(ff_second, "fsdp", 2, 1).astype(F32), c)
        up_total = jnp.concatenate(q[:2], axis=0).astype(F32)
        down_total = jnp.concatenate(q[2:], axis=0).astype(F32)
        down_total = jnp.concatenate(
            [down_total[:, : width // 2], down_total[:, width // 2 :]], axis=0
        )
        q = sum_over_ctx(late_first + swap(late_second, "fsdp", 2, 1).astype(F32), c)
        late = jnp.concatenate(q, axis=0).astype(F32)
        small = jnp.concatenate([late[4 * local : 4 * local + 8], late[4 * local + 8 :][:8]], axis=1)
    else:
        q = sum_over_ctx(scatter_any(ff_first, 0), c)
        up_total = jnp.concatenate(q, axis=0).astype(F32)
        q = sum_over_ctx(scatter_any(ff_second, 1), c)
        down_total = jnp.concatenate(q, axis=0).astype(F32)
        q = sum_over_ctx(scatter_any(late_first, 1), c)
        late = jnp.concatenate(q, axis=0).astype(F32)
        small = butterfly(butterfly(late_second, "fsdp", fsdp), "ctx", 4)
    mix_total = late[: 3 * local].reshape(3, local, -1).transpose(2, 0, 1)
    out_total = late[3 * local : 4 * local]
    norm_small = butterfly(small, "tp", 4)
    bias_total = norm_small[5] * 0.25
    return (
        block_out,
        inputs_grad,
        mix_total,
        small[6, : 3 * local].reshape(3, local),
        out_total,
        bias_total,
        up_total,
        small[4, :hidden],
        down_total,
        bias_total,
        norm_small[0],
        norm_small[1],
        norm_small[2],
        norm_small[3],
    )


def solution(mesh):
    in_specs = (
        P("fsdp", "ctx", None),
        P("fsdp", None),
        P("fsdp", None, "tp"),
        P(None, "tp"),
        P("tp", "fsdp"),
        P(),
        P("fsdp", "tp"),
        P("tp"),
        P("tp", "fsdp"),
        P(),
        P(),
        P(),
        P(),
        P(),
        P("fsdp", "ctx", None),
    )
    out_specs = (
        P("fsdp", "ctx", None),
        P("fsdp", "ctx", None),
        P("fsdp", None, "tp"),
        P(None, "tp"),
        P("tp", "fsdp"),
        P(),
        P("fsdp", "tp"),
        P("tp"),
        P("tp", "fsdp"),
        P(),
        P(),
        P(),
        P(),
        P(),
    )
    body = functools.partial(shards, dict(mesh.shape))
    return jax.shard_map(body, mesh=mesh, in_specs=in_specs, out_specs=out_specs, check_vma=False)
```

time: 300 us -> 286 us (0.953)
  starting transfers between devices: 77.5 us -> 39.1 us
  waiting for transfers between devices: 92.3 us -> 127 us
  local copies, waits for them, and re-layouts: 42.4 us -> 15.9 us
  Pallas kernels: 50.4 us -> 73.1 us
  matrix products: 6.66 us -> 0 us
    ppermute x63 -> x30, starting transfers between devices: 77.5 us -> 39.1 us  [swap(): return lax.ppermute(v, axis, [(i, i ^ distance) for i in range(size)])]
    ppermute x63 -> x30, waiting for transfers between devices: 92.3 us -> 127 us  [swap(): return lax.ppermute(v, axis, [(i, i ^ distance) for i in range(size)])]
    pallas_call x6 -> x9, Pallas kernels: 50.4 us -> 73.1 us  [the longest x3 29.5 us: attention(): pl.pallas_call(attention_kernel, grid=(rows // lanes,), in_specs=[pl.Bloc...]
    unnamed x104 -> x92, local copies, waits for them, and re-layouts: 18.7 us -> 7.87 us
    dot_general x3 -> x0, matrix products: 6.66 us -> none  [mm(): lax.dot_general(a, b, (((ca,), (cb,)), ((), ())), preferred_element_type=...]
    reshape x7 -> x0, local copies, waits for them, and re-layouts: 5.54 us -> none  [the longest x2 1.96 us: shards(): s2, b2 = (second_scale.reshape(1, width), second_shift.reshape(1, width))]
    convert_element_type x11 -> x6, local copies, waits for them, and re-layouts: 6.02 us -> 2.56 us  [the longest x2 1.63 us: sum_over_ctx(): send = lax.dynamic_slice_in_dim(v, (1 - low) * rows, rows, 0).astype(BF16)]
    convert_element_type x14 -> x8, other arithmetic: 7 us -> 3.76 us  [the longest x2 1.16 us: sum_over_ctx(): v = (keep + swap(send, 'ctx', 4, 2).astype(F32)).astype(BF16)]
  transfers between devices with their start and end apart: 63 -> 30, of which waited for: 22 -> 13; matrix products, arithmetic and copies ran while one was open for 22% -> 12% of each run, Pallas kernels for 6% -> 1%
where the time goes in v2:
time: 286 us; the launch traced here: 284 us
  waiting for transfers between devices  127 us (44%)
  Pallas kernels  73.1 us (26%)
  starting transfers between devices  39.1 us (14%)
  other arithmetic  26.6 us (9%)
  local copies, waits for them, and re-layouts  15.9 us (6%)
    ppermute x30, waiting for transfers between devices, swap(): return lax.ppermute(v, axis, [(i, i ^ distance) for i in range(size)])  127 us
    ppermute x30, starting transfers between devices, swap(): return lax.ppermute(v, axis, [(i, i ^ distance) for i in range(size)])  39.1 us
    pallas_call x3, Pallas kernels, attention(): pl.pallas_call(attention_kernel, grid=(rows // lanes,), in_specs=[pl.Bloc...  29.5 us
    pallas_call x1, Pallas kernels, back(): pl.pallas_call(functools.partial(back_kernel, split, heads), grid_spec=pl...  14.7 us
    pallas_call x1, Pallas kernels, feed_forward(): pl.pallas_call(functools.partial(forward_kernel, split), grid_spec=pltpu....  11 us
    pallas_call x1, Pallas kernels, finish(): pl.pallas_call(finish_kernel, grid_spec=pltpu.PrefetchScalarGridSpec(num_...  8.39 us
    unnamed x92, local copies, waits for them, and re-layouts  7.87 us
  transfers between devices with their start and end apart: 30, of which 13 were waited for; matrix products, arithmetic and copies ran while one was open for 12% of the time, Pallas kernels for 1%

profile of v2, /device:TPU:0, one launch (start us, length us, event | category | flops | bytes accessed | tf_op | source)
XLA Modules:
  0.0 283.6 jit_solution(15693569075205093035)
XLA Ops:
  1.9 5.1 %collective-permute-start.6 = (bf16[1,128,768]{2,1,0:T(8,128)(2,1)S(1)}, bf16[1,128,768]{2,1,0:T(8,128)(2,1)S(1)}, u32[]{:S(2)}, u32[]{:S(2)}) collective-permute-start(bf16[1,128,768]{2,1,0:T(8,128)(2,1)S(1)} %get-tuple-element.92), channel_id=1, source_target_pairs={{0,12},{4,8},{8,4},{12,0},{1,13},{5,9},{9,5},{13,1},{2,14},{6,10},... | collective-permute-start | bytes 589832 | tf_op jit(solution)/shard_map/ppermute | solution.py:570
  8.7 1.5 collective-permute-start.4
  11.5 12.3 %collective-permute-done.5 = bf16[1,128,768]{2,1,0:T(8,128)(2,1)S(1)} collective-permute-done((bf16[1,128,768]{2,1,0:T(8,128)(2,1)S(1)}, bf16[1,128,768]{2,1,0:T(8,128)(2,1)S(1)}, u32[]{:S(2)}, u32[]{:S(2)}) %collective-permute-start.5) | collective-permute-done | bytes 196640 | tf_op jit(solution)/shard_map/ppermute | solution.py:570
  23.8 1.5 collective-permute-start.9
  25.4 1.6 collective-permute-start.7
  27.7 4.5 %collective-permute-done.fz = bf16[2,128,768]{2,1,0:T(8,128)(2,1)S(1)} collective-permute-done((bf16[2,128,768]{2,1,0:T(8,128)(2,1)}, bf16[2,128,768]{2,1,0:T(8,128)(2,1)S(1)}, u32[]{:S(2)}, u32[]{:S(2)}) %collective-permute-start) | collective-permute-done | bytes 393248 | tf_op jit(solution)/shard_map/ppermute | solution.py:570
  32.1 1.5 collective-permute-start.1
  33.6 3.0 %collective-permute-done.7.nx = bf16[2,128,768]{2,1,0:T(8,128)(2,1)S(1)} collective-permute-done((bf16[2,128,768]{2,1,0:T(8,128)(2,1)S(1)}, bf16[2,128,768]{2,1,0:T(8,128)(2,1)S(1)}, u32[]{:S(2)}, u32[]{:S(2)}) %collective-permute-start.7) | collective-permute-done | bytes 393248 | tf_op jit(solution)/shard_map/ppermute | solution.py:570
  36.7 12.2 %collective-permute-done.9 = bf16[768,384]{1,0:T(8,128)(2,1)} collective-permute-done((bf16[768,384]{1,0:T(8,128)(2,1)S(1)}, bf16[768,384]{1,0:T(8,128)(2,1)}, u32[]{:S(2)}, u32[]{:S(2)}) %collective-permute-start.9) | collective-permute-done | bytes 589856 | tf_op jit(solution)/shard_map/ppermute | solution.py:570
  51.8 1.3 broadcast_select_fusion.5
  54.1 2.4 shard_map.256
  56.6 2.7 shard_map.254
  59.3 11.0 %shard_map.255 = (bf16[1024,768]{1,0:T(8,128)(2,1)S(1)}, bf16[1024,768]{1,0:T(8,128)(2,1)S(1)}, f32[8,768]{1,0:T(8,128)S(1)}, f32[768,768]{1,0:T(8,128)S(1)}, bf16[768,768]{1,0:T(8,128)(2,1)}) custom-call(s32[4]{0:T(128)S(1)} %pad_add_fusion.at, bf16[1024,768]{1,0:T(8,128)(2,1)S(1)} %get-tuple-element.49.n2_ref, ...), custom_call_target="tpu_custom_call" | custom-call | flops 7247757312 | bytes 16777216 | tf_op jit(solution)/shard_map/pallas_call | solution.py:383
  70.3 4.5 %shard_map.257 = (bf16[192,2048]{1,0:T(8,128)(2,1)S(1)}, bf16[192,2048]{1,0:T(8,128)(2,1)S(1)}, bf16[192,1024]{1,0:T(8,128)(2,1)S(1)}, bf16[192,1024]{1,0:T(8,128)(2,1)S(1)}) custom-call(bf16[1024,768]{1,0:T(8,128)(2,1)S(1)} %get-tuple-element.53.n1o.refs_12_, bf16[1024,768]{1,0:T(8,128)(2,1)S(1)} %get-tuple-element.54.n1x.refs_13_, ...), custom_call_target="tpu_custom_call" | custom-call | flops 1811939328 | bytes 9437184 | tf_op jit(solution)/shard_map/pallas_call | solution.py:206
  74.8 9.8 %shard_map.258 = (bf16[64,1024]{1,0:T(8,128)(2,1)S(1)}, bf16[64,1024]{1,0:T(8,128)(2,1)S(1)}, bf16[64,2048]{1,0:T(8,128)(2,1)S(1)}, bf16[64,2048]{1,0:T(8,128)(2,1)S(1)}) custom-call(f32[8,768]{1,0:T(8,128)S(1)} %get-tuple-element.52.after.refs_21_, bf16[192,1024]{1,0:T(8,128)(2,1)S(1)} %get-tuple-element.57.q_ref, ...), custom_call_target="tpu_custom_call" | custom-call | flops 5368709120 | bytes 2097152 | tf_op jit(solution)/shard_map/pallas_call | solution.py:309
  84.6 9.7 %shard_map.259 = (bf16[64,1024]{1,0:T(8,128)(2,1)S(1)}, bf16[64,1024]{1,0:T(8,128)(2,1)S(1)}, bf16[64,2048]{1,0:T(8,128)(2,1)S(1)}, bf16[64,2048]{1,0:T(8,128)(2,1)S(1)}) custom-call(bf16[64,1024]{1,0:T(8,128)(2,1)S(1)} %get-tuple-element.61.after.refs_0_, bf16[192,1024]{1,0:T(8,128)(2,1)S(1)} %get-tuple-element.57.q_ref, ...), custom_call_target="tpu_custom_call" | custom-call | flops 5368709120 | bytes 2097152 | tf_op jit(solution)/shard_map/pallas_call | solution.py:309
  94.4 10.0 %shard_map.260 = (bf16[64,1024]{1,0:T(8,128)(2,1)S(1)}, bf16[64,1024]{1,0:T(8,128)(2,1)S(1)}, bf16[64,2048]{1,0:T(8,128)(2,1)S(1)}, bf16[64,2048]{1,0:T(8,128)(2,1)S(1)}) custom-call(bf16[64,1024]{1,0:T(8,128)(2,1)S(1)} %get-tuple-element.62.after.refs_1_, bf16[192,1024]{1,0:T(8,128)(2,1)S(1)} %get-tuple-element.57.q_ref, ...), custom_call_target="tpu_custom_call" | custom-call | flops 5368709120 | bytes 2097152 | tf_op jit(solution)/shard_map/pallas_call | solution.py:309
  104.4 14.7 %shard_map.261 = (bf16[6,256,768]{2,1,0:T(8,128)(2,1)S(1)}, bf16[6,256,768]{2,1,0:T(8,128)(2,1)S(1)}, f32[832,384]{1,0:T(8,128)S(1)}, bf16[832,384]{1,0:T(8,128)(2,1)}) custom-call(s32[4]{0:T(128)S(1)} %pad_add_fusion.at, bf16[64,1024]{1,0:T(8,128)(2,1)S(1)} %get-tuple-element.61.after.refs_0_, bf16[64,1024]{1,0:T(8,128)(2,1)S(1)} %get-tuple-element.62.after.refs_1_, ...), custom_call_target="tpu_custom_call" | custom-call | flops 4227858432 | bytes 20971520 | tf_op jit(solution)/shard_map/pallas_call | solution.py:507
  119.1 1.4 copy-done.2
  121.6 1.4 copy-done.16
  123.0 1.5 collective-permute-start.18
  125.0 15.5 %collective-permute-done.18 = bf16[832,384]{1,0:T(8,128)(2,1)} collective-permute-done((bf16[832,384]{1,0:T(8,128)(2,1)}, bf16[832,384]{1,0:T(8,128)(2,1)}, u32[]{:S(2)}, u32[]{:S(2)}) %collective-permute-start.18) | collective-permute-done | bytes 639008 | tf_op jit(solution)/shard_map/ppermute | solution.py:570
  140.5 1.6 convert_add_fusion.2
  144.6 8.3 %collective-permute-done.19 = bf16[416,384]{1,0:T(8,128)(2,1)} collective-permute-done((bf16[416,384]{1,0:T(8,128)(2,1)}, bf16[416,384]{1,0:T(8,128)(2,1)}, u32[]{:S(2)}, u32[]{:S(2)}) %collective-permute-start.19) | collective-permute-done | bytes 319520 | tf_op jit(solution)/shard_map/ppermute | solution.py:570
  155.0 2.6 collective-permute-start.20
  157.6 7.7 %collective-permute-done.25 = bf16[768,768]{1,0:T(8,128)(2,1)} collective-permute-done((bf16[768,768]{1,0:T(8,128)(2,1)}, bf16[768,768]{1,0:T(8,128)(2,1)}, u32[]{:S(2)}, u32[]{:S(2)}) %collective-permute-start.25) | collective-permute-done | bytes 1179680 | tf_op jit(solution)/shard_map/ppermute | solution.py:570
  165.3 2.2 convert_add_fusion.1
  167.6 1.5 copy-done.27
  171.9 2.1 collective-permute-start.21
  174.0 14.6 %collective-permute-done.26 = bf16[384,768]{1,0:T(8,128)(2,1)} collective-permute-done((bf16[384,768]{1,0:T(8,128)(2,1)}, bf16[384,768]{1,0:T(8,128)(2,1)}, u32[]{:S(2)}, u32[]{:S(2)}) %collective-permute-start.26) | collective-permute-done | bytes 589856 | tf_op jit(solution)/shard_map/ppermute | solution.py:570
  188.6 1.6 convert_add_fusion.3
  190.8 2.2 convert_add_fusion
  193.3 1.6 collective-permute-start.12
  195.0 2.4 collective-permute-start.22
  197.4 7.9 %collective-permute-done.27 = bf16[192,768]{1,0:T(8,128)(2,1)S(1)} collective-permute-done((bf16[192,768]{1,0:T(8,128)(2,1)S(1)}, bf16[192,768]{1,0:T(8,128)(2,1)S(1)}, u32[]{:S(2)}, u32[]{:S(2)}) %collective-permute-start.27) | collective-permute-done | bytes 294944 | tf_op jit(solution)/shard_map/ppermute | solution.py:570
  205.6 1.5 collective-permute-start.11
  207.1 6.8 %collective-permute-done.12 = bf16[4,128,768]{2,1,0:T(8,128)(2,1)S(1)} collective-permute-done((bf16[4,128,768]{2,1,0:T(8,128)(2,1)S(1)}, bf16[4,128,768]{2,1,0:T(8,128)(2,1)S(1)}, u32[]{:S(2)}, u32[]{:S(2)}) %collective-permute-start.12) | collective-permute-done | bytes 786464 | tf_op jit(solution)/shard_map/ppermute | solution.py:570
  214.2 2.5 collective-permute-start.14
  216.8 3.3 %collective-permute-done.11 = bf16[2,128,768]{2,1,0:T(8,128)(2,1)S(1)} collective-permute-done((bf16[2,128,768]{2,1,0:T(8,128)(2,1)S(1)}, bf16[2,128,768]{2,1,0:T(8,128)(2,1)S(1)}, u32[]{:S(2)}, u32[]{:S(2)}) %collective-permute-start.11) | collective-permute-done | bytes 393248 | tf_op jit(solution)/shard_map/ppermute | solution.py:570
  220.2 2.3 collective-permute-start.15
  222.6 19.2 %collective-permute-done.13 = bf16[2,128,768]{2,1,0:T(8,128)(2,1)S(1)} collective-permute-done((bf16[2,128,768]{2,1,0:T(8,128)(2,1)S(1)}, bf16[2,128,768]{2,1,0:T(8,128)(2,1)S(1)}, u32[]{:S(2)}, u32[]{:S(2)}) %collective-permute-start.13) | collective-permute-done | bytes 393248 | tf_op jit(solution)/shard_map/ppermute | solution.py:570
  242.7 1.5 collective-permute-start.16
  245.3 4.6 %collective-permute-start.29 = (bf16[2,192,768]{2,1,0:T(8,128)(2,1)}, bf16[2,192,768]{2,1,0:T(8,128)(2,1)}, u32[]{:S(2)}, u32[]{:S(2)}) collective-permute-start(bf16[2,192,768]{2,1,0:T(8,128)(2,1)} %pad_maximum_fusion.10), channel_id=1, source_target_pairs={{0,4},{4,0},{8,12},{12,8},{1,5},{5,1},{9,13},{13,9},{2,6},{6,2},{1... | collective-permute-start | bytes 1769480 | tf_op jit(solution)/shard_map/ppermute | solution.py:570
  250.2 11.9 %collective-permute-done.16 = bf16[2,2,128,768]{3,2,1,0:T(8,128)(2,1)S(1)} collective-permute-done((bf16[2,2,128,768]{3,2,1,0:T(8,128)(2,1)S(1)}, bf16[2,2,128,768]{3,2,1,0:T(8,128)(2,1)S(1)}, u32[]{:S(2)}, u32[]{:S(2)}) %collective-permute-start.16) | collective-permute-done | bytes 786464 | tf_op jit(solution)/shard_map/ppermute | solution.py:570
  262.1 1.3 pad_maximum_fusion.pair
  264.6 1.5 collective-permute-start.24
  267.5 2.2 slice.147
  274.6 8.4 %shard_map.262 = (f32[2,512,768]{2,1,0:T(8,128)}, f32[2,512,768]{2,1,0:T(8,128)}) custom-call(s32[4]{0:T(128)S(1)} %pad_add_fusion.at, bf16[2,2,2,128,768]{4,3,2,1,0:T(8,128)(2,1)} %pad_maximum_fusion.pair, bf16[2,2,2,128,768]{4,3,2,1,0:T(8,128)(2,1)} %collective-permute-done.17.core, bf16[2,512,768]{2,1,0:T(8,128)(2,1)S(1)} %copy-done, ...), custom_call_target="tpu_custom_call" | custom-call | bytes 12582912 | tf_op jit(solution)/shard_map/pallas_call | solution.py:555
  (186 shorter events, 29.7 us)
Async XLA Ops:
  0.7 10.7 %copy-start.44 = (s32[2,2048]{1,0:T(2,128)S(1)}, s32[2,2048]{1,0:T(2,128)}, u32[]{:S(2)}) copy-start(s32[2,2048]{1,0:T(2,128)} %param.16) | copy-start | bytes 49156
  0.7 10.7 %copy-start.34 = (bf16[384,3,192]{0,2,1:T(8,128)(2,1)S(1)}, bf16[384,3,192]{0,2,1:T(8,128)(2,1)}, u32[]{:S(2)}) copy-start(bf16[384,3,192]{0,2,1:T(8,128)(2,1)} %param.17) | copy-start | bytes 1327108
  0.7 10.7 %copy-start.37 = (bf16[192,384]{1,0:T(8,128)(2,1)S(1)}, bf16[192,384]{1,0:T(8,128)(2,1)}, u32[]{:S(2)}) copy-start(bf16[192,384]{1,0:T(8,128)(2,1)} %param.19) | copy-start | bytes 442372
  1.9 23.5 %copy-start.25 = (bf16[1,128,768]{2,1,0:T(8,128)(2,1)}, bf16[1,128,768]{2,1,0:T(8,128)(2,1)S(1)}, u32[]{:S(2)}) copy-start(bf16[1,128,768]{2,1,0:T(8,128)(2,1)S(1)} %get-tuple-element.92) | copy-start | bytes 589828
  1.9 23.5 %copy-start.28 = (bf16[1,128,768]{2,1,0:T(8,128)(2,1)}, bf16[1,128,768]{2,1,0:T(8,128)(2,1)S(1)}, u32[]{:S(2)}) copy-start(bf16[1,128,768]{2,1,0:T(8,128)(2,1)S(1)} %get-tuple-element.91) | copy-start | bytes 589828
  1.9 23.5 %collective-permute-start.6 = (bf16[1,128,768]{2,1,0:T(8,128)(2,1)S(1)}, bf16[1,128,768]{2,1,0:T(8,128)(2,1)S(1)}, u32[]{:S(2)}, u32[]{:S(2)}) collective-permute-start(bf16[1,128,768]{2,1,0:T(8,128)(2,1)S(1)} %get-tuple-element.92), channel_id=1, source_target_pairs={{0,12},{4,8},{8,4},{12,0},{1,13},{5,9},{9,5},{13,1},{2,14},{6,10},... | collective-permute-start | bytes 589832 | tf_op jit(solution)/shard_map/ppermute | solution.py:570
  8.7 23.4 %collective-permute-start = (bf16[2,128,768]{2,1,0:T(8,128)(2,1)}, bf16[2,128,768]{2,1,0:T(8,128)(2,1)S(1)}, u32[]{:S(2)}, u32[]{:S(2)}) collective-permute-start(bf16[2,128,768]{2,1,0:T(8,128)(2,1)} %pad_maximum_fusion.11), channel_id=1, source_target_pairs={{0,8},{4,12},{8,0},{12,4},{1,9},{5,13},{9,1},{13,5},{2,10},{6,14},... | collective-permute-start | bytes 1179656 | tf_op jit(solution)/shard_map/ppermute | solution.py:570
  8.7 41.8 %collective-permute-start.4 = (bf16[768,384]{1,0:T(8,128)(2,1)S(1)}, bf16[768,384]{1,0:T(8,128)(2,1)}, u32[]{:S(2)}, u32[]{:S(2)}) collective-permute-start(bf16[768,384]{1,0:T(8,128)(2,1)S(1)} %copy-done.38), channel_id=1, source_target_pairs={{0,16},{16,0},{1,17},{17,1},{2,18},{18,2},{3,19},{19,3},{4,20},{20... | collective-permute-start | bytes 1769480 | tf_op jit(solution)/shard_map/ppermute | solution.py:570
  10.2 41.5 %collective-permute-start.3 = (bf16[384,768]{1,0:T(8,128)(2,1)}, bf16[384,768]{1,0:T(8,128)(2,1)}, u32[]{:S(2)}, u32[]{:S(2)}) collective-permute-start(bf16[384,768]{1,0:T(8,128)(2,1)} %param.21), channel_id=1, source_target_pairs={{0,16},{16,0},{1,17},{17,1},{2,18},{18,2},{3,19},{19,3},{4,20},{20... | collective-permute-start | bytes 1769480 | tf_op jit(solution)/shard_map/ppermute | solution.py:570
  10.8 13.1 %collective-permute-start.5 = (bf16[1,128,768]{2,1,0:T(8,128)(2,1)S(1)}, bf16[1,128,768]{2,1,0:T(8,128)(2,1)S(1)}, u32[]{:S(2)}, u32[]{:S(2)}) collective-permute-start(bf16[1,128,768]{2,1,0:T(8,128)(2,1)S(1)} %get-tuple-element.91), channel_id=1, source_target_pairs={{0,4},{4,0},{8,12},{12,8},{1,5},{5,1},{9,13},{13,9},{2,6},{6,2},{1... | collective-permute-start | bytes 589832 | tf_op jit(solution)/shard_map/ppermute | solution.py:570
  23.8 25.1 %collective-permute-start.9 = (bf16[768,384]{1,0:T(8,128)(2,1)S(1)}, bf16[768,384]{1,0:T(8,128)(2,1)}, u32[]{:S(2)}, u32[]{:S(2)}) collective-permute-start(bf16[768,384]{1,0:T(8,128)(2,1)S(1)} %pad_maximum_fusion.9), channel_id=1, source_target_pairs={{0,16},{16,0},{1,17},{17,1},{2,18},{18,2},{3,19},{19,3},{4,20},{20... | collective-permute-start | bytes 1769480 | tf_op jit(solution)/shard_map/ppermute | solution.py:570
  25.4 11.1 %collective-permute-start.7 = (bf16[2,128,768]{2,1,0:T(8,128)(2,1)S(1)}, bf16[2,128,768]{2,1,0:T(8,128)(2,1)S(1)}, u32[]{:S(2)}, u32[]{:S(2)}) collective-permute-start(bf16[2,128,768]{2,1,0:T(8,128)(2,1)S(1)} %constant_dynamic-update-slice_fusion.nz), channel_id=1, source_target_pairs={{0,2},{1,3},{2,0},{3,1},{4,6},{5,7},{6,4},{7,5},{8,10},{9,11},{10,... | collective-permute-start | bytes 1179656 | tf_op jit(solution)/shard_map/ppermute | solution.py:570
  32.1 18.1 %copy-start.5 = (bf16[2,128,768]{2,1,0:T(8,128)(2,1)}, bf16[2,128,768]{2,1,0:T(8,128)(2,1)S(1)}, u32[]{:S(2)}) copy-start(bf16[2,128,768]{2,1,0:T(8,128)(2,1)S(1)} %collective-permute-done.fz) | copy-start | bytes 1179652
  32.1 18.1 %collective-permute-start.1 = (bf16[2,128,768]{2,1,0:T(8,128)(2,1)S(1)}, bf16[2,128,768]{2,1,0:T(8,128)(2,1)S(1)}, u32[]{:S(2)}, u32[]{:S(2)}) collective-permute-start(bf16[2,128,768]{2,1,0:T(8,128)(2,1)S(1)} %collective-permute-done.fz), channel_id=1, source_target_pairs={{0,2},{1,3},{2,0},{3,1},{4,6},{5,7},{6,4},{7,5},{8,10},{9,11},{10,... | collective-permute-start | bytes 1179656 | tf_op jit(solution)/shard_map/ppermute | solution.py:570
  36.6 13.7 %copy-start.7 = (bf16[2,128,768]{2,1,0:T(8,128)(2,1)}, bf16[2,128,768]{2,1,0:T(8,128)(2,1)S(1)}, u32[]{:S(2)}) copy-start(bf16[2,128,768]{2,1,0:T(8,128)(2,1)S(1)} %collective-permute-done.7.nx) | copy-start | bytes 1179652
  36.6 16.7 %collective-permute-start.8 = (bf16[2,2,128,768]{3,2,1,0:T(8,128)(2,1)S(1)}, bf16[2,2,128,768]{3,2,1,0:T(8,128)(2,1)S(1)}, u32[]{:S(2)}, u32[]{:S(2)}) collective-permute-start(bf16[2,2,128,768]{3,2,1,0:T(8,128)(2,1)S(1)} %pad_maximum_fusion.6), channel_id=1, source_target_pairs={{0,1},{1,0},{2,3},{3,2},{4,5},{5,4},{6,7},{7,6},{8,9},{9,8},{10,11... | collective-permute-start | bytes 2359304 | tf_op jit(solution)/shard_map/ppermute | solution.py:570
  50.3 6.2 %collective-permute-start.2 = (bf16[2,2,128,768]{3,2,1,0:T(8,128)(2,1)S(1)}, bf16[2,2,128,768]{3,2,1,0:T(8,128)(2,1)S(1)}, u32[]{:S(2)}, u32[]{:S(2)}) collective-permute-start(bf16[2,2,128,768]{3,2,1,0:T(8,128)(2,1)S(1)} %pad_maximum_fusion.5), channel_id=1, source_target_pairs={{0,1},{1,0},{2,3},{3,2},{4,5},{5,4},{6,7},{7,6},{8,9},{9,8},{10,11... | collective-permute-start | bytes 2359304 | tf_op jit(solution)/shard_map/ppermute | solution.py:570
  59.3 11.0 %copy-start.17 = (bf16[1024,768]{1,0:T(8,128)(2,1)}, bf16[1024,768]{1,0:T(8,128)(2,1)S(1)}, u32[]{:S(2)}) copy-start(bf16[1024,768]{1,0:T(8,128)(2,1)S(1)} %get-tuple-element.50.g_ref.refs_16_) | copy-start | bytes 4718596
  59.3 11.0 %copy-start.20 = (f32[3,192]{1,0:T(4,128)S(1)}, f32[3,192]{1,0:T(4,128)}, u32[]{:S(2)}) copy-start(f32[3,192]{1,0:T(4,128)} %b_ref.1) | copy-start | bytes 6916
  94.3 10.0 %copy-start.18 = (bf16[1024,768]{1,0:T(8,128)(2,1)S(1)}, bf16[1024,768]{1,0:T(8,128)(2,1)}, u32[]{:S(2)}) copy-start(bf16[1024,768]{1,0:T(8,128)(2,1)} %copy-done.17) | copy-start | bytes 4718596
  94.3 10.0 %copy-start.22 = (bf16[1024,768]{1,0:T(8,128)(2,1)S(1)}, bf16[1024,768]{1,0:T(8,128)(2,1)}, u32[]{:S(2)}) copy-start(bf16[1024,768]{1,0:T(8,128)(2,1)} %copy-done.21) | copy-start | bytes 4718596
  94.4 10.0 %copy-start.24 = (bf16[1024,768]{1,0:T(8,128)(2,1)S(1)}, bf16[1024,768]{1,0:T(8,128)(2,1)}, u32[]{:S(2)}) copy-start(bf16[1024,768]{1,0:T(8,128)(2,1)} %copy-done.23) | copy-start | bytes 4718596
  123.0 17.5 %collective-permute-start.18 = (bf16[832,384]{1,0:T(8,128)(2,1)}, bf16[832,384]{1,0:T(8,128)(2,1)}, u32[]{:S(2)}, u32[]{:S(2)}) collective-permute-start(bf16[832,384]{1,0:T(8,128)(2,1)} %get-tuple-element.81), channel_id=1, source_target_pairs={{0,16},{16,0},{1,17},{17,1},{2,18},{18,2},{3,19},{19,3},{4,20},{20... | collective-permute-start | bytes 1916936 | tf_op jit(solution)/shard_map/ppermute | solution.py:570
  124.5 40.9 %collective-permute-start.25 = (bf16[768,768]{1,0:T(8,128)(2,1)}, bf16[768,768]{1,0:T(8,128)(2,1)}, u32[]{:S(2)}, u32[]{:S(2)}) collective-permute-start(bf16[768,768]{1,0:T(8,128)(2,1)} %get-tuple-element.83), channel_id=1, source_target_pairs={{0,16},{16,0},{1,17},{17,1},{2,18},{18,2},{3,19},{19,3},{4,20},{20... | collective-permute-start | bytes 3538952 | tf_op jit(solution)/shard_map/ppermute | solution.py:570
  125.0 65.8 %collective-permute-start.10 = (bf16[6,256,768]{2,1,0:T(8,128)(2,1)}, bf16[6,256,768]{2,1,0:T(8,128)(2,1)}, u32[]{:S(2)}, u32[]{:S(2)}) collective-permute-start(bf16[6,256,768]{2,1,0:T(8,128)(2,1)} %copy-done.16), channel_id=1, source_target_pairs={{0,1},{1,0},{2,3},{3,2},{4,5},{5,4},{6,7},{7,6},{8,9},{9,8},{10,11... | collective-permute-start | bytes 7077896 | tf_op jit(solution)/shard_map/ppermute | solution.py:570
  143.9 9.1 %collective-permute-start.19 = (bf16[416,384]{1,0:T(8,128)(2,1)}, bf16[416,384]{1,0:T(8,128)(2,1)}, u32[]{:S(2)}, u32[]{:S(2)}) collective-permute-start(bf16[416,384]{1,0:T(8,128)(2,1)} %dynamic-slice_convert_fusion.1), channel_id=1, source_target_pairs={{0,4},{4,0},{8,12},{12,8},{1,5},{5,1},{9,13},{13,9},{2,6},{6,2},{1... | collective-permute-start | bytes 958472 | tf_op jit(solution)/shard_map/ppermute | solution.py:570
  154.2 11.1 %copy-start.33 = (f32[416,384]{1,0:T(8,128)}, f32[416,384]{1,0:T(8,128)S(1)}, u32[]{:S(2)}) copy-start(f32[416,384]{1,0:T(8,128)S(1)} %convert_add_fusion.4) | copy-start | bytes 1916932
  155.0 15.8 %collective-permute-start.20 = (bf16[208,384]{1,0:T(8,128)(2,1)}, bf16[208,384]{1,0:T(8,128)(2,1)}, u32[]{:S(2)}, u32[]{:S(2)}) collective-permute-start(bf16[208,384]{1,0:T(8,128)(2,1)} %dynamic-slice_convert_fusion.3), channel_id=1, source_target_pairs={{0,8},{4,12},{8,0},{12,4},{1,9},{5,13},{9,1},{13,5},{2,10},{6,14},... | collective-permute-start | bytes 479240 | tf_op jit(solution)/shard_map/ppermute | solution.py:570
  169.9 18.7 %collective-permute-start.26 = (bf16[384,768]{1,0:T(8,128)(2,1)}, bf16[384,768]{1,0:T(8,128)(2,1)}, u32[]{:S(2)}, u32[]{:S(2)}) collective-permute-start(bf16[384,768]{1,0:T(8,128)(2,1)} %dynamic-slice_convert_fusion), channel_id=1, source_target_pairs={{0,4},{4,0},{8,12},{12,8},{1,5},{5,1},{9,13},{13,9},{2,6},{6,2},{1... | collective-permute-start | bytes 1769480 | tf_op jit(solution)/shard_map/ppermute | solution.py:570
  170.5 71.8 %copy-start.41 = (f32[2,128]{1,0:T(2,128)}, f32[2,128]{1,0:T(2,128)S(1)}, u32[]{:S(2)}) copy-start(f32[2,128]{1,0:T(2,128)S(1)} %broadcast_multiply_fusion.2) | copy-start | bytes 3076
  171.9 18.9 %copy-start.3 = (bf16[6,256,768]{2,1,0:T(8,128)(2,1)S(1)}, bf16[6,256,768]{2,1,0:T(8,128)(2,1)}, u32[]{:S(2)}) copy-start(bf16[6,256,768]{2,1,0:T(8,128)(2,1)} %copy-done.2) | copy-start | bytes 7077892
  171.9 23.0 %collective-permute-start.21 = (bf16[208,384]{1,0:T(8,128)(2,1)S(1)}, bf16[208,384]{1,0:T(8,128)(2,1)S(1)}, u32[]{:S(2)}, u32[]{:S(2)}) collective-permute-start(bf16[208,384]{1,0:T(8,128)(2,1)S(1)} %add_convert_fusion.1), channel_id=1, source_target_pairs={{0,8},{4,12},{8,0},{12,4},{1,9},{5,13},{9,1},{13,5},{2,10},{6,14},... | collective-permute-start | bytes 479240 | tf_op jit(solution)/shard_map/ppermute | solution.py:570
  190.2 15.1 %collective-permute-start.27 = (bf16[192,768]{1,0:T(8,128)(2,1)S(1)}, bf16[192,768]{1,0:T(8,128)(2,1)S(1)}, u32[]{:S(2)}, u32[]{:S(2)}) collective-permute-start(bf16[192,768]{1,0:T(8,128)(2,1)S(1)} %dynamic-slice_convert_fusion.2), channel_id=1, source_target_pairs={{0,8},{4,12},{8,0},{12,4},{1,9},{5,13},{9,1},{13,5},{2,10},{6,14},... | collective-permute-start | bytes 884744 | tf_op jit(solution)/shard_map/ppermute | solution.py:570
  193.3 20.5 %collective-permute-start.12 = (bf16[4,128,768]{2,1,0:T(8,128)(2,1)S(1)}, bf16[4,128,768]{2,1,0:T(8,128)(2,1)S(1)}, u32[]{:S(2)}, u32[]{:S(2)}) collective-permute-start(bf16[4,128,768]{2,1,0:T(8,128)(2,1)S(1)} %fusion.7), channel_id=1, source_target_pairs={{0,2},{1,3},{2,0},{3,1},{4,6},{5,7},{6,4},{7,5},{8,10},{9,11},{10,... | collective-permute-start | bytes 2359304 | tf_op jit(solution)/shard_map/ppermute | solution.py:570
  195.0 49.2 %collective-permute-start.22 = (bf16[2,208,384]{2,1,0:T(8,128)(2,1)S(1)}, bf16[2,208,384]{2,1,0:T(8,128)(2,1)S(1)}, u32[]{:S(2)}, u32[]{:S(2)}) collective-permute-start(bf16[2,208,384]{2,1,0:T(8,128)(2,1)S(1)} %pad_maximum_fusion.14), channel_id=1, source_target_pairs={{0,4},{4,0},{8,12},{12,8},{1,5},{5,1},{9,13},{13,9},{2,6},{6,2},{1... | collective-permute-start | bytes 958472 | tf_op jit(solution)/shard_map/ppermute | solution.py:570
  205.4 39.0 %copy-start.31 = (bf16[192,768]{1,0:T(8,128)(2,1)}, bf16[192,768]{1,0:T(8,128)(2,1)S(1)}, u32[]{:S(2)}) copy-start(bf16[192,768]{1,0:T(8,128)(2,1)S(1)} %add_convert_fusion) | copy-start | bytes 884740
  205.4 39.0 %collective-permute-start.28 = (bf16[192,768]{1,0:T(8,128)(2,1)S(1)}, bf16[192,768]{1,0:T(8,128)(2,1)S(1)}, u32[]{:S(2)}, u32[]{:S(2)}) collective-permute-start(bf16[192,768]{1,0:T(8,128)(2,1)S(1)} %add_convert_fusion), channel_id=1, source_target_pairs={{0,8},{4,12},{8,0},{12,4},{1,9},{5,13},{9,1},{13,5},{2,10},{6,14},... | collective-permute-start | bytes 884744 | tf_op jit(solution)/shard_map/ppermute | solution.py:570
  205.6 14.5 %collective-permute-start.11 = (bf16[2,128,768]{2,1,0:T(8,128)(2,1)S(1)}, bf16[2,128,768]{2,1,0:T(8,128)(2,1)S(1)}, u32[]{:S(2)}, u32[]{:S(2)}) collective-permute-start(bf16[2,128,768]{2,1,0:T(8,128)(2,1)S(1)} %fusion.13), channel_id=1, source_target_pairs={{0,2},{1,3},{2,0},{3,1},{4,6},{5,7},{6,4},{7,5},{8,10},{9,11},{10,... | collective-permute-start | bytes 1179656 | tf_op jit(solution)/shard_map/ppermute | solution.py:570
  214.2 8.3 %collective-permute-start.14 = (bf16[128,768]{1,0:T(8,128)(2,1)S(1)}, bf16[128,768]{1,0:T(8,128)(2,1)S(1)}, u32[]{:S(2)}, u32[]{:S(2)}) collective-permute-start(bf16[128,768]{1,0:T(8,128)(2,1)S(1)} %get-tuple-element.109), channel_id=1, source_target_pairs={{0,4},{4,0},{8,12},{12,8},{1,5},{5,1},{9,13},{13,9},{2,6},{6,2},{1... | collective-permute-start | bytes 589832 | tf_op jit(solution)/shard_map/ppermute | solution.py:570
  216.7 25.1 %collective-permute-start.13 = (bf16[2,128,768]{2,1,0:T(8,128)(2,1)S(1)}, bf16[2,128,768]{2,1,0:T(8,128)(2,1)S(1)}, u32[]{:S(2)}, u32[]{:S(2)}) collective-permute-start(bf16[2,128,768]{2,1,0:T(8,128)(2,1)S(1)} %slice.139), channel_id=1, source_target_pairs={{0,8},{4,12},{8,0},{12,4},{1,9},{5,13},{9,1},{13,5},{2,10},{6,14},... | collective-permute-start | bytes 1179656 | tf_op jit(solution)/shard_map/ppermute | solution.py:570
  220.2 21.6 %collective-permute-start.15 = (bf16[128,768]{1,0:T(8,128)(2,1)S(1)}, bf16[128,768]{1,0:T(8,128)(2,1)S(1)}, u32[]{:S(2)}, u32[]{:S(2)}) collective-permute-start(bf16[128,768]{1,0:T(8,128)(2,1)S(1)} %get-tuple-element.110), channel_id=1, source_target_pairs={{0,12},{4,8},{8,4},{12,0},{1,13},{5,9},{9,5},{13,1},{2,14},{6,10},... | collective-permute-start | bytes 589832 | tf_op jit(solution)/shard_map/ppermute | solution.py:570
  242.7 19.4 %collective-permute-start.16 = (bf16[2,2,128,768]{3,2,1,0:T(8,128)(2,1)S(1)}, bf16[2,2,128,768]{3,2,1,0:T(8,128)(2,1)S(1)}, u32[]{:S(2)}, u32[]{:S(2)}) collective-permute-start(bf16[2,2,128,768]{3,2,1,0:T(8,128)(2,1)S(1)} %pad_maximum_fusion.8), channel_id=1, source_target_pairs={{0,2},{1,3},{2,0},{3,1},{4,6},{5,7},{6,4},{7,5},{8,10},{9,11},{10,... | collective-permute-start | bytes 2359304 | tf_op jit(solution)/shard_map/ppermute | solution.py:570
  244.3 22.5 %copy-start.39 = (f32[8,384]{1,0:T(8,128)}, f32[8,384]{1,0:T(8,128)S(1)}, u32[]{:S(2)}) copy-start(f32[8,384]{1,0:T(8,128)S(1)} %get-tuple-element.112) | copy-start | bytes 36868
  244.3 20.3 %collective-permute-start.23 = (f32[8,768]{1,0:T(8,128)S(1)}, f32[8,768]{1,0:T(8,128)S(1)}, u32[]{:S(2)}, u32[]{:S(2)}) collective-permute-start(f32[8,768]{1,0:T(8,128)S(1)} %pad_maximum_fusion.15), channel_id=1, source_target_pairs={{0,1},{1,0},{2,3},{3,2},{4,5},{5,4},{6,7},{7,6},{8,9},{9,8},{10,11... | collective-permute-start | bytes 73736 | tf_op jit(solution)/shard_map/ppermute | solution.py:570
  245.3 25.6 %collective-permute-start.29 = (bf16[2,192,768]{2,1,0:T(8,128)(2,1)}, bf16[2,192,768]{2,1,0:T(8,128)(2,1)}, u32[]{:S(2)}, u32[]{:S(2)}) collective-permute-start(bf16[2,192,768]{2,1,0:T(8,128)(2,1)} %pad_maximum_fusion.10), channel_id=1, source_target_pairs={{0,4},{4,0},{8,12},{12,8},{1,5},{5,1},{9,13},{13,9},{2,6},{6,2},{1... | collective-permute-start | bytes 1769480 | tf_op jit(solution)/shard_map/ppermute | solution.py:570
  263.5 11.1 %collective-permute-start.17 = (bf16[2,2,2,128,768]{4,3,2,1,0:T(8,128)(2,1)}, bf16[2,2,2,128,768]{4,3,2,1,0:T(8,128)(2,1)}, u32[]{:S(2)}, u32[]{:S(2)}) collective-permute-start(bf16[2,2,2,128,768]{4,3,2,1,0:T(8,128)(2,1)} %pad_maximum_fusion.pair), channel_id=1, source_target_pairs={{0,1},{1,0},{2,3},{3,2},{4,5},{5,4},{6,7},{7,6},{8,9},{9,8},{10,11... | collective-permute-start | bytes 4718600 | tf_op jit(solution)/shard_map/ppermute | solution.py:570
  264.6 5.7 %collective-permute-start.24 = (f32[8,768]{1,0:T(8,128)S(1)}, f32[8,768]{1,0:T(8,128)S(1)}, u32[]{:S(2)}, u32[]{:S(2)}) collective-permute-start(f32[8,768]{1,0:T(8,128)S(1)} %fusion.27), channel_id=1, source_target_pairs={{0,2},{1,3},{2,0},{3,1},{4,6},{5,7},{6,4},{7,5},{8,10},{9,11},{10,... | collective-permute-start | bytes 73736 | tf_op jit(solution)/shard_map/ppermute | solution.py:570
  271.0 12.0 %copy-start.43 = (f32[768]{0:T(1024)}, f32[768]{0:T(1024)S(1)}, u32[]{:S(2)}) copy-start(f32[768]{0:T(1024)S(1)} %get-tuple-element.146) | copy-start | bytes 9220
  (27 other events, 88.3 us)

commit v3 on v2

--- a/solution.py
+++ b/solution.py
@@ -398,172 +398,143 @@
     )(at, n2, g, xhat, up, bias, down, scale)
 
 
-def back_kernel(split, heads, at, *refs):
-    o, dq, dk, dv = (refs[j * heads : (j + 1) * heads] for j in range(4))
-    (n1o, n1x, xho, xhx, g_ref, ff_ref, a2_ref, w_ref, s1_ref, small_ff,
-     keep_ref, send_ref, first_ref, second_ref, mix, out, small) = refs[4 * heads :]
+def emit(keep_ref, send_ref, v):
     i = pl.program_id(0)
+
+    @pl.when(i % 2 == 0)
+    def _():
+        keep_ref[0] = v.astype(BF16)
+
+    @pl.when(i % 2 == 1)
+    def _():
+        send_ref[0] = v.astype(BF16)
+
+
+def branch_kernel(heads, *refs):
+    o = refs[:heads]
+    g_ref, ff_ref, w_ref, keep_ref, send_ref, out = refs[heads:]
     wide = heads * HEAD
 
-    @pl.when(i == 0)
-    def _():
-        mix[...] = jnp.zeros_like(mix)
+    @pl.when(pl.program_id(0) == 0)
+    def _():
         out[...] = jnp.zeros_like(out)
-        small[...] = jnp.zeros_like(small)
-
-    def emit(v):
-        @pl.when(i % 2 == 0)
-        def _():
-            keep_ref[0] = v.astype(BF16)
-
-        @pl.when(i % 2 == 1)
-        def _():
-            send_ref[0] = v.astype(BF16)
-
-    @pl.when(i < 4)
-    def _():
-        ot = jnp.concatenate([r[...] for r in o], axis=0)
-        emit(mm(ot, w_ref[3 * wide :, :], 0, 0) + ff_ref[...].astype(F32))
-        out[...] += mm(ot, g_ref[...])
-
-    def through(grad, low, n1, xhat, extra):
-        rows = slice(low, 3 * wide)
-        first = mm(grad, w_ref[rows, :], 0, 0)
-        a = first * row_of(s1_ref)
-        emit(a if extra is None else a + extra)
-        mix[rows, :] += mm(grad, n1)
-        small[0:1, :] += jnp.sum(first * xhat.astype(F32), axis=0, keepdims=True)
-        small[1:2, :] += jnp.sum(first, axis=0, keepdims=True)
-        ones = jnp.ones((8, grad.shape[1]), BF16)
-        small[6:7, low : 3 * wide] += mm(ones, grad, 1, 1)[0:1]
-
-    @pl.when((i >= 4) & (i < 8))
-    def _():
-        grad = jnp.concatenate([r[...] for r in (*dq, *dk, *dv)], axis=0)
-        through(grad, 0, n1o[...], xho[...], a2_ref[...].astype(F32))
-
-    @pl.when(i >= 8)
-    def _():
-        grad = jnp.concatenate([r[...] for r in (*dk, *dv)], axis=0)
-        through(grad, wide, n1x[...], xhx[...], None)
-
-    @pl.when(i == 11)
-    def _():
-        small[2:4, :] = small_ff[2:4, :]
-        small[4:6, :] = small_ff[0:2, :]
-        if split:
-            half = mix.shape[1] // 2
-            vectors = small[...].astype(BF16)
-            for ref, f in ((first_ref, at[3]), (second_ref, 1 - at[3])):
-                piece = pl.ds(pl.multiple_of(f * half, 128), half)
-                ref[: 3 * wide, :] = mix[:, piece].astype(ref.dtype)
-                ref[3 * wide : 4 * wide, :] = out[:, piece].astype(ref.dtype)
-                both = jnp.concatenate([vectors[:, :half], vectors[:, half:]], axis=0)
-                ref[4 * wide : 4 * wide + 16, :] = both.astype(ref.dtype)
-                ref[4 * wide + 16 :, :] = jnp.zeros((48, half), ref.dtype)
-        else:
-            first_ref[: 3 * wide, :] = mix[...]
-            first_ref[3 * wide :, :] = out[...]
-            second_ref[...] = small[...]
-
-
-def back(split, at, o, dq, dk, dv, n1_own, n1_other, xhat_own, xhat_other, g, ff, a2, weights,
-         scale, small_ff):
+
+    ot = jnp.concatenate([r[...] for r in o], axis=0)
+    emit(keep_ref, send_ref, mm(ot, w_ref[...], 0, 0) + ff_ref[...].astype(F32))
+    out[...] += mm(ot, g_ref[...])
+
+
+def branch(o, g, ff, weights):
     rows, width = g.shape
     heads = len(o)
     wide = heads * HEAD
-
-    def branch(i, at):
-        return jnp.minimum(i, 3)
-
-    def own(i, at):
-        return jnp.clip(i - 4, 0, 3)
-
-    def other(i, at):
-        return jnp.maximum(i - 8, 0)
-
-    def key(i, at):
-        return jnp.maximum(i - 4, 0)
-
-    def row(of):
-        return pl.BlockSpec((STEP, width), lambda i, at: (of(i, at), 0))
-
-    def col(of):
-        return [pl.BlockSpec((HEAD, STEP), lambda i, at: (0, of(i, at)))] * heads
+    row = pl.BlockSpec((STEP, width), lambda i: (i, 0))
+    slots = pl.BlockSpec((1, STEP, width), lambda i: (i // 2, 0, 0))
+    return pl.pallas_call(
+        functools.partial(branch_kernel, heads),
+        grid=(rows // STEP,),
+        in_specs=[pl.BlockSpec((HEAD, STEP), lambda i: (0, i))] * heads
+        + [row, row, pl.BlockSpec((wide, width), lambda i: (3, 0))],
+        out_specs=[slots, slots, pl.BlockSpec((wide, width), lambda i: (0, 0))],
+        out_shape=[low_shape(2, STEP, width)] * 2 + [shape(wide, width)],
+        compiler_params=params(24),
+        cost_estimate=cost(4 * rows * width * wide, 8 * MIB),
+    )(*o, g, ff, weights)
+
+
+def back_kernel(own, split, heads, at, *refs):
+    count = 3 if own else 2
+    grads, refs = refs[: count * heads], refs[count * heads :]
+    n1_ref, xhat_ref, w_ref, s1_ref, *refs = refs
+    if own:
+        (a2_ref, small_ff, small_other, mix_other, out_part, after,
+         keep_ref, send_ref, first_ref, second_ref, mix, small) = refs
+    else:
+        keep_ref, send_ref, mix, small = refs
+    i = pl.program_id(0)
+    wide = heads * HEAD
+    tall = mix.shape[0]
+
+    @pl.when(i == 0)
+    def _():
+        if own:
+            mix[:wide, :] = jnp.zeros((wide, mix.shape[1]), F32)
+            mix[wide:, :] = mix_other[...]
+            small[...] = small_other[...]
+        else:
+            mix[...] = jnp.zeros_like(mix)
+            small[...] = jnp.zeros_like(small)
+
+    grad = jnp.concatenate([r[...] for r in grads], axis=0)
+    first = mm(grad, w_ref[3 * wide - tall : 3 * wide, :], 0, 0)
+    a = first * row_of(s1_ref)
+    emit(keep_ref, send_ref, a + a2_ref[...].astype(F32) if own else a)
+    mix[...] += mm(grad, n1_ref[...])
+    small[0:1, :] += jnp.sum(first * xhat_ref[...].astype(F32), axis=0, keepdims=True)
+    small[1:2, :] += jnp.sum(first, axis=0, keepdims=True)
+    ones = jnp.ones((8, grad.shape[1]), BF16)
+    small[6:7, 3 * wide - tall : 3 * wide] += mm(ones, grad, 1, 1)[0:1]
+
+    if own:
+        @pl.when(i == pl.num_programs(0) - 1)
+        def _():
+            small[2:4, :] = small_ff[2:4, :]
+            small[4:6, :] = small_ff[0:2, :]
+            if split:
+                half = mix.shape[1] // 2
+                vectors = small[...].astype(BF16)
+                for ref, f in ((first_ref, at[3]), (second_ref, 1 - at[3])):
+                    piece = pl.ds(pl.multiple_of(f * half, 128), half)
+                    ref[: 3 * wide, :] = mix[:, piece].astype(ref.dtype)
+                    ref[3 * wide : 4 * wide, :] = out_part[:, piece].astype(ref.dtype)
+                    both = jnp.concatenate([vectors[:, :half], vectors[:, half:]], axis=0)
+                    ref[4 * wide : 4 * wide + 16, :] = both.astype(ref.dtype)
+                    ref[4 * wide + 16 :, :] = jnp.zeros((48, half), ref.dtype)
+            else:
+                first_ref[: 3 * wide, :] = mix[...]
+                first_ref[3 * wide :, :] = out_part[...]
+                second_ref[...] = small[...]
+
+
+def back(own, split, at, grads, n1, xhat, weights, scale, extra):
+    rows, width = n1.shape
+    heads = len(grads[0])
+    wide = heads * HEAD
+    tall = 3 * wide if own else 2 * wide
+    offset = 0 if own else rows // STEP
+    row = pl.BlockSpec((STEP, width), lambda i, at: (i, 0))
+    col = pl.BlockSpec((HEAD, STEP), lambda i, at: (0, i + offset))
+    slots = pl.BlockSpec((1, STEP, width), lambda i, at: (i // 2, 0, 0))
 
     def whole(*dims):
         return pl.BlockSpec(dims, lambda i, at: (0,) * len(dims))
 
-    def slot(i, at):
-        b = jnp.maximum(i - 4, 0) // 2
-        return (jnp.where(i < 4, 4 * (1 - i // 2), jnp.where(b == 0, 5, b)), 0, 0)
-
     half = width // 2
-    if split:
-        parts = [shape(4 * wide + 64, half), low_shape(4 * wide + 64, half)]
+    specs = [col] * (len(grads) * heads) + [row, row, whole(4 * wide, width), whole(width)]
+    if not own:
+        parts = [shape(tall, width), shape(8, width)]
+        scratch = []
     else:
-        parts = [shape(4 * wide, width), shape(8, width)]
-    slots = pl.BlockSpec((1, STEP, width), slot)
+        specs += [row, whole(8, width), whole(8, width), whole(2 * wide, width),
+                  whole(wide, width), pl.BlockSpec(memory_space=pl.ANY)]
+        scratch = [pltpu.VMEM((tall, width), F32), pltpu.VMEM((8, width), F32)]
+        if split:
+            parts = [shape(4 * wide + 64, half), low_shape(4 * wide + 64, half)]
+        else:
+            parts = [shape(4 * wide, width), shape(8, width)]
     return pl.pallas_call(
-        functools.partial(back_kernel, split, heads),
+        functools.partial(back_kernel, own, split, heads),
         grid_spec=pltpu.PrefetchScalarGridSpec(
             num_scalar_prefetch=1,
-            grid=(12,),
-            in_specs=col(branch) + col(own) + col(key) + col(key)
-            + [row(own), row(other), row(own), row(other), row(branch), row(branch), row(own),
-               whole(4 * wide, width), whole(width), whole(8, width)],
+            grid=(rows // STEP,),
+            in_specs=specs,
             out_specs=[slots, slots] + [whole(*p.shape) for p in parts],
-            scratch_shapes=[pltpu.VMEM((3 * wide, width), F32), pltpu.VMEM((wide, width), F32),
-                            pltpu.VMEM((8, width), F32)],
+            scratch_shapes=scratch,
         ),
-        out_shape=[low_shape(6, STEP, width)] * 2 + parts,
+        out_shape=[low_shape(2, STEP, width)] * 2 + parts,
         compiler_params=params(32),
-        cost_estimate=cost(28 * rows * width * wide, 20 * MIB),
-    )(at, *o, *dq, *dk, *dv, n1_own, n1_other, xhat_own, xhat_other, g, ff, a2, weights, scale,
-      small_ff)
-
-
-def finish_kernel(at, pair, core, x_ref, g_ref, bias_a, bias_b, out_ref, grad_ref):
-    j = at[2] ^ pl.program_id(1)
-
-    def write(part):
-        bias = row_of(bias_a) + row_of(bias_b)
-        out_ref[0] = x_ref[0].astype(F32) + part[0, 0, 0].astype(F32) + bias
-        grad_ref[0] = g_ref[0].astype(F32) + part[0, 1, 0].astype(F32)
-
-    @pl.when(j % 2 == 0)
-    def _():
-        write(pair)
-
-    @pl.when(j % 2 == 1)
-    def _():
-        write(core)
-
-
-def finish(at, pair, core, x, g, bias_a, bias_b):
-    seqs, block, width = x.shape
-    q = block // 4
-
-    def place(i, j, at):
-        return (i, j, 0)
-
-    piece = pl.BlockSpec(
-        (1, 2, 1, q, width), lambda i, j, at: ((at[2] ^ j) // 2, 0, at[0] ^ i, 0, 0)
-    )
-    rows = pl.BlockSpec((1, q, width), place)
-    vec = pl.BlockSpec((width,), lambda i, j, at: (0,))
-    return pl.pallas_call(
-        finish_kernel,
-        grid_spec=pltpu.PrefetchScalarGridSpec(
-            num_scalar_prefetch=1,
-            grid=(seqs, 4),
-            in_specs=[piece, piece, rows, rows, vec, vec],
-            out_specs=[rows, rows],
-        ),
-        out_shape=[shape(seqs, block, width)] * 2,
-        compiler_params=params(24),
-        cost_estimate=cost(0, 16 * seqs * block * width),
-    )(at, pair, core, x, g, bias_a, bias_b)
+        cost_estimate=cost(4 * rows * width * tall, 10 * MIB),
+    )(at, *[v for vs in grads for v in vs], n1, xhat, weights, scale, *extra)
 
 
 def swap(v, axis, size, distance):
@@ -579,10 +550,16 @@
             jnp.where(high, a, c), jnp.where(high, b, d))
 
 
-def gather_halves(shard, size, mine, dim):
+def tie(v, *earlier):
+    return lax.optimization_barrier((v, *earlier))[0]
+
+
+def gather_halves(shard, size, mine, dim, *earlier):
     if size != 2:
         return lax.all_gather(shard, "fsdp", axis=dim, tiled=True)
     other = swap(shard, "fsdp", 2, 1)
+    if earlier:
+        other = tie(other, *earlier)
     first = mine == 0
     return jnp.concatenate(
         [jnp.where(first, shard, other), jnp.where(first, other, shard)], axis=dim
@@ -595,19 +572,22 @@
     ).astype(F32)
 
 
-def sum_over_ctx(v, c):
-    low, high = c % 2, c // 2
+def halve(v, distance, bit):
     rows = v.shape[0] // 2
-    keep = lax.dynamic_slice_in_dim(v, low * rows, rows, 0)
-    send = lax.dynamic_slice_in_dim(v, (1 - low) * rows, rows, 0).astype(BF16)
-    v = keep + swap(send, "ctx", 4, 1).astype(F32)
-    rows = rows // 2
-    keep = lax.dynamic_slice_in_dim(v, high * rows, rows, 0)
-    send = lax.dynamic_slice_in_dim(v, (1 - high) * rows, rows, 0).astype(BF16)
-    v = (keep + swap(send, "ctx", 4, 2).astype(F32)).astype(BF16)
+    keep = lax.dynamic_slice_in_dim(v, bit * rows, rows, 0)
+    send = lax.dynamic_slice_in_dim(v, (1 - bit) * rows, rows, 0).astype(BF16)
+    return keep + swap(send, "ctx", 4, distance).astype(F32)
+
+
+def double(v, c):
+    v = v.astype(BF16)
     pair = jnp.stack([v, swap(v, "ctx", 4, 2)])
     others = swap(pair, "ctx", 4, 1)
-    return by_xor([pair[0], pair[1], others[0], others[1]], 2 * low + high)
+    return by_xor([pair[0], pair[1], others[0], others[1]], 2 * (c % 2) + c // 2)
+
+
+def sum_over_ctx(v, c):
+    return double(halve(halve(v, 1, c % 2), 2, c // 2), c)
 
 
 def butterfly(v, axis_name, size):
@@ -670,9 +650,7 @@
     wup = gather_halves(up_projection_weight, fsdp, f, 0)
     wdown = gather_halves(down_projection_weight, fsdp, f, 1)
     mix_shard = query_key_value_weight.transpose(1, 2, 0).reshape(3 * local, -1)
-    weights = gather_halves(
-        jnp.concatenate([mix_shard, attention_output_weight], axis=0), fsdp, f, 1
-    )
+    mix_out_shard = jnp.concatenate([mix_shard, attention_output_weight], axis=0)
 
     inverse = 10000.0 ** (-2.0 * jnp.arange(HALF, dtype=F32) / ROT)
     places = positions.astype(F32)[:, None, :]
@@ -688,58 +666,82 @@
     ff, a2, small_ff, ff_first, ff_second = feed_forward(
         split, at, n2, g, xhat_own, wup, up_projection_bias, wdown, second_scale
     )
+    weights = gather_halves(mix_out_shard, fsdp, f, 1, small_ff)
     n1_other, xhat_other, trig_other = norms(
-        at, False, others, trig, (first_scale, first_shift)
+        at, False, (others[0], others[1], tie(others[2], small_ff)), trig,
+        (first_scale, first_shift),
     )
     kt, vt, qt, dot = project(
         n1_own, n1_other, trig_own, trig_other, g, weights, query_key_value_bias
     )
+    if split:
+        ff_rest = ff_first + swap(ff_second, "fsdp", 2, 1).astype(F32)
+    else:
+        ff_rest = small_ff
     per_head = []
-    after = small_ff
     for h in range(heads):
+        after = ff_rest if h == heads - 1 else small_ff
         per_head.append(attention(h, after, qt, dot, kt, vt, trig_own, trig_other))
-        after = per_head[-1][0]
     o, dq, dk, dv = zip(*per_head)
-    keep, send, late_first, late_second = back(
-        split, at, o, dq, dk, dv, n1_own, n1_other, xhat_own, xhat_other, g, ff, a2, weights,
-        first_scale, small_ff,
-    )
-
-    half_sums = keep.astype(F32) + swap(send, "tp", 4, 1).astype(F32)
-    half_sums = half_sums.reshape(6, 2, quarter, width)
-
-    def over_x(v):
+    keep_b, send_b, out_part = branch(o, g, ff, weights)
+    if split:
+        ff_half = halve(ff_rest, 1, c % 2)
+    else:
+        ff_half = small_ff
+    keep_o, send_o, mix_other, small_other = back(
+        False, split, at, (dk, dv), n1_other, xhat_other, weights, first_scale, ()
+    )
+    keep_w, send_w, late_first, late_second = back(
+        True, split, at, (dq, dk, dv), n1_own, xhat_own, weights, first_scale,
+        (a2, small_ff, small_other, mix_other, out_part, ff_half),
+    )
+
+    def scatter_tp(keep, send):
+        v = keep.astype(F32) + swap(send, "tp", 4, 1).astype(F32)
+        v = v.reshape(2, 2, quarter, width)
         return v[:, 0] + swap(v[:, 1].astype(BF16), "tp", 4, 2).astype(F32)
 
-    travel = over_x(half_sums[0:4]).astype(BF16)
-    far_back = swap(travel[0:2], "ctx", 4, 2).astype(F32)
-    near_back = swap(travel[2], "ctx", 4, 1).astype(F32)
-    cross_back = swap(travel[3], "ctx", 4, 3).astype(F32)
-    stay = over_x(half_sums[4:6])
-    branches = jnp.stack([stay[0], far_back[0]])
-    a = jnp.stack([stay[1] + near_back, far_back[1] + cross_back])
+    def over_ctx(v, distance):
+        return swap(v.astype(BF16), "ctx", 4, distance).astype(F32)
+
+    def gather_tp(mine, theirs):
+        ours = jnp.stack([mine, theirs]).astype(BF16)
+        pair = jnp.stack([ours, swap(ours, "tp", 4, 2)])
+        core = swap(pair, "tp", 4, 1)
+        pieces = by_xor((pair[0], core[0], pair[1], core[1]), t)
+        pieces = jnp.concatenate(pieces, axis=1)
+        return jnp.stack([jnp.where(s == 0, pieces[0], pieces[1]),
+                          jnp.where(s == 0, pieces[1], pieces[0])]).astype(F32)
+
+    sums_b = scatter_tp(keep_b, send_b)
+    block_out = gather_tp(sums_b[0], over_ctx(sums_b[1], 2))
+    block_out = (
+        inputs.astype(F32) + block_out + (attention_output_bias + down_projection_bias)
+    )
+
+    sums_o = scatter_tp(keep_o, send_o)
+    sums_w = scatter_tp(keep_w, send_w)
+    a = jnp.stack([
+        sums_w[0] + over_ctx(sums_o[0], 1),
+        over_ctx(sums_w[1], 2) + over_ctx(sums_o[1], 3),
+    ])
     xhat, inv = xhat_of(jnp.concatenate([x_mine, x_theirs], axis=0).astype(F32))
     norm_grad = inv * (
         a
         - jnp.mean(a, axis=-1, keepdims=True)
         - xhat * jnp.mean(a * xhat, axis=-1, keepdims=True)
     )
-    ours = jnp.stack([branches, norm_grad]).astype(BF16)
-    pair = jnp.stack([ours, swap(ours, "tp", 4, 2)])
-    core = swap(pair, "tp", 4, 1)
-    block_out, inputs_grad = finish(
-        at, pair, core, inputs, cotangent, attention_output_bias, down_projection_bias
-    )
+    inputs_grad = cotangent.astype(F32) + gather_tp(norm_grad[0], norm_grad[1])
 
     if split:
-        q = sum_over_ctx(ff_first + swap(ff_second, "fsdp", 2, 1).astype(F32), c)
+        q = double(halve(ff_half, 2, c // 2), c)
         up_total = jnp.concatenate(q[:2], axis=0).astype(F32)
         down_total = jnp.concatenate(q[2:], axis=0).astype(F32)
         down_total = jnp.concatenate(
             [down_total[:, : width // 2], down_total[:, width // 2 :]], axis=0
         )
-        q = sum_over_ctx(late_first + swap(late_second, "fsdp", 2, 1).astype(F32), c)
-        late = jnp.concatenate(q, axis=0).astype(F32)
+        late = late_first + swap(late_second, "fsdp", 2, 1).astype(F32)
+        late = jnp.concatenate(sum_over_ctx(late, c), axis=0).astype(F32)
         small = jnp.concatenate([late[4 * local : 4 * local + 8], late[4 * local + 8 :][:8]], axis=1)
     else:
         q = sum_over_ctx(scatter_any(ff_first, 0), c)

time: 286 us -> 230 us (0.80)
  waiting for transfers between devices: 127 us -> 85.9 us
  Pallas kernels: 73.1 us -> 62.4 us
  local copies, waits for them, and re-layouts: 15.9 us -> 10.7 us
    ppermute x30 -> x36, waiting for transfers between devices: 127 us -> 85.9 us  [swap(): return lax.ppermute(v, axis, [(i, i ^ distance) for i in range(size)])]
    pallas_call x2 -> x3, Pallas kernels: 23.1 us -> 13.9 us  [the longest x2 11.2 us: back(): pl.pallas_call(functools.partial(back_kernel, own, split, heads), grid_sp...]
    unnamed x92 -> x100, local copies, waits for them, and re-layouts: 7.87 us -> 4.59 us
    add x6 -> x12, other arithmetic: 8.91 us -> 6.74 us  [the longest x1 2.08 us: shards(): inputs.astype(F32) + block_out]
    ppermute x30 -> x36, starting transfers between devices: 39.1 us -> 40.6 us  [swap(): return lax.ppermute(v, axis, [(i, i ^ distance) for i in range(size)])]
  transfers between devices with their start and end apart: 30 -> 36, of which waited for: 13 -> 12; matrix products, arithmetic and copies ran while one was open for 12% -> 13% of each run, Pallas kernels for 1% -> 27%
where the time goes in v3:
time: 230 us
  waiting for transfers between devices  85.9 us (37%)
  Pallas kernels  62.4 us (27%)
  starting transfers between devices  40.6 us (18%)
  other arithmetic  28.3 us (12%)
  local copies, waits for them, and re-layouts  10.7 us (5%)
    ppermute x36, waiting for transfers between devices, swap(): return lax.ppermute(v, axis, [(i, i ^ distance) for i in range(size)])  85.9 us
    ppermute x36, starting transfers between devices, swap(): return lax.ppermute(v, axis, [(i, i ^ distance) for i in range(size)])  40.6 us
    pallas_call x3, Pallas kernels, attention(): pl.pallas_call(attention_kernel, grid=(rows // lanes,), in_specs=[pl.Bloc...  29.1 us
    pallas_call x2, Pallas kernels, back(): pl.pallas_call(functools.partial(back_kernel, own, split, heads), grid_sp...  11.2 us
    pallas_call x1, Pallas kernels, feed_forward(): pl.pallas_call(functools.partial(forward_kernel, split), grid_spec=pltpu....  9.8 us
    pallas_call x2, Pallas kernels, norms(): pl.pallas_call(kernel, grid_spec=pltpu.PrefetchScalarGridSpec(num_scalar_...  5.07 us
  transfers between devices with their start and end apart: 36, of which 12 were waited for; matrix products, arithmetic and copies ran while one was open for 13% of the time, Pallas kernels for 27%

profile of v3, /device:TPU:0, one launch (start us, length us, event | category | flops | bytes accessed | tf_op | source)
XLA Modules:
  0.0 229.7 jit_solution(14218894254916172864)
XLA Ops:
  0.7 1.1 constant_dynamic-slice_fusion
  1.9 5.1 %collective-permute-start.6 = (bf16[1,128,768]{2,1,0:T(8,128)(2,1)S(1)}, bf16[1,128,768]{2,1,0:T(8,128)(2,1)S(1)}, u32[]{:S(2)}, u32[]{:S(2)}) collective-permute-start(bf16[1,128,768]{2,1,0:T(8,128)(2,1)S(1)} %get-tuple-element.118), channel_id=1, source_target_pairs={{0,12},{4,8},{8,4},{12,0},{1,13},{5,9},{9,5},{13,1},{2,14},{6,10},... | collective-permute-start | bytes 589832 | tf_op jit(solution)/shard_map/ppermute | solution.py:541
  8.1 1.6 collective-permute-start.4
  12.5 11.3 %collective-permute-done.5 = bf16[1,128,768]{2,1,0:T(8,128)(2,1)S(1)} collective-permute-done((bf16[1,128,768]{2,1,0:T(8,128)(2,1)S(1)}, bf16[1,128,768]{2,1,0:T(8,128)(2,1)S(1)}, u32[]{:S(2)}, u32[]{:S(2)}) %collective-permute-start.5) | collective-permute-done | bytes 196640 | tf_op jit(solution)/shard_map/ppermute | solution.py:541
  23.9 1.5 collective-permute-start.9
  25.4 1.6 collective-permute-start.7
  27.0 5.1 %collective-permute-done.fz = bf16[2,128,768]{2,1,0:T(8,128)(2,1)S(1)} collective-permute-done((bf16[2,128,768]{2,1,0:T(8,128)(2,1)S(1)}, bf16[2,128,768]{2,1,0:T(8,128)(2,1)S(1)}, u32[]{:S(2)}, u32[]{:S(2)}) %collective-permute-start) | collective-permute-done | bytes 393248 | tf_op jit(solution)/shard_map/ppermute | solution.py:541
  32.1 1.5 collective-permute-start.1
  34.0 1.3 add.132
  35.3 8.4 %collective-permute-done.1.fx = bf16[2,128,768]{2,1,0:T(8,128)(2,1)S(1)} collective-permute-done((bf16[2,128,768]{2,1,0:T(8,128)(2,1)S(1)}, bf16[2,128,768]{2,1,0:T(8,128)(2,1)S(1)}, u32[]{:S(2)}, u32[]{:S(2)}) %collective-permute-start.1) | collective-permute-done | bytes 393248 | tf_op jit(solution)/shard_map/ppermute | solution.py:541
  44.5 1.2 broadcast_select_fusion.7
  45.8 1.2 broadcast_select_fusion.9
  49.0 2.8 %shard_map.254 = (bf16[1024,768]{1,0:T(8,128)(2,1)S(1)}, bf16[1024,768]{1,0:T(8,128)(2,1)S(1)}, bf16[1024,768]{1,0:T(8,128)(2,1)S(1)}, bf16[1024,768]{1,0:T(8,128)(2,1)S(1)}, f32[24,1024]{1,0:T(8,128)S(1)}) custom-call(s32[4]{0:T(128)S(1)} %pad_add_fusion.at, bf16[2,512,768]{2,1,0:T(8,128)(2,1)S(1)} %copy-done, bf16[2,512,768]{2,1,0:T(8,128)(2,1)S(1)} %copy-done, ...), custom_call_target="tpu_custom_call" | custom-call | bytes 4718592 | tf_op jit(solution)/shard_map/pallas_call | solution.py:142
  51.9 9.8 %shard_map.255 = (bf16[1024,768]{1,0:T(8,128)(2,1)S(1)}, bf16[1024,768]{1,0:T(8,128)(2,1)S(1)}, f32[8,768]{1,0:T(8,128)S(1)}, f32[768,768]{1,0:T(8,128)S(1)}, bf16[768,768]{1,0:T(8,128)(2,1)S(1)}) custom-call(s32[4]{0:T(128)S(1)} %pad_add_fusion.at, bf16[1024,768]{1,0:T(8,128)(2,1)S(1)} %get-tuple-element.56.n2_ref, ...), custom_call_target="tpu_custom_call" | custom-call | flops 7247757312 | bytes 16777216 | tf_op jit(solution)/shard_map/pallas_call | solution.py:383
  62.3 1.3 broadcast_select_fusion.5
  64.7 2.2 shard_map.256
  66.9 4.5 %shard_map.257 = (bf16[192,2048]{1,0:T(8,128)(2,1)S(1)}, bf16[192,2048]{1,0:T(8,128)(2,1)S(1)}, bf16[192,1024]{1,0:T(8,128)(2,1)S(1)}, bf16[192,1024]{1,0:T(8,128)(2,1)S(1)}) custom-call(bf16[1024,768]{1,0:T(8,128)(2,1)S(1)} %get-tuple-element.60.n1o.refs_9_, bf16[1024,768]{1,0:T(8,128)(2,1)S(1)} %get-tuple-element.62.n1x.refs_6_, ...), custom_call_target="tpu_custom_call" | custom-call | flops 1811939328 | bytes 9437184 | tf_op jit(solution)/shard_map/pallas_call | solution.py:206
  71.5 9.7 %shard_map.259 = (bf16[64,1024]{1,0:T(8,128)(2,1)S(1)}, bf16[64,1024]{1,0:T(8,128)(2,1)S(1)}, bf16[64,2048]{1,0:T(8,128)(2,1)S(1)}, bf16[64,2048]{1,0:T(8,128)(2,1)S(1)}) custom-call(f32[8,768]{1,0:T(8,128)S(1)} %get-tuple-element.59.after.refs_14_, bf16[192,1024]{1,0:T(8,128)(2,1)S(1)} %get-tuple-element.66.q_ref, ...), custom_call_target="tpu_custom_call" | custom-call | flops 5368709120 | bytes 2097152 | tf_op jit(solution)/shard_map/pallas_call | solution.py:309
  81.2 9.7 %shard_map.258 = (bf16[64,1024]{1,0:T(8,128)(2,1)S(1)}, bf16[64,1024]{1,0:T(8,128)(2,1)S(1)}, bf16[64,2048]{1,0:T(8,128)(2,1)S(1)}, bf16[64,2048]{1,0:T(8,128)(2,1)S(1)}) custom-call(f32[8,768]{1,0:T(8,128)S(1)} %get-tuple-element.59.after.refs_14_, bf16[192,1024]{1,0:T(8,128)(2,1)S(1)} %get-tuple-element.66.q_ref, ...), custom_call_target="tpu_custom_call" | custom-call | flops 5368709120 | bytes 2097152 | tf_op jit(solution)/shard_map/pallas_call | solution.py:309
  91.4 2.6 %collective-permute-start.16 = (bf16[384,768]{1,0:T(8,128)(2,1)S(1)}, bf16[384,768]{1,0:T(8,128)(2,1)S(1)}, u32[]{:S(2)}, u32[]{:S(2)}) collective-permute-start(bf16[384,768]{1,0:T(8,128)(2,1)S(1)} %dynamic-slice_convert_fusion), channel_id=1, source_target_pairs={{0,4},{4,0},{8,12},{12,8},{1,5},{5,1},{9,13},{13,9},{2,6},{6,2},{1... | collective-permute-start | bytes 1769480 | tf_op jit(solution)/shard_map/ppermute | solution.py:541
  94.0 9.7 %shard_map.260 = (bf16[64,1024]{1,0:T(8,128)(2,1)S(1)}, bf16[64,1024]{1,0:T(8,128)(2,1)S(1)}, bf16[64,2048]{1,0:T(8,128)(2,1)S(1)}, bf16[64,2048]{1,0:T(8,128)(2,1)S(1)}) custom-call(f32[768,768]{1,0:T(8,128)S(1)} %convert_add_fusion.1.after, bf16[192,1024]{1,0:T(8,128)(2,1)S(1)} %get-tuple-element.66.q_ref, bf16[192,1024]{1,0:T(8,128)(2,1)S(1)} %get-tuple-element.67.do_ref, ...), custom_call_target="tpu_custom_call" | custom-call | flops 5368709120 | bytes 2097152 | tf_op jit(solution)/shard_map/pallas_call | solution.py:309
  103.7 4.9 %shard_map.262 = (bf16[2,256,768]{2,1,0:T(8,128)(2,1)S(1)}, bf16[2,256,768]{2,1,0:T(8,128)(2,1)S(1)}, f32[384,768]{1,0:T(8,128)S(1)}, f32[8,768]{1,0:T(8,128)S(1)}) custom-call(s32[4]{0:T(128)S(1)} %pad_add_fusion.at, bf16[64,2048]{1,0:T(8,128)(2,1)S(1)} %get-tuple-element.81.refs_0_.refs_3_, bf16[64,2048]{1,0:T(8,128)(2,1)S(1)} %get-tuple-element.82.refs_1_.refs_4_, ...), custom_call_target="tpu_custom_call" | custom-call | flops 1207959552 | bytes 10485760 | tf_op jit(solution)/shard_map/pallas_call | solution.py:525
  108.8 2.7 %shard_map.261 = (bf16[2,256,768]{2,1,0:T(8,128)(2,1)S(1)}, bf16[2,256,768]{2,1,0:T(8,128)(2,1)S(1)}, f32[192,768]{1,0:T(8,128)S(1)}) custom-call(bf16[64,1024]{1,0:T(8,128)(2,1)S(1)} %get-tuple-element.70.refs_0_, bf16[64,1024]{1,0:T(8,128)(2,1)S(1)} %get-tuple-element.71.refs_1_, bf16[64,1024]{1,0:T(8,128)(2,1)S(1)} %get-tuple-element.74.refs_2_, ...), custom_call_target="tpu_custom_call" | custom-call | flops 603979776 | bytes 8388608 | tf_op jit(solution)/shard_map/pallas_call | solution.py:433
  112.3 6.2 %shard_map.263 = (bf16[2,256,768]{2,1,0:T(8,128)(2,1)S(1)}, bf16[2,256,768]{2,1,0:T(8,128)(2,1)S(1)}, f32[832,384]{1,0:T(8,128)S(1)}, bf16[832,384]{1,0:T(8,128)(2,1)S(1)}) custom-call(s32[4]{0:T(128)S(1)} %pad_add_fusion.at, bf16[64,1024]{1,0:T(8,128)(2,1)S(1)} %get-tuple-element.78.refs_0_, bf16[64,1024]{1,0:T(8,128)(2,1)S(1)} %get-tuple-element.79.refs_1_, ...), custom_call_target="tpu_custom_call" | custom-call | flops 1811939328 | bytes 10485760 | tf_op jit(solution)/shard_map/pallas_call | solution.py:525
  118.5 1.6 collective-permute-start.26
  120.4 1.6 collective-permute-start.20
  121.9 6.3 %collective-permute-done.33 = bf16[192,768]{1,0:T(8,128)(2,1)S(1)} collective-permute-done((bf16[192,768]{1,0:T(8,128)(2,1)S(1)}, bf16[192,768]{1,0:T(8,128)(2,1)S(1)}, u32[]{:S(2)}, u32[]{:S(2)}) %collective-permute-start.33) | collective-permute-done | bytes 294944 | tf_op jit(solution)/shard_map/ppermute | solution.py:541
  128.6 1.6 collective-permute-start.12
  130.2 11.8 %collective-permute-done.34 = bf16[192,768]{1,0:T(8,128)(2,1)S(1)} collective-permute-done((bf16[192,768]{1,0:T(8,128)(2,1)S(1)}, bf16[192,768]{1,0:T(8,128)(2,1)S(1)}, u32[]{:S(2)}, u32[]{:S(2)}) %collective-permute-start.34) | collective-permute-done | bytes 294944 | tf_op jit(solution)/shard_map/ppermute | solution.py:541
  142.3 2.1 collective-permute-start.21
  144.4 2.6 %collective-permute-start.23 = (bf16[128,768]{1,0:T(8,128)(2,1)S(1)}, bf16[128,768]{1,0:T(8,128)(2,1)S(1)}, u32[]{:S(2)}, u32[]{:S(2)}) collective-permute-start(bf16[128,768]{1,0:T(8,128)(2,1)S(1)} %get-tuple-element.142), channel_id=1, source_target_pairs={{0,12},{4,8},{8,4},{12,0},{1,13},{5,9},{9,5},{13,1},{2,14},{6,10},... | collective-permute-start | bytes 589832 | tf_op jit(solution)/shard_map/ppermute | solution.py:541
  147.4 1.8 collective-permute-start.13
  149.4 27.5 %collective-permute-done.27 = bf16[416,384]{1,0:T(8,128)(2,1)S(1)} collective-permute-done((bf16[416,384]{1,0:T(8,128)(2,1)S(1)}, bf16[416,384]{1,0:T(8,128)(2,1)S(1)}, u32[]{:S(2)}, u32[]{:S(2)}) %collective-permute-start.27) | collective-permute-done | bytes 319520 | tf_op jit(solution)/shard_map/ppermute | solution.py:541
  177.2 1.1 collective-permute-start.18
  178.3 7.2 %collective-permute-done.28 = bf16[208,384]{1,0:T(8,128)(2,1)S(1)} collective-permute-done((bf16[208,384]{1,0:T(8,128)(2,1)S(1)}, bf16[208,384]{1,0:T(8,128)(2,1)S(1)}, u32[]{:S(2)}, u32[]{:S(2)}) %collective-permute-start.28) | collective-permute-done | bytes 159776 | tf_op jit(solution)/shard_map/ppermute | solution.py:541
  187.5 4.8 %collective-permute-start.22 = (bf16[128,768]{1,0:T(8,128)(2,1)S(1)}, bf16[128,768]{1,0:T(8,128)(2,1)S(1)}, u32[]{:S(2)}, u32[]{:S(2)}) collective-permute-start(bf16[128,768]{1,0:T(8,128)(2,1)S(1)} %fusion.26), channel_id=1, source_target_pairs={{0,8},{4,12},{8,0},{12,4},{1,9},{5,13},{9,1},{13,5},{2,10},{6,14},... | collective-permute-start | bytes 589832 | tf_op jit(solution)/shard_map/ppermute | solution.py:541
  194.7 1.9 collective-permute-done.14
  198.3 1.4 collective-permute-start.30
  199.7 2.8 %collective-permute-done.22 = bf16[128,768]{1,0:T(8,128)(2,1)S(1)} collective-permute-done((bf16[128,768]{1,0:T(8,128)(2,1)S(1)}, bf16[128,768]{1,0:T(8,128)(2,1)S(1)}, u32[]{:S(2)}, u32[]{:S(2)}) %collective-permute-start.22) | collective-permute-done | bytes 196640 | tf_op jit(solution)/shard_map/ppermute | solution.py:541
  204.0 1.8 collective-permute-start.24
  206.8 2.4 %collective-permute-done.30 = bf16[2,208,384]{2,1,0:T(8,128)(2,1)S(1)} collective-permute-done((bf16[2,208,384]{2,1,0:T(8,128)(2,1)S(1)}, bf16[2,208,384]{2,1,0:T(8,128)(2,1)S(1)}, u32[]{:S(2)}, u32[]{:S(2)}) %collective-permute-start.30) | collective-permute-done | bytes 319520 | tf_op jit(solution)/shard_map/ppermute | solution.py:541
  211.3 1.8 collective-permute-start.32
  214.4 1.4 reshape_squeeze.3
  215.8 2.2 slice.186
  221.3 1.3 broadcast_select_fusion.25
  223.4 2.1 add_add_fusion
  225.5 1.4 broadcast_select_fusion.21
  227.1 2.0 convert_add_fusion
  (216 shorter events, 28.1 us)
Async XLA Ops:
  0.7 10.2 %copy-start.46 = (s32[2,2048]{1,0:T(2,128)S(1)}, s32[2,2048]{1,0:T(2,128)}, u32[]{:S(2)}) copy-start(s32[2,2048]{1,0:T(2,128)} %param.16) | copy-start | bytes 49156
  1.8 31.8 %copy-start.16 = (bf16[1,128,768]{2,1,0:T(8,128)(2,1)}, bf16[1,128,768]{2,1,0:T(8,128)(2,1)S(1)}, u32[]{:S(2)}) copy-start(bf16[1,128,768]{2,1,0:T(8,128)(2,1)S(1)} %get-tuple-element.118) | copy-start | bytes 589828
  1.9 31.8 %copy-start.18 = (bf16[1,128,768]{2,1,0:T(8,128)(2,1)}, bf16[1,128,768]{2,1,0:T(8,128)(2,1)S(1)}, u32[]{:S(2)}) copy-start(bf16[1,128,768]{2,1,0:T(8,128)(2,1)S(1)} %get-tuple-element.117) | copy-start | bytes 589828
  1.9 9.8 %copy-start.26 = (bf16[384,3,192]{0,2,1:T(8,128)(2,1)S(1)}, bf16[384,3,192]{0,2,1:T(8,128)(2,1)}, u32[]{:S(2)}) copy-start(bf16[384,3,192]{0,2,1:T(8,128)(2,1)} %param.17) | copy-start | bytes 1327108
  1.9 23.5 %collective-permute-start.6 = (bf16[1,128,768]{2,1,0:T(8,128)(2,1)S(1)}, bf16[1,128,768]{2,1,0:T(8,128)(2,1)S(1)}, u32[]{:S(2)}, u32[]{:S(2)}) collective-permute-start(bf16[1,128,768]{2,1,0:T(8,128)(2,1)S(1)} %get-tuple-element.118), channel_id=1, source_target_pairs={{0,12},{4,8},{8,4},{12,0},{1,13},{5,9},{9,5},{13,1},{2,14},{6,10},... | collective-permute-start | bytes 589832 | tf_op jit(solution)/shard_map/ppermute | solution.py:541
  8.0 24.1 %collective-permute-start = (bf16[2,128,768]{2,1,0:T(8,128)(2,1)S(1)}, bf16[2,128,768]{2,1,0:T(8,128)(2,1)S(1)}, u32[]{:S(2)}, u32[]{:S(2)}) collective-permute-start(bf16[2,128,768]{2,1,0:T(8,128)(2,1)S(1)} %pad_maximum_fusion.13), channel_id=1, source_target_pairs={{0,8},{4,12},{8,0},{12,4},{1,9},{5,13},{9,1},{13,5},{2,10},{6,14},... | collective-permute-start | bytes 1179656 | tf_op jit(solution)/shard_map/ppermute | solution.py:541
  8.1 36.4 %collective-permute-start.4 = (bf16[768,384]{1,0:T(8,128)(2,1)S(1)}, bf16[768,384]{1,0:T(8,128)(2,1)}, u32[]{:S(2)}, u32[]{:S(2)}) collective-permute-start(bf16[768,384]{1,0:T(8,128)(2,1)S(1)} %copy-done.35), channel_id=1, source_target_pairs={{0,16},{16,0},{1,17},{17,1},{2,18},{18,2},{3,19},{19,3},{4,20},{20... | collective-permute-start | bytes 1769480 | tf_op jit(solution)/shard_map/ppermute | solution.py:541
  9.7 36.1 %collective-permute-start.3 = (bf16[384,768]{1,0:T(8,128)(2,1)S(1)}, bf16[384,768]{1,0:T(8,128)(2,1)}, u32[]{:S(2)}, u32[]{:S(2)}) collective-permute-start(bf16[384,768]{1,0:T(8,128)(2,1)S(1)} %copy-done.36), channel_id=1, source_target_pairs={{0,16},{16,0},{1,17},{17,1},{2,18},{18,2},{3,19},{19,3},{4,20},{20... | collective-permute-start | bytes 1769480 | tf_op jit(solution)/shard_map/ppermute | solution.py:541
  10.2 13.7 %collective-permute-start.5 = (bf16[1,128,768]{2,1,0:T(8,128)(2,1)S(1)}, bf16[1,128,768]{2,1,0:T(8,128)(2,1)S(1)}, u32[]{:S(2)}, u32[]{:S(2)}) collective-permute-start(bf16[1,128,768]{2,1,0:T(8,128)(2,1)S(1)} %get-tuple-element.117), channel_id=1, source_target_pairs={{0,4},{4,0},{8,12},{12,8},{1,5},{5,1},{9,13},{13,9},{2,6},{6,2},{1... | collective-permute-start | bytes 589832 | tf_op jit(solution)/shard_map/ppermute | solution.py:541
  11.5 22.5 %copy-start.48 = (f32[768]{0:T(1024)S(1)}, f32[768]{0:T(1024)}, u32[]{:S(2)}) copy-start(f32[768]{0:T(1024)} %param.20) | copy-start | bytes 9220
  23.9 38.4 %collective-permute-start.9 = (bf16[768,384]{1,0:T(8,128)(2,1)}, bf16[768,384]{1,0:T(8,128)(2,1)}, u32[]{:S(2)}, u32[]{:S(2)}) collective-permute-start(bf16[768,384]{1,0:T(8,128)(2,1)} %pad_maximum_fusion.11), channel_id=1, source_target_pairs={{0,16},{16,0},{1,17},{17,1},{2,18},{18,2},{3,19},{19,3},{4,20},{20... | collective-permute-start | bytes 1769480 | tf_op jit(solution)/shard_map/ppermute | solution.py:541
  25.4 18.5 %copy-start.2 = (bf16[2,128,768]{2,1,0:T(8,128)(2,1)}, bf16[2,128,768]{2,1,0:T(8,128)(2,1)S(1)}, u32[]{:S(2)}) copy-start(bf16[2,128,768]{2,1,0:T(8,128)(2,1)S(1)} %constant_dynamic-update-slice_fusion.nz) | copy-start | bytes 1179652
  25.4 18.4 %collective-permute-start.7 = (bf16[2,128,768]{2,1,0:T(8,128)(2,1)S(1)}, bf16[2,128,768]{2,1,0:T(8,128)(2,1)S(1)}, u32[]{:S(2)}, u32[]{:S(2)}) collective-permute-start(bf16[2,128,768]{2,1,0:T(8,128)(2,1)S(1)} %constant_dynamic-update-slice_fusion.nz), channel_id=1, source_target_pairs={{0,2},{1,3},{2,0},{3,1},{4,6},{5,7},{6,4},{7,5},{8,10},{9,11},{10,... | collective-permute-start | bytes 1179656 | tf_op jit(solution)/shard_map/ppermute | solution.py:541
  32.1 11.8 %copy-start.4 = (bf16[2,128,768]{2,1,0:T(8,128)(2,1)}, bf16[2,128,768]{2,1,0:T(8,128)(2,1)S(1)}, u32[]{:S(2)}) copy-start(bf16[2,128,768]{2,1,0:T(8,128)(2,1)S(1)} %collective-permute-done.fz) | copy-start | bytes 1179652
  32.1 11.5 %collective-permute-start.1 = (bf16[2,128,768]{2,1,0:T(8,128)(2,1)S(1)}, bf16[2,128,768]{2,1,0:T(8,128)(2,1)S(1)}, u32[]{:S(2)}, u32[]{:S(2)}) collective-permute-start(bf16[2,128,768]{2,1,0:T(8,128)(2,1)S(1)} %collective-permute-done.fz), channel_id=1, source_target_pairs={{0,2},{1,3},{2,0},{3,1},{4,6},{5,7},{6,4},{7,5},{8,10},{9,11},{10,... | collective-permute-start | bytes 1179656 | tf_op jit(solution)/shard_map/ppermute | solution.py:541
  43.8 3.4 %collective-permute-start.2 = (bf16[2,2,128,768]{3,2,1,0:T(8,128)(2,1)S(1)}, bf16[2,2,128,768]{3,2,1,0:T(8,128)(2,1)S(1)}, u32[]{:S(2)}, u32[]{:S(2)}) collective-permute-start(bf16[2,2,128,768]{3,2,1,0:T(8,128)(2,1)S(1)} %pad_maximum_fusion.6), channel_id=1, source_target_pairs={{0,1},{1,0},{2,3},{3,2},{4,5},{5,4},{6,7},{7,6},{8,9},{9,8},{10,11... | collective-permute-start | bytes 2359304 | tf_op jit(solution)/shard_map/ppermute | solution.py:541
  44.4 19.3 %collective-permute-start.8 = (bf16[2,2,128,768]{3,2,1,0:T(8,128)(2,1)S(1)}, bf16[2,2,128,768]{3,2,1,0:T(8,128)(2,1)S(1)}, u32[]{:S(2)}, u32[]{:S(2)}) collective-permute-start(bf16[2,2,128,768]{3,2,1,0:T(8,128)(2,1)S(1)} %pad_maximum_fusion.7), channel_id=1, source_target_pairs={{0,1},{1,0},{2,3},{3,2},{4,5},{5,4},{6,7},{7,6},{8,9},{9,8},{10,11... | collective-permute-start | bytes 2359304 | tf_op jit(solution)/shard_map/ppermute | solution.py:541
  51.8 10.4 %copy-start.27 = (bf16[384,3,192]{0,2,1:T(8,128)(2,1)S(1)}, bf16[384,3,192]{0,2,1:T(8,128)(2,1)}, u32[]{:S(2)}) copy-start(bf16[384,3,192]{0,2,1:T(8,128)(2,1)} %param.17) | copy-start | bytes 1327108
  51.9 10.4 %copy-start.34 = (bf16[192,384]{1,0:T(8,128)(2,1)S(1)}, bf16[192,384]{1,0:T(8,128)(2,1)}, u32[]{:S(2)}) copy-start(bf16[192,384]{1,0:T(8,128)(2,1)} %param.19) | copy-start | bytes 442372
  61.7 29.2 %collective-permute-start.10 = (bf16[768,768]{1,0:T(8,128)(2,1)S(1)}, bf16[768,768]{1,0:T(8,128)(2,1)S(1)}, u32[]{:S(2)}, u32[]{:S(2)}) collective-permute-start(bf16[768,768]{1,0:T(8,128)(2,1)S(1)} %get-tuple-element.73), channel_id=1, source_target_pairs={{0,16},{16,0},{1,17},{17,1},{2,18},{18,2},{3,19},{19,3},{4,20},{20... | collective-permute-start | bytes 3538952 | tf_op jit(solution)/shard_map/ppermute | solution.py:541
  91.4 20.7 %collective-permute-start.16 = (bf16[384,768]{1,0:T(8,128)(2,1)S(1)}, bf16[384,768]{1,0:T(8,128)(2,1)S(1)}, u32[]{:S(2)}, u32[]{:S(2)}) collective-permute-start(bf16[384,768]{1,0:T(8,128)(2,1)S(1)} %dynamic-slice_convert_fusion), channel_id=1, source_target_pairs={{0,4},{4,0},{8,12},{12,8},{1,5},{5,1},{9,13},{13,9},{2,6},{6,2},{1... | collective-permute-start | bytes 1769480 | tf_op jit(solution)/shard_map/ppermute | solution.py:541
  108.6 11.5 %collective-permute-start.19 = (bf16[2,256,768]{2,1,0:T(8,128)(2,1)S(1)}, bf16[2,256,768]{2,1,0:T(8,128)(2,1)S(1)}, u32[]{:S(2)}, u32[]{:S(2)}) collective-permute-start(bf16[2,256,768]{2,1,0:T(8,128)(2,1)S(1)} %get-tuple-element.95), channel_id=1, source_target_pairs={{0,1},{1,0},{2,3},{3,2},{4,5},{5,4},{6,7},{7,6},{8,9},{9,8},{10,11... | collective-permute-start | bytes 2359304 | tf_op jit(solution)/shard_map/ppermute | solution.py:541
  108.7 97.0 %copy-start.39 = (f32[2,128]{1,0:T(2,128)}, f32[2,128]{1,0:T(2,128)S(1)}, u32[]{:S(2)}) copy-start(f32[2,128]{1,0:T(2,128)S(1)} %add_rsqrt_fusion) | copy-start | bytes 3076
  111.5 16.9 %collective-permute-start.11 = (bf16[2,256,768]{2,1,0:T(8,128)(2,1)S(1)}, bf16[2,256,768]{2,1,0:T(8,128)(2,1)S(1)}, u32[]{:S(2)}, u32[]{:S(2)}) collective-permute-start(bf16[2,256,768]{2,1,0:T(8,128)(2,1)S(1)} %get-tuple-element.77), channel_id=1, source_target_pairs={{0,1},{1,0},{2,3},{3,2},{4,5},{5,4},{6,7},{7,6},{8,9},{9,8},{10,11... | collective-permute-start | bytes 2359304 | tf_op jit(solution)/shard_map/ppermute | solution.py:541
  112.2 16.0 %collective-permute-start.33 = (bf16[192,768]{1,0:T(8,128)(2,1)S(1)}, bf16[192,768]{1,0:T(8,128)(2,1)S(1)}, u32[]{:S(2)}, u32[]{:S(2)}) collective-permute-start(bf16[192,768]{1,0:T(8,128)(2,1)S(1)} %dynamic-slice_convert_fusion.2), channel_id=1, source_target_pairs={{0,8},{4,12},{8,0},{12,4},{1,9},{5,13},{9,1},{13,5},{2,10},{6,14},... | collective-permute-start | bytes 884744 | tf_op jit(solution)/shard_map/ppermute | solution.py:541
  118.5 28.6 %collective-permute-start.26 = (bf16[832,384]{1,0:T(8,128)(2,1)S(1)}, bf16[832,384]{1,0:T(8,128)(2,1)S(1)}, u32[]{:S(2)}, u32[]{:S(2)}) collective-permute-start(bf16[832,384]{1,0:T(8,128)(2,1)S(1)} %get-tuple-element.97), channel_id=1, source_target_pairs={{0,16},{16,0},{1,17},{17,1},{2,18},{18,2},{3,19},{19,3},{4,20},{20... | collective-permute-start | bytes 1916936 | tf_op jit(solution)/shard_map/ppermute | solution.py:541
  120.1 27.3 %collective-permute-start.17 = (bf16[2,256,768]{2,1,0:T(8,128)(2,1)S(1)}, bf16[2,256,768]{2,1,0:T(8,128)(2,1)S(1)}, u32[]{:S(2)}, u32[]{:S(2)}) collective-permute-start(bf16[2,256,768]{2,1,0:T(8,128)(2,1)S(1)} %get-tuple-element.93), channel_id=1, source_target_pairs={{0,1},{1,0},{2,3},{3,2},{4,5},{5,4},{6,7},{7,6},{8,9},{9,8},{10,11... | collective-permute-start | bytes 2359304 | tf_op jit(solution)/shard_map/ppermute | solution.py:541
  120.4 21.8 %collective-permute-start.20 = (bf16[2,128,768]{2,1,0:T(8,128)(2,1)S(1)}, bf16[2,128,768]{2,1,0:T(8,128)(2,1)S(1)}, u32[]{:S(2)}, u32[]{:S(2)}) collective-permute-start(bf16[2,128,768]{2,1,0:T(8,128)(2,1)S(1)} %fusion.19), channel_id=1, source_target_pairs={{0,2},{1,3},{2,0},{3,1},{4,6},{5,7},{6,4},{7,5},{8,10},{9,11},{10,... | collective-permute-start | bytes 1179656 | tf_op jit(solution)/shard_map/ppermute | solution.py:541
  128.3 13.7 %collective-permute-start.34 = (bf16[192,768]{1,0:T(8,128)(2,1)S(1)}, bf16[192,768]{1,0:T(8,128)(2,1)S(1)}, u32[]{:S(2)}, u32[]{:S(2)}) collective-permute-start(bf16[192,768]{1,0:T(8,128)(2,1)S(1)} %add_convert_fusion), channel_id=1, source_target_pairs={{0,8},{4,12},{8,0},{12,4},{1,9},{5,13},{9,1},{13,5},{2,10},{6,14},... | collective-permute-start | bytes 884744 | tf_op jit(solution)/shard_map/ppermute | solution.py:541
  128.6 15.7 %collective-permute-start.12 = (bf16[2,128,768]{2,1,0:T(8,128)(2,1)S(1)}, bf16[2,128,768]{2,1,0:T(8,128)(2,1)S(1)}, u32[]{:S(2)}, u32[]{:S(2)}) collective-permute-start(bf16[2,128,768]{2,1,0:T(8,128)(2,1)S(1)} %fusion.17), channel_id=1, source_target_pairs={{0,2},{1,3},{2,0},{3,1},{4,6},{5,7},{6,4},{7,5},{8,10},{9,11},{10,... | collective-permute-start | bytes 1179656 | tf_op jit(solution)/shard_map/ppermute | solution.py:541
  142.1 44.6 %collective-permute-start.35 = (bf16[2,192,768]{2,1,0:T(8,128)(2,1)S(1)}, bf16[2,192,768]{2,1,0:T(8,128)(2,1)S(1)}, u32[]{:S(2)}, u32[]{:S(2)}) collective-permute-start(bf16[2,192,768]{2,1,0:T(8,128)(2,1)S(1)} %pad_maximum_fusion.12), channel_id=1, source_target_pairs={{0,4},{4,0},{8,12},{12,8},{1,5},{5,1},{9,13},{13,9},{2,6},{6,2},{1... | collective-permute-start | bytes 1769480 | tf_op jit(solution)/shard_map/ppermute | solution.py:541
  142.3 51.2 %collective-permute-start.21 = (bf16[128,768]{1,0:T(8,128)(2,1)S(1)}, bf16[128,768]{1,0:T(8,128)(2,1)S(1)}, u32[]{:S(2)}, u32[]{:S(2)}) collective-permute-start(bf16[128,768]{1,0:T(8,128)(2,1)S(1)} %get-tuple-element.141), channel_id=1, source_target_pairs={{0,4},{4,0},{8,12},{12,8},{1,5},{5,1},{9,13},{13,9},{2,6},{6,2},{1... | collective-permute-start | bytes 589832 | tf_op jit(solution)/shard_map/ppermute | solution.py:541
  144.4 55.3 %collective-permute-start.23 = (bf16[128,768]{1,0:T(8,128)(2,1)S(1)}, bf16[128,768]{1,0:T(8,128)(2,1)S(1)}, u32[]{:S(2)}, u32[]{:S(2)}) collective-permute-start(bf16[128,768]{1,0:T(8,128)(2,1)S(1)} %get-tuple-element.142), channel_id=1, source_target_pairs={{0,12},{4,8},{8,4},{12,0},{1,13},{5,9},{9,5},{13,1},{2,14},{6,10},... | collective-permute-start | bytes 589832 | tf_op jit(solution)/shard_map/ppermute | solution.py:541
  147.3 29.6 %collective-permute-start.27 = (bf16[416,384]{1,0:T(8,128)(2,1)S(1)}, bf16[416,384]{1,0:T(8,128)(2,1)S(1)}, u32[]{:S(2)}, u32[]{:S(2)}) collective-permute-start(bf16[416,384]{1,0:T(8,128)(2,1)S(1)} %dynamic-slice_convert_fusion.1), channel_id=1, source_target_pairs={{0,4},{4,0},{8,12},{12,8},{1,5},{5,1},{9,13},{13,9},{2,6},{6,2},{1... | collective-permute-start | bytes 958472 | tf_op jit(solution)/shard_map/ppermute | solution.py:541
  147.4 49.2 %copy-start.24 = (bf16[1,128,768]{2,1,0:T(8,128)(2,1)}, bf16[1,128,768]{2,1,0:T(8,128)(2,1)S(1)}, u32[]{:S(2)}) copy-start(bf16[1,128,768]{2,1,0:T(8,128)(2,1)S(1)} %get-tuple-element.143) | copy-start | bytes 589828
  147.4 29.7 %collective-permute-start.13 = (bf16[128,768]{1,0:T(8,128)(2,1)S(1)}, bf16[128,768]{1,0:T(8,128)(2,1)S(1)}, u32[]{:S(2)}, u32[]{:S(2)}) collective-permute-start(bf16[128,768]{1,0:T(8,128)(2,1)S(1)} %get-tuple-element.144), channel_id=1, source_target_pairs={{0,8},{4,12},{8,0},{12,4},{1,9},{5,13},{9,1},{13,5},{2,10},{6,14},... | collective-permute-start | bytes 589832 | tf_op jit(solution)/shard_map/ppermute | solution.py:541
  177.0 8.6 %collective-permute-start.28 = (bf16[208,384]{1,0:T(8,128)(2,1)S(1)}, bf16[208,384]{1,0:T(8,128)(2,1)S(1)}, u32[]{:S(2)}, u32[]{:S(2)}) collective-permute-start(bf16[208,384]{1,0:T(8,128)(2,1)S(1)} %dynamic-slice_convert_fusion.3), channel_id=1, source_target_pairs={{0,8},{4,12},{8,0},{12,4},{1,9},{5,13},{9,1},{13,5},{2,10},{6,14},... | collective-permute-start | bytes 479240 | tf_op jit(solution)/shard_map/ppermute | solution.py:541
  177.1 19.5 %copy-start.28 = (bf16[128,768]{1,0:T(8,128)(2,1)}, bf16[128,768]{1,0:T(8,128)(2,1)S(1)}, u32[]{:S(2)}) copy-start(bf16[128,768]{1,0:T(8,128)(2,1)S(1)} %collective-permute-done.13) | copy-start | bytes 589828
  177.2 10.3 %collective-permute-start.18 = (bf16[2,128,768]{2,1,0:T(8,128)(2,1)S(1)}, bf16[2,128,768]{2,1,0:T(8,128)(2,1)S(1)}, u32[]{:S(2)}, u32[]{:S(2)}) collective-permute-start(bf16[2,128,768]{2,1,0:T(8,128)(2,1)S(1)} %fusion.18), channel_id=1, source_target_pairs={{0,2},{1,3},{2,0},{3,1},{4,6},{5,7},{6,4},{7,5},{8,10},{9,11},{10,... | collective-permute-start | bytes 1179656 | tf_op jit(solution)/shard_map/ppermute | solution.py:541
  185.6 11.0 %collective-permute-start.14 = (bf16[2,128,768]{2,1,0:T(8,128)(2,1)S(1)}, bf16[2,128,768]{2,1,0:T(8,128)(2,1)S(1)}, u32[]{:S(2)}, u32[]{:S(2)}) collective-permute-start(bf16[2,128,768]{2,1,0:T(8,128)(2,1)S(1)} %pad_maximum_fusion.15), channel_id=1, source_target_pairs={{0,2},{1,3},{2,0},{3,1},{4,6},{5,7},{6,4},{7,5},{8,10},{9,11},{10,... | collective-permute-start | bytes 1179656 | tf_op jit(solution)/shard_map/ppermute | solution.py:541
  186.7 11.5 %collective-permute-start.29 = (bf16[208,384]{1,0:T(8,128)(2,1)S(1)}, bf16[208,384]{1,0:T(8,128)(2,1)S(1)}, u32[]{:S(2)}, u32[]{:S(2)}) collective-permute-start(bf16[208,384]{1,0:T(8,128)(2,1)S(1)} %add_convert_fusion.1), channel_id=1, source_target_pairs={{0,8},{4,12},{8,0},{12,4},{1,9},{5,13},{9,1},{13,5},{2,10},{6,14},... | collective-permute-start | bytes 479240 | tf_op jit(solution)/shard_map/ppermute | solution.py:541
  187.5 14.9 %collective-permute-start.22 = (bf16[128,768]{1,0:T(8,128)(2,1)S(1)}, bf16[128,768]{1,0:T(8,128)(2,1)S(1)}, u32[]{:S(2)}, u32[]{:S(2)}) collective-permute-start(bf16[128,768]{1,0:T(8,128)(2,1)S(1)} %fusion.26), channel_id=1, source_target_pairs={{0,8},{4,12},{8,0},{12,4},{1,9},{5,13},{9,1},{13,5},{2,10},{6,14},... | collective-permute-start | bytes 589832 | tf_op jit(solution)/shard_map/ppermute | solution.py:541
  197.6 23.7 %collective-permute-start.15 = (bf16[2,2,128,768]{3,2,1,0:T(8,128)(2,1)}, bf16[2,2,128,768]{3,2,1,0:T(8,128)(2,1)}, u32[]{:S(2)}, u32[]{:S(2)}) collective-permute-start(bf16[2,2,128,768]{3,2,1,0:T(8,128)(2,1)} %pad_maximum_fusion.8), channel_id=1, source_target_pairs={{0,1},{1,0},{2,3},{3,2},{4,5},{5,4},{6,7},{7,6},{8,9},{9,8},{10,11... | collective-permute-start | bytes 2359304 | tf_op jit(solution)/shard_map/ppermute | solution.py:541
  198.3 10.9 %collective-permute-start.30 = (bf16[2,208,384]{2,1,0:T(8,128)(2,1)S(1)}, bf16[2,208,384]{2,1,0:T(8,128)(2,1)S(1)}, u32[]{:S(2)}, u32[]{:S(2)}) collective-permute-start(bf16[2,208,384]{2,1,0:T(8,128)(2,1)S(1)} %pad_maximum_fusion.17), channel_id=1, source_target_pairs={{0,4},{4,0},{8,12},{12,8},{1,5},{5,1},{9,13},{13,9},{2,6},{6,2},{1... | collective-permute-start | bytes 958472 | tf_op jit(solution)/shard_map/ppermute | solution.py:541
  204.0 16.1 %collective-permute-start.24 = (bf16[2,128,768]{2,1,0:T(8,128)(2,1)}, bf16[2,128,768]{2,1,0:T(8,128)(2,1)}, u32[]{:S(2)}, u32[]{:S(2)}) collective-permute-start(bf16[2,128,768]{2,1,0:T(8,128)(2,1)} %fusion.7), channel_id=1, source_target_pairs={{0,2},{1,3},{2,0},{3,1},{4,6},{5,7},{6,4},{7,5},{8,10},{9,11},{10,... | collective-permute-start | bytes 1179656 | tf_op jit(solution)/shard_map/ppermute | solution.py:541
  209.3 1.3 collective-permute-start.31
  211.3 7.4 %collective-permute-start.32 = (f32[8,768]{1,0:T(8,128)}, f32[8,768]{1,0:T(8,128)}, u32[]{:S(2)}, u32[]{:S(2)}) collective-permute-start(f32[8,768]{1,0:T(8,128)} %fusion.32), channel_id=1, source_target_pairs={{0,2},{1,3},{2,0},{3,1},{4,6},{5,7},{6,4},{7,5},{8,10},{9,11},{10,... | collective-permute-start | bytes 73736 | tf_op jit(solution)/shard_map/ppermute | solution.py:541
  221.1 4.3 %collective-permute-start.25 = (bf16[2,2,128,768]{3,2,1,0:T(8,128)(2,1)S(1)}, bf16[2,2,128,768]{3,2,1,0:T(8,128)(2,1)S(1)}, u32[]{:S(2)}, u32[]{:S(2)}) collective-permute-start(bf16[2,2,128,768]{3,2,1,0:T(8,128)(2,1)S(1)} %pad_maximum_fusion.10), channel_id=1, source_target_pairs={{0,1},{1,0},{2,3},{3,2},{4,5},{5,4},{6,7},{7,6},{8,9},{9,8},{10,11... | collective-permute-start | bytes 2359304 | tf_op jit(solution)/shard_map/ppermute | solution.py:541
  (37 other events, 141.1 us)

commit v4 on v3

--- a/solution.py
+++ b/solution.py
@@ -50,10 +50,27 @@
     return jax.ShapeDtypeStruct(dims, BF16)
 
 
-def norm_own_kernel(at, xa, xb, ga, gb, fz, fx, fc, ta, tb, s1, b1, s2, b2,
-                    n1_ref, n2_ref, xhat_ref, g_ref, trig_ref, x):
+def two_quarters(width, seq_of):
+    def piece(high):
+        return pl.BlockSpec(
+            (1, STEP // 2, width), lambda i, at: (seq_of(i, at), at[2] ^ (i % 2 + high), 0)
+        )
+
+    return [piece(0), piece(2)]
+
+
+def project_kernel(at, xa, xb, ga, gb, fz, fx, fc, nz, nx, nc, ta, tb, w_ref, b_ref, s1, b1,
+                   n1_ref, xhat_ref, g_ref, trig_ref, k_ref, v_ref, q_ref, do_ref, x, bias):
     i = pl.program_id(0)
-    q = xa.shape[1]
+    wide = k_ref.shape[0]
+    q = STEP // 2
+    b = jnp.maximum(i // 2 - 2, 0)
+
+    @pl.when(i == 0)
+    def _():
+        for j in range(3):
+            line = jnp.broadcast_to(b_ref[j : j + 1, :], (8, wide))
+            bias[j * wide : (j + 1) * wide, :] = line.T[:, 0:1]
 
     @pl.when(i < 2)
     def _():
@@ -76,158 +93,95 @@
         g_ref[:q, :] = fc[0, 1]
         g_ref[q:, :] = fc[1, 1]
 
+    @pl.when((i >= 4) & (i % 2 == 0))
+    def _():
+        x[:q, :] = nz[b]
+        x[q:, :] = nx[b]
+
+    @pl.when((i >= 4) & (i % 2 == 1))
+    def _():
+        x[:q, :] = nc[0, b]
+        x[q:, :] = nc[1, b]
+
     trig_ref[:, :q] = ta[0]
     trig_ref[:, q:] = tb[0]
+    trig = trig_ref[...]
+    cosine, sine = trig[:HALF], trig[HALF:ROT]
     xhat, _ = xhat_of(x[...].astype(F32))
     xhat_ref[...] = xhat.astype(BF16)
-    n1_ref[...] = (xhat * row_of(s1) + row_of(b1)).astype(BF16)
-    n2_ref[...] = (xhat * row_of(s2) + row_of(b2)).astype(BF16)
-
-
-def norm_other_kernel(at, nz, nx, nc, ta, tb, s1, b1, n1_ref, xhat_ref, trig_ref, x):
-    i = pl.program_id(0)
-    q = nz.shape[1]
-    b = i // 2
-
-    @pl.when(i % 2 == 0)
-    def _():
-        x[:q, :] = nz[b]
-        x[q:, :] = nx[b]
-
-    @pl.when(i % 2 == 1)
-    def _():
-        x[:q, :] = nc[0, b]
-        x[q:, :] = nc[1, b]
-
-    trig_ref[:, :q] = ta[0]
-    trig_ref[:, q:] = tb[0]
-    xhat, _ = xhat_of(x[...].astype(F32))
-    xhat_ref[...] = xhat.astype(BF16)
-    n1_ref[...] = (xhat * row_of(s1) + row_of(b1)).astype(BF16)
-
-
-def norms(at, own, arrays, trig, vectors):
-    width = vectors[0].shape[0]
-    rows, q = 4 * STEP, STEP // 2
-    tall = trig.shape[1]
-    first = 0 if own else 1
-
-    def pick(high):
-        def place(i, at):
-            block = at[1] ^ (first + 2 * (i // 2))
-            return (at[0], 0, block * 4 + (at[2] ^ (i % 2 + high)))
-
-        return pl.BlockSpec((1, tall, q), place)
-
-    def piece(high):
-        return pl.BlockSpec(
-            (1, q, width), lambda i, at: (at[0], at[2] ^ (jnp.minimum(i, 1) + high), 0)
-        )
-
-    def whole(v):
-        return pl.BlockSpec(v.shape, lambda i, at: (0,) * v.ndim)
-
-    row = pl.BlockSpec((STEP, width), lambda i, at: (i, 0))
-    out_trig = pl.BlockSpec((tall, STEP), lambda i, at: (0, i))
-    if own:
-        x, g, received = arrays[0], arrays[1], arrays[2:]
-        specs = [piece(0), piece(2), piece(0), piece(2)]
-        operands = [x, x, g, g]
-        kernel, count = norm_own_kernel, 4
-    else:
-        received, specs, operands = arrays, [], []
-        kernel, count = norm_other_kernel, 2
-    specs += [whole(v) for v in received] + [pick(0), pick(2)] + [whole(v) for v in vectors]
-    operands += [*received, trig, trig, *vectors]
-    return pl.pallas_call(
-        kernel,
-        grid_spec=pltpu.PrefetchScalarGridSpec(
-            num_scalar_prefetch=1,
-            grid=(rows // STEP,),
-            in_specs=specs,
-            out_specs=[row] * count + [out_trig],
-            scratch_shapes=[pltpu.VMEM((STEP, width), BF16)],
-        ),
-        out_shape=[low_shape(rows, width)] * count + [shape(tall, rows)],
-        compiler_params=params(24),
-        cost_estimate=cost(0, 6 * rows * width),
-    )(at, *operands)
-
-
-def project_kernel(n1o, n1x, to, tx, g_ref, w_ref, b_ref, k_ref, v_ref, q_ref, do_ref, bias):
-    i = pl.program_id(0)
-    wide = k_ref.shape[0]
-
-    @pl.when(i == 0)
-    def _():
-        for j in range(3):
-            line = jnp.broadcast_to(b_ref[j : j + 1, :], (8, wide))
-            bias[j * wide : (j + 1) * wide, :] = line.T[:, 0:1]
-
-    def rotated(ref, mixed, trig, factor):
-        cosine, sine = trig[:HALF], trig[HALF:ROT]
+    n1 = (xhat * row_of(s1) + row_of(b1)).astype(BF16)
+    n1_ref[...] = n1
+
+    def rotated(ref, mixed, factor):
         for h in range(0, wide, HEAD):
             a, b = mixed[h : h + HALF], mixed[h + HALF : h + ROT]
             turned = jnp.concatenate([a * cosine - b * sine, b * cosine + a * sine], axis=0)
             ref[h : h + ROT, :] = turned.astype(BF16) * factor
             ref[h + ROT : h + HEAD, :] = mixed[h + ROT : h + HEAD].astype(BF16) * factor
 
-    def keys_values(mixed, trig):
-        rotated(k_ref, mixed[:wide], trig, BF16(1.0))
-        v_ref[...] = mixed[wide:].astype(BF16)
+    mixed = mm(w_ref[wide : 3 * wide, :], n1, 1, 1) + bias[wide:, :]
+    rotated(k_ref, mixed[:wide], BF16(1.0))
+    v_ref[...] = mixed[wide:].astype(BF16)
 
     @pl.when(i < 4)
     def _():
-        trig = to[...]
-        mixed = mm(w_ref[: 3 * wide, :], n1o[...], 1, 1) + bias[...]
-        rotated(q_ref, mixed[:wide], trig, BF16(HEAD**-0.5))
-        keys_values(mixed[wide:], trig)
+        rotated(q_ref, mm(w_ref[:wide, :], n1, 1, 1) + bias[:wide, :], BF16(HEAD**-0.5))
         do_ref[...] = mm(w_ref[3 * wide :, :], g_ref[...], 1, 1).astype(BF16)
 
-    @pl.when(i >= 4)
-    def _():
-        mixed = mm(w_ref[wide : 3 * wide, :], n1x[...], 1, 1) + bias[wide:, :]
-        keys_values(mixed, tx[...])
-
-
-def project(n1_own, n1_other, trig_own, trig_other, g, weights, bias):
-    rows, width = n1_own.shape
+
+def project(at, x, g, far, others, trig, weights, bias, scale, offset):
+    width = x.shape[2]
+    rows = 8 * STEP
     wide = bias.shape[1]
-    tall = trig_own.shape[0]
-
-    def own(i):
-        return jnp.minimum(i, 3)
-
-    def other(i):
-        return jnp.maximum(i - 4, 0)
-
-    col = pl.BlockSpec((wide, STEP), lambda i: (0, i))
-    own_col = pl.BlockSpec((wide, STEP), lambda i: (0, own(i)))
+    tall = trig.shape[1]
+
+    def pick(high):
+        def place(i, at):
+            b = i // 2
+            block = at[1] ^ (b % 2 * 2 + b // 2)
+            return (at[0], 0, block * 4 + (at[2] ^ (i % 2 + high)))
+
+        return pl.BlockSpec((1, tall, STEP // 2), place)
+
+    def whole(v):
+        return pl.BlockSpec(v.shape, lambda i, at: (0,) * v.ndim)
+
+    def piece(high):
+        return pl.BlockSpec(
+            (1, STEP // 2, width), lambda i, at: (at[0], at[2] ^ (jnp.minimum(i, 1) + high), 0)
+        )
+
+    pieces = [piece(0), piece(2)]
+    row = pl.BlockSpec((STEP, width), lambda i, at: (i, 0))
+    own_row = pl.BlockSpec((STEP, width), lambda i, at: (jnp.minimum(i, 3), 0))
+    col = pl.BlockSpec((wide, STEP), lambda i, at: (0, i))
+    own_col = pl.BlockSpec((wide, STEP), lambda i, at: (0, jnp.minimum(i, 3)))
+    received = (*far, *others)
+    fixed = (weights, bias, scale, offset)
     return pl.pallas_call(
         project_kernel,
-        grid=(8,),
-        in_specs=[
-            pl.BlockSpec((STEP, width), lambda i: (own(i), 0)),
-            pl.BlockSpec((STEP, width), lambda i: (other(i), 0)),
-            pl.BlockSpec((tall, STEP), lambda i: (0, own(i))),
-            pl.BlockSpec((tall, STEP), lambda i: (0, other(i))),
-            pl.BlockSpec((STEP, width), lambda i: (own(i), 0)),
-            pl.BlockSpec((4 * wide, width), lambda i: (0, 0)),
-            pl.BlockSpec((3, wide), lambda i: (0, 0)),
-        ],
-        out_specs=[col, col, own_col, own_col],
-        out_shape=[low_shape(wide, 2 * rows)] * 2 + [low_shape(wide, rows)] * 2,
-        scratch_shapes=[pltpu.VMEM((3 * wide, 1), F32)],
-        compiler_params=params(24),
-        cost_estimate=cost(12 * rows * width * wide, 12 * rows * width),
-    )(n1_own, n1_other, trig_own, trig_other, g, weights, bias)
-
-
-def attention_kernel(after, q_ref, do_ref, k_ref, v_ref, tq_ref, to_ref, tx_ref,
-                     o_ref, dq_ref, dk_ref, dv_ref, kn, vn, kp, dk, dv, es, dps):
+        grid_spec=pltpu.PrefetchScalarGridSpec(
+            num_scalar_prefetch=1,
+            grid=(8,),
+            in_specs=pieces * 2 + [whole(v) for v in received] + [pick(0), pick(2)]
+            + [whole(v) for v in fixed],
+            out_specs=[row, row, own_row, pl.BlockSpec((tall, STEP), lambda i, at: (0, i)),
+                       col, col, own_col, own_col],
+            scratch_shapes=[pltpu.VMEM((STEP, width), BF16), pltpu.VMEM((3 * wide, 1), F32)],
+        ),
+        out_shape=[low_shape(rows, width)] * 2
+        + [low_shape(rows // 2, width), shape(tall, rows)]
+        + [low_shape(wide, rows)] * 2 + [low_shape(wide, rows // 2)] * 2,
+        compiler_params=params(32),
+        cost_estimate=cost(6 * rows * width * wide, 8 * rows * width),
+    )(at, x, x, g, g, *received, trig, trig, *fixed)
+
+
+def attention_kernel(count, *refs):
+    (q_ref, do_ref, k_ref, v_ref, tq_ref, tk_ref,
+     o_ref, dq_ref, dk_ref, dv_ref, kn, vn, kp, dk, dv, es, dps) = refs[count:]
     i = pl.program_id(0)
     length = k_ref.shape[1]
-    half = length // 2
     chunk = STEP
     steps = length // chunk
 
@@ -235,8 +189,7 @@
     def _():
         kn[...] = k_ref[...].T
         vn[...] = v_ref[...].T
-        kp[:half, :] = to_ref[ROT:, :].T[:, 0:1]
-        kp[half:, :] = tx_ref[ROT:, :].T[:, 0:1]
+        kp[...] = tk_ref[ROT:, :].T[:, 0:1]
         dk[...] = jnp.zeros_like(dk)
         dv[...] = jnp.zeros_like(dv)
 
@@ -293,24 +246,22 @@
 
     @pl.when(i == pl.num_programs(0) - 1)
     def _():
-        grad = dk[...].T
-        dk_ref[:ROT, :half], dk_ref[ROT:, :half] = unrotated(grad[:, :half], to_ref[...])
-        dk_ref[:ROT, half:], dk_ref[ROT:, half:] = unrotated(grad[:, half:], tx_ref[...])
+        dk_ref[:ROT, :], dk_ref[ROT:, :] = unrotated(dk[...].T, tk_ref[...])
         dv_ref[...] = dv[...].T.astype(BF16)
 
 
-def attention(h, after, qt, dot, kt, vt, trig_own, trig_other):
+def attention(h, after, qt, dot, kt, vt, trig):
     rows, length = qt.shape[1], kt.shape[1]
     lanes = STEP
-    tall = trig_own.shape[0]
+    tall = trig.shape[0]
     q_spec = pl.BlockSpec((HEAD, lanes), lambda i: (h, i))
     k_spec = pl.BlockSpec((HEAD, length), lambda i: (h, 0))
-    trig_spec = pl.BlockSpec((tall, rows), lambda i: (0, 0))
     return pl.pallas_call(
-        attention_kernel,
+        functools.partial(attention_kernel, len(after)),
         grid=(rows // lanes,),
-        in_specs=[pl.BlockSpec(memory_space=pl.ANY), q_spec, q_spec, k_spec, k_spec,
-                  pl.BlockSpec((tall, lanes), lambda i: (0, i)), trig_spec, trig_spec],
+        in_specs=[pl.BlockSpec(memory_space=pl.ANY)] * len(after)
+        + [q_spec, q_spec, k_spec, k_spec, pl.BlockSpec((tall, lanes), lambda i: (0, i)),
+           pl.BlockSpec((tall, length), lambda i: (0, 0))],
         out_specs=[pl.BlockSpec((HEAD, lanes), lambda i: (0, i))] * 2
         + [pl.BlockSpec((HEAD, length), lambda i: (0, 0))] * 2,
         out_shape=[low_shape(HEAD, rows)] * 2 + [low_shape(HEAD, length)] * 2,
@@ -325,11 +276,11 @@
         ],
         compiler_params=params(32),
         cost_estimate=cost(40 * rows * length * HEAD, 16 * HEAD * length, rows * length),
-    )(after, qt, dot, kt, vt, trig_own, trig_own, trig_other)
-
-
-def forward_kernel(split, at, n2_ref, g_ref, xhat_ref, up_ref, bias_ref, down_ref, s2_ref,
-                   ff_ref, a_ref, small_ref, first_ref, second_ref, *scratch):
+    )(*after, qt, dot, kt, vt, trig, trig)
+
+
+def forward_kernel(split, at, xa, xb, ga, gb, up_ref, bias_ref, down_ref, s2_ref, b2_ref,
+                   ff_ref, a_ref, keep_ref, send_ref, small_ref, first_ref, second_ref, *scratch):
     i = pl.program_id(0)
     up_part, down_part = scratch if split else (first_ref, second_ref)
 
@@ -339,20 +290,39 @@
         down_part[...] = jnp.zeros_like(down_part)
         small_ref[...] = jnp.zeros_like(small_ref)
 
-    n2, g = n2_ref[...], g_ref[...]
+    xhat, _ = xhat_of(jnp.concatenate([xa[0], xb[0]], axis=0).astype(F32))
+    g = jnp.concatenate([ga[0], gb[0]], axis=0)
+    scale = row_of(s2_ref)
+    n2 = (xhat * scale + row_of(b2_ref)).astype(BF16)
     up = mm(n2, up_ref[...]) + row_of(bias_ref)
     cdf = 0.5 + 0.5 * lax.erf(up * (0.5**0.5))
     act = (up * cdf).astype(BF16)
     slope = cdf + up * (jnp.exp(up * up * -0.5) * 0.3989422804014327)
     up_grad = (mm(g, down_ref[...], 1, 1) * slope).astype(BF16)
-    ff_ref[...] = mm(act, down_ref[...]).astype(BF16)
+    ff = mm(act, down_ref[...]).astype(BF16)
     second = mm(up_grad, up_ref[...], 1, 1)
+    a = (second * scale).astype(BF16)
+
+    @pl.when(i < 2)
+    def _():
+        ff_ref[...] = ff
+        a_ref[...] = a
+
+    @pl.when(i == 2)
+    def _():
+        keep_ref[0] = ff
+        keep_ref[1] = a
+
+    @pl.when(i == 3)
+    def _():
+        send_ref[0] = ff
+        send_ref[1] = a
+
     up_part[...] += mm(n2, up_grad, 0, 0)
     down_part[...] += mm(act, g, 0, 0)
-    a_ref[...] = (second * row_of(s2_ref)).astype(BF16)
     small_ref[0:1, :] += jnp.sum(up_grad.astype(F32), axis=0, keepdims=True)
     small_ref[1:2, :] += jnp.sum(g.astype(F32), axis=0, keepdims=True)
-    small_ref[2:3, :] += jnp.sum(second * xhat_ref[...].astype(F32), axis=0, keepdims=True)
+    small_ref[2:3, :] += jnp.sum(second * xhat, axis=0, keepdims=True)
     small_ref[3:4, :] += jnp.sum(second, axis=0, keepdims=True)
 
     if split:
@@ -367,10 +337,11 @@
                 ref[half:, half:] = down_part[half:, piece].astype(ref.dtype)
 
 
-def feed_forward(split, at, n2, g, xhat, up, bias, down, scale):
-    rows, width = n2.shape
+def feed_forward(split, at, x, g, up, bias, down, scale, offset):
+    width = x.shape[2]
     hidden = up.shape[1]
-    row = pl.BlockSpec((STEP, width), lambda i, at: (i, 0))
+    pieces = two_quarters(width, lambda i, at: at[0] ^ (i // 2))
+    own_row = pl.BlockSpec((STEP, width), lambda i, at: (jnp.minimum(i, 1), 0))
 
     def whole(*dims):
         return pl.BlockSpec(dims, lambda i, at: (0,) * len(dims))
@@ -380,26 +351,31 @@
         parts = [shape(width, hidden), low_shape(width, hidden)]
     else:
         parts = [shape(width, hidden), shape(hidden, width)]
+    slots = whole(2, STEP, width)
     return pl.pallas_call(
         functools.partial(forward_kernel, split),
         grid_spec=pltpu.PrefetchScalarGridSpec(
             num_scalar_prefetch=1,
-            grid=(rows // STEP,),
-            in_specs=[row, row, row, whole(width, hidden), whole(hidden), whole(hidden, width),
-                      whole(width)],
-            out_specs=[row, row, whole(8, width)] + [whole(*p.shape) for p in parts],
+            grid=(4,),
+            in_specs=pieces * 2 + [whole(width, hidden), whole(hidden), whole(hidden, width),
+                                   whole(width), whole(width)],
+            out_specs=[own_row, own_row, slots, slots, whole(8, width)]
+            + [whole(*p.shape) for p in parts],
             scratch_shapes=[pltpu.VMEM((width, hidden), F32), pltpu.VMEM((hidden, width), F32)]
             if split
             else [],
         ),
-        out_shape=[low_shape(rows, width)] * 2 + [shape(8, width)] + parts,
+        out_shape=[low_shape(2 * STEP, width)] * 2 + [low_shape(2, STEP, width)] * 2
+        + [shape(8, width)] + parts,
         compiler_params=params(40),
-        cost_estimate=cost(12 * rows * width * hidden, 16 * MIB, 2 * rows * hidden),
-    )(at, n2, g, xhat, up, bias, down, scale)
-
-
-def emit(keep_ref, send_ref, v):
+        cost_estimate=cost(48 * STEP * width * hidden, 16 * MIB, 8 * STEP * hidden),
+    )(at, x, x, g, g, up, bias, down, scale, offset)
+
+
+def emit(keep_ref, send_ref, v, own_ref=None):
     i = pl.program_id(0)
+    if own_ref is not None:
+        v = jnp.where(i < 2, v + own_ref[...].astype(F32), v)
 
     @pl.when(i % 2 == 0)
     def _():
@@ -420,7 +396,7 @@
         out[...] = jnp.zeros_like(out)
 
     ot = jnp.concatenate([r[...] for r in o], axis=0)
-    emit(keep_ref, send_ref, mm(ot, w_ref[...], 0, 0) + ff_ref[...].astype(F32))
+    emit(keep_ref, send_ref, mm(ot, w_ref[...], 0, 0), ff_ref)
     out[...] += mm(ot, g_ref[...])
 
 
@@ -434,7 +410,8 @@
         functools.partial(branch_kernel, heads),
         grid=(rows // STEP,),
         in_specs=[pl.BlockSpec((HEAD, STEP), lambda i: (0, i))] * heads
-        + [row, row, pl.BlockSpec((wide, width), lambda i: (3, 0))],
+        + [row, pl.BlockSpec((STEP, width), lambda i: (jnp.minimum(i, 1), 0)),
+           pl.BlockSpec((wide, width), lambda i: (3, 0))],
         out_specs=[slots, slots, pl.BlockSpec((wide, width), lambda i: (0, 0))],
         out_shape=[low_shape(2, STEP, width)] * 2 + [shape(wide, width)],
         compiler_params=params(24),
@@ -468,7 +445,7 @@
     grad = jnp.concatenate([r[...] for r in grads], axis=0)
     first = mm(grad, w_ref[3 * wide - tall : 3 * wide, :], 0, 0)
     a = first * row_of(s1_ref)
-    emit(keep_ref, send_ref, a + a2_ref[...].astype(F32) if own else a)
+    emit(keep_ref, send_ref, a, a2_ref if own else None)
     mix[...] += mm(grad, n1_ref[...])
     small[0:1, :] += jnp.sum(first * xhat_ref[...].astype(F32), axis=0, keepdims=True)
     small[1:2, :] += jnp.sum(first, axis=0, keepdims=True)
@@ -497,12 +474,12 @@
 
 
 def back(own, split, at, grads, n1, xhat, weights, scale, extra):
-    rows, width = n1.shape
+    rows, width = n1.shape[0] // 2, n1.shape[1]
     heads = len(grads[0])
     wide = heads * HEAD
     tall = 3 * wide if own else 2 * wide
     offset = 0 if own else rows // STEP
-    row = pl.BlockSpec((STEP, width), lambda i, at: (i, 0))
+    row = pl.BlockSpec((STEP, width), lambda i, at: (i + offset, 0))
     col = pl.BlockSpec((HEAD, STEP), lambda i, at: (0, i + offset))
     slots = pl.BlockSpec((1, STEP, width), lambda i, at: (i // 2, 0, 0))
 
@@ -515,7 +492,8 @@
         parts = [shape(tall, width), shape(8, width)]
         scratch = []
     else:
-        specs += [row, whole(8, width), whole(8, width), whole(2 * wide, width),
+        specs += [pl.BlockSpec((STEP, width), lambda i, at: (jnp.minimum(i, 1), 0)),
+                  whole(8, width), whole(8, width), whole(2 * wide, width),
                   whole(wide, width), pl.BlockSpec(memory_space=pl.ANY)]
         scratch = [pltpu.VMEM((tall, width), F32), pltpu.VMEM((8, width), F32)]
         if split:
@@ -637,8 +615,8 @@
     x_mine, x_theirs = my_quarter(inputs, s), my_quarter(inputs, 1 - s)
     g_theirs = my_quarter(cotangent, 1 - s)
     far_z = swap(jnp.concatenate([x_theirs, g_theirs], axis=0), "ctx", 4, 2)
-    cross = swap(x_theirs, "ctx", 4, 3)
-    near = swap(x_mine, "ctx", 4, 1)
+    cross = swap(tie(x_theirs, far_z), "ctx", 4, 3)
+    near = swap(tie(x_mine, far_z), "ctx", 4, 1)
 
     def over_tp(v):
         v_x = swap(v, "tp", 4, 2)
@@ -659,29 +637,40 @@
         [jnp.cos(angles), jnp.sin(angles), jnp.broadcast_to(places, angles.shape)], axis=1
     )
 
-    n1_own, n2, xhat_own, g, trig_own = norms(
-        at, True, (inputs, cotangent, *far), trig,
-        (first_scale, first_shift, second_scale, second_shift),
-    )
-    ff, a2, small_ff, ff_first, ff_second = feed_forward(
-        split, at, n2, g, xhat_own, wup, up_projection_bias, wdown, second_scale
-    )
+    ff, a2, keep_e, send_e, small_ff, ff_first, ff_second = feed_forward(
+        split, at, inputs, cotangent, wup, up_projection_bias, wdown, second_scale, second_shift
+    )
+
     weights = gather_halves(mix_out_shard, fsdp, f, 1, small_ff)
-    n1_other, xhat_other, trig_other = norms(
-        at, False, (others[0], others[1], tie(others[2], small_ff)), trig,
-        (first_scale, first_shift),
-    )
-    kt, vt, qt, dot = project(
-        n1_own, n1_other, trig_own, trig_other, g, weights, query_key_value_bias
-    )
-    if split:
-        ff_rest = ff_first + swap(ff_second, "fsdp", 2, 1).astype(F32)
-    else:
-        ff_rest = small_ff
+    n1, xhat_all, g, trig, kt, vt, qt, dot = project(
+        at, inputs, cotangent, (far[0], far[1], tie(far[2], small_ff)),
+        (others[0], others[1], tie(others[2], small_ff)), trig, weights, query_key_value_bias,
+        first_scale, first_shift,
+    )
+    def over_core(keep, send, *earlier):
+        v = keep.astype(F32) + tie(swap(send, "tp", 4, 1), *earlier).astype(F32)
+        return v.reshape(2, 2, quarter, width)
+
+    def over_x(v, *earlier):
+        return v[:, 0] + tie(swap(v[:, 1].astype(BF16), "tp", 4, 2), *earlier).astype(F32)
+
+    def scatter_tp(keep, send):
+        return over_x(over_core(keep, send))
+
     per_head = []
     for h in range(heads):
-        after = ff_rest if h == heads - 1 else small_ff
-        per_head.append(attention(h, after, qt, dot, kt, vt, trig_own, trig_other))
+        after = ()
+        if h == 1:
+            early = over_core(keep_e, send_e, per_head[0][0])
+            after = (early,)
+        if h == heads - 1:
+            early = over_x(early, per_head[h - 1][0])
+            ff_rest = small_ff
+            if split:
+                ff_rest = tie(swap(ff_second, "fsdp", 2, 1), per_head[h - 1][0])
+                ff_rest = ff_first + ff_rest.astype(F32)
+            after = (early, ff_rest)
+        per_head.append(attention(h, after, qt, dot, kt, vt, trig))
     o, dq, dk, dv = zip(*per_head)
     keep_b, send_b, out_part = branch(o, g, ff, weights)
     if split:
@@ -689,17 +678,12 @@
     else:
         ff_half = small_ff
     keep_o, send_o, mix_other, small_other = back(
-        False, split, at, (dk, dv), n1_other, xhat_other, weights, first_scale, ()
+        False, split, at, (dk, dv), n1, xhat_all, weights, first_scale, ()
     )
     keep_w, send_w, late_first, late_second = back(
-        True, split, at, (dq, dk, dv), n1_own, xhat_own, weights, first_scale,
+        True, split, at, (dq, dk, dv), n1, xhat_all, weights, first_scale,
         (a2, small_ff, small_other, mix_other, out_part, ff_half),
     )
-
-    def scatter_tp(keep, send):
-        v = keep.astype(F32) + swap(send, "tp", 4, 1).astype(F32)
-        v = v.reshape(2, 2, quarter, width)
-        return v[:, 0] + swap(v[:, 1].astype(BF16), "tp", 4, 2).astype(F32)
 
     def over_ctx(v, distance):
         return swap(v.astype(BF16), "ctx", 4, distance).astype(F32)
@@ -714,7 +698,7 @@
                           jnp.where(s == 0, pieces[1], pieces[0])]).astype(F32)
 
     sums_b = scatter_tp(keep_b, send_b)
-    block_out = gather_tp(sums_b[0], over_ctx(sums_b[1], 2))
+    block_out = gather_tp(sums_b[0], over_ctx(sums_b[1], 2) + early[0])
     block_out = (
         inputs.astype(F32) + block_out + (attention_output_bias + down_projection_bias)
     )
@@ -723,7 +707,7 @@
     sums_w = scatter_tp(keep_w, send_w)
     a = jnp.stack([
         sums_w[0] + over_ctx(sums_o[0], 1),
-        over_ctx(sums_w[1], 2) + over_ctx(sums_o[1], 3),
+        over_ctx(sums_w[1], 2) + over_ctx(sums_o[1], 3) + early[1],
     ])
     xhat, inv = xhat_of(jnp.concatenate([x_mine, x_theirs], axis=0).astype(F32))
     norm_grad = inv * (
@@ -740,7 +724,7 @@
         down_total = jnp.concatenate(
             [down_total[:, : width // 2], down_total[:, width // 2 :]], axis=0
         )
-        late = late_first + swap(late_second, "fsdp", 2, 1).astype(F32)
+        late = late_first + tie(swap(late_second, "fsdp", 2, 1), sums_w).astype(F32)
         late = jnp.concatenate(sum_over_ctx(late, c), axis=0).astype(F32)
         small = jnp.concatenate([late[4 * local : 4 * local + 8], late[4 * local + 8 :][:8]], axis=1)
     else:

time: 230 us -> 261 us (1.13)
  local copies, waits for them, and re-layouts: 10.7 us -> 30.5 us
  waiting for transfers between devices: 85.9 us -> 94.1 us
  Pallas kernels: 62.4 us -> 65.7 us
    unnamed x100 -> x154, local copies, waits for them, and re-layouts: 4.59 us -> 24.7 us
    ppermute x36 -> x38, waiting for transfers between devices: 85.9 us -> 94.1 us  [swap(): return lax.ppermute(v, axis, [(i, i ^ distance) for i in range(size)])]
    pallas_call x1, Pallas kernels: 9.8 us -> 12.9 us  [feed_forward(): pl.pallas_call(functools.partial(forward_kernel, split), grid_spec=pltpu....]
    ppermute x36 -> x38, starting transfers between devices: 40.6 us -> 39.7 us  [swap(): return lax.ppermute(v, axis, [(i, i ^ distance) for i in range(size)])]
    pallas_call x6 -> x4, Pallas kernels: 38.7 us -> 38.3 us  [the longest x3 29.2 us: attention(): pl.pallas_call(functools.partial(attention_kernel, len(after)), grid=(row...]
  transfers between devices with their start and end apart: 36 -> 38, of which waited for: 12 -> 15; matrix products, arithmetic and copies ran while one was open for 13% -> 11% of each run, Pallas kernels for 27% -> 25%
where the time goes in v4:
time: 261 us; the launch traced here: 260 us
  waiting for transfers between devices  94.1 us (36%)
  Pallas kernels  65.7 us (25%)
  starting transfers between devices  39.7 us (15%)
  local copies, waits for them, and re-layouts  30.5 us (12%)
  other arithmetic  27.7 us (11%)
    ppermute x38, waiting for transfers between devices, swap(): return lax.ppermute(v, axis, [(i, i ^ distance) for i in range(size)])  94.1 us
    ppermute x38, starting transfers between devices, swap(): return lax.ppermute(v, axis, [(i, i ^ distance) for i in range(size)])  39.7 us
    pallas_call x3, Pallas kernels, attention(): pl.pallas_call(functools.partial(attention_kernel, len(after)), grid=(row...  29.2 us
    unnamed x154, local copies, waits for them, and re-layouts  24.7 us
    pallas_call x1, Pallas kernels, feed_forward(): pl.pallas_call(functools.partial(forward_kernel, split), grid_spec=pltpu....  12.9 us
    pallas_call x2, Pallas kernels, back(): pl.pallas_call(functools.partial(back_kernel, own, split, heads), grid_sp...  11.7 us
    pallas_call x1, Pallas kernels, project(): pl.pallas_call(project_kernel, grid_spec=pltpu.PrefetchScalarGridSpec(num...  9.08 us
  transfers between devices with their start and end apart: 38, of which 15 were waited for; matrix products, arithmetic and copies ran while one was open for 11% of the time, Pallas kernels for 25%

profile of v4, /device:TPU:0, one launch (start us, length us, event | category | flops | bytes accessed | tf_op | source)
XLA Modules:
  0.0 259.5 jit_solution(4319953975089413234)
XLA Ops:
  0.7 3.0 %collective-permute-start.3 = (bf16[384,768]{1,0:T(8,128)(2,1)}, bf16[384,768]{1,0:T(8,128)(2,1)}, u32[]{:S(2)}, u32[]{:S(2)}) collective-permute-start(bf16[384,768]{1,0:T(8,128)(2,1)} %param.21), channel_id=1, source_target_pairs={{0,16},{16,0},{1,17},{17,1},{2,18},{18,2},{3,19},{19,3},{4,20},{20... | collective-permute-start | bytes 1769480 | tf_op jit(solution)/shard_map/ppermute | solution.py:519
  5.9 3.1 %collective-permute-start = (bf16[2,128,768]{2,1,0:T(8,128)(2,1)S(1)}, bf16[2,128,768]{2,1,0:T(8,128)(2,1)S(1)}, u32[]{:S(2)}, u32[]{:S(2)}) collective-permute-start(bf16[2,128,768]{2,1,0:T(8,128)(2,1)S(1)} %pad_maximum_fusion.13), channel_id=1, source_target_pairs={{0,8},{4,12},{8,0},{12,4},{1,9},{5,13},{9,1},{13,5},{2,10},{6,14},... | collective-permute-start | bytes 1179656 | tf_op jit(solution)/shard_map/ppermute | solution.py:519
  9.8 1.5 collective-permute-start.9
  12.2 13.8 %collective-permute-done.fz = bf16[2,128,768]{2,1,0:T(8,128)(2,1)S(1)} collective-permute-done((bf16[2,128,768]{2,1,0:T(8,128)(2,1)S(1)}, bf16[2,128,768]{2,1,0:T(8,128)(2,1)S(1)}, u32[]{:S(2)}, u32[]{:S(2)}) %collective-permute-start) | collective-permute-done | bytes 393248 | tf_op jit(solution)/shard_map/ppermute | solution.py:519
  26.9 2.9 %collective-permute-start.6 = (bf16[1,128,768]{2,1,0:T(8,128)(2,1)S(1)}, bf16[1,128,768]{2,1,0:T(8,128)(2,1)S(1)}, u32[]{:S(2)}, u32[]{:S(2)}) collective-permute-start(bf16[1,128,768]{2,1,0:T(8,128)(2,1)S(1)} %get-tuple-element.64), channel_id=1, source_target_pairs={{0,12},{4,8},{8,4},{12,0},{1,13},{5,9},{9,5},{13,1},{2,14},{6,10},... | collective-permute-start | bytes 589832 | tf_op jit(solution)/shard_map/ppermute | solution.py:519
  29.9 2.1 collective-permute-done.5
  31.9 1.5 collective-permute-start.1
  33.4 5.4 %collective-permute-done.6 = bf16[1,128,768]{2,1,0:T(8,128)(2,1)S(1)} collective-permute-done((bf16[1,128,768]{2,1,0:T(8,128)(2,1)S(1)}, bf16[1,128,768]{2,1,0:T(8,128)(2,1)S(1)}, u32[]{:S(2)}, u32[]{:S(2)}) %collective-permute-start.6) | collective-permute-done | bytes 196640 | tf_op jit(solution)/shard_map/ppermute | solution.py:519
  38.9 1.6 collective-permute-start.7
  42.2 7.4 %collective-permute-done.7.nx = bf16[2,128,768]{2,1,0:T(8,128)(2,1)S(1)} collective-permute-done((bf16[2,128,768]{2,1,0:T(8,128)(2,1)S(1)}, bf16[2,128,768]{2,1,0:T(8,128)(2,1)S(1)}, u32[]{:S(2)}, u32[]{:S(2)}) %collective-permute-start.7) | collective-permute-done | bytes 393248 | tf_op jit(solution)/shard_map/ppermute | solution.py:519
  49.8 12.9 %shard_map.254 = (bf16[512,768]{1,0:T(8,128)(2,1)S(1)}, bf16[512,768]{1,0:T(8,128)(2,1)S(1)}, bf16[2,256,768]{2,1,0:T(8,128)(2,1)S(1)}, bf16[2,256,768]{2,1,0:T(...) custom-call(s32[4]{0:T(128)S(1)} %pad_add_fusion.at, ...), custom_call_target="tpu_custom_call" | custom-call | flops 7247757312 | bytes 16777216 | tf_op jit(solution)/shard_map/pallas_call | solution.py:355
  63.4 1.5 collective-permute-start.12
  64.9 1.3 broadcast_select_fusion.5
  66.9 9.1 %shard_map.255 = (bf16[2048,768]{1,0:T(8,128)(2,1)S(1)}, bf16[2048,768]{1,0:T(8,128)(2,1)S(1)}, bf16[1024,768]{1,0:T(8,128)(2,1)S(1)}, f32[24,2048]{1,0:T(8,128)...) custom-call(s32[4]{0:T(128)S(1)} %pad_add_fusion.at, ...), custom_call_target="tpu_custom_call" | custom-call | flops 1811939328 | bytes 12582912 | tf_op jit(solution)/shard_map/pallas_call | solution.py:161
  76.0 9.7 %shard_map.256 = (bf16[64,1024]{1,0:T(8,128)(2,1)S(1)}, bf16[64,1024]{1,0:T(8,128)(2,1)S(1)}, bf16[64,2048]{1,0:T(8,128)(2,1)S(1)}, bf16[64,2048]{1,0:T(8,128)(2,1)S(1)}) custom-call(bf16[192,1024]{1,0:T(8,128)(2,1)S(1)} %get-tuple-element.67.refs_0_.refs_1_.refs_2_, bf16[192,1024]{1,0:T(8,128)(2,1)S(1)} %get-tuple-element.68.refs_1_.refs_2_.refs_3_, ...), custom_call_target="tpu_custom_call" | custom-call | flops 5368709120 | bytes 2097152 | tf_op jit(solution)/shard_map/pallas_call | solution.py:259
  86.5 1.6 collective-permute-start.11
  88.1 9.7 %shard_map.257 = (bf16[64,1024]{1,0:T(8,128)(2,1)S(1)}, bf16[64,1024]{1,0:T(8,128)(2,1)S(1)}, bf16[64,2048]{1,0:T(8,128)(2,1)S(1)}, bf16[64,2048]{1,0:T(8,128)(2,1)S(1)}) custom-call(f32[2,2,128,768]{3,2,1,0:T(8,128)S(1)} %bitcast.168, bf16[192,1024]{1,0:T(8,128)(2,1)S(1)} %get-tuple-element.67.refs_0_.refs_1_.refs_2_, ...), custom_call_target="tpu_custom_call" | custom-call | flops 5368709120 | bytes 2097152 | tf_op jit(solution)/shard_map/pallas_call | solution.py:259
  98.5 2.5 collective-permute-start.18
  101.1 9.9 %shard_map.258 = (bf16[64,1024]{1,0:T(8,128)(2,1)S(1)}, bf16[64,1024]{1,0:T(8,128)(2,1)S(1)}, bf16[64,2048]{1,0:T(8,128)(2,1)S(1)}, bf16[64,2048]{1,0:T(8,128)(2,1)S(1)}) custom-call(f32[2,128,768]{2,1,0:T(8,128)S(1)} %fusion.13.refs_0_, f32[768,768]{1,0:T(8,128)S(1)} %convert_add_fusion.1.refs_1_, ...), custom_call_target="tpu_custom_call" | custom-call | flops 5368709120 | bytes 2097152 | tf_op jit(solution)/shard_map/pallas_call | solution.py:259
  111.8 5.5 %shard_map.260 = (bf16[2,256,768]{2,1,0:T(8,128)(2,1)S(1)}, bf16[2,256,768]{2,1,0:T(8,128)(2,1)}, f32[384,768]{1,0:T(8,128)S(1)}, f32[8,768]{1,0:T(8,128)S(1)}) custom-call(s32[4]{0:T(128)S(1)} %pad_add_fusion.at, bf16[64,2048]{1,0:T(8,128)(2,1)S(1)} %get-tuple-element.89.refs_0_.refs_3_, bf16[64,2048]{1,0:T(8,128)(2,1)S(1)} %get-tuple-element.90.refs_1_.refs_4_, ...), custom_call_target="tpu_custom_call" | custom-call | flops 1207959552 | bytes 10485760 | tf_op jit(solution)/shard_map/pallas_call | solution.py:503
  119.7 4.4 %collective-permute-start.35 = (bf16[192,768]{1,0:T(8,128)(2,1)}, bf16[192,768]{1,0:T(8,128)(2,1)}, u32[]{:S(2)}, u32[]{:S(2)}) collective-permute-start(bf16[192,768]{1,0:T(8,128)(2,1)} %dynamic-slice_convert_fusion.2), channel_id=1, source_target_pairs={{0,8},{4,12},{8,0},{12,4},{1,9},{5,13},{9,1},{13,5},{2,10},{6,14},... | collective-permute-start | bytes 884744 | tf_op jit(solution)/shard_map/ppermute | solution.py:519
  124.1 1.3 add.147
  125.4 1.4 copy-done.10
  130.7 2.7 %shard_map.259 = (bf16[2,256,768]{2,1,0:T(8,128)(2,1)S(1)}, bf16[2,256,768]{2,1,0:T(8,128)(2,1)S(1)}, f32[192,768]{1,0:T(8,128)S(1)}) custom-call(bf16[64,1024]{1,0:T(8,128)(2,1)S(1)} %copy-done.40, bf16[64,1024]{1,0:T(8,128)(2,1)S(1)} %copy-done.42, bf16[64,1024]{1,0:T(8,128)(2,1)S(1)} %copy-done.44, bf16[1024,768]{1,0:T(8,128)(2,1)S(1)} %copy-done.10, ...), custom_call_target="tpu_custom_call" | custom-call | flops 603979776 | bytes 8388608 | tf_op jit(solution)/shard_map/pallas_call | solution.py:409
  133.6 1.9 copy-done.6
  146.2 6.2 %shard_map.261 = (bf16[2,256,768]{2,1,0:T(8,128)(2,1)S(1)}, bf16[2,256,768]{2,1,0:T(8,128)(2,1)S(1)}, f32[832,384]{1,0:T(8,128)S(1)}, bf16[832,384]{1,0:T(8,128)(2,1)S(1)}) custom-call(s32[4]{0:T(128)S(1)} %pad_add_fusion.at, bf16[64,1024]{1,0:T(8,128)(2,1)S(1)} %copy-done.34, bf16[64,1024]{1,0:T(8,128)(2,1)S(1)} %copy-done.36, ...), custom_call_target="tpu_custom_call" | custom-call | flops 1811939328 | bytes 10485760 | tf_op jit(solution)/shard_map/pallas_call | solution.py:503
  154.5 1.3 convert_add_fusion.2
  156.7 1.5 collective-permute-start.14
  158.3 11.8 %collective-permute-done.36 = bf16[192,768]{1,0:T(8,128)(2,1)S(1)} collective-permute-done((bf16[192,768]{1,0:T(8,128)(2,1)S(1)}, bf16[192,768]{1,0:T(8,128)(2,1)S(1)}, u32[]{:S(2)}, u32[]{:S(2)}) %collective-permute-start.36) | collective-permute-done | bytes 294944 | tf_op jit(solution)/shard_map/ppermute | solution.py:519
  172.3 4.1 %collective-permute-done.14 = bf16[2,128,768]{2,1,0:T(8,128)(2,1)S(1)} collective-permute-done((bf16[2,128,768]{2,1,0:T(8,128)(2,1)S(1)}, bf16[2,128,768]{2,1,0:T(8,128)(2,1)S(1)}, u32[]{:S(2)}, u32[]{:S(2)}) %collective-permute-start.14) | collective-permute-done | bytes 393248 | tf_op jit(solution)/shard_map/ppermute | solution.py:519
  176.6 3.0 %collective-permute-start.15 = (bf16[128,768]{1,0:T(8,128)(2,1)S(1)}, bf16[128,768]{1,0:T(8,128)(2,1)S(1)}, u32[]{:S(2)}, u32[]{:S(2)}) collective-permute-start(bf16[128,768]{1,0:T(8,128)(2,1)S(1)} %get-tuple-element.158), channel_id=1, source_target_pairs={{0,8},{4,12},{8,0},{12,4},{1,9},{5,13},{9,1},{13,5},{2,10},{6,14},... | collective-permute-start | bytes 589832 | tf_op jit(solution)/shard_map/ppermute | solution.py:519
  179.5 4.1 %collective-permute-done.20 = bf16[2,128,768]{2,1,0:T(8,128)(2,1)S(1)} collective-permute-done((bf16[2,128,768]{2,1,0:T(8,128)(2,1)S(1)}, bf16[2,128,768]{2,1,0:T(8,128)(2,1)S(1)}, u32[]{:S(2)}, u32[]{:S(2)}) %collective-permute-start.20) | collective-permute-done | bytes 393248 | tf_op jit(solution)/shard_map/ppermute | solution.py:519
  184.0 2.7 %collective-permute-start.24 = (bf16[128,768]{1,0:T(8,128)(2,1)S(1)}, bf16[128,768]{1,0:T(8,128)(2,1)S(1)}, u32[]{:S(2)}, u32[]{:S(2)}) collective-permute-start(bf16[128,768]{1,0:T(8,128)(2,1)S(1)} %fusion.29), channel_id=1, source_target_pairs={{0,8},{4,12},{8,0},{12,4},{1,9},{5,13},{9,1},{13,5},{2,10},{6,14},... | collective-permute-start | bytes 589832 | tf_op jit(solution)/shard_map/ppermute | solution.py:519
  186.9 12.2 %collective-permute-done.37 = bf16[2,192,768]{2,1,0:T(8,128)(2,1)S(1)} collective-permute-done((bf16[2,192,768]{2,1,0:T(8,128)(2,1)S(1)}, bf16[2,192,768]{2,1,0:T(8,128)(2,1)S(1)}, u32[]{:S(2)}, u32[]{:S(2)}) %collective-permute-start.37) | collective-permute-done | bytes 589856 | tf_op jit(solution)/shard_map/ppermute | solution.py:519
  201.5 1.7 collective-permute-done.23
  204.7 4.5 %collective-permute-done.29 = bf16[416,384]{1,0:T(8,128)(2,1)S(1)} collective-permute-done((bf16[416,384]{1,0:T(8,128)(2,1)S(1)}, bf16[416,384]{1,0:T(8,128)(2,1)S(1)}, u32[]{:S(2)}, u32[]{:S(2)}) %collective-permute-start.29) | collective-permute-done | bytes 319520 | tf_op jit(solution)/shard_map/ppermute | solution.py:519
  209.4 9.5 %collective-permute-done.30 = bf16[208,384]{1,0:T(8,128)(2,1)S(1)} collective-permute-done((bf16[208,384]{1,0:T(8,128)(2,1)S(1)}, bf16[208,384]{1,0:T(8,128)(2,1)S(1)}, u32[]{:S(2)}, u32[]{:S(2)}) %collective-permute-start.30) | collective-permute-done | bytes 159776 | tf_op jit(solution)/shard_map/ppermute | solution.py:519
  219.9 1.6 collective-permute-start.16
  221.5 4.8 %collective-permute-done.31 = bf16[208,384]{1,0:T(8,128)(2,1)S(1)} collective-permute-done((bf16[208,384]{1,0:T(8,128)(2,1)S(1)}, bf16[208,384]{1,0:T(8,128)(2,1)S(1)}, u32[]{:S(2)}, u32[]{:S(2)}) %collective-permute-start.31) | collective-permute-done | bytes 159776 | tf_op jit(solution)/shard_map/ppermute | solution.py:519
  226.7 4.6 %collective-permute-done.26 = bf16[2,128,768]{2,1,0:T(8,128)(2,1)S(1)} collective-permute-done((bf16[2,128,768]{2,1,0:T(8,128)(2,1)S(1)}, bf16[2,128,768]{2,1,0:T(8,128)(2,1)S(1)}, u32[]{:S(2)}, u32[]{:S(2)}) %collective-permute-start.26) | collective-permute-done | bytes 393248 | tf_op jit(solution)/shard_map/ppermute | solution.py:519
  232.3 6.4 %collective-permute-done.16 = bf16[2,128,768]{2,1,0:T(8,128)(2,1)S(1)} collective-permute-done((bf16[2,128,768]{2,1,0:T(8,128)(2,1)S(1)}, bf16[2,128,768]{2,1,0:T(8,128)(2,1)S(1)}, u32[]{:S(2)}, u32[]{:S(2)}) %collective-permute-start.16) | collective-permute-done | bytes 393248 | tf_op jit(solution)/shard_map/ppermute | solution.py:519
  240.5 1.5 collective-permute-done.33
  245.4 1.4 reshape_squeeze.3
  246.8 1.3 fusion.34
  249.5 1.5 broadcast_select_fusion.21
  252.0 1.3 broadcast_select_fusion.25
  254.8 2.0 convert_add_fusion
  256.8 2.1 add_add_fusion
  (275 shorter events, 48.8 us)
Async XLA Ops:
  0.7 39.8 %collective-permute-start.3 = (bf16[384,768]{1,0:T(8,128)(2,1)}, bf16[384,768]{1,0:T(8,128)(2,1)}, u32[]{:S(2)}, u32[]{:S(2)}) collective-permute-start(bf16[384,768]{1,0:T(8,128)(2,1)} %param.21), channel_id=1, source_target_pairs={{0,16},{16,0},{1,17},{17,1},{2,18},{18,2},{3,19},{19,3},{4,20},{20... | collective-permute-start | bytes 1769480 | tf_op jit(solution)/shard_map/ppermute | solution.py:519
  3.7 37.9 %collective-permute-start.4 = (bf16[768,384]{1,0:T(8,128)(2,1)}, bf16[768,384]{1,0:T(8,128)(2,1)S(1)}, u32[]{:S(2)}, u32[]{:S(2)}) collective-permute-start(bf16[768,384]{1,0:T(8,128)(2,1)} %param.23), channel_id=1, source_target_pairs={{0,16},{16,0},{1,17},{17,1},{2,18},{18,2},{3,19},{19,3},{4,20},{20... | collective-permute-start | bytes 1769480 | tf_op jit(solution)/shard_map/ppermute | solution.py:519
  5.8 21.1 %copy-start.55 = (bf16[1,128,768]{2,1,0:T(8,128)(2,1)}, bf16[1,128,768]{2,1,0:T(8,128)(2,1)S(1)}, u32[]{:S(2)}) copy-start(bf16[1,128,768]{2,1,0:T(8,128)(2,1)S(1)} %get-tuple-element.64) | copy-start | bytes 589828
  5.9 20.1 %collective-permute-start = (bf16[2,128,768]{2,1,0:T(8,128)(2,1)S(1)}, bf16[2,128,768]{2,1,0:T(8,128)(2,1)S(1)}, u32[]{:S(2)}, u32[]{:S(2)}) collective-permute-start(bf16[2,128,768]{2,1,0:T(8,128)(2,1)S(1)} %pad_maximum_fusion.13), channel_id=1, source_target_pairs={{0,8},{4,12},{8,0},{12,4},{1,9},{5,13},{9,1},{13,5},{2,10},{6,14},... | collective-permute-start | bytes 1179656 | tf_op jit(solution)/shard_map/ppermute | solution.py:519
  9.8 30.6 %copy-start.67 = (bf16[384,768]{1,0:T(8,128)(2,1)S(1)}, bf16[384,768]{1,0:T(8,128)(2,1)}, u32[]{:S(2)}) copy-start(bf16[384,768]{1,0:T(8,128)(2,1)} %param.21) | copy-start | bytes 1769476
  9.8 53.5 %collective-permute-start.9 = (bf16[768,384]{1,0:T(8,128)(2,1)}, bf16[768,384]{1,0:T(8,128)(2,1)}, u32[]{:S(2)}, u32[]{:S(2)}) collective-permute-start(bf16[768,384]{1,0:T(8,128)(2,1)} %pad_maximum_fusion.11), channel_id=1, source_target_pairs={{0,16},{16,0},{1,17},{17,1},{2,18},{18,2},{3,19},{19,3},{4,20},{20... | collective-permute-start | bytes 1769480 | tf_op jit(solution)/shard_map/ppermute | solution.py:519
  25.9 6.0 %collective-permute-start.5 = (bf16[1,128,768]{2,1,0:T(8,128)(2,1)S(1)}, bf16[1,128,768]{2,1,0:T(8,128)(2,1)S(1)}, u32[]{:S(2)}, u32[]{:S(2)}) collective-permute-start(bf16[1,128,768]{2,1,0:T(8,128)(2,1)S(1)} %get-tuple-element.63), channel_id=1, source_target_pairs={{0,4},{4,0},{8,12},{12,8},{1,5},{5,1},{9,13},{13,9},{2,6},{6,2},{1... | collective-permute-start | bytes 589832 | tf_op jit(solution)/shard_map/ppermute | solution.py:519
  26.9 12.0 %collective-permute-start.6 = (bf16[1,128,768]{2,1,0:T(8,128)(2,1)S(1)}, bf16[1,128,768]{2,1,0:T(8,128)(2,1)S(1)}, u32[]{:S(2)}, u32[]{:S(2)}) collective-permute-start(bf16[1,128,768]{2,1,0:T(8,128)(2,1)S(1)} %get-tuple-element.64), channel_id=1, source_target_pairs={{0,12},{4,8},{8,4},{12,0},{1,13},{5,9},{9,5},{13,1},{2,14},{6,10},... | collective-permute-start | bytes 589832 | tf_op jit(solution)/shard_map/ppermute | solution.py:519
  31.9 10.0 %collective-permute-start.1 = (bf16[2,128,768]{2,1,0:T(8,128)(2,1)S(1)}, bf16[2,128,768]{2,1,0:T(8,128)(2,1)S(1)}, u32[]{:S(2)}, u32[]{:S(2)}) collective-permute-start(bf16[2,128,768]{2,1,0:T(8,128)(2,1)S(1)} %collective-permute-done.fz), channel_id=1, source_target_pairs={{0,2},{1,3},{2,0},{3,1},{4,6},{5,7},{6,4},{7,5},{8,10},{9,11},{10,... | collective-permute-start | bytes 1179656 | tf_op jit(solution)/shard_map/ppermute | solution.py:519
  38.9 10.7 %collective-permute-start.7 = (bf16[2,128,768]{2,1,0:T(8,128)(2,1)S(1)}, bf16[2,128,768]{2,1,0:T(8,128)(2,1)S(1)}, u32[]{:S(2)}, u32[]{:S(2)}) collective-permute-start(bf16[2,128,768]{2,1,0:T(8,128)(2,1)S(1)} %constant_dynamic-update-slice_fusion.nz), channel_id=1, source_target_pairs={{0,2},{1,3},{2,0},{3,1},{4,6},{5,7},{6,4},{7,5},{8,10},{9,11},{10,... | collective-permute-start | bytes 1179656 | tf_op jit(solution)/shard_map/ppermute | solution.py:519
  42.1 24.3 %collective-permute-start.2 = (bf16[2,2,128,768]{3,2,1,0:T(8,128)(2,1)S(1)}, bf16[2,2,128,768]{3,2,1,0:T(8,128)(2,1)S(1)}, u32[]{:S(2)}, u32[]{:S(2)}) collective-permute-start(bf16[2,2,128,768]{3,2,1,0:T(8,128)(2,1)S(1)} %pad_maximum_fusion.6), channel_id=1, source_target_pairs={{0,1},{1,0},{2,3},{3,2},{4,5},{5,4},{6,7},{7,6},{8,9},{9,8},{10,11... | collective-permute-start | bytes 2359304 | tf_op jit(solution)/shard_map/ppermute | solution.py:519
  49.7 16.7 %collective-permute-start.8 = (bf16[2,2,128,768]{3,2,1,0:T(8,128)(2,1)S(1)}, bf16[2,2,128,768]{3,2,1,0:T(8,128)(2,1)S(1)}, u32[]{:S(2)}, u32[]{:S(2)}) collective-permute-start(bf16[2,2,128,768]{3,2,1,0:T(8,128)(2,1)S(1)} %pad_maximum_fusion.7), channel_id=1, source_target_pairs={{0,1},{1,0},{2,3},{3,2},{4,5},{5,4},{6,7},{7,6},{8,9},{9,8},{10,11... | collective-permute-start | bytes 2359304 | tf_op jit(solution)/shard_map/ppermute | solution.py:519
  62.8 23.0 %collective-permute-start.10 = (bf16[2,256,768]{2,1,0:T(8,128)(2,1)S(1)}, bf16[2,256,768]{2,1,0:T(8,128)(2,1)S(1)}, u32[]{:S(2)}, u32[]{:S(2)}) collective-permute-start(bf16[2,256,768]{2,1,0:T(8,128)(2,1)S(1)} %get-tuple-element.74), channel_id=1, source_target_pairs={{0,1},{1,0},{2,3},{3,2},{4,5},{5,4},{6,7},{7,6},{8,9},{9,8},{10,11... | collective-permute-start | bytes 2359304 | tf_op jit(solution)/shard_map/ppermute | solution.py:519
  63.4 34.4 %collective-permute-start.12 = (bf16[768,768]{1,0:T(8,128)(2,1)S(1)}, bf16[768,768]{1,0:T(8,128)(2,1)S(1)}, u32[]{:S(2)}, u32[]{:S(2)}) collective-permute-start(bf16[768,768]{1,0:T(8,128)(2,1)S(1)} %get-tuple-element.79), channel_id=1, source_target_pairs={{0,16},{16,0},{1,17},{17,1},{2,18},{18,2},{3,19},{19,3},{4,20},{20... | collective-permute-start | bytes 3538952 | tf_op jit(solution)/shard_map/ppermute | solution.py:519
  76.0 35.7 %copy-start.3 = (bf16[2048,768]{1,0:T(8,128)(2,1)}, bf16[2048,768]{1,0:T(8,128)(2,1)S(1)}, u32[]{:S(2)}) copy-start(bf16[2048,768]{1,0:T(8,128)(2,1)S(1)} %get-tuple-element.95.refs_6_.refs_9_) | copy-start | bytes 9437188
  76.0 35.7 %copy-start.5 = (bf16[2048,768]{1,0:T(8,128)(2,1)}, bf16[2048,768]{1,0:T(8,128)(2,1)S(1)}, u32[]{:S(2)}) copy-start(bf16[2048,768]{1,0:T(8,128)(2,1)S(1)} %get-tuple-element.96.refs_7_.refs_10_) | copy-start | bytes 9437188
  85.8 26.0 %copy-start.13 = (bf16[64,2048]{1,0:T(8,128)(2,1)}, bf16[64,2048]{1,0:T(8,128)(2,1)S(1)}, u32[]{:S(2)}) copy-start(bf16[64,2048]{1,0:T(8,128)(2,1)S(1)} %get-tuple-element.89.refs_0_.refs_3_) | copy-start | bytes 786436
  85.8 26.0 %copy-start.15 = (bf16[64,2048]{1,0:T(8,128)(2,1)}, bf16[64,2048]{1,0:T(8,128)(2,1)S(1)}, u32[]{:S(2)}) copy-start(bf16[64,2048]{1,0:T(8,128)(2,1)S(1)} %get-tuple-element.92.refs_3_.refs_6_) | copy-start | bytes 786436
  86.5 14.6 %collective-permute-start.11 = (bf16[2,128,768]{2,1,0:T(8,128)(2,1)S(1)}, bf16[2,128,768]{2,1,0:T(8,128)(2,1)S(1)}, u32[]{:S(2)}, u32[]{:S(2)}) collective-permute-start(bf16[2,128,768]{2,1,0:T(8,128)(2,1)S(1)} %fusion.18), channel_id=1, source_target_pairs={{0,2},{1,3},{2,0},{3,1},{4,6},{5,7},{6,4},{7,5},{8,10},{9,11},{10,... | collective-permute-start | bytes 1179656 | tf_op jit(solution)/shard_map/ppermute | solution.py:519
  98.5 18.9 %collective-permute-start.18 = (bf16[384,768]{1,0:T(8,128)(2,1)S(1)}, bf16[384,768]{1,0:T(8,128)(2,1)S(1)}, u32[]{:S(2)}, u32[]{:S(2)}) collective-permute-start(bf16[384,768]{1,0:T(8,128)(2,1)S(1)} %dynamic-slice_convert_fusion), channel_id=1, source_target_pairs={{0,4},{4,0},{8,12},{12,8},{1,5},{5,1},{9,13},{13,9},{2,6},{6,2},{1... | collective-permute-start | bytes 1769480 | tf_op jit(solution)/shard_map/ppermute | solution.py:519
  117.3 37.2 %collective-permute-start.21 = (bf16[2,256,768]{2,1,0:T(8,128)(2,1)}, bf16[2,256,768]{2,1,0:T(8,128)(2,1)}, u32[]{:S(2)}, u32[]{:S(2)}) collective-permute-start(bf16[2,256,768]{2,1,0:T(8,128)(2,1)} %get-tuple-element.104), channel_id=1, source_target_pairs={{0,1},{1,0},{2,3},{3,2},{4,5},{5,4},{6,7},{7,6},{8,9},{9,8},{10,11... | collective-permute-start | bytes 2359304 | tf_op jit(solution)/shard_map/ppermute | solution.py:519
  119.7 33.7 %collective-permute-start.35 = (bf16[192,768]{1,0:T(8,128)(2,1)}, bf16[192,768]{1,0:T(8,128)(2,1)}, u32[]{:S(2)}, u32[]{:S(2)}) collective-permute-start(bf16[192,768]{1,0:T(8,128)(2,1)} %dynamic-slice_convert_fusion.2), channel_id=1, source_target_pairs={{0,8},{4,12},{8,0},{12,4},{1,9},{5,13},{9,1},{13,5},{2,10},{6,14},... | collective-permute-start | bytes 884744 | tf_op jit(solution)/shard_map/ppermute | solution.py:519
  124.1 102.3 %copy-start.70 = (f32[2,128]{1,0:T(2,128)}, f32[2,128]{1,0:T(2,128)S(1)}, u32[]{:S(2)}) copy-start(f32[2,128]{1,0:T(2,128)S(1)} %add_rsqrt_fusion) | copy-start | bytes 3076
  133.4 23.1 %collective-permute-start.13 = (bf16[2,256,768]{2,1,0:T(8,128)(2,1)S(1)}, bf16[2,256,768]{2,1,0:T(8,128)(2,1)S(1)}, u32[]{:S(2)}, u32[]{:S(2)}) collective-permute-start(bf16[2,256,768]{2,1,0:T(8,128)(2,1)S(1)} %get-tuple-element.85), channel_id=1, source_target_pairs={{0,1},{1,0},{2,3},{3,2},{4,5},{5,4},{6,7},{7,6},{8,9},{9,8},{10,11... | collective-permute-start | bytes 2359304 | tf_op jit(solution)/shard_map/ppermute | solution.py:519
  152.3 17.9 %collective-permute-start.19 = (bf16[2,256,768]{2,1,0:T(8,128)(2,1)S(1)}, bf16[2,256,768]{2,1,0:T(8,128)(2,1)S(1)}, u32[]{:S(2)}, u32[]{:S(2)}) collective-permute-start(bf16[2,256,768]{2,1,0:T(8,128)(2,1)S(1)} %get-tuple-element.102), channel_id=1, source_target_pairs={{0,1},{1,0},{2,3},{3,2},{4,5},{5,4},{6,7},{7,6},{8,9},{9,8},{10,11... | collective-permute-start | bytes 2359304 | tf_op jit(solution)/shard_map/ppermute | solution.py:519
  152.9 31.2 %collective-permute-start.28 = (bf16[832,384]{1,0:T(8,128)(2,1)S(1)}, bf16[832,384]{1,0:T(8,128)(2,1)S(1)}, u32[]{:S(2)}, u32[]{:S(2)}) collective-permute-start(bf16[832,384]{1,0:T(8,128)(2,1)S(1)} %get-tuple-element.106), channel_id=1, source_target_pairs={{0,16},{16,0},{1,17},{17,1},{2,18},{18,2},{3,19},{19,3},{4,20},{20... | collective-permute-start | bytes 1916936 | tf_op jit(solution)/shard_map/ppermute | solution.py:519
  154.4 15.7 %collective-permute-start.36 = (bf16[192,768]{1,0:T(8,128)(2,1)S(1)}, bf16[192,768]{1,0:T(8,128)(2,1)S(1)}, u32[]{:S(2)}, u32[]{:S(2)}) collective-permute-start(bf16[192,768]{1,0:T(8,128)(2,1)S(1)} %add_convert_fusion), channel_id=1, source_target_pairs={{0,8},{4,12},{8,0},{12,4},{1,9},{5,13},{9,1},{13,5},{2,10},{6,14},... | collective-permute-start | bytes 884744 | tf_op jit(solution)/shard_map/ppermute | solution.py:519
  155.9 15.2 %collective-permute-start.22 = (bf16[2,128,768]{2,1,0:T(8,128)(2,1)S(1)}, bf16[2,128,768]{2,1,0:T(8,128)(2,1)S(1)}, u32[]{:S(2)}, u32[]{:S(2)}) collective-permute-start(bf16[2,128,768]{2,1,0:T(8,128)(2,1)S(1)} %fusion.21), channel_id=1, source_target_pairs={{0,2},{1,3},{2,0},{3,1},{4,6},{5,7},{6,4},{7,5},{8,10},{9,11},{10,... | collective-permute-start | bytes 1179656 | tf_op jit(solution)/shard_map/ppermute | solution.py:519
  156.7 19.7 %collective-permute-start.14 = (bf16[2,128,768]{2,1,0:T(8,128)(2,1)S(1)}, bf16[2,128,768]{2,1,0:T(8,128)(2,1)S(1)}, u32[]{:S(2)}, u32[]{:S(2)}) collective-permute-start(bf16[2,128,768]{2,1,0:T(8,128)(2,1)S(1)} %fusion.19), channel_id=1, source_target_pairs={{0,2},{1,3},{2,0},{3,1},{4,6},{5,7},{6,4},{7,5},{8,10},{9,11},{10,... | collective-permute-start | bytes 1179656 | tf_op jit(solution)/shard_map/ppermute | solution.py:519
  170.2 28.9 %collective-permute-start.37 = (bf16[2,192,768]{2,1,0:T(8,128)(2,1)S(1)}, bf16[2,192,768]{2,1,0:T(8,128)(2,1)S(1)}, u32[]{:S(2)}, u32[]{:S(2)}) collective-permute-start(bf16[2,192,768]{2,1,0:T(8,128)(2,1)S(1)} %pad_maximum_fusion.12), channel_id=1, source_target_pairs={{0,4},{4,0},{8,12},{12,8},{1,5},{5,1},{9,13},{13,9},{2,6},{6,2},{1... | collective-permute-start | bytes 1769480 | tf_op jit(solution)/shard_map/ppermute | solution.py:519
  170.5 13.1 %collective-permute-start.20 = (bf16[2,128,768]{2,1,0:T(8,128)(2,1)S(1)}, bf16[2,128,768]{2,1,0:T(8,128)(2,1)S(1)}, u32[]{:S(2)}, u32[]{:S(2)}) collective-permute-start(bf16[2,128,768]{2,1,0:T(8,128)(2,1)S(1)} %fusion.20), channel_id=1, source_target_pairs={{0,2},{1,3},{2,0},{3,1},{4,6},{5,7},{6,4},{7,5},{8,10},{9,11},{10,... | collective-permute-start | bytes 1179656 | tf_op jit(solution)/shard_map/ppermute | solution.py:519
  171.3 32.1 %collective-permute-start.25 = (bf16[128,768]{1,0:T(8,128)(2,1)S(1)}, bf16[128,768]{1,0:T(8,128)(2,1)S(1)}, u32[]{:S(2)}, u32[]{:S(2)}) collective-permute-start(bf16[128,768]{1,0:T(8,128)(2,1)S(1)} %get-tuple-element.156), channel_id=1, source_target_pairs={{0,12},{4,8},{8,4},{12,0},{1,13},{5,9},{9,5},{13,1},{2,14},{6,10},... | collective-permute-start | bytes 589832 | tf_op jit(solution)/shard_map/ppermute | solution.py:519
  176.5 62.1 %copy-start.59 = (bf16[1,128,768]{2,1,0:T(8,128)(2,1)}, bf16[1,128,768]{2,1,0:T(8,128)(2,1)S(1)}, u32[]{:S(2)}) copy-start(bf16[1,128,768]{2,1,0:T(8,128)(2,1)S(1)} %get-tuple-element.157) | copy-start | bytes 589828
  176.6 26.8 %collective-permute-start.15 = (bf16[128,768]{1,0:T(8,128)(2,1)S(1)}, bf16[128,768]{1,0:T(8,128)(2,1)S(1)}, u32[]{:S(2)}, u32[]{:S(2)}) collective-permute-start(bf16[128,768]{1,0:T(8,128)(2,1)S(1)} %get-tuple-element.158), channel_id=1, source_target_pairs={{0,8},{4,12},{8,0},{12,4},{1,9},{5,13},{9,1},{13,5},{2,10},{6,14},... | collective-permute-start | bytes 589832 | tf_op jit(solution)/shard_map/ppermute | solution.py:519
  183.6 19.7 %collective-permute-start.23 = (bf16[128,768]{1,0:T(8,128)(2,1)S(1)}, bf16[128,768]{1,0:T(8,128)(2,1)S(1)}, u32[]{:S(2)}, u32[]{:S(2)}) collective-permute-start(bf16[128,768]{1,0:T(8,128)(2,1)S(1)} %get-tuple-element.155), channel_id=1, source_target_pairs={{0,4},{4,0},{8,12},{12,8},{1,5},{5,1},{9,13},{13,9},{2,6},{6,2},{1... | collective-permute-start | bytes 589832 | tf_op jit(solution)/shard_map/ppermute | solution.py:519
  184.0 19.4 %collective-permute-start.24 = (bf16[128,768]{1,0:T(8,128)(2,1)S(1)}, bf16[128,768]{1,0:T(8,128)(2,1)S(1)}, u32[]{:S(2)}, u32[]{:S(2)}) collective-permute-start(bf16[128,768]{1,0:T(8,128)(2,1)S(1)} %fusion.29), channel_id=1, source_target_pairs={{0,8},{4,12},{8,0},{12,4},{1,9},{5,13},{9,1},{13,5},{2,10},{6,14},... | collective-permute-start | bytes 589832 | tf_op jit(solution)/shard_map/ppermute | solution.py:519
  199.1 10.1 %collective-permute-start.29 = (bf16[416,384]{1,0:T(8,128)(2,1)S(1)}, bf16[416,384]{1,0:T(8,128)(2,1)S(1)}, u32[]{:S(2)}, u32[]{:S(2)}) collective-permute-start(bf16[416,384]{1,0:T(8,128)(2,1)S(1)} %dynamic-slice_convert_fusion.1), channel_id=1, source_target_pairs={{0,4},{4,0},{8,12},{12,8},{1,5},{5,1},{9,13},{13,9},{2,6},{6,2},{1... | collective-permute-start | bytes 958472 | tf_op jit(solution)/shard_map/ppermute | solution.py:519
  204.7 35.0 %copy-start.71 = (f32[2,128]{1,0:T(2,128)}, f32[2,128]{1,0:T(2,128)S(1)}, u32[]{:S(2)}) copy-start(f32[2,128]{1,0:T(2,128)S(1)} %broadcast_multiply_fusion) | copy-start | bytes 3076
  209.3 9.6 %collective-permute-start.30 = (bf16[208,384]{1,0:T(8,128)(2,1)S(1)}, bf16[208,384]{1,0:T(8,128)(2,1)S(1)}, u32[]{:S(2)}, u32[]{:S(2)}) collective-permute-start(bf16[208,384]{1,0:T(8,128)(2,1)S(1)} %dynamic-slice_convert_fusion.3), channel_id=1, source_target_pairs={{0,8},{4,12},{8,0},{12,4},{1,9},{5,13},{9,1},{13,5},{2,10},{6,14},... | collective-permute-start | bytes 479240 | tf_op jit(solution)/shard_map/ppermute | solution.py:519
  209.4 30.4 %copy-start.72 = (f32[2,128]{1,0:T(2,128)}, f32[2,128]{1,0:T(2,128)S(1)}, u32[]{:S(2)}) copy-start(f32[2,128]{1,0:T(2,128)S(1)} %broadcast_multiply_fusion.1) | copy-start | bytes 3076
  218.9 7.4 %collective-permute-start.31 = (bf16[208,384]{1,0:T(8,128)(2,1)S(1)}, bf16[208,384]{1,0:T(8,128)(2,1)S(1)}, u32[]{:S(2)}, u32[]{:S(2)}) collective-permute-start(bf16[208,384]{1,0:T(8,128)(2,1)S(1)} %add_convert_fusion.1), channel_id=1, source_target_pairs={{0,8},{4,12},{8,0},{12,4},{1,9},{5,13},{9,1},{13,5},{2,10},{6,14},... | collective-permute-start | bytes 479240 | tf_op jit(solution)/shard_map/ppermute | solution.py:519
  219.3 12.1 %collective-permute-start.26 = (bf16[2,128,768]{2,1,0:T(8,128)(2,1)S(1)}, bf16[2,128,768]{2,1,0:T(8,128)(2,1)S(1)}, u32[]{:S(2)}, u32[]{:S(2)}) collective-permute-start(bf16[2,128,768]{2,1,0:T(8,128)(2,1)S(1)} %fusion.7), channel_id=1, source_target_pairs={{0,2},{1,3},{2,0},{3,1},{4,6},{5,7},{6,4},{7,5},{8,10},{9,11},{10,... | collective-permute-start | bytes 1179656 | tf_op jit(solution)/shard_map/ppermute | solution.py:519
  219.9 18.7 %collective-permute-start.16 = (bf16[2,128,768]{2,1,0:T(8,128)(2,1)S(1)}, bf16[2,128,768]{2,1,0:T(8,128)(2,1)S(1)}, u32[]{:S(2)}, u32[]{:S(2)}) collective-permute-start(bf16[2,128,768]{2,1,0:T(8,128)(2,1)S(1)} %pad_maximum_fusion.15), channel_id=1, source_target_pairs={{0,2},{1,3},{2,0},{3,1},{4,6},{5,7},{6,4},{7,5},{8,10},{9,11},{10,... | collective-permute-start | bytes 1179656 | tf_op jit(solution)/shard_map/ppermute | solution.py:519
  226.4 13.3 %collective-permute-start.32 = (bf16[2,208,384]{2,1,0:T(8,128)(2,1)S(1)}, bf16[2,208,384]{2,1,0:T(8,128)(2,1)S(1)}, u32[]{:S(2)}, u32[]{:S(2)}) collective-permute-start(bf16[2,208,384]{2,1,0:T(8,128)(2,1)S(1)} %pad_maximum_fusion.17), channel_id=1, source_target_pairs={{0,4},{4,0},{8,12},{12,8},{1,5},{5,1},{9,13},{13,9},{2,6},{6,2},{1... | collective-permute-start | bytes 958472 | tf_op jit(solution)/shard_map/ppermute | solution.py:519
  232.3 17.2 %collective-permute-start.27 = (bf16[2,2,128,768]{3,2,1,0:T(8,128)(2,1)}, bf16[2,2,128,768]{3,2,1,0:T(8,128)(2,1)}, u32[]{:S(2)}, u32[]{:S(2)}) collective-permute-start(bf16[2,2,128,768]{3,2,1,0:T(8,128)(2,1)} %pad_maximum_fusion.10), channel_id=1, source_target_pairs={{0,1},{1,0},{2,3},{3,2},{4,5},{5,4},{6,7},{7,6},{8,9},{9,8},{10,11... | collective-permute-start | bytes 2359304 | tf_op jit(solution)/shard_map/ppermute | solution.py:519
  239.6 11.5 %collective-permute-start.17 = (bf16[2,2,128,768]{3,2,1,0:T(8,128)(2,1)}, bf16[2,2,128,768]{3,2,1,0:T(8,128)(2,1)}, u32[]{:S(2)}, u32[]{:S(2)}) collective-permute-start(bf16[2,2,128,768]{3,2,1,0:T(8,128)(2,1)} %pad_maximum_fusion.8), channel_id=1, source_target_pairs={{0,1},{1,0},{2,3},{3,2},{4,5},{5,4},{6,7},{7,6},{8,9},{9,8},{10,11... | collective-permute-start | bytes 2359304 | tf_op jit(solution)/shard_map/ppermute | solution.py:519
  239.8 2.2 collective-permute-start.33
  242.6 5.5 %collective-permute-start.34 = (f32[8,768]{1,0:T(8,128)}, f32[8,768]{1,0:T(8,128)}, u32[]{:S(2)}, u32[]{:S(2)}) collective-permute-start(f32[8,768]{1,0:T(8,128)} %fusion.37), channel_id=1, source_target_pairs={{0,2},{1,3},{2,0},{3,1},{4,6},{5,7},{6,4},{7,5},{8,10},{9,11},{10,... | collective-permute-start | bytes 73736 | tf_op jit(solution)/shard_map/ppermute | solution.py:519
  (66 other events, 285.1 us)

commit v5 on v4

--- a/solution.py
+++ b/solution.py
@@ -172,7 +172,7 @@
         out_shape=[low_shape(rows, width)] * 2
         + [low_shape(rows // 2, width), shape(tall, rows)]
         + [low_shape(wide, rows)] * 2 + [low_shape(wide, rows // 2)] * 2,
-        compiler_params=params(32),
+        compiler_params=params(56),
         cost_estimate=cost(6 * rows * width * wide, 8 * rows * width),
     )(at, x, x, g, g, *received, trig, trig, *fixed)
 
@@ -274,7 +274,7 @@
             pltpu.VMEM((length, lanes), F32),
             pltpu.VMEM((length, lanes), F32),
         ],
-        compiler_params=params(32),
+        compiler_params=params(56),
         cost_estimate=cost(40 * rows * length * HEAD, 16 * HEAD * length, rows * length),
     )(*after, qt, dot, kt, vt, trig, trig)
 
@@ -367,7 +367,7 @@
         ),
         out_shape=[low_shape(2 * STEP, width)] * 2 + [low_shape(2, STEP, width)] * 2
         + [shape(8, width)] + parts,
-        compiler_params=params(40),
+        compiler_params=params(56),
         cost_estimate=cost(48 * STEP * width * hidden, 16 * MIB, 8 * STEP * hidden),
     )(at, x, x, g, g, up, bias, down, scale, offset)
 
@@ -414,7 +414,7 @@
            pl.BlockSpec((wide, width), lambda i: (3, 0))],
         out_specs=[slots, slots, pl.BlockSpec((wide, width), lambda i: (0, 0))],
         out_shape=[low_shape(2, STEP, width)] * 2 + [shape(wide, width)],
-        compiler_params=params(24),
+        compiler_params=params(56),
         cost_estimate=cost(4 * rows * width * wide, 8 * MIB),
     )(*o, g, ff, weights)
 
@@ -424,7 +424,7 @@
     grads, refs = refs[: count * heads], refs[count * heads :]
     n1_ref, xhat_ref, w_ref, s1_ref, *refs = refs
     if own:
-        (a2_ref, small_ff, small_other, mix_other, out_part, after,
+        (a2_ref, small_ff, small_other, mix_other, out_part,
          keep_ref, send_ref, first_ref, second_ref, mix, small) = refs
     else:
         keep_ref, send_ref, mix, small = refs
@@ -494,7 +494,7 @@
     else:
         specs += [pl.BlockSpec((STEP, width), lambda i, at: (jnp.minimum(i, 1), 0)),
                   whole(8, width), whole(8, width), whole(2 * wide, width),
-                  whole(wide, width), pl.BlockSpec(memory_space=pl.ANY)]
+                  whole(wide, width)]
         scratch = [pltpu.VMEM((tall, width), F32), pltpu.VMEM((8, width), F32)]
         if split:
             parts = [shape(4 * wide + 64, half), low_shape(4 * wide + 64, half)]
@@ -510,7 +510,7 @@
             scratch_shapes=scratch,
         ),
         out_shape=[low_shape(2, STEP, width)] * 2 + parts,
-        compiler_params=params(32),
+        compiler_params=params(56),
         cost_estimate=cost(4 * rows * width * tall, 10 * MIB),
     )(at, *[v for vs in grads for v in vs], n1, xhat, weights, scale, *extra)
 
@@ -550,22 +550,29 @@
     ).astype(F32)
 
 
-def halve(v, distance, bit):
-    rows = v.shape[0] // 2
-    keep = lax.dynamic_slice_in_dim(v, bit * rows, rows, 0)
-    send = lax.dynamic_slice_in_dim(v, (1 - bit) * rows, rows, 0).astype(BF16)
-    return keep + swap(send, "ctx", 4, distance).astype(F32)
-
-
-def double(v, c):
+def quarter_sum(v, c, *earlier):
+    rows = v.shape[0] // 4
+    mine = 2 * (c % 2) + c // 2
+
+    def part(j):
+        return lax.dynamic_slice_in_dim(v, (mine ^ j) * rows, rows, 0)
+
+    total = part(0)
+    for distance, j in ((3, 3), (2, 1), (1, 2)):
+        sent = swap(part(j).astype(BF16), "ctx", 4, distance)
+        total = total + tie(sent, *earlier).astype(F32)
+    return total
+
+
+def double(v, c, first=(), second=()):
     v = v.astype(BF16)
-    pair = jnp.stack([v, swap(v, "ctx", 4, 2)])
-    others = swap(pair, "ctx", 4, 1)
+    pair = jnp.stack([v, tie(swap(v, "ctx", 4, 2), *first)])
+    others = tie(swap(pair, "ctx", 4, 1), *second)
     return by_xor([pair[0], pair[1], others[0], others[1]], 2 * (c % 2) + c // 2)
 
 
 def sum_over_ctx(v, c):
-    return double(halve(halve(v, 1, c % 2), 2, c // 2), c)
+    return double(quarter_sum(v, c), c)
 
 
 def butterfly(v, axis_name, size):
@@ -615,15 +622,12 @@
     x_mine, x_theirs = my_quarter(inputs, s), my_quarter(inputs, 1 - s)
     g_theirs = my_quarter(cotangent, 1 - s)
     far_z = swap(jnp.concatenate([x_theirs, g_theirs], axis=0), "ctx", 4, 2)
-    cross = swap(tie(x_theirs, far_z), "ctx", 4, 3)
-    near = swap(tie(x_mine, far_z), "ctx", 4, 1)
-
-    def over_tp(v):
-        v_x = swap(v, "tp", 4, 2)
-        return v, v_x, swap(jnp.stack([v, v_x]), "tp", 4, 1)
-
-    far = over_tp(far_z)
-    others = over_tp(jnp.concatenate([near, cross], axis=0))
+    cross = swap(x_theirs, "ctx", 4, 3)
+    near = swap(x_mine, "ctx", 4, 1)
+
+    others_z = jnp.concatenate([near, cross], axis=0)
+    others_x = swap(others_z, "tp", 4, 2)
+    far_x = swap(far_z, "tp", 4, 2)
 
     wup = gather_halves(up_projection_weight, fsdp, f, 0)
     wdown = gather_halves(down_projection_weight, fsdp, f, 1)
@@ -641,11 +645,14 @@
         split, at, inputs, cotangent, wup, up_projection_bias, wdown, second_scale, second_shift
     )
 
+    def over_tp(v_z, v_x):
+        v_x = tie(v_x, small_ff)
+        return v_z, v_x, swap(jnp.stack([v_z, v_x]), "tp", 4, 1)
+
     weights = gather_halves(mix_out_shard, fsdp, f, 1, small_ff)
     n1, xhat_all, g, trig, kt, vt, qt, dot = project(
-        at, inputs, cotangent, (far[0], far[1], tie(far[2], small_ff)),
-        (others[0], others[1], tie(others[2], small_ff)), trig, weights, query_key_value_bias,
-        first_scale, first_shift,
+        at, inputs, cotangent, over_tp(far_z, far_x), over_tp(others_z, others_x), trig, weights,
+        query_key_value_bias, first_scale, first_shift,
     )
     def over_core(keep, send, *earlier):
         v = keep.astype(F32) + tie(swap(send, "tp", 4, 1), *earlier).astype(F32)
@@ -653,37 +660,34 @@
 
     def over_x(v, *earlier):
         return v[:, 0] + tie(swap(v[:, 1].astype(BF16), "tp", 4, 2), *earlier).astype(F32)
-
-    def scatter_tp(keep, send):
-        return over_x(over_core(keep, send))
 
     per_head = []
     for h in range(heads):
         after = ()
         if h == 1:
             early = over_core(keep_e, send_e, per_head[0][0])
-            after = (early,)
+            ff_rest = small_ff
+            if split:
+                ff_rest = tie(swap(ff_second, "fsdp", 2, 1), per_head[0][0])
+                ff_rest = ff_first + ff_rest.astype(F32)
+            after = (early, ff_rest)
         if h == heads - 1:
             early = over_x(early, per_head[h - 1][0])
-            ff_rest = small_ff
-            if split:
-                ff_rest = tie(swap(ff_second, "fsdp", 2, 1), per_head[h - 1][0])
-                ff_rest = ff_first + ff_rest.astype(F32)
-            after = (early, ff_rest)
+            after = (early,)
         per_head.append(attention(h, after, qt, dot, kt, vt, trig))
     o, dq, dk, dv = zip(*per_head)
-    keep_b, send_b, out_part = branch(o, g, ff, weights)
-    if split:
-        ff_half = halve(ff_rest, 1, c % 2)
-    else:
-        ff_half = small_ff
+    ff_quarter = quarter_sum(ff_rest, c, o[-1]) if split else small_ff
     keep_o, send_o, mix_other, small_other = back(
         False, split, at, (dk, dv), n1, xhat_all, weights, first_scale, ()
     )
+    keep_b, send_b, out_part = branch(o, g, tie(ff, keep_o), weights)
     keep_w, send_w, late_first, late_second = back(
-        True, split, at, (dq, dk, dv), n1, xhat_all, weights, first_scale,
-        (a2, small_ff, small_other, mix_other, out_part, ff_half),
-    )
+        True, split, at, (dq, dk, dv), n1, xhat_all, weights, tie(first_scale, ff_quarter),
+        (a2, small_ff, small_other, mix_other, out_part),
+    )
+    half_o = over_core(keep_o, send_o)
+    half_b = over_core(keep_b, send_b)
+    half_w = over_core(keep_w, send_w)
 
     def over_ctx(v, distance):
         return swap(v.astype(BF16), "ctx", 4, distance).astype(F32)
@@ -697,14 +701,14 @@
         return jnp.stack([jnp.where(s == 0, pieces[0], pieces[1]),
                           jnp.where(s == 0, pieces[1], pieces[0])]).astype(F32)
 
-    sums_b = scatter_tp(keep_b, send_b)
+    sums_b = over_x(half_b)
     block_out = gather_tp(sums_b[0], over_ctx(sums_b[1], 2) + early[0])
     block_out = (
         inputs.astype(F32) + block_out + (attention_output_bias + down_projection_bias)
     )
 
-    sums_o = scatter_tp(keep_o, send_o)
-    sums_w = scatter_tp(keep_w, send_w)
+    sums_o = over_x(half_o)
+    sums_w = over_x(half_w)
     a = jnp.stack([
         sums_w[0] + over_ctx(sums_o[0], 1),
         over_ctx(sums_w[1], 2) + over_ctx(sums_o[1], 3) + early[1],
@@ -718,14 +722,15 @@
     inputs_grad = cotangent.astype(F32) + gather_tp(norm_grad[0], norm_grad[1])
 
     if split:
-        q = double(halve(ff_half, 2, c // 2), c)
+        q = double(ff_quarter, c, (sums_w,), (norm_grad,))
         up_total = jnp.concatenate(q[:2], axis=0).astype(F32)
         down_total = jnp.concatenate(q[2:], axis=0).astype(F32)
         down_total = jnp.concatenate(
             [down_total[:, : width // 2], down_total[:, width // 2 :]], axis=0
         )
-        late = late_first + tie(swap(late_second, "fsdp", 2, 1), sums_w).astype(F32)
-        late = jnp.concatenate(sum_over_ctx(late, c), axis=0).astype(F32)
+        late = late_first + tie(swap(late_second, "fsdp", 2, 1), sums_o).astype(F32)
+        late = double(quarter_sum(late, c, sums_w), c)
+        late = jnp.concatenate(late, axis=0).astype(F32)
         small = jnp.concatenate([late[4 * local : 4 * local + 8], late[4 * local + 8 :][:8]], axis=1)
     else:
         q = sum_over_ctx(scatter_any(ff_first, 0), c)

time: 261 us -> 246 us (0.943)
  waiting for transfers between devices: 94.1 us -> 67.6 us
  Pallas kernels: 65.7 us -> 89.2 us
  local copies, waits for them, and re-layouts: 30.5 us -> 13.5 us
  other arithmetic: 27.7 us -> 33.1 us
    ppermute x38 -> x40, waiting for transfers between devices: 94.1 us -> 67.6 us  [swap(): return lax.ppermute(v, axis, [(i, i ^ distance) for i in range(size)])]
    unnamed x154 -> x82, local copies, waits for them, and re-layouts: 24.7 us -> 7.74 us
    pallas_call x2, Pallas kernels: 11.7 us -> 17.8 us  [back(): pl.pallas_call(functools.partial(back_kernel, own, split, heads), grid_sp...]
    pallas_call x3, Pallas kernels: 29.2 us -> 35.3 us  [attention(): pl.pallas_call(functools.partial(attention_kernel, len(after)), grid=(row...]
    pallas_call x1, Pallas kernels: 12.9 us -> 17.3 us  [feed_forward(): pl.pallas_call(functools.partial(forward_kernel, split), grid_spec=pltpu....]
    pallas_call x1, Pallas kernels: 9.08 us -> 13.4 us  [project(): pl.pallas_call(project_kernel, grid_spec=pltpu.PrefetchScalarGridSpec(num...]
    concatenate x3, other arithmetic: 0.27 us -> 3.31 us  [gather_halves(): jnp.concatenate([jnp.where(first, shard, other), jnp.where(first, other,...]
    pallas_call x1, Pallas kernels: 2.72 us -> 5.37 us  [branch(): pl.pallas_call(functools.partial(branch_kernel, heads), grid=(rows // STE...]
  transfers between devices with their start and end apart: 38 -> 40, of which waited for: 15 -> 12; matrix products, arithmetic and copies ran while one was open for 11% -> 14% of each run, Pallas kernels for 25% -> 36%
where the time goes in v5:
time: 246 us
  Pallas kernels  89.2 us (36%)
  waiting for transfers between devices  67.6 us (27%)
  starting transfers between devices  40.7 us (17%)
  other arithmetic  33.1 us (13%)
  local copies, waits for them, and re-layouts  13.5 us (5%)
    ppermute x40, waiting for transfers between devices, swap(): return lax.ppermute(v, axis, [(i, i ^ distance) for i in range(size)])  67.6 us
    ppermute x40, starting transfers between devices, swap(): return lax.ppermute(v, axis, [(i, i ^ distance) for i in range(size)])  40.7 us
    pallas_call x3, Pallas kernels, attention(): pl.pallas_call(functools.partial(attention_kernel, len(after)), grid=(row...  35.3 us
    pallas_call x2, Pallas kernels, back(): pl.pallas_call(functools.partial(back_kernel, own, split, heads), grid_sp...  17.8 us
    pallas_call x1, Pallas kernels, feed_forward(): pl.pallas_call(functools.partial(forward_kernel, split), grid_spec=pltpu....  17.3 us
    pallas_call x1, Pallas kernels, project(): pl.pallas_call(project_kernel, grid_spec=pltpu.PrefetchScalarGridSpec(num...  13.4 us
    unnamed x82, local copies, waits for them, and re-layouts  7.74 us
    pallas_call x1, Pallas kernels, branch(): pl.pallas_call(functools.partial(branch_kernel, heads), grid=(rows // STE...  5.37 us
  transfers between devices with their start and end apart: 40, of which 12 were waited for; matrix products, arithmetic and copies ran while one was open for 14% of the time, Pallas kernels for 36%

profile of v5, /device:TPU:0, one launch (start us, length us, event | category | flops | bytes accessed | tf_op | source)
XLA Modules:
  0.0 245.5 jit_solution(3479445954307783243)
XLA Ops:
  0.7 3.0 %collective-permute-start.3 = (bf16[768,384]{1,0:T(8,128)(2,1)}, bf16[768,384]{1,0:T(8,128)(2,1)S(1)}, u32[]{:S(2)}, u32[]{:S(2)}) collective-permute-start(bf16[768,384]{1,0:T(8,128)(2,1)} %param.23), channel_id=1, source_target_pairs={{0,16},{16,0},{1,17},{17,1},{2,18},{18,2},{3,19},{19,3},{4,20},{20... | collective-permute-start | bytes 1769480 | tf_op jit(solution)/shard_map/ppermute | solution.py:519
  4.8 2.1 collective-permute-start.5
  6.9 2.5 %collective-permute-start.6 = (bf16[1,128,768]{2,1,0:T(8,128)(2,1)S(1)}, bf16[1,128,768]{2,1,0:T(8,128)(2,1)}, u32[]{:S(2)}, u32[]{:S(2)}) collective-permute-start(bf16[1,128,768]{2,1,0:T(8,128)(2,1)S(1)} %get-tuple-element.147), channel_id=1, source_target_pairs={{0,12},{4,8},{8,4},{12,0},{1,13},{5,9},{9,5},{13,1},{2,14},{6,10},... | collective-permute-start | bytes 589832 | tf_op jit(solution)/shard_map/ppermute | solution.py:519
  13.4 1.5 collective-permute-start.9
  15.9 3.7 %collective-permute-done.6 = bf16[1,128,768]{2,1,0:T(8,128)(2,1)} collective-permute-done((bf16[1,128,768]{2,1,0:T(8,128)(2,1)S(1)}, bf16[1,128,768]{2,1,0:T(8,128)(2,1)}, u32[]{:S(2)}, u32[]{:S(2)}) %collective-permute-start.6) | collective-permute-done | bytes 196640 | tf_op jit(solution)/shard_map/ppermute | solution.py:519
  20.6 1.6 collective-permute-start.7
  22.1 12.5 %collective-permute-done.fz = bf16[2,128,768]{2,1,0:T(8,128)(2,1)S(1)} collective-permute-done((bf16[2,128,768]{2,1,0:T(8,128)(2,1)}, bf16[2,128,768]{2,1,0:T(8,128)(2,1)S(1)}, u32[]{:S(2)}, u32[]{:S(2)}) %collective-permute-start) | collective-permute-done | bytes 393248 | tf_op jit(solution)/shard_map/ppermute | solution.py:519
  34.6 1.5 collective-permute-start.1
  36.3 1.1 pad_maximum_fusion.3.down_ref
  38.6 17.3 %shard_map.254 = (bf16[512,768]{1,0:T(8,128)(2,1)}, bf16[512,768]{1,0:T(8,128)(2,1)}, bf16[2,256,768]{2,1,0:T(8,128)(2,1)}, bf16[2,256,768]{2,1,0:T(8,128)(2,1)}...) custom-call(s32[4]{0:T(128)} %pad_add_fusion.at, bf16[2,512,768]{2,1,0:T(8,128)(2,1)} %xb.3, ...), custom_call_target="tpu_custom_call" | custom-call | flops 7247757312 | bytes 16777216 | tf_op jit(solution)/shard_map/pallas_call | solution.py:355
  57.6 1.5 collective-permute-start.11
  59.3 1.3 broadcast_select_fusion.5
  60.6 1.1 pad_maximum_fusion.4.w_ref.refs_8_.refs_5_.refs_11_
  63.5 13.4 %shard_map.255 = (bf16[2048,768]{1,0:T(8,128)(2,1)}, bf16[2048,768]{1,0:T(8,128)(2,1)}, bf16[1024,768]{1,0:T(8,128)(2,1)}, f32[24,2048]{1,0:T(8,128)}, bf16[192,...) custom-call(s32[4]{0:T(128)} %pad_add_fusion.at, ...), custom_call_target="tpu_custom_call" | custom-call | flops 1811939328 | bytes 12582912 | tf_op jit(solution)/shard_map/pallas_call | solution.py:161
  76.9 11.8 %shard_map.256 = (bf16[64,1024]{1,0:T(8,128)(2,1)}, bf16[64,1024]{1,0:T(8,128)(2,1)}, bf16[64,2048]{1,0:T(8,128)(2,1)}, bf16[64,2048]{1,0:T(8,128)(2,1)}) custom-call(bf16[192,1024]{1,0:T(8,128)(2,1)} %get-tuple-element.73.refs_0_.refs_2_.refs_1_, bf16[192,1024]{1,0:T(8,128)(2,1)} %get-tuple-element.74.refs_1_.refs_3_.refs_2_, ...), custom_call_target="tpu_custom_call" | custom-call | flops 5368709120 | bytes 2097152 | tf_op jit(solution)/shard_map/pallas_call | solution.py:259
  89.5 1.4 copy-done.7
  91.4 2.7 %collective-permute-start.18 = (bf16[192,768]{1,0:T(8,128)(2,1)S(1)}, bf16[192,768]{1,0:T(8,128)(2,1)S(1)}, u32[]{:S(2)}, u32[]{:S(2)}) collective-permute-start(bf16[192,768]{1,0:T(8,128)(2,1)S(1)} %get-tuple-element.131), channel_id=1, source_target_pairs={{0,12},{4,8},{8,4},{12,0},{1,13},{5,9},{9,5},{13,1},{2,14},{6,10},... | collective-permute-start | bytes 884744 | tf_op jit(solution)/shard_map/ppermute | solution.py:519
  94.2 1.7 collective-permute-start.20
  95.9 11.9 %shard_map.257 = (bf16[64,1024]{1,0:T(8,128)(2,1)}, bf16[64,1024]{1,0:T(8,128)(2,1)}, bf16[64,2048]{1,0:T(8,128)(2,1)}, bf16[64,2048]{1,0:T(8,128)(2,1)}) custom-call(f32[2,2,128,768]{3,2,1,0:T(8,128)} %bitcast.172, f32[768,768]{1,0:T(8,128)} %copy-done.2, bf16[192,1024]{1,0:T(8,128)(2,1)} %get-tuple-element.73.refs_0_.refs_2_.refs_1_, ...), custom_call_target="tpu_custom_call" | custom-call | flops 5368709120 | bytes 2097152 | tf_op jit(solution)/shard_map/pallas_call | solution.py:259
  108.8 11.7 %shard_map.258 = (bf16[64,1024]{1,0:T(8,128)(2,1)}, bf16[64,1024]{1,0:T(8,128)(2,1)}, bf16[64,2048]{1,0:T(8,128)(2,1)}, bf16[64,2048]{1,0:T(8,128)(2,1)}) custom-call(f32[2,128,768]{2,1,0:T(8,128)} %fusion.11.refs_0_, bf16[192,1024]{1,0:T(8,128)(2,1)} %get-tuple-element.73.refs_0_.refs_2_.refs_1_, ...), custom_call_target="tpu_custom_call" | custom-call | flops 5368709120 | bytes 2097152 | tf_op jit(solution)/shard_map/pallas_call | solution.py:259
  120.5 7.6 %shard_map.259 = (bf16[2,256,768]{2,1,0:T(8,128)(2,1)}, bf16[2,256,768]{2,1,0:T(8,128)(2,1)}, f32[384,768]{1,0:T(8,128)}, f32[8,768]{1,0:T(8,128)}) custom-call(s32[4]{0:T(128)} %pad_add_fusion.at, bf16[64,2048]{1,0:T(8,128)(2,1)} %get-tuple-element.90.refs_0_.refs_3_, bf16[64,2048]{1,0:T(8,128)(2,1)} %get-tuple-element.91.refs_1_.refs_4_, ...), custom_call_target="tpu_custom_call" | custom-call | flops 1207959552 | bytes 10485760 | tf_op jit(solution)/shard_map/pallas_call | solution.py:503
  129.1 5.4 %shard_map.260 = (bf16[2,256,768]{2,1,0:T(8,128)(2,1)}, bf16[2,256,768]{2,1,0:T(8,128)(2,1)}, f32[192,768]{1,0:T(8,128)}) custom-call(bf16[64,1024]{1,0:T(8,128)(2,1)} %get-tuple-element.78.refs_0_, bf16[64,1024]{1,0:T(8,128)(2,1)} %get-tuple-element.85.refs_1_, bf16[64,1024]{1,0:T(8,128)(2,1)} %get-tuple-element.87.refs_2_, ...), custom_call_target="tpu_custom_call" | custom-call | flops 603979776 | bytes 8388608 | tf_op jit(solution)/shard_map/pallas_call | solution.py:409
  135.0 1.3 convert_add_fusion.7
  136.3 1.4 collective-permute-start.38
  137.7 10.2 %shard_map.261 = (bf16[2,256,768]{2,1,0:T(8,128)(2,1)}, bf16[2,256,768]{2,1,0:T(8,128)(2,1)}, f32[832,384]{1,0:T(8,128)}, bf16[832,384]{1,0:T(8,128)(2,1)}) custom-call(s32[4]{0:T(128)} %pad_add_fusion.at, bf16[64,1024]{1,0:T(8,128)(2,1)} %get-tuple-element.102.refs_0_, bf16[64,1024]{1,0:T(8,128)(2,1)} %get-tuple-element.103.refs_1_, ...), custom_call_target="tpu_custom_call" | custom-call | flops 1811939328 | bytes 10485760 | tf_op jit(solution)/shard_map/pallas_call | solution.py:503
  148.0 1.2 collective-permute-start.30
  150.3 1.6 collective-permute-start.14
  152.9 8.5 %collective-permute-done.24 = bf16[2,128,768]{2,1,0:T(8,128)(2,1)S(1)} collective-permute-done((bf16[2,128,768]{2,1,0:T(8,128)(2,1)S(1)}, bf16[2,128,768]{2,1,0:T(8,128)(2,1)S(1)}, u32[]{:S(2)}, u32[]{:S(2)}) %collective-permute-start.24) | collective-permute-done | bytes 393248 | tf_op jit(solution)/shard_map/ppermute | solution.py:519
  161.6 2.0 collective-permute-start.25
  163.5 1.4 collective-permute-done.30
  165.2 1.5 collective-permute-start.31
  166.7 3.2 %collective-permute-done.14 = bf16[2,128,768]{2,1,0:T(8,128)(2,1)S(1)} collective-permute-done((bf16[2,128,768]{2,1,0:T(8,128)(2,1)S(1)}, bf16[2,128,768]{2,1,0:T(8,128)(2,1)S(1)}, u32[]{:S(2)}, u32[]{:S(2)}) %collective-permute-start.14) | collective-permute-done | bytes 393248 | tf_op jit(solution)/shard_map/ppermute | solution.py:519
  169.9 1.6 collective-permute-start.32
  171.6 5.9 %collective-permute-done.22 = bf16[2,128,768]{2,1,0:T(8,128)(2,1)S(1)} collective-permute-done((bf16[2,128,768]{2,1,0:T(8,128)(2,1)S(1)}, bf16[2,128,768]{2,1,0:T(8,128)(2,1)S(1)}, u32[]{:S(2)}, u32[]{:S(2)}) %collective-permute-start.22) | collective-permute-done | bytes 393248 | tf_op jit(solution)/shard_map/ppermute | solution.py:519
  177.5 1.9 collective-permute-start.33
  180.5 2.4 collective-permute-start.27
  184.0 4.5 %collective-permute-done.33 = bf16[208,384]{1,0:T(8,128)(2,1)S(1)} collective-permute-done((bf16[208,384]{1,0:T(8,128)(2,1)S(1)}, bf16[208,384]{1,0:T(8,128)(2,1)S(1)}, u32[]{:S(2)}, u32[]{:S(2)}) %collective-permute-start.33) | collective-permute-done | bytes 159776 | tf_op jit(solution)/shard_map/ppermute | solution.py:519
  188.9 2.6 %collective-permute-start.34 = (bf16[208,384]{1,0:T(8,128)(2,1)S(1)}, bf16[208,384]{1,0:T(8,128)(2,1)S(1)}, u32[]{:S(2)}, u32[]{:S(2)}) collective-permute-start(bf16[208,384]{1,0:T(8,128)(2,1)S(1)} %add_convert_fusion), channel_id=1, source_target_pairs={{0,8},{4,12},{8,0},{12,4},{1,9},{5,13},{9,1},{13,5},{2,10},{6,14},... | collective-permute-start | bytes 479240 | tf_op jit(solution)/shard_map/ppermute | solution.py:519
  191.6 4.3 %collective-permute-done.15 = bf16[128,768]{1,0:T(8,128)(2,1)S(1)} collective-permute-done((bf16[128,768]{1,0:T(8,128)(2,1)S(1)}, bf16[128,768]{1,0:T(8,128)(2,1)S(1)}, u32[]{:S(2)}, u32[]{:S(2)}) %collective-permute-start.15) | collective-permute-done | bytes 196640 | tf_op jit(solution)/shard_map/ppermute | solution.py:519
  195.9 13.5 %collective-permute-done.26 = bf16[128,768]{1,0:T(8,128)(2,1)S(1)} collective-permute-done((bf16[128,768]{1,0:T(8,128)(2,1)S(1)}, bf16[128,768]{1,0:T(8,128)(2,1)S(1)}, u32[]{:S(2)}, u32[]{:S(2)}) %collective-permute-start.26) | collective-permute-done | bytes 196640 | tf_op jit(solution)/shard_map/ppermute | solution.py:519
  211.8 3.0 %collective-permute-done.34 = bf16[208,384]{1,0:T(8,128)(2,1)S(1)} collective-permute-done((bf16[208,384]{1,0:T(8,128)(2,1)S(1)}, bf16[208,384]{1,0:T(8,128)(2,1)S(1)}, u32[]{:S(2)}, u32[]{:S(2)}) %collective-permute-start.34) | collective-permute-done | bytes 159776 | tf_op jit(solution)/shard_map/ppermute | solution.py:519
  217.7 6.2 %collective-permute-done.35 = bf16[2,208,384]{2,1,0:T(8,128)(2,1)S(1)} collective-permute-done((bf16[2,208,384]{2,1,0:T(8,128)(2,1)S(1)}, bf16[2,208,384]{2,1,0:T(8,128)(2,1)S(1)}, u32[]{:S(2)}, u32[]{:S(2)}) %collective-permute-start.35) | collective-permute-done | bytes 319520 | tf_op jit(solution)/shard_map/ppermute | solution.py:519
  226.0 1.4 reshape_squeeze.3
  230.3 1.2 bitcast_select_fusion.2
  236.8 1.2 broadcast_select_fusion.25
  239.6 1.2 copy-done.1
  240.8 2.0 convert_add_fusion
  242.8 2.1 add_add_fusion
  (203 shorter events, 38.8 us)
Async XLA Ops:
  0.7 35.4 %collective-permute-start.3 = (bf16[768,384]{1,0:T(8,128)(2,1)}, bf16[768,384]{1,0:T(8,128)(2,1)S(1)}, u32[]{:S(2)}, u32[]{:S(2)}) collective-permute-start(bf16[768,384]{1,0:T(8,128)(2,1)} %param.23), channel_id=1, source_target_pairs={{0,16},{16,0},{1,17},{17,1},{2,18},{18,2},{3,19},{19,3},{4,20},{20... | collective-permute-start | bytes 1769480 | tf_op jit(solution)/shard_map/ppermute | solution.py:519
  3.7 33.7 %collective-permute-start.2 = (bf16[384,768]{1,0:T(8,128)(2,1)}, bf16[384,768]{1,0:T(8,128)(2,1)S(1)}, u32[]{:S(2)}, u32[]{:S(2)}) collective-permute-start(bf16[384,768]{1,0:T(8,128)(2,1)} %param.21), channel_id=1, source_target_pairs={{0,16},{16,0},{1,17},{17,1},{2,18},{18,2},{3,19},{19,3},{4,20},{20... | collective-permute-start | bytes 1769480 | tf_op jit(solution)/shard_map/ppermute | solution.py:519
  4.8 8.6 %collective-permute-start.5 = (bf16[1,128,768]{2,1,0:T(8,128)(2,1)S(1)}, bf16[1,128,768]{2,1,0:T(8,128)(2,1)}, u32[]{:S(2)}, u32[]{:S(2)}) collective-permute-start(bf16[1,128,768]{2,1,0:T(8,128)(2,1)S(1)} %get-tuple-element.146), channel_id=1, source_target_pairs={{0,4},{4,0},{8,12},{12,8},{1,5},{5,1},{9,13},{13,9},{2,6},{6,2},{1... | collective-permute-start | bytes 589832 | tf_op jit(solution)/shard_map/ppermute | solution.py:519
  6.9 12.7 %collective-permute-start.6 = (bf16[1,128,768]{2,1,0:T(8,128)(2,1)S(1)}, bf16[1,128,768]{2,1,0:T(8,128)(2,1)}, u32[]{:S(2)}, u32[]{:S(2)}) collective-permute-start(bf16[1,128,768]{2,1,0:T(8,128)(2,1)S(1)} %get-tuple-element.147), channel_id=1, source_target_pairs={{0,12},{4,8},{8,4},{12,0},{1,13},{5,9},{9,5},{13,1},{2,14},{6,10},... | collective-permute-start | bytes 589832 | tf_op jit(solution)/shard_map/ppermute | solution.py:519
  10.3 25.8 %copy-start.24 = (bf16[768,384]{1,0:T(8,128)(2,1)S(1)}, bf16[768,384]{1,0:T(8,128)(2,1)}, u32[]{:S(2)}) copy-start(bf16[768,384]{1,0:T(8,128)(2,1)} %param.23) | copy-start | bytes 1769476
  11.1 23.5 %collective-permute-start = (bf16[2,128,768]{2,1,0:T(8,128)(2,1)}, bf16[2,128,768]{2,1,0:T(8,128)(2,1)S(1)}, u32[]{:S(2)}, u32[]{:S(2)}) collective-permute-start(bf16[2,128,768]{2,1,0:T(8,128)(2,1)} %pad_maximum_fusion.13), channel_id=1, source_target_pairs={{0,8},{4,12},{8,0},{12,4},{1,9},{5,13},{9,1},{13,5},{2,10},{6,14},... | collective-permute-start | bytes 1179656 | tf_op jit(solution)/shard_map/ppermute | solution.py:519
  13.4 44.2 %collective-permute-start.9 = (bf16[768,384]{1,0:T(8,128)(2,1)}, bf16[768,384]{1,0:T(8,128)(2,1)S(1)}, u32[]{:S(2)}, u32[]{:S(2)}) collective-permute-start(bf16[768,384]{1,0:T(8,128)(2,1)} %pad_maximum_fusion.11), channel_id=1, source_target_pairs={{0,16},{16,0},{1,17},{17,1},{2,18},{18,2},{3,19},{19,3},{4,20},{20... | collective-permute-start | bytes 1769480 | tf_op jit(solution)/shard_map/ppermute | solution.py:519
  20.6 35.4 %copy-start.6 = (bf16[2,128,768]{2,1,0:T(8,128)(2,1)}, bf16[2,128,768]{2,1,0:T(8,128)(2,1)S(1)}, u32[]{:S(2)}) copy-start(bf16[2,128,768]{2,1,0:T(8,128)(2,1)S(1)} %constant_dynamic-update-slice_fusion.nz) | copy-start | bytes 1179652
  20.6 35.4 %collective-permute-start.7 = (bf16[2,128,768]{2,1,0:T(8,128)(2,1)S(1)}, bf16[2,128,768]{2,1,0:T(8,128)(2,1)S(1)}, u32[]{:S(2)}, u32[]{:S(2)}) collective-permute-start(bf16[2,128,768]{2,1,0:T(8,128)(2,1)S(1)} %constant_dynamic-update-slice_fusion.nz), channel_id=1, source_target_pairs={{0,2},{1,3},{2,0},{3,1},{4,6},{5,7},{6,4},{7,5},{8,10},{9,11},{10,... | collective-permute-start | bytes 1179656 | tf_op jit(solution)/shard_map/ppermute | solution.py:519
  34.6 21.6 %copy-start.9 = (bf16[2,128,768]{2,1,0:T(8,128)(2,1)}, bf16[2,128,768]{2,1,0:T(8,128)(2,1)S(1)}, u32[]{:S(2)}) copy-start(bf16[2,128,768]{2,1,0:T(8,128)(2,1)S(1)} %collective-permute-done.fz) | copy-start | bytes 1179652
  34.6 21.5 %collective-permute-start.1 = (bf16[2,128,768]{2,1,0:T(8,128)(2,1)S(1)}, bf16[2,128,768]{2,1,0:T(8,128)(2,1)S(1)}, u32[]{:S(2)}, u32[]{:S(2)}) collective-permute-start(bf16[2,128,768]{2,1,0:T(8,128)(2,1)S(1)} %collective-permute-done.fz), channel_id=1, source_target_pairs={{0,2},{1,3},{2,0},{3,1},{4,6},{5,7},{6,4},{7,5},{8,10},{9,11},{10,... | collective-permute-start | bytes 1179656 | tf_op jit(solution)/shard_map/ppermute | solution.py:519
  56.1 5.7 %collective-permute-start.8 = (bf16[2,2,128,768]{3,2,1,0:T(8,128)(2,1)S(1)}, bf16[2,2,128,768]{3,2,1,0:T(8,128)(2,1)S(1)}, u32[]{:S(2)}, u32[]{:S(2)}) collective-permute-start(bf16[2,2,128,768]{3,2,1,0:T(8,128)(2,1)S(1)} %pad_maximum_fusion.7), channel_id=1, source_target_pairs={{0,1},{1,0},{2,3},{3,2},{4,5},{5,4},{6,7},{7,6},{8,9},{9,8},{10,11... | collective-permute-start | bytes 2359304 | tf_op jit(solution)/shard_map/ppermute | solution.py:519
  56.8 5.0 %collective-permute-start.4 = (bf16[2,2,128,768]{3,2,1,0:T(8,128)(2,1)S(1)}, bf16[2,2,128,768]{3,2,1,0:T(8,128)(2,1)S(1)}, u32[]{:S(2)}, u32[]{:S(2)}) collective-permute-start(bf16[2,2,128,768]{3,2,1,0:T(8,128)(2,1)S(1)} %pad_maximum_fusion.6), channel_id=1, source_target_pairs={{0,1},{1,0},{2,3},{3,2},{4,5},{5,4},{6,7},{7,6},{8,9},{9,8},{10,11... | collective-permute-start | bytes 2359304 | tf_op jit(solution)/shard_map/ppermute | solution.py:519
  57.6 31.9 %collective-permute-start.11 = (bf16[768,768]{1,0:T(8,128)(2,1)}, bf16[768,768]{1,0:T(8,128)(2,1)S(1)}, u32[]{:S(2)}, u32[]{:S(2)}) collective-permute-start(bf16[768,768]{1,0:T(8,128)(2,1)} %get-tuple-element.83), channel_id=1, source_target_pairs={{0,16},{16,0},{1,17},{17,1},{2,18},{18,2},{3,19},{19,3},{4,20},{20... | collective-permute-start | bytes 3538952 | tf_op jit(solution)/shard_map/ppermute | solution.py:519
  59.1 29.5 %collective-permute-start.10 = (bf16[2,256,768]{2,1,0:T(8,128)(2,1)}, bf16[2,256,768]{2,1,0:T(8,128)(2,1)S(1)}, u32[]{:S(2)}, u32[]{:S(2)}) collective-permute-start(bf16[2,256,768]{2,1,0:T(8,128)(2,1)} %get-tuple-element.80), channel_id=1, source_target_pairs={{0,1},{1,0},{2,3},{3,2},{4,5},{5,4},{6,7},{7,6},{8,9},{9,8},{10,11... | collective-permute-start | bytes 2359304 | tf_op jit(solution)/shard_map/ppermute | solution.py:519
  88.9 18.8 %collective-permute-start.12 = (bf16[2,128,768]{2,1,0:T(8,128)(2,1)S(1)}, bf16[2,128,768]{2,1,0:T(8,128)(2,1)S(1)}, u32[]{:S(2)}, u32[]{:S(2)}) collective-permute-start(bf16[2,128,768]{2,1,0:T(8,128)(2,1)S(1)} %fusion.16), channel_id=1, source_target_pairs={{0,2},{1,3},{2,0},{3,1},{4,6},{5,7},{6,4},{7,5},{8,10},{9,11},{10,... | collective-permute-start | bytes 1179656 | tf_op jit(solution)/shard_map/ppermute | solution.py:519
  91.4 43.6 %collective-permute-start.18 = (bf16[192,768]{1,0:T(8,128)(2,1)S(1)}, bf16[192,768]{1,0:T(8,128)(2,1)S(1)}, u32[]{:S(2)}, u32[]{:S(2)}) collective-permute-start(bf16[192,768]{1,0:T(8,128)(2,1)S(1)} %get-tuple-element.131), channel_id=1, source_target_pairs={{0,12},{4,8},{8,4},{12,0},{1,13},{5,9},{9,5},{13,1},{2,14},{6,10},... | collective-permute-start | bytes 884744 | tf_op jit(solution)/shard_map/ppermute | solution.py:519
  94.1 40.9 %collective-permute-start.19 = (bf16[192,768]{1,0:T(8,128)(2,1)S(1)}, bf16[192,768]{1,0:T(8,128)(2,1)S(1)}, u32[]{:S(2)}, u32[]{:S(2)}) collective-permute-start(bf16[192,768]{1,0:T(8,128)(2,1)S(1)} %get-tuple-element.133), channel_id=1, source_target_pairs={{0,8},{4,12},{8,0},{12,4},{1,9},{5,13},{9,1},{13,5},{2,10},{6,14},... | collective-permute-start | bytes 884744 | tf_op jit(solution)/shard_map/ppermute | solution.py:519
  94.2 13.6 %copy-start.4 = (f32[2,256,768]{2,1,0:T(8,128)S(1)}, f32[2,256,768]{2,1,0:T(8,128)}, u32[]{:S(2)}) copy-start(f32[2,256,768]{2,1,0:T(8,128)} %copy-done.3) | copy-start | bytes 4718596
  94.2 40.9 %collective-permute-start.20 = (bf16[192,768]{1,0:T(8,128)(2,1)S(1)}, bf16[192,768]{1,0:T(8,128)(2,1)}, u32[]{:S(2)}, u32[]{:S(2)}) collective-permute-start(bf16[192,768]{1,0:T(8,128)(2,1)S(1)} %get-tuple-element.132), channel_id=1, source_target_pairs={{0,4},{4,0},{8,12},{12,8},{1,5},{5,1},{9,13},{13,9},{2,6},{6,2},{1... | collective-permute-start | bytes 884744 | tf_op jit(solution)/shard_map/ppermute | solution.py:519
  128.1 21.1 %collective-permute-start.23 = (bf16[2,256,768]{2,1,0:T(8,128)(2,1)}, bf16[2,256,768]{2,1,0:T(8,128)(2,1)S(1)}, u32[]{:S(2)}, u32[]{:S(2)}) collective-permute-start(bf16[2,256,768]{2,1,0:T(8,128)(2,1)} %get-tuple-element.115), channel_id=1, source_target_pairs={{0,1},{1,0},{2,3},{3,2},{4,5},{5,4},{6,7},{7,6},{8,9},{9,8},{10,11... | collective-permute-start | bytes 2359304 | tf_op jit(solution)/shard_map/ppermute | solution.py:519
  129.1 87.6 %copy-start.29 = (f32[2,128]{1,0:T(2,128)}, f32[2,128]{1,0:T(2,128)S(1)}, u32[]{:S(2)}) copy-start(f32[2,128]{1,0:T(2,128)S(1)} %add_rsqrt_fusion) | copy-start | bytes 3076
  134.5 15.6 %collective-permute-start.13 = (bf16[2,256,768]{2,1,0:T(8,128)(2,1)}, bf16[2,256,768]{2,1,0:T(8,128)(2,1)S(1)}, u32[]{:S(2)}, u32[]{:S(2)}) collective-permute-start(bf16[2,256,768]{2,1,0:T(8,128)(2,1)} %get-tuple-element.101), channel_id=1, source_target_pairs={{0,1},{1,0},{2,3},{3,2},{4,5},{5,4},{6,7},{7,6},{8,9},{9,8},{10,11... | collective-permute-start | bytes 2359304 | tf_op jit(solution)/shard_map/ppermute | solution.py:519
  136.3 43.2 %collective-permute-start.38 = (bf16[192,768]{1,0:T(8,128)(2,1)S(1)}, bf16[192,768]{1,0:T(8,128)(2,1)S(1)}, u32[]{:S(2)}, u32[]{:S(2)}) collective-permute-start(bf16[192,768]{1,0:T(8,128)(2,1)S(1)} %convert_add_fusion.7), channel_id=1, source_target_pairs={{0,8},{4,12},{8,0},{12,4},{1,9},{5,13},{9,1},{13,5},{2,10},{6,14},... | collective-permute-start | bytes 884744 | tf_op jit(solution)/shard_map/ppermute | solution.py:519
  147.9 3.9 %collective-permute-start.21 = (bf16[2,256,768]{2,1,0:T(8,128)(2,1)}, bf16[2,256,768]{2,1,0:T(8,128)(2,1)S(1)}, u32[]{:S(2)}, u32[]{:S(2)}) collective-permute-start(bf16[2,256,768]{2,1,0:T(8,128)(2,1)} %get-tuple-element.114), channel_id=1, source_target_pairs={{0,1},{1,0},{2,3},{3,2},{4,5},{5,4},{6,7},{7,6},{8,9},{9,8},{10,11... | collective-permute-start | bytes 2359304 | tf_op jit(solution)/shard_map/ppermute | solution.py:519
  148.0 17.0 %collective-permute-start.30 = (bf16[832,384]{1,0:T(8,128)(2,1)}, bf16[832,384]{1,0:T(8,128)(2,1)S(1)}, u32[]{:S(2)}, u32[]{:S(2)}) collective-permute-start(bf16[832,384]{1,0:T(8,128)(2,1)} %get-tuple-element.117), channel_id=1, source_target_pairs={{0,16},{16,0},{1,17},{17,1},{2,18},{18,2},{3,19},{19,3},{4,20},{20... | collective-permute-start | bytes 1916936 | tf_op jit(solution)/shard_map/ppermute | solution.py:519
  149.4 12.0 %collective-permute-start.24 = (bf16[2,128,768]{2,1,0:T(8,128)(2,1)S(1)}, bf16[2,128,768]{2,1,0:T(8,128)(2,1)S(1)}, u32[]{:S(2)}, u32[]{:S(2)}) collective-permute-start(bf16[2,128,768]{2,1,0:T(8,128)(2,1)S(1)} %fusion.19), channel_id=1, source_target_pairs={{0,2},{1,3},{2,0},{3,1},{4,6},{5,7},{6,4},{7,5},{8,10},{9,11},{10,... | collective-permute-start | bytes 1179656 | tf_op jit(solution)/shard_map/ppermute | solution.py:519
  150.3 19.6 %collective-permute-start.14 = (bf16[2,128,768]{2,1,0:T(8,128)(2,1)S(1)}, bf16[2,128,768]{2,1,0:T(8,128)(2,1)S(1)}, u32[]{:S(2)}, u32[]{:S(2)}) collective-permute-start(bf16[2,128,768]{2,1,0:T(8,128)(2,1)S(1)} %fusion.17), channel_id=1, source_target_pairs={{0,2},{1,3},{2,0},{3,1},{4,6},{5,7},{6,4},{7,5},{8,10},{9,11},{10,... | collective-permute-start | bytes 1179656 | tf_op jit(solution)/shard_map/ppermute | solution.py:519
  152.0 13.0 %copy-start.13 = (f32[832,384]{1,0:T(8,128)S(1)}, f32[832,384]{1,0:T(8,128)}, u32[]{:S(2)}) copy-start(f32[832,384]{1,0:T(8,128)} %get-tuple-element.116) | copy-start | bytes 3833860
  152.1 25.4 %collective-permute-start.22 = (bf16[2,128,768]{2,1,0:T(8,128)(2,1)S(1)}, bf16[2,128,768]{2,1,0:T(8,128)(2,1)S(1)}, u32[]{:S(2)}, u32[]{:S(2)}) collective-permute-start(bf16[2,128,768]{2,1,0:T(8,128)(2,1)S(1)} %fusion.18), channel_id=1, source_target_pairs={{0,2},{1,3},{2,0},{3,1},{4,6},{5,7},{6,4},{7,5},{8,10},{9,11},{10,... | collective-permute-start | bytes 1179656 | tf_op jit(solution)/shard_map/ppermute | solution.py:519
  161.6 27.3 %collective-permute-start.25 = (bf16[128,768]{1,0:T(8,128)(2,1)S(1)}, bf16[128,768]{1,0:T(8,128)(2,1)S(1)}, u32[]{:S(2)}, u32[]{:S(2)}) collective-permute-start(bf16[128,768]{1,0:T(8,128)(2,1)S(1)} %get-tuple-element.177), channel_id=1, source_target_pairs={{0,4},{4,0},{8,12},{12,8},{1,5},{5,1},{9,13},{13,9},{2,6},{6,2},{1... | collective-permute-start | bytes 589832 | tf_op jit(solution)/shard_map/ppermute | solution.py:519
  165.2 15.3 %collective-permute-start.31 = (bf16[208,384]{1,0:T(8,128)(2,1)S(1)}, bf16[208,384]{1,0:T(8,128)(2,1)S(1)}, u32[]{:S(2)}, u32[]{:S(2)}) collective-permute-start(bf16[208,384]{1,0:T(8,128)(2,1)S(1)} %get-tuple-element.148), channel_id=1, source_target_pairs={{0,12},{4,8},{8,4},{12,0},{1,13},{5,9},{9,5},{13,1},{2,14},{6,10},... | collective-permute-start | bytes 479240 | tf_op jit(solution)/shard_map/ppermute | solution.py:519
  169.9 13.9 %collective-permute-start.32 = (bf16[208,384]{1,0:T(8,128)(2,1)S(1)}, bf16[208,384]{1,0:T(8,128)(2,1)S(1)}, u32[]{:S(2)}, u32[]{:S(2)}) collective-permute-start(bf16[208,384]{1,0:T(8,128)(2,1)S(1)} %get-tuple-element.150), channel_id=1, source_target_pairs={{0,8},{4,12},{8,0},{12,4},{1,9},{5,13},{9,1},{13,5},{2,10},{6,14},... | collective-permute-start | bytes 479240 | tf_op jit(solution)/shard_map/ppermute | solution.py:519
  177.5 10.9 %collective-permute-start.33 = (bf16[208,384]{1,0:T(8,128)(2,1)S(1)}, bf16[208,384]{1,0:T(8,128)(2,1)S(1)}, u32[]{:S(2)}, u32[]{:S(2)}) collective-permute-start(bf16[208,384]{1,0:T(8,128)(2,1)S(1)} %get-tuple-element.149), channel_id=1, source_target_pairs={{0,4},{4,0},{8,12},{12,8},{1,5},{5,1},{9,13},{13,9},{2,6},{6,2},{1... | collective-permute-start | bytes 479240 | tf_op jit(solution)/shard_map/ppermute | solution.py:519
  179.5 12.1 %copy-start.14 = (bf16[192,768]{1,0:T(8,128)(2,1)}, bf16[192,768]{1,0:T(8,128)(2,1)S(1)}, u32[]{:S(2)}) copy-start(bf16[192,768]{1,0:T(8,128)(2,1)S(1)} %collective-permute-done.38) | copy-start | bytes 884740
  179.6 16.3 %collective-permute-start.15 = (bf16[128,768]{1,0:T(8,128)(2,1)S(1)}, bf16[128,768]{1,0:T(8,128)(2,1)S(1)}, u32[]{:S(2)}, u32[]{:S(2)}) collective-permute-start(bf16[128,768]{1,0:T(8,128)(2,1)S(1)} %get-tuple-element.180), channel_id=1, source_target_pairs={{0,8},{4,12},{8,0},{12,4},{1,9},{5,13},{9,1},{13,5},{2,10},{6,14},... | collective-permute-start | bytes 589832 | tf_op jit(solution)/shard_map/ppermute | solution.py:519
  179.7 29.7 %copy-start.5 = (f32[2,128,768]{2,1,0:T(8,128)S(1)}, f32[2,128,768]{2,1,0:T(8,128)}, u32[]{:S(2)}) copy-start(f32[2,128,768]{2,1,0:T(8,128)} %fusion.11.refs_0_) | copy-start | bytes 2359300
  180.5 15.4 %collective-permute-start.27 = (bf16[128,768]{1,0:T(8,128)(2,1)S(1)}, bf16[128,768]{1,0:T(8,128)(2,1)S(1)}, u32[]{:S(2)}, u32[]{:S(2)}) collective-permute-start(bf16[128,768]{1,0:T(8,128)(2,1)S(1)} %get-tuple-element.178), channel_id=1, source_target_pairs={{0,12},{4,8},{8,4},{12,0},{1,13},{5,9},{9,5},{13,1},{2,14},{6,10},... | collective-permute-start | bytes 589832 | tf_op jit(solution)/shard_map/ppermute | solution.py:519
  183.7 46.5 %collective-permute-start.39 = (bf16[2,192,768]{2,1,0:T(8,128)(2,1)}, bf16[2,192,768]{2,1,0:T(8,128)(2,1)}, u32[]{:S(2)}, u32[]{:S(2)}) collective-permute-start(bf16[2,192,768]{2,1,0:T(8,128)(2,1)} %pad_maximum_fusion.12), channel_id=1, source_target_pairs={{0,4},{4,0},{8,12},{12,8},{1,5},{5,1},{9,13},{13,9},{2,6},{6,2},{1... | collective-permute-start | bytes 1769480 | tf_op jit(solution)/shard_map/ppermute | solution.py:519
  188.4 20.9 %collective-permute-start.26 = (bf16[128,768]{1,0:T(8,128)(2,1)S(1)}, bf16[128,768]{1,0:T(8,128)(2,1)S(1)}, u32[]{:S(2)}, u32[]{:S(2)}) collective-permute-start(bf16[128,768]{1,0:T(8,128)(2,1)S(1)} %fusion.27), channel_id=1, source_target_pairs={{0,8},{4,12},{8,0},{12,4},{1,9},{5,13},{9,1},{13,5},{2,10},{6,14},... | collective-permute-start | bytes 589832 | tf_op jit(solution)/shard_map/ppermute | solution.py:519
  188.9 25.9 %collective-permute-start.34 = (bf16[208,384]{1,0:T(8,128)(2,1)S(1)}, bf16[208,384]{1,0:T(8,128)(2,1)S(1)}, u32[]{:S(2)}, u32[]{:S(2)}) collective-permute-start(bf16[208,384]{1,0:T(8,128)(2,1)S(1)} %add_convert_fusion), channel_id=1, source_target_pairs={{0,8},{4,12},{8,0},{12,4},{1,9},{5,13},{9,1},{13,5},{2,10},{6,14},... | collective-permute-start | bytes 479240 | tf_op jit(solution)/shard_map/ppermute | solution.py:519
  211.2 20.3 %collective-permute-start.16 = (bf16[2,128,768]{2,1,0:T(8,128)(2,1)}, bf16[2,128,768]{2,1,0:T(8,128)(2,1)}, u32[]{:S(2)}, u32[]{:S(2)}) collective-permute-start(bf16[2,128,768]{2,1,0:T(8,128)(2,1)} %pad_maximum_fusion.15), channel_id=1, source_target_pairs={{0,2},{1,3},{2,0},{3,1},{4,6},{5,7},{6,4},{7,5},{8,10},{9,11},{10,... | collective-permute-start | bytes 1179656 | tf_op jit(solution)/shard_map/ppermute | solution.py:519
  214.9 9.0 %collective-permute-start.35 = (bf16[2,208,384]{2,1,0:T(8,128)(2,1)S(1)}, bf16[2,208,384]{2,1,0:T(8,128)(2,1)S(1)}, u32[]{:S(2)}, u32[]{:S(2)}) collective-permute-start(bf16[2,208,384]{2,1,0:T(8,128)(2,1)S(1)} %pad_maximum_fusion.17), channel_id=1, source_target_pairs={{0,4},{4,0},{8,12},{12,8},{1,5},{5,1},{9,13},{13,9},{2,6},{6,2},{1... | collective-permute-start | bytes 958472 | tf_op jit(solution)/shard_map/ppermute | solution.py:519
  215.9 17.0 %collective-permute-start.28 = (bf16[2,128,768]{2,1,0:T(8,128)(2,1)}, bf16[2,128,768]{2,1,0:T(8,128)(2,1)S(1)}, u32[]{:S(2)}, u32[]{:S(2)}) collective-permute-start(bf16[2,128,768]{2,1,0:T(8,128)(2,1)} %fusion.6), channel_id=1, source_target_pairs={{0,2},{1,3},{2,0},{3,1},{4,6},{5,7},{6,4},{7,5},{8,10},{9,11},{10,... | collective-permute-start | bytes 1179656 | tf_op jit(solution)/shard_map/ppermute | solution.py:519
  224.6 4.4 %collective-permute-start.36 = (f32[8,768]{1,0:T(8,128)}, f32[8,768]{1,0:T(8,128)}, u32[]{:S(2)}, u32[]{:S(2)}) collective-permute-start(f32[8,768]{1,0:T(8,128)} %pad_maximum_fusion.18), channel_id=1, source_target_pairs={{0,1},{1,0},{2,3},{3,2},{4,5},{5,4},{6,7},{7,6},{8,9},{9,8},{10,11... | collective-permute-start | bytes 73736 | tf_op jit(solution)/shard_map/ppermute | solution.py:519
  229.7 6.4 %collective-permute-start.37 = (f32[8,768]{1,0:T(8,128)S(1)}, f32[8,768]{1,0:T(8,128)S(1)}, u32[]{:S(2)}, u32[]{:S(2)}) collective-permute-start(f32[8,768]{1,0:T(8,128)S(1)} %fusion.35), channel_id=1, source_target_pairs={{0,2},{1,3},{2,0},{3,1},{4,6},{5,7},{6,4},{7,5},{8,10},{9,11},{10,... | collective-permute-start | bytes 73736 | tf_op jit(solution)/shard_map/ppermute | solution.py:519
  232.6 4.2 %collective-permute-start.17 = (bf16[2,2,128,768]{3,2,1,0:T(8,128)(2,1)S(1)}, bf16[2,2,128,768]{3,2,1,0:T(8,128)(2,1)S(1)}, u32[]{:S(2)}, u32[]{:S(2)}) collective-permute-start(bf16[2,2,128,768]{3,2,1,0:T(8,128)(2,1)S(1)} %pad_maximum_fusion.8), channel_id=1, source_target_pairs={{0,1},{1,0},{2,3},{3,2},{4,5},{5,4},{6,7},{7,6},{8,9},{9,8},{10,11... | collective-permute-start | bytes 2359304 | tf_op jit(solution)/shard_map/ppermute | solution.py:519
  233.7 4.4 %collective-permute-start.29 = (bf16[2,2,128,768]{3,2,1,0:T(8,128)(2,1)S(1)}, bf16[2,2,128,768]{3,2,1,0:T(8,128)(2,1)S(1)}, u32[]{:S(2)}, u32[]{:S(2)}) collective-permute-start(bf16[2,2,128,768]{3,2,1,0:T(8,128)(2,1)S(1)} %pad_maximum_fusion.10), channel_id=1, source_target_pairs={{0,1},{1,0},{2,3},{3,2},{4,5},{5,4},{6,7},{7,6},{8,9},{9,8},{10,11... | collective-permute-start | bytes 2359304 | tf_op jit(solution)/shard_map/ppermute | solution.py:519
  (32 other events, 131.8 us)

commit v6 on v5

--- a/solution.py
+++ b/solution.py
@@ -172,7 +172,7 @@
         out_shape=[low_shape(rows, width)] * 2
         + [low_shape(rows // 2, width), shape(tall, rows)]
         + [low_shape(wide, rows)] * 2 + [low_shape(wide, rows // 2)] * 2,
-        compiler_params=params(56),
+        compiler_params=params(20),
         cost_estimate=cost(6 * rows * width * wide, 8 * rows * width),
     )(at, x, x, g, g, *received, trig, trig, *fixed)
 
@@ -274,7 +274,7 @@
             pltpu.VMEM((length, lanes), F32),
             pltpu.VMEM((length, lanes), F32),
         ],
-        compiler_params=params(56),
+        compiler_params=params(16),
         cost_estimate=cost(40 * rows * length * HEAD, 16 * HEAD * length, rows * length),
     )(*after, qt, dot, kt, vt, trig, trig)
 
@@ -367,7 +367,7 @@
         ),
         out_shape=[low_shape(2 * STEP, width)] * 2 + [low_shape(2, STEP, width)] * 2
         + [shape(8, width)] + parts,
-        compiler_params=params(56),
+        compiler_params=params(28),
         cost_estimate=cost(48 * STEP * width * hidden, 16 * MIB, 8 * STEP * hidden),
     )(at, x, x, g, g, up, bias, down, scale, offset)
 
@@ -414,7 +414,7 @@
            pl.BlockSpec((wide, width), lambda i: (3, 0))],
         out_specs=[slots, slots, pl.BlockSpec((wide, width), lambda i: (0, 0))],
         out_shape=[low_shape(2, STEP, width)] * 2 + [shape(wide, width)],
-        compiler_params=params(56),
+        compiler_params=params(12),
         cost_estimate=cost(4 * rows * width * wide, 8 * MIB),
     )(*o, g, ff, weights)
 
@@ -510,7 +510,7 @@
             scratch_shapes=scratch,
         ),
         out_shape=[low_shape(2, STEP, width)] * 2 + parts,
-        compiler_params=params(56),
+        compiler_params=params(20),
         cost_estimate=cost(4 * rows * width * tall, 10 * MIB),
     )(at, *[v for vs in grads for v in vs], n1, xhat, weights, scale, *extra)
 
@@ -564,15 +564,18 @@
     return total
 
 
-def double(v, c, first=(), second=()):
+def pair_up(v, *earlier):
     v = v.astype(BF16)
-    pair = jnp.stack([v, tie(swap(v, "ctx", 4, 2), *first)])
-    others = tie(swap(pair, "ctx", 4, 1), *second)
+    return jnp.stack([v, tie(swap(v, "ctx", 4, 2), *earlier)])
+
+
+def double(pair, c, *earlier):
+    others = tie(swap(pair, "ctx", 4, 1), *earlier)
     return by_xor([pair[0], pair[1], others[0], others[1]], 2 * (c % 2) + c // 2)
 
 
 def sum_over_ctx(v, c):
-    return double(quarter_sum(v, c), c)
+    return double(pair_up(quarter_sum(v, c)), c)
 
 
 def butterfly(v, axis_name, size):
@@ -677,23 +680,23 @@
         per_head.append(attention(h, after, qt, dot, kt, vt, trig))
     o, dq, dk, dv = zip(*per_head)
     ff_quarter = quarter_sum(ff_rest, c, o[-1]) if split else small_ff
+    keep_b, send_b, out_part = branch(o, g, ff, weights)
     keep_o, send_o, mix_other, small_other = back(
-        False, split, at, (dk, dv), n1, xhat_all, weights, first_scale, ()
-    )
-    keep_b, send_b, out_part = branch(o, g, tie(ff, keep_o), weights)
+        False, split, at, (dk, dv), n1, xhat_all, weights, tie(first_scale, keep_b), ()
+    )
+    half_b = over_core(keep_b, send_b)
     keep_w, send_w, late_first, late_second = back(
-        True, split, at, (dq, dk, dv), n1, xhat_all, weights, tie(first_scale, ff_quarter),
-        (a2, small_ff, small_other, mix_other, out_part),
+        True, split, at, (dq, dk, dv), n1, xhat_all, weights,
+        tie(first_scale, ff_quarter, half_b), (a2, small_ff, small_other, mix_other, out_part),
     )
     half_o = over_core(keep_o, send_o)
-    half_b = over_core(keep_b, send_b)
     half_w = over_core(keep_w, send_w)
-
-    def over_ctx(v, distance):
-        return swap(v.astype(BF16), "ctx", 4, distance).astype(F32)
-
-    def gather_tp(mine, theirs):
-        ours = jnp.stack([mine, theirs]).astype(BF16)
+    ff_pair = pair_up(ff_quarter, half_w) if split else half_w
+
+    def over_ctx(v, distance, *earlier):
+        return tie(swap(v.astype(BF16), "ctx", 4, distance), *earlier).astype(F32)
+
+    def gather_tp(ours):
         pair = jnp.stack([ours, swap(ours, "tp", 4, 2)])
         core = swap(pair, "tp", 4, 1)
         pieces = by_xor((pair[0], core[0], pair[1], core[1]), t)
@@ -701,35 +704,35 @@
         return jnp.stack([jnp.where(s == 0, pieces[0], pieces[1]),
                           jnp.where(s == 0, pieces[1], pieces[0])]).astype(F32)
 
-    sums_b = over_x(half_b)
-    block_out = gather_tp(sums_b[0], over_ctx(sums_b[1], 2) + early[0])
+    sums_b = over_x(half_b, half_w)
+    branches = jnp.stack([sums_b[0], over_ctx(sums_b[1], 2) + early[0]]).astype(BF16)
+    block_out = gather_tp(branches)
     block_out = (
         inputs.astype(F32) + block_out + (attention_output_bias + down_projection_bias)
     )
 
-    sums_o = over_x(half_o)
+    sums_o = over_x(half_o, ff_pair)
     sums_w = over_x(half_w)
-    a = jnp.stack([
-        sums_w[0] + over_ctx(sums_o[0], 1),
-        over_ctx(sums_w[1], 2) + over_ctx(sums_o[1], 3) + early[1],
-    ])
+    sums_w = sums_w + over_ctx(sums_o, 1)
+    a = jnp.stack([sums_w[0], over_ctx(sums_w[1], 2, branches) + early[1]])
     xhat, inv = xhat_of(jnp.concatenate([x_mine, x_theirs], axis=0).astype(F32))
     norm_grad = inv * (
         a
         - jnp.mean(a, axis=-1, keepdims=True)
         - xhat * jnp.mean(a * xhat, axis=-1, keepdims=True)
     )
-    inputs_grad = cotangent.astype(F32) + gather_tp(norm_grad[0], norm_grad[1])
+    norm_grad = norm_grad.astype(BF16)
+    inputs_grad = cotangent.astype(F32) + gather_tp(norm_grad)
 
     if split:
-        q = double(ff_quarter, c, (sums_w,), (norm_grad,))
+        q = double(ff_pair, c, norm_grad)
         up_total = jnp.concatenate(q[:2], axis=0).astype(F32)
         down_total = jnp.concatenate(q[2:], axis=0).astype(F32)
         down_total = jnp.concatenate(
             [down_total[:, : width // 2], down_total[:, width // 2 :]], axis=0
         )
         late = late_first + tie(swap(late_second, "fsdp", 2, 1), sums_o).astype(F32)
-        late = double(quarter_sum(late, c, sums_w), c)
+        late = double(pair_up(quarter_sum(late, c, sums_w), norm_grad), c)
         late = jnp.concatenate(late, axis=0).astype(F32)
         small = jnp.concatenate([late[4 * local : 4 * local + 8], late[4 * local + 8 :][:8]], axis=1)
     else:

time: 246 us -> 242 us (0.984)
  Pallas kernels: 89.2 us -> 65.4 us
  waiting for transfers between devices: 67.6 us -> 90.6 us
  local copies, waits for them, and re-layouts: 13.5 us -> 19.2 us
  other arithmetic: 33.1 us -> 28.1 us
  starting transfers between devices: 40.7 us -> 35.8 us
    ppermute x40 -> x39, waiting for transfers between devices: 67.6 us -> 90.6 us  [swap(): return lax.ppermute(v, axis, [(i, i ^ distance) for i in range(size)])]
    pallas_call x2, Pallas kernels: 17.8 us -> 11 us  [back(): pl.pallas_call(functools.partial(back_kernel, own, split, heads), grid_sp...]
    pallas_call x3, Pallas kernels: 35.3 us -> 29.2 us  [attention(): pl.pallas_call(functools.partial(attention_kernel, len(after)), grid=(row...]
    ppermute x40 -> x39, starting transfers between devices: 40.7 us -> 35.8 us  [swap(): return lax.ppermute(v, axis, [(i, i ^ distance) for i in range(size)])]
    pallas_call x1, Pallas kernels: 17.3 us -> 12.7 us  [feed_forward(): pl.pallas_call(functools.partial(forward_kernel, split), grid_spec=pltpu....]
    unnamed x82 -> x136, local copies, waits for them, and re-layouts: 7.74 us -> 12.4 us
    pallas_call x1, Pallas kernels: 13.4 us -> 9.13 us  [project(): pl.pallas_call(project_kernel, grid_spec=pltpu.PrefetchScalarGridSpec(num...]
    concatenate x3, other arithmetic: 3.31 us -> 0.27 us  [gather_halves(): jnp.concatenate([jnp.where(first, shard, other), jnp.where(first, other,...]
  transfers between devices with their start and end apart: 40 -> 39, of which waited for: 12 -> 13; matrix products, arithmetic and copies ran while one was open for 14% -> 12% of each run, Pallas kernels for 36% -> 22%
where the time goes in v6:
time: 242 us; the launch traced here: 241 us
  waiting for transfers between devices  90.6 us (37%)
  Pallas kernels  65.4 us (27%)
  starting transfers between devices  35.8 us (15%)
  other arithmetic  28.1 us (12%)
  local copies, waits for them, and re-layouts  19.2 us (8%)
    ppermute x39, waiting for transfers between devices, swap(): return lax.ppermute(v, axis, [(i, i ^ distance) for i in range(size)])  90.6 us
    ppermute x39, starting transfers between devices, swap(): return lax.ppermute(v, axis, [(i, i ^ distance) for i in range(size)])  35.8 us
    pallas_call x3, Pallas kernels, attention(): pl.pallas_call(functools.partial(attention_kernel, len(after)), grid=(row...  29.2 us
    pallas_call x1, Pallas kernels, feed_forward(): pl.pallas_call(functools.partial(forward_kernel, split), grid_spec=pltpu....  12.7 us
    unnamed x136, local copies, waits for them, and re-layouts  12.4 us
    pallas_call x2, Pallas kernels, back(): pl.pallas_call(functools.partial(back_kernel, own, split, heads), grid_sp...  11 us
    pallas_call x1, Pallas kernels, project(): pl.pallas_call(project_kernel, grid_spec=pltpu.PrefetchScalarGridSpec(num...  9.13 us
  transfers between devices with their start and end apart: 39, of which 13 were waited for; matrix products, arithmetic and copies ran while one was open for 12% of the time, Pallas kernels for 22%

profile of v6, /device:TPU:0, one launch (start us, length us, event | category | flops | bytes accessed | tf_op | source)
XLA Modules:
  0.0 241.0 jit_solution(4559462747353863077)
XLA Ops:
  1.8 3.1 %collective-permute-start.5 = (bf16[1,128,768]{2,1,0:T(8,128)(2,1)S(1)}, bf16[1,128,768]{2,1,0:T(8,128)(2,1)S(1)}, u32[]{:S(2)}, u32[]{:S(2)}) collective-permute-start(bf16[1,128,768]{2,1,0:T(8,128)(2,1)S(1)} %get-tuple-element.154), channel_id=1, source_target_pairs={{0,4},{4,0},{8,12},{12,8},{1,5},{5,1},{9,13},{13,9},{2,6},{6,2},{1... | collective-permute-start | bytes 589832 | tf_op jit(solution)/shard_map/ppermute | solution.py:519
  4.9 2.5 %collective-permute-start.6 = (bf16[1,128,768]{2,1,0:T(8,128)(2,1)S(1)}, bf16[1,128,768]{2,1,0:T(8,128)(2,1)S(1)}, u32[]{:S(2)}, u32[]{:S(2)}) collective-permute-start(bf16[1,128,768]{2,1,0:T(8,128)(2,1)S(1)} %get-tuple-element.155), channel_id=1, source_target_pairs={{0,12},{4,8},{8,4},{12,0},{1,13},{5,9},{9,5},{13,1},{2,14},{6,10},... | collective-permute-start | bytes 589832 | tf_op jit(solution)/shard_map/ppermute | solution.py:519
  7.4 1.5 collective-permute-start.3
  10.7 1.3 multiply_cosine_fusion
  13.0 1.5 collective-permute-start.9
  14.6 2.9 %collective-permute-done.6 = bf16[1,128,768]{2,1,0:T(8,128)(2,1)S(1)} collective-permute-done((bf16[1,128,768]{2,1,0:T(8,128)(2,1)S(1)}, bf16[1,128,768]{2,1,0:T(8,128)(2,1)S(1)}, u32[]{:S(2)}, u32[]{:S(2)}) %collective-permute-start.6) | collective-permute-done | bytes 196640 | tf_op jit(solution)/shard_map/ppermute | solution.py:519
  17.5 1.6 collective-permute-start.7
  19.1 14.1 %collective-permute-done.fz = bf16[2,128,768]{2,1,0:T(8,128)(2,1)S(1)} collective-permute-done((bf16[2,128,768]{2,1,0:T(8,128)(2,1)S(1)}, bf16[2,128,768]{2,1,0:T(8,128)(2,1)S(1)}, u32[]{:S(2)}, u32[]{:S(2)}) %collective-permute-start) | collective-permute-done | bytes 393248 | tf_op jit(solution)/shard_map/ppermute | solution.py:519
  33.2 1.5 collective-permute-start.1
  37.0 1.3 broadcast_select_fusion.9
  39.7 12.7 %shard_map.254 = (bf16[512,768]{1,0:T(8,128)(2,1)S(1)}, bf16[512,768]{1,0:T(8,128)(2,1)S(1)}, bf16[2,256,768]{2,1,0:T(8,128)(2,1)S(1)}, bf16[2,256,768]{2,1,0:T(...) custom-call(s32[4]{0:T(128)S(1)} %pad_add_fusion.at, ...), custom_call_target="tpu_custom_call" | custom-call | flops 7247757312 | bytes 16777216 | tf_op jit(solution)/shard_map/pallas_call | solution.py:355
  53.8 1.6 collective-permute-start.11
  56.3 9.1 %shard_map.255 = (bf16[2048,768]{1,0:T(8,128)(2,1)S(1)}, bf16[2048,768]{1,0:T(8,128)(2,1)S(1)}, bf16[1024,768]{1,0:T(8,128)(2,1)S(1)}, f32[24,2048]{1,0:T(8,128)...) custom-call(s32[4]{0:T(128)S(1)} %pad_add_fusion.at, ...), custom_call_target="tpu_custom_call" | custom-call | flops 1811939328 | bytes 12582912 | tf_op jit(solution)/shard_map/pallas_call | solution.py:161
  65.5 9.7 %shard_map.256 = (bf16[64,1024]{1,0:T(8,128)(2,1)S(1)}, bf16[64,1024]{1,0:T(8,128)(2,1)S(1)}, bf16[64,2048]{1,0:T(8,128)(2,1)S(1)}, bf16[64,2048]{1,0:T(8,128)(2,1)S(1)}) custom-call(bf16[192,1024]{1,0:T(8,128)(2,1)S(1)} %get-tuple-element.77.refs_0_.refs_2_.refs_1_, bf16[192,1024]{1,0:T(8,128)(2,1)S(1)} %get-tuple-element.78.refs_1_.refs_3_.refs_2_, ...), custom_call_target="tpu_custom_call" | custom-call | flops 5368709120 | bytes 2097152 | tf_op jit(solution)/shard_map/pallas_call | solution.py:259
  76.1 1.2 collective-permute-start.12
  77.3 4.6 %collective-permute-done.11 = bf16[768,768]{1,0:T(8,128)(2,1)S(1)} collective-permute-done((bf16[768,768]{1,0:T(8,128)(2,1)S(1)}, bf16[768,768]{1,0:T(8,128)(2,1)S(1)}, u32[]{:S(2)}, u32[]{:S(2)}) %collective-permute-start.11) | collective-permute-done | bytes 1179680 | tf_op jit(solution)/shard_map/ppermute | solution.py:519
  82.2 9.7 %shard_map.257 = (bf16[64,1024]{1,0:T(8,128)(2,1)S(1)}, bf16[64,1024]{1,0:T(8,128)(2,1)S(1)}, bf16[64,2048]{1,0:T(8,128)(2,1)S(1)}, bf16[64,2048]{1,0:T(8,128)(2,1)S(1)}) custom-call(f32[2,2,128,768]{3,2,1,0:T(8,128)S(1)} %bitcast.154, f32[768,768]{1,0:T(8,128)S(1)} %convert_add_fusion.1.refs_1_, ...), custom_call_target="tpu_custom_call" | custom-call | flops 5368709120 | bytes 2097152 | tf_op jit(solution)/shard_map/pallas_call | solution.py:259
  92.1 9.9 %shard_map.258 = (bf16[64,1024]{1,0:T(8,128)(2,1)S(1)}, bf16[64,1024]{1,0:T(8,128)(2,1)S(1)}, bf16[64,2048]{1,0:T(8,128)(2,1)S(1)}, bf16[64,2048]{1,0:T(8,128)(2,1)S(1)}) custom-call(f32[2,128,768]{2,1,0:T(8,128)S(1)} %fusion.13.refs_0_, bf16[192,1024]{1,0:T(8,128)(2,1)S(1)} %get-tuple-element.77.refs_0_.refs_2_.refs_1_, ...), custom_call_target="tpu_custom_call" | custom-call | flops 5368709120 | bytes 2097152 | tf_op jit(solution)/shard_map/pallas_call | solution.py:259
  102.0 3.3 %shard_map.259 = (bf16[2,256,768]{2,1,0:T(8,128)(2,1)S(1)}, bf16[2,256,768]{2,1,0:T(8,128)(2,1)}, f32[192,768]{1,0:T(8,128)S(1)}) custom-call(bf16[64,1024]{1,0:T(8,128)(2,1)S(1)} %get-tuple-element.82.refs_0_, bf16[64,1024]{1,0:T(8,128)(2,1)S(1)} %get-tuple-element.89.refs_1_, bf16[64,1024]{1,0:T(8,128)(2,1)S(1)} %get-tuple-element.91.refs_2_, ...), custom_call_target="tpu_custom_call" | custom-call | flops 603979776 | bytes 8388608 | tf_op jit(solution)/shard_map/pallas_call | solution.py:409
  108.0 1.4 add.162
  109.3 1.5 dynamic-slice_convert_fusion.2
  110.9 2.7 %collective-permute-start.15 = (bf16[192,768]{1,0:T(8,128)(2,1)S(1)}, bf16[192,768]{1,0:T(8,128)(2,1)S(1)}, u32[]{:S(2)}, u32[]{:S(2)}) collective-permute-start(bf16[192,768]{1,0:T(8,128)(2,1)S(1)} %get-tuple-element.139), channel_id=1, source_target_pairs={{0,12},{4,8},{8,4},{12,0},{1,13},{5,9},{9,5},{13,1},{2,14},{6,10},... | collective-permute-start | bytes 884744 | tf_op jit(solution)/shard_map/ppermute | solution.py:519
  113.6 1.7 collective-permute-start.17
  115.4 1.9 copy-done.4
  117.3 1.9 copy-done.7
  119.2 4.9 %shard_map.260 = (bf16[2,256,768]{2,1,0:T(8,128)(2,1)S(1)}, bf16[2,256,768]{2,1,0:T(8,128)(2,1)S(1)}, f32[384,768]{1,0:T(8,128)S(1)}, f32[8,768]{1,0:T(8,128)S(1)}) custom-call(s32[4]{0:T(128)S(1)} %pad_add_fusion.at, bf16[64,2048]{1,0:T(8,128)(2,1)S(1)} %copy-done.11, bf16[64,2048]{1,0:T(8,128)(2,1)S(1)} %copy-done.15, bf16[64,2048]{1,0:T(8,128)(2,1)S(1)} %copy-done.19, ...), custom_call_target="tpu_custom_call" | custom-call | flops 1207959552 | bytes 10485760 | tf_op jit(solution)/shard_map/pallas_call | solution.py:503
  124.1 15.0 %collective-permute-done.16 = bf16[192,768]{1,0:T(8,128)(2,1)S(1)} collective-permute-done((bf16[192,768]{1,0:T(8,128)(2,1)S(1)}, bf16[192,768]{1,0:T(8,128)(2,1)S(1)}, u32[]{:S(2)}, u32[]{:S(2)}) %collective-permute-start.16) | collective-permute-done | bytes 294944 | tf_op jit(solution)/shard_map/ppermute | solution.py:519
  139.1 1.3 convert_add_fusion.7
  140.5 1.5 convert_add_fusion.4
  142.6 6.1 %shard_map.261 = (bf16[2,256,768]{2,1,0:T(8,128)(2,1)S(1)}, bf16[2,256,768]{2,1,0:T(8,128)(2,1)S(1)}, f32[832,384]{1,0:T(8,128)S(1)}, bf16[832,384]{1,0:T(8,128)(2,1)S(1)}) custom-call(s32[4]{0:T(128)S(1)} %pad_add_fusion.at, bf16[64,1024]{1,0:T(8,128)(2,1)S(1)} %copy-done.29, bf16[64,1024]{1,0:T(8,128)(2,1)S(1)} %copy-done.31, ...), custom_call_target="tpu_custom_call" | custom-call | flops 1811939328 | bytes 10485760 | tf_op jit(solution)/shard_map/pallas_call | solution.py:503
  148.8 1.6 collective-permute-start.14
  151.2 1.5 collective-permute-start.30
  152.9 7.9 %collective-permute-done.14 = bf16[2,128,768]{2,1,0:T(8,128)(2,1)S(1)} collective-permute-done((bf16[2,128,768]{2,1,0:T(8,128)(2,1)S(1)}, bf16[2,128,768]{2,1,0:T(8,128)(2,1)S(1)}, u32[]{:S(2)}, u32[]{:S(2)}) %collective-permute-start.14) | collective-permute-done | bytes 393248 | tf_op jit(solution)/shard_map/ppermute | solution.py:519
  160.9 2.4 collective-permute-start.19
  163.4 5.4 %collective-permute-done.24 = bf16[2,128,768]{2,1,0:T(8,128)(2,1)S(1)} collective-permute-done((bf16[2,128,768]{2,1,0:T(8,128)(2,1)S(1)}, bf16[2,128,768]{2,1,0:T(8,128)(2,1)S(1)}, u32[]{:S(2)}, u32[]{:S(2)}) %collective-permute-start.24) | collective-permute-done | bytes 393248 | tf_op jit(solution)/shard_map/ppermute | solution.py:519
  168.9 1.2 collective-permute-start.26
  170.2 1.6 collective-permute-start.22
  171.9 2.7 %collective-permute-start.31 = (bf16[208,384]{1,0:T(8,128)(2,1)S(1)}, bf16[208,384]{1,0:T(8,128)(2,1)S(1)}, u32[]{:S(2)}, u32[]{:S(2)}) collective-permute-start(bf16[208,384]{1,0:T(8,128)(2,1)S(1)} %get-tuple-element.156), channel_id=1, source_target_pairs={{0,12},{4,8},{8,4},{12,0},{1,13},{5,9},{9,5},{13,1},{2,14},{6,10},... | collective-permute-start | bytes 479240 | tf_op jit(solution)/shard_map/ppermute | solution.py:519
  174.8 21.7 %collective-permute-done.26 = bf16[2,128,768]{2,1,0:T(8,128)(2,1)S(1)} collective-permute-done((bf16[2,128,768]{2,1,0:T(8,128)(2,1)S(1)}, bf16[2,128,768]{2,1,0:T(8,128)(2,1)S(1)}, u32[]{:S(2)}, u32[]{:S(2)}) %collective-permute-start.26) | collective-permute-done | bytes 393248 | tf_op jit(solution)/shard_map/ppermute | solution.py:519
  196.5 1.6 collective-permute-start.20
  199.1 3.2 %collective-permute-done.33 = bf16[208,384]{1,0:T(8,128)(2,1)S(1)} collective-permute-done((bf16[208,384]{1,0:T(8,128)(2,1)S(1)}, bf16[208,384]{1,0:T(8,128)(2,1)S(1)}, u32[]{:S(2)}, u32[]{:S(2)}) %collective-permute-start.33) | collective-permute-done | bytes 159776 | tf_op jit(solution)/shard_map/ppermute | solution.py:519
  202.5 10.0 %collective-permute-done.27 = bf16[128,768]{1,0:T(8,128)(2,1)S(1)} collective-permute-done((bf16[128,768]{1,0:T(8,128)(2,1)S(1)}, bf16[128,768]{1,0:T(8,128)(2,1)S(1)}, u32[]{:S(2)}, u32[]{:S(2)}) %collective-permute-start.27) | collective-permute-done | bytes 196640 | tf_op jit(solution)/shard_map/ppermute | solution.py:519
  218.5 4.5 %collective-permute-done.35 = bf16[2,208,384]{2,1,0:T(8,128)(2,1)S(1)} collective-permute-done((bf16[2,208,384]{2,1,0:T(8,128)(2,1)S(1)}, bf16[2,208,384]{2,1,0:T(8,128)(2,1)S(1)}, u32[]{:S(2)}, u32[]{:S(2)}) %collective-permute-start.35) | collective-permute-done | bytes 319520 | tf_op jit(solution)/shard_map/ppermute | solution.py:519
  227.5 2.1 slice.192
  230.8 1.4 broadcast_select_fusion.25
  233.3 1.5 broadcast_select_fusion.21
  236.3 2.0 convert_add_fusion
  238.3 2.1 add_add_fusion
  (255 shorter events, 32.0 us)
Async XLA Ops:
  1.8 11.2 %collective-permute-start.5 = (bf16[1,128,768]{2,1,0:T(8,128)(2,1)S(1)}, bf16[1,128,768]{2,1,0:T(8,128)(2,1)S(1)}, u32[]{:S(2)}, u32[]{:S(2)}) collective-permute-start(bf16[1,128,768]{2,1,0:T(8,128)(2,1)S(1)} %get-tuple-element.154), channel_id=1, source_target_pairs={{0,4},{4,0},{8,12},{12,8},{1,5},{5,1},{9,13},{13,9},{2,6},{6,2},{1... | collective-permute-start | bytes 589832 | tf_op jit(solution)/shard_map/ppermute | solution.py:519
  4.9 12.6 %collective-permute-start.6 = (bf16[1,128,768]{2,1,0:T(8,128)(2,1)S(1)}, bf16[1,128,768]{2,1,0:T(8,128)(2,1)S(1)}, u32[]{:S(2)}, u32[]{:S(2)}) collective-permute-start(bf16[1,128,768]{2,1,0:T(8,128)(2,1)S(1)} %get-tuple-element.155), channel_id=1, source_target_pairs={{0,12},{4,8},{8,4},{12,0},{1,13},{5,9},{9,5},{13,1},{2,14},{6,10},... | collective-permute-start | bytes 589832 | tf_op jit(solution)/shard_map/ppermute | solution.py:519
  7.4 27.3 %collective-permute-start.3 = (bf16[768,384]{1,0:T(8,128)(2,1)}, bf16[768,384]{1,0:T(8,128)(2,1)}, u32[]{:S(2)}, u32[]{:S(2)}) collective-permute-start(bf16[768,384]{1,0:T(8,128)(2,1)} %param.23), channel_id=1, source_target_pairs={{0,16},{16,0},{1,17},{17,1},{2,18},{18,2},{3,19},{19,3},{4,20},{20... | collective-permute-start | bytes 1769480 | tf_op jit(solution)/shard_map/ppermute | solution.py:519
  8.9 27.7 %collective-permute-start.2 = (bf16[384,768]{1,0:T(8,128)(2,1)}, bf16[384,768]{1,0:T(8,128)(2,1)}, u32[]{:S(2)}, u32[]{:S(2)}) collective-permute-start(bf16[384,768]{1,0:T(8,128)(2,1)} %param.21), channel_id=1, source_target_pairs={{0,16},{16,0},{1,17},{17,1},{2,18},{18,2},{3,19},{19,3},{4,20},{20... | collective-permute-start | bytes 1769480 | tf_op jit(solution)/shard_map/ppermute | solution.py:519
  10.4 24.3 %copy-start.56 = (bf16[768,384]{1,0:T(8,128)(2,1)S(1)}, bf16[768,384]{1,0:T(8,128)(2,1)}, u32[]{:S(2)}) copy-start(bf16[768,384]{1,0:T(8,128)(2,1)} %param.23) | copy-start | bytes 1769476
  10.4 22.8 %collective-permute-start = (bf16[2,128,768]{2,1,0:T(8,128)(2,1)S(1)}, bf16[2,128,768]{2,1,0:T(8,128)(2,1)S(1)}, u32[]{:S(2)}, u32[]{:S(2)}) collective-permute-start(bf16[2,128,768]{2,1,0:T(8,128)(2,1)S(1)} %pad_maximum_fusion.13), channel_id=1, source_target_pairs={{0,8},{4,12},{8,0},{12,4},{1,9},{5,13},{9,1},{13,5},{2,10},{6,14},... | collective-permute-start | bytes 1179656 | tf_op jit(solution)/shard_map/ppermute | solution.py:519
  10.6 24.1 %copy-start.60 = (f32[2,2048]{1,0:T(2,128)}, f32[2,2048]{1,0:T(2,128)S(1)}, u32[]{:S(2)}) copy-start(f32[2,2048]{1,0:T(2,128)S(1)} %convert_element_type.177) | copy-start | bytes 49156
  13.0 40.8 %collective-permute-start.9 = (bf16[768,384]{1,0:T(8,128)(2,1)}, bf16[768,384]{1,0:T(8,128)(2,1)S(1)}, u32[]{:S(2)}, u32[]{:S(2)}) collective-permute-start(bf16[768,384]{1,0:T(8,128)(2,1)} %pad_maximum_fusion.11), channel_id=1, source_target_pairs={{0,16},{16,0},{1,17},{17,1},{2,18},{18,2},{3,19},{19,3},{4,20},{20... | collective-permute-start | bytes 1769480 | tf_op jit(solution)/shard_map/ppermute | solution.py:519
  17.5 35.0 %collective-permute-start.7 = (bf16[2,128,768]{2,1,0:T(8,128)(2,1)S(1)}, bf16[2,128,768]{2,1,0:T(8,128)(2,1)S(1)}, u32[]{:S(2)}, u32[]{:S(2)}) collective-permute-start(bf16[2,128,768]{2,1,0:T(8,128)(2,1)S(1)} %constant_dynamic-update-slice_fusion.nz), channel_id=1, source_target_pairs={{0,2},{1,3},{2,0},{3,1},{4,6},{5,7},{6,4},{7,5},{8,10},{9,11},{10,... | collective-permute-start | bytes 1179656 | tf_op jit(solution)/shard_map/ppermute | solution.py:519
  33.2 19.5 %collective-permute-start.1 = (bf16[2,128,768]{2,1,0:T(8,128)(2,1)S(1)}, bf16[2,128,768]{2,1,0:T(8,128)(2,1)S(1)}, u32[]{:S(2)}, u32[]{:S(2)}) collective-permute-start(bf16[2,128,768]{2,1,0:T(8,128)(2,1)S(1)} %collective-permute-done.fz), channel_id=1, source_target_pairs={{0,2},{1,3},{2,0},{3,1},{4,6},{5,7},{6,4},{7,5},{8,10},{9,11},{10,... | collective-permute-start | bytes 1179656 | tf_op jit(solution)/shard_map/ppermute | solution.py:519
  52.6 3.2 %collective-permute-start.8 = (bf16[2,2,128,768]{3,2,1,0:T(8,128)(2,1)S(1)}, bf16[2,2,128,768]{3,2,1,0:T(8,128)(2,1)S(1)}, u32[]{:S(2)}, u32[]{:S(2)}) collective-permute-start(bf16[2,2,128,768]{3,2,1,0:T(8,128)(2,1)S(1)} %pad_maximum_fusion.7), channel_id=1, source_target_pairs={{0,1},{1,0},{2,3},{3,2},{4,5},{5,4},{6,7},{7,6},{8,9},{9,8},{10,11... | collective-permute-start | bytes 2359304 | tf_op jit(solution)/shard_map/ppermute | solution.py:519
  53.3 2.7 %collective-permute-start.4 = (bf16[2,2,128,768]{3,2,1,0:T(8,128)(2,1)S(1)}, bf16[2,2,128,768]{3,2,1,0:T(8,128)(2,1)S(1)}, u32[]{:S(2)}, u32[]{:S(2)}) collective-permute-start(bf16[2,2,128,768]{3,2,1,0:T(8,128)(2,1)S(1)} %pad_maximum_fusion.6), channel_id=1, source_target_pairs={{0,1},{1,0},{2,3},{3,2},{4,5},{5,4},{6,7},{7,6},{8,9},{9,8},{10,11... | collective-permute-start | bytes 2359304 | tf_op jit(solution)/shard_map/ppermute | solution.py:519
  53.8 28.1 %collective-permute-start.11 = (bf16[768,768]{1,0:T(8,128)(2,1)S(1)}, bf16[768,768]{1,0:T(8,128)(2,1)S(1)}, u32[]{:S(2)}, u32[]{:S(2)}) collective-permute-start(bf16[768,768]{1,0:T(8,128)(2,1)S(1)} %get-tuple-element.87), channel_id=1, source_target_pairs={{0,16},{16,0},{1,17},{17,1},{2,18},{18,2},{3,19},{19,3},{4,20},{20... | collective-permute-start | bytes 3538952 | tf_op jit(solution)/shard_map/ppermute | solution.py:519
  55.4 19.9 %collective-permute-start.10 = (bf16[2,256,768]{2,1,0:T(8,128)(2,1)S(1)}, bf16[2,256,768]{2,1,0:T(8,128)(2,1)S(1)}, u32[]{:S(2)}, u32[]{:S(2)}) collective-permute-start(bf16[2,256,768]{2,1,0:T(8,128)(2,1)S(1)} %get-tuple-element.84), channel_id=1, source_target_pairs={{0,1},{1,0},{2,3},{3,2},{4,5},{5,4},{6,7},{7,6},{8,9},{9,8},{10,11... | collective-permute-start | bytes 2359304 | tf_op jit(solution)/shard_map/ppermute | solution.py:519
  76.1 15.9 %collective-permute-start.12 = (bf16[2,128,768]{2,1,0:T(8,128)(2,1)S(1)}, bf16[2,128,768]{2,1,0:T(8,128)(2,1)S(1)}, u32[]{:S(2)}, u32[]{:S(2)}) collective-permute-start(bf16[2,128,768]{2,1,0:T(8,128)(2,1)S(1)} %fusion.18), channel_id=1, source_target_pairs={{0,2},{1,3},{2,0},{3,1},{4,6},{5,7},{6,4},{7,5},{8,10},{9,11},{10,... | collective-permute-start | bytes 1179656 | tf_op jit(solution)/shard_map/ppermute | solution.py:519
  107.1 33.4 %collective-permute-start.13 = (bf16[2,256,768]{2,1,0:T(8,128)(2,1)}, bf16[2,256,768]{2,1,0:T(8,128)(2,1)}, u32[]{:S(2)}, u32[]{:S(2)}) collective-permute-start(bf16[2,256,768]{2,1,0:T(8,128)(2,1)} %get-tuple-element.95), channel_id=1, source_target_pairs={{0,1},{1,0},{2,3},{3,2},{4,5},{5,4},{6,7},{7,6},{8,9},{9,8},{10,11... | collective-permute-start | bytes 2359304 | tf_op jit(solution)/shard_map/ppermute | solution.py:519
  110.9 13.3 %collective-permute-start.15 = (bf16[192,768]{1,0:T(8,128)(2,1)S(1)}, bf16[192,768]{1,0:T(8,128)(2,1)S(1)}, u32[]{:S(2)}, u32[]{:S(2)}) collective-permute-start(bf16[192,768]{1,0:T(8,128)(2,1)S(1)} %get-tuple-element.139), channel_id=1, source_target_pairs={{0,12},{4,8},{8,4},{12,0},{1,13},{5,9},{9,5},{13,1},{2,14},{6,10},... | collective-permute-start | bytes 884744 | tf_op jit(solution)/shard_map/ppermute | solution.py:519
  113.6 25.5 %collective-permute-start.16 = (bf16[192,768]{1,0:T(8,128)(2,1)S(1)}, bf16[192,768]{1,0:T(8,128)(2,1)S(1)}, u32[]{:S(2)}, u32[]{:S(2)}) collective-permute-start(bf16[192,768]{1,0:T(8,128)(2,1)S(1)} %get-tuple-element.141), channel_id=1, source_target_pairs={{0,8},{4,12},{8,0},{12,4},{1,9},{5,13},{9,1},{13,5},{2,10},{6,14},... | collective-permute-start | bytes 884744 | tf_op jit(solution)/shard_map/ppermute | solution.py:519
  113.6 25.5 %collective-permute-start.17 = (bf16[192,768]{1,0:T(8,128)(2,1)S(1)}, bf16[192,768]{1,0:T(8,128)(2,1)S(1)}, u32[]{:S(2)}, u32[]{:S(2)}) collective-permute-start(bf16[192,768]{1,0:T(8,128)(2,1)S(1)} %get-tuple-element.140), channel_id=1, source_target_pairs={{0,4},{4,0},{8,12},{12,8},{1,5},{5,1},{9,13},{13,9},{2,6},{6,2},{1... | collective-permute-start | bytes 884744 | tf_op jit(solution)/shard_map/ppermute | solution.py:519
  119.2 22.9 %copy-start.8 = (bf16[2048,768]{1,0:T(8,128)(2,1)S(1)}, bf16[2048,768]{1,0:T(8,128)(2,1)}, u32[]{:S(2)}) copy-start(bf16[2048,768]{1,0:T(8,128)(2,1)} %copy-done.6) | copy-start | bytes 9437188
  119.2 22.9 %copy-start.27 = (f32[192,768]{1,0:T(8,128)S(1)}, f32[192,768]{1,0:T(8,128)}, u32[]{:S(2)}) copy-start(f32[192,768]{1,0:T(8,128)} %copy-done.26) | copy-start | bytes 1769476
  119.2 22.9 %copy-start.31 = (bf16[64,1024]{1,0:T(8,128)(2,1)S(1)}, bf16[64,1024]{1,0:T(8,128)(2,1)}, u32[]{:S(2)}) copy-start(bf16[64,1024]{1,0:T(8,128)(2,1)} %copy-done.30) | copy-start | bytes 393220
  119.2 22.9 %copy-start.33 = (bf16[64,1024]{1,0:T(8,128)(2,1)S(1)}, bf16[64,1024]{1,0:T(8,128)(2,1)}, u32[]{:S(2)}) copy-start(bf16[64,1024]{1,0:T(8,128)(2,1)} %copy-done.32) | copy-start | bytes 393220
  124.0 16.5 %copy-start.25 = (bf16[2,256,768]{2,1,0:T(8,128)(2,1)S(1)}, bf16[2,256,768]{2,1,0:T(8,128)(2,1)}, u32[]{:S(2)}) copy-start(bf16[2,256,768]{2,1,0:T(8,128)(2,1)} %copy-done.24) | copy-start | bytes 2359300
  124.0 26.3 %collective-permute-start.23 = (bf16[2,256,768]{2,1,0:T(8,128)(2,1)S(1)}, bf16[2,256,768]{2,1,0:T(8,128)(2,1)S(1)}, u32[]{:S(2)}, u32[]{:S(2)}) collective-permute-start(bf16[2,256,768]{2,1,0:T(8,128)(2,1)S(1)} %get-tuple-element.120), channel_id=1, source_target_pairs={{0,1},{1,0},{2,3},{3,2},{4,5},{5,4},{6,7},{7,6},{8,9},{9,8},{10,11... | collective-permute-start | bytes 2359304 | tf_op jit(solution)/shard_map/ppermute | solution.py:519
  140.4 22.9 %collective-permute-start.25 = (bf16[192,768]{1,0:T(8,128)(2,1)S(1)}, bf16[192,768]{1,0:T(8,128)(2,1)S(1)}, u32[]{:S(2)}, u32[]{:S(2)}) collective-permute-start(bf16[192,768]{1,0:T(8,128)(2,1)S(1)} %convert_add_fusion.7), channel_id=1, source_target_pairs={{0,8},{4,12},{8,0},{12,4},{1,9},{5,13},{9,1},{13,5},{2,10},{6,14},... | collective-permute-start | bytes 884744 | tf_op jit(solution)/shard_map/ppermute | solution.py:519
  148.7 4.0 %collective-permute-start.18 = (bf16[2,256,768]{2,1,0:T(8,128)(2,1)S(1)}, bf16[2,256,768]{2,1,0:T(8,128)(2,1)S(1)}, u32[]{:S(2)}, u32[]{:S(2)}) collective-permute-start(bf16[2,256,768]{2,1,0:T(8,128)(2,1)S(1)} %get-tuple-element.117), channel_id=1, source_target_pairs={{0,1},{1,0},{2,3},{3,2},{4,5},{5,4},{6,7},{7,6},{8,9},{9,8},{10,11... | collective-permute-start | bytes 2359304 | tf_op jit(solution)/shard_map/ppermute | solution.py:519
  148.8 12.0 %collective-permute-start.14 = (bf16[2,128,768]{2,1,0:T(8,128)(2,1)S(1)}, bf16[2,128,768]{2,1,0:T(8,128)(2,1)S(1)}, u32[]{:S(2)}, u32[]{:S(2)}) collective-permute-start(bf16[2,128,768]{2,1,0:T(8,128)(2,1)S(1)} %fusion.19), channel_id=1, source_target_pairs={{0,2},{1,3},{2,0},{3,1},{4,6},{5,7},{6,4},{7,5},{8,10},{9,11},{10,... | collective-permute-start | bytes 1179656 | tf_op jit(solution)/shard_map/ppermute | solution.py:519
  150.6 18.2 %collective-permute-start.24 = (bf16[2,128,768]{2,1,0:T(8,128)(2,1)S(1)}, bf16[2,128,768]{2,1,0:T(8,128)(2,1)S(1)}, u32[]{:S(2)}, u32[]{:S(2)}) collective-permute-start(bf16[2,128,768]{2,1,0:T(8,128)(2,1)S(1)} %fusion.21), channel_id=1, source_target_pairs={{0,2},{1,3},{2,0},{3,1},{4,6},{5,7},{6,4},{7,5},{8,10},{9,11},{10,... | collective-permute-start | bytes 1179656 | tf_op jit(solution)/shard_map/ppermute | solution.py:519
  151.2 20.5 %collective-permute-start.30 = (bf16[832,384]{1,0:T(8,128)(2,1)S(1)}, bf16[832,384]{1,0:T(8,128)(2,1)S(1)}, u32[]{:S(2)}, u32[]{:S(2)}) collective-permute-start(bf16[832,384]{1,0:T(8,128)(2,1)S(1)} %get-tuple-element.125), channel_id=1, source_target_pairs={{0,16},{16,0},{1,17},{17,1},{2,18},{18,2},{3,19},{19,3},{4,20},{20... | collective-permute-start | bytes 1916936 | tf_op jit(solution)/shard_map/ppermute | solution.py:519
  160.9 54.1 %copy-start.48 = (bf16[1,128,768]{2,1,0:T(8,128)(2,1)}, bf16[1,128,768]{2,1,0:T(8,128)(2,1)S(1)}, u32[]{:S(2)}) copy-start(bf16[1,128,768]{2,1,0:T(8,128)(2,1)S(1)} %get-tuple-element.183) | copy-start | bytes 589828
  160.9 13.7 %collective-permute-start.19 = (bf16[128,768]{1,0:T(8,128)(2,1)S(1)}, bf16[128,768]{1,0:T(8,128)(2,1)S(1)}, u32[]{:S(2)}, u32[]{:S(2)}) collective-permute-start(bf16[128,768]{1,0:T(8,128)(2,1)S(1)} %get-tuple-element.184), channel_id=1, source_target_pairs={{0,8},{4,12},{8,0},{12,4},{1,9},{5,13},{9,1},{13,5},{2,10},{6,14},... | collective-permute-start | bytes 589832 | tf_op jit(solution)/shard_map/ppermute | solution.py:519
  163.4 50.9 %collective-permute-start.38 = (bf16[2,192,768]{2,1,0:T(8,128)(2,1)S(1)}, bf16[2,192,768]{2,1,0:T(8,128)(2,1)S(1)}, u32[]{:S(2)}, u32[]{:S(2)}) collective-permute-start(bf16[2,192,768]{2,1,0:T(8,128)(2,1)S(1)} %pad_maximum_fusion.12), channel_id=1, source_target_pairs={{0,4},{4,0},{8,12},{12,8},{1,5},{5,1},{9,13},{13,9},{2,6},{6,2},{1... | collective-permute-start | bytes 1769480 | tf_op jit(solution)/shard_map/ppermute | solution.py:519
  168.9 27.6 %collective-permute-start.26 = (bf16[2,128,768]{2,1,0:T(8,128)(2,1)S(1)}, bf16[2,128,768]{2,1,0:T(8,128)(2,1)S(1)}, u32[]{:S(2)}, u32[]{:S(2)}) collective-permute-start(bf16[2,128,768]{2,1,0:T(8,128)(2,1)S(1)} %fusion.9), channel_id=1, source_target_pairs={{0,4},{4,0},{8,12},{12,8},{1,5},{5,1},{9,13},{13,9},{2,6},{6,2},{1... | collective-permute-start | bytes 1179656 | tf_op jit(solution)/shard_map/ppermute | solution.py:519
  170.2 26.4 %collective-permute-start.22 = (bf16[2,128,768]{2,1,0:T(8,128)(2,1)S(1)}, bf16[2,128,768]{2,1,0:T(8,128)(2,1)S(1)}, u32[]{:S(2)}, u32[]{:S(2)}) collective-permute-start(bf16[2,128,768]{2,1,0:T(8,128)(2,1)S(1)} %fusion.20), channel_id=1, source_target_pairs={{0,2},{1,3},{2,0},{3,1},{4,6},{5,7},{6,4},{7,5},{8,10},{9,11},{10,... | collective-permute-start | bytes 1179656 | tf_op jit(solution)/shard_map/ppermute | solution.py:519
  171.9 26.3 %collective-permute-start.31 = (bf16[208,384]{1,0:T(8,128)(2,1)S(1)}, bf16[208,384]{1,0:T(8,128)(2,1)S(1)}, u32[]{:S(2)}, u32[]{:S(2)}) collective-permute-start(bf16[208,384]{1,0:T(8,128)(2,1)S(1)} %get-tuple-element.156), channel_id=1, source_target_pairs={{0,12},{4,8},{8,4},{12,0},{1,13},{5,9},{9,5},{13,1},{2,14},{6,10},... | collective-permute-start | bytes 479240 | tf_op jit(solution)/shard_map/ppermute | solution.py:519
  174.6 24.5 %collective-permute-start.32 = (bf16[208,384]{1,0:T(8,128)(2,1)S(1)}, bf16[208,384]{1,0:T(8,128)(2,1)S(1)}, u32[]{:S(2)}, u32[]{:S(2)}) collective-permute-start(bf16[208,384]{1,0:T(8,128)(2,1)S(1)} %get-tuple-element.158), channel_id=1, source_target_pairs={{0,8},{4,12},{8,0},{12,4},{1,9},{5,13},{9,1},{13,5},{2,10},{6,14},... | collective-permute-start | bytes 479240 | tf_op jit(solution)/shard_map/ppermute | solution.py:519
  174.7 21.8 %copy-start.51 = (bf16[1,128,768]{2,1,0:T(8,128)(2,1)}, bf16[1,128,768]{2,1,0:T(8,128)(2,1)S(1)}, u32[]{:S(2)}) copy-start(bf16[1,128,768]{2,1,0:T(8,128)(2,1)S(1)} %get-tuple-element.174) | copy-start | bytes 589828
  196.5 5.8 %collective-permute-start.33 = (bf16[208,384]{1,0:T(8,128)(2,1)S(1)}, bf16[208,384]{1,0:T(8,128)(2,1)S(1)}, u32[]{:S(2)}, u32[]{:S(2)}) collective-permute-start(bf16[208,384]{1,0:T(8,128)(2,1)S(1)} %get-tuple-element.157), channel_id=1, source_target_pairs={{0,4},{4,0},{8,12},{12,8},{1,5},{5,1},{9,13},{13,9},{2,6},{6,2},{1... | collective-permute-start | bytes 479240 | tf_op jit(solution)/shard_map/ppermute | solution.py:519
  196.5 18.5 %collective-permute-start.20 = (bf16[2,128,768]{2,1,0:T(8,128)(2,1)S(1)}, bf16[2,128,768]{2,1,0:T(8,128)(2,1)S(1)}, u32[]{:S(2)}, u32[]{:S(2)}) collective-permute-start(bf16[2,128,768]{2,1,0:T(8,128)(2,1)S(1)} %pad_maximum_fusion.15), channel_id=1, source_target_pairs={{0,2},{1,3},{2,0},{3,1},{4,6},{5,7},{6,4},{7,5},{8,10},{9,11},{10,... | collective-permute-start | bytes 1179656 | tf_op jit(solution)/shard_map/ppermute | solution.py:519
  198.3 14.2 %collective-permute-start.27 = (bf16[128,768]{1,0:T(8,128)(2,1)S(1)}, bf16[128,768]{1,0:T(8,128)(2,1)S(1)}, u32[]{:S(2)}, u32[]{:S(2)}) collective-permute-start(bf16[128,768]{1,0:T(8,128)(2,1)S(1)} %fusion.28), channel_id=1, source_target_pairs={{0,8},{4,12},{8,0},{12,4},{1,9},{5,13},{9,1},{13,5},{2,10},{6,14},... | collective-permute-start | bytes 589832 | tf_op jit(solution)/shard_map/ppermute | solution.py:519
  202.4 12.3 %collective-permute-start.34 = (bf16[208,384]{1,0:T(8,128)(2,1)S(1)}, bf16[208,384]{1,0:T(8,128)(2,1)S(1)}, u32[]{:S(2)}, u32[]{:S(2)}) collective-permute-start(bf16[208,384]{1,0:T(8,128)(2,1)S(1)} %add_convert_fusion), channel_id=1, source_target_pairs={{0,8},{4,12},{8,0},{12,4},{1,9},{5,13},{9,1},{13,5},{2,10},{6,14},... | collective-permute-start | bytes 479240 | tf_op jit(solution)/shard_map/ppermute | solution.py:519
  213.2 11.2 %collective-permute-start.28 = (bf16[2,128,768]{2,1,0:T(8,128)(2,1)S(1)}, bf16[2,128,768]{2,1,0:T(8,128)(2,1)S(1)}, u32[]{:S(2)}, u32[]{:S(2)}) collective-permute-start(bf16[2,128,768]{2,1,0:T(8,128)(2,1)S(1)} %fusion.7), channel_id=1, source_target_pairs={{0,2},{1,3},{2,0},{3,1},{4,6},{5,7},{6,4},{7,5},{8,10},{9,11},{10,... | collective-permute-start | bytes 1179656 | tf_op jit(solution)/shard_map/ppermute | solution.py:519
  214.7 8.3 %collective-permute-start.35 = (bf16[2,208,384]{2,1,0:T(8,128)(2,1)S(1)}, bf16[2,208,384]{2,1,0:T(8,128)(2,1)S(1)}, u32[]{:S(2)}, u32[]{:S(2)}) collective-permute-start(bf16[2,208,384]{2,1,0:T(8,128)(2,1)S(1)} %pad_maximum_fusion.17), channel_id=1, source_target_pairs={{0,4},{4,0},{8,12},{12,8},{1,5},{5,1},{9,13},{13,9},{2,6},{6,2},{1... | collective-permute-start | bytes 958472 | tf_op jit(solution)/shard_map/ppermute | solution.py:519
  216.0 14.8 %collective-permute-start.21 = (bf16[2,2,128,768]{3,2,1,0:T(8,128)(2,1)}, bf16[2,2,128,768]{3,2,1,0:T(8,128)(2,1)}, u32[]{:S(2)}, u32[]{:S(2)}) collective-permute-start(bf16[2,2,128,768]{3,2,1,0:T(8,128)(2,1)} %pad_maximum_fusion.8), channel_id=1, source_target_pairs={{0,1},{1,0},{2,3},{3,2},{4,5},{5,4},{6,7},{7,6},{8,9},{9,8},{10,11... | collective-permute-start | bytes 2359304 | tf_op jit(solution)/shard_map/ppermute | solution.py:519
  223.1 2.7 %collective-permute-start.36 = (f32[8,768]{1,0:T(8,128)S(1)}, f32[8,768]{1,0:T(8,128)S(1)}, u32[]{:S(2)}, u32[]{:S(2)}) collective-permute-start(f32[8,768]{1,0:T(8,128)S(1)} %pad_maximum_fusion.18), channel_id=1, source_target_pairs={{0,1},{1,0},{2,3},{3,2},{4,5},{5,4},{6,7},{7,6},{8,9},{9,8},{10,11... | collective-permute-start | bytes 73736 | tf_op jit(solution)/shard_map/ppermute | solution.py:519
  225.4 7.0 %collective-permute-start.29 = (bf16[2,2,128,768]{3,2,1,0:T(8,128)(2,1)}, bf16[2,2,128,768]{3,2,1,0:T(8,128)(2,1)}, u32[]{:S(2)}, u32[]{:S(2)}) collective-permute-start(bf16[2,2,128,768]{3,2,1,0:T(8,128)(2,1)} %pad_maximum_fusion.10), channel_id=1, source_target_pairs={{0,1},{1,0},{2,3},{3,2},{4,5},{5,4},{6,7},{7,6},{8,9},{9,8},{10,11... | collective-permute-start | bytes 2359304 | tf_op jit(solution)/shard_map/ppermute | solution.py:519
  225.9 4.3 %collective-permute-start.37 = (f32[8,768]{1,0:T(8,128)S(1)}, f32[8,768]{1,0:T(8,128)S(1)}, u32[]{:S(2)}, u32[]{:S(2)}) collective-permute-start(f32[8,768]{1,0:T(8,128)S(1)} %fusion.34), channel_id=1, source_target_pairs={{0,2},{1,3},{2,0},{3,1},{4,6},{5,7},{6,4},{7,5},{8,10},{9,11},{10,... | collective-permute-start | bytes 73736 | tf_op jit(solution)/shard_map/ppermute | solution.py:519
  (58 other events, 289.5 us)

commit v7 on v6

--- a/solution.py
+++ b/solution.py
@@ -562,6 +562,13 @@
         sent = swap(part(j).astype(BF16), "ctx", 4, distance)
         total = total + tie(sent, *earlier).astype(F32)
     return total
+
+
+def halve(v, distance, bit, *earlier):
+    rows = v.shape[0] // 2
+    keep = lax.dynamic_slice_in_dim(v, bit * rows, rows, 0)
+    send = lax.dynamic_slice_in_dim(v, (1 - bit) * rows, rows, 0).astype(BF16)
+    return keep + tie(swap(send, "ctx", 4, distance), *earlier).astype(F32)
 
 
 def pair_up(v, *earlier):
@@ -676,18 +683,19 @@
             after = (early, ff_rest)
         if h == heads - 1:
             early = over_x(early, per_head[h - 1][0])
-            after = (early,)
+            ff_half = halve(ff_rest, 1, c % 2, per_head[h - 1][0]) if split else small_ff
+            after = (early, ff_half)
         per_head.append(attention(h, after, qt, dot, kt, vt, trig))
     o, dq, dk, dv = zip(*per_head)
-    ff_quarter = quarter_sum(ff_rest, c, o[-1]) if split else small_ff
-    keep_b, send_b, out_part = branch(o, g, ff, weights)
+    ff_quarter = halve(ff_half, 2, c // 2, o[-1]) if split else small_ff
+    keep_b, send_b, out_part = branch(o, g, tie(ff, ff_quarter), weights)
     keep_o, send_o, mix_other, small_other = back(
         False, split, at, (dk, dv), n1, xhat_all, weights, tie(first_scale, keep_b), ()
     )
     half_b = over_core(keep_b, send_b)
     keep_w, send_w, late_first, late_second = back(
         True, split, at, (dq, dk, dv), n1, xhat_all, weights,
-        tie(first_scale, ff_quarter, half_b), (a2, small_ff, small_other, mix_other, out_part),
+        tie(first_scale, half_b), (a2, small_ff, small_other, mix_other, out_part),
     )
     half_o = over_core(keep_o, send_o)
     half_w = over_core(keep_w, send_w)

time: 242 us -> 242 us (level)
  waiting for transfers between devices: 90.6 us -> 73.4 us
  local copies, waits for them, and re-layouts: 19.2 us -> 30.6 us
    ppermute x39 -> x38, waiting for transfers between devices: 90.6 us -> 73.4 us  [swap(): return lax.ppermute(v, axis, [(i, i ^ distance) for i in range(size)])]
    unnamed x136 -> x168, local copies, waits for them, and re-layouts: 12.4 us -> 22.9 us
    ppermute x39 -> x38, starting transfers between devices: 35.8 us -> 37.2 us  [swap(): return lax.ppermute(v, axis, [(i, i ^ distance) for i in range(size)])]
  transfers between devices with their start and end apart: 39 -> 38, of which waited for: 13 -> 16; matrix products, arithmetic and copies ran while one was open for 12% -> 15% of each run, Pallas kernels for 22% -> 27%
where the time goes in v7:
time: 242 us; the launch traced here: 241 us
  waiting for transfers between devices  73.4 us (30%)
  Pallas kernels  67.5 us (28%)
  starting transfers between devices  37.2 us (15%)
  local copies, waits for them, and re-layouts  30.6 us (13%)
  other arithmetic  30.5 us (13%)
    ppermute x38, waiting for transfers between devices, swap(): return lax.ppermute(v, axis, [(i, i ^ distance) for i in range(size)])  73.4 us
    ppermute x38, starting transfers between devices, swap(): return lax.ppermute(v, axis, [(i, i ^ distance) for i in range(size)])  37.2 us
    pallas_call x3, Pallas kernels, attention(): pl.pallas_call(functools.partial(attention_kernel, len(after)), grid=(row...  29.2 us
    unnamed x168, local copies, waits for them, and re-layouts  22.9 us
    pallas_call x1, Pallas kernels, feed_forward(): pl.pallas_call(functools.partial(forward_kernel, split), grid_spec=pltpu....  13.6 us
    pallas_call x2, Pallas kernels, back(): pl.pallas_call(functools.partial(back_kernel, own, split, heads), grid_sp...  11 us
    pallas_call x1, Pallas kernels, project(): pl.pallas_call(project_kernel, grid_spec=pltpu.PrefetchScalarGridSpec(num...  10.5 us
  transfers between devices with their start and end apart: 38, of which 16 were waited for; matrix products, arithmetic and copies ran while one was open for 15% of the time, Pallas kernels for 27%

profile of v7, /device:TPU:0, one launch (start us, length us, event | category | flops | bytes accessed | tf_op | source)
XLA Modules:
  0.0 241.1 jit_solution(1789900867685240602)
XLA Ops:
  0.7 3.0 %collective-permute-start.3 = (bf16[768,384]{1,0:T(8,128)(2,1)}, bf16[768,384]{1,0:T(8,128)(2,1)}, u32[]{:S(2)}, u32[]{:S(2)}) collective-permute-start(bf16[768,384]{1,0:T(8,128)(2,1)} %param.23), channel_id=1, source_target_pairs={{0,16},{16,0},{1,17},{17,1},{2,18},{18,2},{3,19},{19,3},{4,20},{20... | collective-permute-start | bytes 1769480 | tf_op jit(solution)/shard_map/ppermute | solution.py:519
  4.9 2.1 collective-permute-start.5
  6.9 2.5 %collective-permute-start.6 = (bf16[1,128,768]{2,1,0:T(8,128)(2,1)S(1)}, bf16[1,128,768]{2,1,0:T(8,128)(2,1)}, u32[]{:S(2)}, u32[]{:S(2)}) collective-permute-start(bf16[1,128,768]{2,1,0:T(8,128)(2,1)S(1)} %get-tuple-element.152), channel_id=1, source_target_pairs={{0,12},{4,8},{8,4},{12,0},{1,13},{5,9},{9,5},{13,1},{2,14},{6,10},... | collective-permute-start | bytes 589832 | tf_op jit(solution)/shard_map/ppermute | solution.py:519
  13.0 1.5 collective-permute-start.9
  15.4 4.2 %collective-permute-done.6 = bf16[1,128,768]{2,1,0:T(8,128)(2,1)} collective-permute-done((bf16[1,128,768]{2,1,0:T(8,128)(2,1)S(1)}, bf16[1,128,768]{2,1,0:T(8,128)(2,1)}, u32[]{:S(2)}, u32[]{:S(2)}) %collective-permute-start.6) | collective-permute-done | bytes 196640 | tf_op jit(solution)/shard_map/ppermute | solution.py:519
  20.6 1.6 collective-permute-start.7
  22.2 12.5 %collective-permute-done.fz = bf16[2,128,768]{2,1,0:T(8,128)(2,1)S(1)} collective-permute-done((bf16[2,128,768]{2,1,0:T(8,128)(2,1)S(1)}, bf16[2,128,768]{2,1,0:T(8,128)(2,1)S(1)}, u32[]{:S(2)}, u32[]{:S(2)}) %collective-permute-start) | collective-permute-done | bytes 393248 | tf_op jit(solution)/shard_map/ppermute | solution.py:519
  34.6 1.5 collective-permute-start.1
  36.1 1.2 broadcast_select_fusion.7
  40.4 13.6 %shard_map.254 = (bf16[512,768]{1,0:T(8,128)(2,1)S(1)}, bf16[512,768]{1,0:T(8,128)(2,1)S(1)}, bf16[2,256,768]{2,1,0:T(8,128)(2,1)S(1)}, bf16[2,256,768]{2,1,0:T(...) custom-call(s32[4]{0:T(128)S(1)} %pad_add_fusion.at, ...), custom_call_target="tpu_custom_call" | custom-call | flops 7247757312 | bytes 16777216 | tf_op jit(solution)/shard_map/pallas_call | solution.py:355
  59.8 1.2 multiply_cosine_fusion
  62.8 1.6 collective-permute-start.11
  66.2 10.5 %shard_map.255 = (bf16[2048,768]{1,0:T(8,128)(2,1)S(1)}, bf16[2048,768]{1,0:T(8,128)(2,1)S(1)}, bf16[1024,768]{1,0:T(8,128)(2,1)S(1)}, f32[24,2048]{1,0:T(8,128)...) custom-call(s32[4]{0:T(128)S(1)} %pad_add_fusion.at, ...), custom_call_target="tpu_custom_call" | custom-call | flops 1811939328 | bytes 12582912 | tf_op jit(solution)/shard_map/pallas_call | solution.py:161
  76.7 9.7 %shard_map.256 = (bf16[64,1024]{1,0:T(8,128)(2,1)S(1)}, bf16[64,1024]{1,0:T(8,128)(2,1)S(1)}, bf16[64,2048]{1,0:T(8,128)(2,1)S(1)}, bf16[64,2048]{1,0:T(8,128)(2,1)S(1)}) custom-call(bf16[192,1024]{1,0:T(8,128)(2,1)S(1)} %get-tuple-element.77.refs_0_.refs_2_, bf16[192,1024]{1,0:T(8,128)(2,1)S(1)} %get-tuple-element.78.refs_1_.refs_3_, ...), custom_call_target="tpu_custom_call" | custom-call | flops 5368709120 | bytes 2097152 | tf_op jit(solution)/shard_map/pallas_call | solution.py:259
  87.9 3.2 %collective-permute-done.11 = bf16[768,768]{1,0:T(8,128)(2,1)S(1)} collective-permute-done((bf16[768,768]{1,0:T(8,128)(2,1)}, bf16[768,768]{1,0:T(8,128)(2,1)S(1)}, u32[]{:S(2)}, u32[]{:S(2)}) %collective-permute-start.11) | collective-permute-done | bytes 1179680 | tf_op jit(solution)/shard_map/ppermute | solution.py:519
  91.4 9.9 %shard_map.257 = (bf16[64,1024]{1,0:T(8,128)(2,1)S(1)}, bf16[64,1024]{1,0:T(8,128)(2,1)S(1)}, bf16[64,2048]{1,0:T(8,128)(2,1)S(1)}, bf16[64,2048]{1,0:T(8,128)(2,1)S(1)}) custom-call(f32[2,2,128,768]{3,2,1,0:T(8,128)S(1)} %bitcast.154, f32[768,768]{1,0:T(8,128)S(1)} %convert_add_fusion.1.refs_1_, bf16[192,1024]{1,0:T(8,128)(2,1)S(1)} %get-tuple-element.77.refs_0_.refs_2_, ...), custom_call_target="tpu_custom_call" | custom-call | flops 5368709120 | bytes 2097152 | tf_op jit(solution)/shard_map/pallas_call | solution.py:259
  101.4 4.5 %collective-permute-done.13 = bf16[384,768]{1,0:T(8,128)(2,1)S(1)} collective-permute-done((bf16[384,768]{1,0:T(8,128)(2,1)S(1)}, bf16[384,768]{1,0:T(8,128)(2,1)S(1)}, u32[]{:S(2)}, u32[]{:S(2)}) %collective-permute-start.13) | collective-permute-done | bytes 589856 | tf_op jit(solution)/shard_map/ppermute | solution.py:519
  106.1 1.5 collective-permute-start.14
  107.6 9.7 %shard_map.258 = (bf16[64,1024]{1,0:T(8,128)(2,1)S(1)}, bf16[64,1024]{1,0:T(8,128)(2,1)S(1)}, bf16[64,2048]{1,0:T(8,128)(2,1)S(1)}, bf16[64,2048]{1,0:T(8,128)(2,1)S(1)}) custom-call(f32[2,128,768]{2,1,0:T(8,128)S(1)} %fusion.13.refs_0_, f32[384,768]{1,0:T(8,128)S(1)} %convert_add_fusion.7.refs_1_, bf16[192,1024]{1,0:T(8,128)(2,1)S(1)} %get-tuple-element.77.refs_0_.refs_2_, ...), custom_call_target="tpu_custom_call" | custom-call | flops 5368709120 | bytes 2097152 | tf_op jit(solution)/shard_map/pallas_call | solution.py:259
  117.3 3.3 %collective-permute-done.14 = bf16[192,768]{1,0:T(8,128)(2,1)S(1)} collective-permute-done((bf16[192,768]{1,0:T(8,128)(2,1)S(1)}, bf16[192,768]{1,0:T(8,128)(2,1)S(1)}, u32[]{:S(2)}, u32[]{:S(2)}) %collective-permute-start.14) | collective-permute-done | bytes 294944 | tf_op jit(solution)/shard_map/ppermute | solution.py:519
  121.4 3.3 %shard_map.259 = (bf16[2,256,768]{2,1,0:T(8,128)(2,1)S(1)}, bf16[2,256,768]{2,1,0:T(8,128)(2,1)}, f32[192,768]{1,0:T(8,128)S(1)}) custom-call(bf16[64,1024]{1,0:T(8,128)(2,1)S(1)} %get-tuple-element.82.refs_0_, bf16[64,1024]{1,0:T(8,128)(2,1)S(1)} %get-tuple-element.89.refs_1_, bf16[64,1024]{1,0:T(8,128)(2,1)S(1)} %get-tuple-element.92.refs_2_, ...), custom_call_target="tpu_custom_call" | custom-call | flops 603979776 | bytes 8388608 | tf_op jit(solution)/shard_map/pallas_call | solution.py:409
  128.3 1.9 copy-done.5
  130.2 1.9 copy-done.8
  137.8 4.9 %shard_map.260 = (bf16[2,256,768]{2,1,0:T(8,128)(2,1)S(1)}, bf16[2,256,768]{2,1,0:T(8,128)(2,1)S(1)}, f32[384,768]{1,0:T(8,128)S(1)}, f32[8,768]{1,0:T(8,128)S(1)}) custom-call(s32[4]{0:T(128)S(1)} %pad_add_fusion.at, bf16[64,2048]{1,0:T(8,128)(2,1)S(1)} %copy-done.17, bf16[64,2048]{1,0:T(8,128)(2,1)S(1)} %copy-done.21, bf16[64,2048]{1,0:T(8,128)(2,1)S(1)} %copy-done.26, ...), custom_call_target="tpu_custom_call" | custom-call | flops 1207959552 | bytes 10485760 | tf_op jit(solution)/shard_map/pallas_call | solution.py:503
  143.7 1.4 convert_add_fusion.4
  145.7 6.1 %shard_map.261 = (bf16[2,256,768]{2,1,0:T(8,128)(2,1)S(1)}, bf16[2,256,768]{2,1,0:T(8,128)(2,1)S(1)}, f32[832,384]{1,0:T(8,128)S(1)}, bf16[832,384]{1,0:T(8,128)(2,1)S(1)}) custom-call(s32[4]{0:T(128)S(1)} %pad_add_fusion.at, bf16[64,1024]{1,0:T(8,128)(2,1)S(1)} %copy-done.42, bf16[64,1024]{1,0:T(8,128)(2,1)S(1)} %copy-done.44, ...), custom_call_target="tpu_custom_call" | custom-call | flops 1811939328 | bytes 10485760 | tf_op jit(solution)/shard_map/pallas_call | solution.py:503
  152.8 1.6 collective-permute-start.16
  154.4 1.5 collective-permute-start.29
  156.1 3.7 %collective-permute-done.24 = bf16[192,768]{1,0:T(8,128)(2,1)S(1)} collective-permute-done((bf16[192,768]{1,0:T(8,128)(2,1)S(1)}, bf16[192,768]{1,0:T(8,128)(2,1)S(1)}, u32[]{:S(2)}, u32[]{:S(2)}) %collective-permute-start.24) | collective-permute-done | bytes 294944 | tf_op jit(solution)/shard_map/ppermute | solution.py:519
  160.0 4.2 %collective-permute-done.23 = bf16[2,128,768]{2,1,0:T(8,128)(2,1)S(1)} collective-permute-done((bf16[2,128,768]{2,1,0:T(8,128)(2,1)S(1)}, bf16[2,128,768]{2,1,0:T(8,128)(2,1)S(1)}, u32[]{:S(2)}, u32[]{:S(2)}) %collective-permute-start.23) | collective-permute-done | bytes 393248 | tf_op jit(solution)/shard_map/ppermute | solution.py:519
  164.2 2.6 %collective-permute-start.25 = (bf16[2,128,768]{2,1,0:T(8,128)(2,1)S(1)}, bf16[2,128,768]{2,1,0:T(8,128)(2,1)S(1)}, u32[]{:S(2)}, u32[]{:S(2)}) collective-permute-start(bf16[2,128,768]{2,1,0:T(8,128)(2,1)S(1)} %fusion.9), channel_id=1, source_target_pairs={{0,4},{4,0},{8,12},{12,8},{1,5},{5,1},{9,13},{13,9},{2,6},{6,2},{1... | collective-permute-start | bytes 1179656 | tf_op jit(solution)/shard_map/ppermute | solution.py:519
  167.5 5.1 %collective-permute-done.16 = bf16[2,128,768]{2,1,0:T(8,128)(2,1)S(1)} collective-permute-done((bf16[2,128,768]{2,1,0:T(8,128)(2,1)S(1)}, bf16[2,128,768]{2,1,0:T(8,128)(2,1)S(1)}, u32[]{:S(2)}, u32[]{:S(2)}) %collective-permute-start.16) | collective-permute-done | bytes 393248 | tf_op jit(solution)/shard_map/ppermute | solution.py:519
  172.7 2.3 collective-permute-start.18
  175.3 2.7 %collective-permute-start.30 = (bf16[208,384]{1,0:T(8,128)(2,1)S(1)}, bf16[208,384]{1,0:T(8,128)(2,1)S(1)}, u32[]{:S(2)}, u32[]{:S(2)}) collective-permute-start(bf16[208,384]{1,0:T(8,128)(2,1)S(1)} %get-tuple-element.153), channel_id=1, source_target_pairs={{0,12},{4,8},{8,4},{12,0},{1,13},{5,9},{9,5},{13,1},{2,14},{6,10},... | collective-permute-start | bytes 479240 | tf_op jit(solution)/shard_map/ppermute | solution.py:519
  177.9 8.3 %collective-permute-done.18 = bf16[128,768]{1,0:T(8,128)(2,1)S(1)} collective-permute-done((bf16[128,768]{1,0:T(8,128)(2,1)S(1)}, bf16[128,768]{1,0:T(8,128)(2,1)S(1)}, u32[]{:S(2)}, u32[]{:S(2)}) %collective-permute-start.18) | collective-permute-done | bytes 196640 | tf_op jit(solution)/shard_map/ppermute | solution.py:519
  186.3 3.4 %collective-permute-start.31 = (bf16[208,384]{1,0:T(8,128)(2,1)S(1)}, bf16[208,384]{1,0:T(8,128)(2,1)S(1)}, u32[]{:S(2)}, u32[]{:S(2)}) collective-permute-start(bf16[208,384]{1,0:T(8,128)(2,1)S(1)} %get-tuple-element.155), channel_id=1, source_target_pairs={{0,8},{4,12},{8,0},{12,4},{1,9},{5,13},{9,1},{13,5},{2,10},{6,14},... | collective-permute-start | bytes 479240 | tf_op jit(solution)/shard_map/ppermute | solution.py:519
  189.8 1.5 collective-permute-done.25
  192.0 2.3 collective-permute-start.26
  194.3 7.6 %collective-permute-done.31 = bf16[208,384]{1,0:T(8,128)(2,1)S(1)} collective-permute-done((bf16[208,384]{1,0:T(8,128)(2,1)S(1)}, bf16[208,384]{1,0:T(8,128)(2,1)S(1)}, u32[]{:S(2)}, u32[]{:S(2)}) %collective-permute-start.31) | collective-permute-done | bytes 159776 | tf_op jit(solution)/shard_map/ppermute | solution.py:519
  202.1 7.4 %collective-permute-done.26 = bf16[128,768]{1,0:T(8,128)(2,1)S(1)} collective-permute-done((bf16[128,768]{1,0:T(8,128)(2,1)S(1)}, bf16[128,768]{1,0:T(8,128)(2,1)S(1)}, u32[]{:S(2)}, u32[]{:S(2)}) %collective-permute-start.26) | collective-permute-done | bytes 196640 | tf_op jit(solution)/shard_map/ppermute | solution.py:519
  211.5 1.4 collective-permute-done.33
  217.0 5.6 %collective-permute-done.34 = bf16[2,208,384]{2,1,0:T(8,128)(2,1)S(1)} collective-permute-done((bf16[2,208,384]{2,1,0:T(8,128)(2,1)S(1)}, bf16[2,208,384]{2,1,0:T(8,128)(2,1)S(1)}, u32[]{:S(2)}, u32[]{:S(2)}) %collective-permute-start.34) | collective-permute-done | bytes 319520 | tf_op jit(solution)/shard_map/ppermute | solution.py:519
  226.5 1.4 reshape_squeeze.3
  227.9 2.2 slice.192
  232.4 1.3 broadcast_select_fusion.25
  234.5 2.1 add_add_fusion
  237.3 1.3 copy-done.3
  238.6 2.0 convert_add_fusion
  (287 shorter events, 49.7 us)
Async XLA Ops:
  0.6 10.0 %copy-start.62 = (bf16[384,3,192]{0,2,1:T(8,128)(2,1)S(1)}, bf16[384,3,192]{0,2,1:T(8,128)(2,1)}, u32[]{:S(2)}) copy-start(bf16[384,3,192]{0,2,1:T(8,128)(2,1)} %param.17) | copy-start | bytes 1327108
  0.7 10.0 %copy-start.65 = (bf16[192,384]{1,0:T(8,128)(2,1)S(1)}, bf16[192,384]{1,0:T(8,128)(2,1)}, u32[]{:S(2)}) copy-start(bf16[192,384]{1,0:T(8,128)(2,1)} %param.19) | copy-start | bytes 442372
  0.7 35.5 %collective-permute-start.3 = (bf16[768,384]{1,0:T(8,128)(2,1)}, bf16[768,384]{1,0:T(8,128)(2,1)}, u32[]{:S(2)}, u32[]{:S(2)}) collective-permute-start(bf16[768,384]{1,0:T(8,128)(2,1)} %param.23), channel_id=1, source_target_pairs={{0,16},{16,0},{1,17},{17,1},{2,18},{18,2},{3,19},{19,3},{4,20},{20... | collective-permute-start | bytes 1769480 | tf_op jit(solution)/shard_map/ppermute | solution.py:519
  3.7 33.6 %collective-permute-start.2 = (bf16[384,768]{1,0:T(8,128)(2,1)}, bf16[384,768]{1,0:T(8,128)(2,1)}, u32[]{:S(2)}, u32[]{:S(2)}) collective-permute-start(bf16[384,768]{1,0:T(8,128)(2,1)} %param.21), channel_id=1, source_target_pairs={{0,16},{16,0},{1,17},{17,1},{2,18},{18,2},{3,19},{19,3},{4,20},{20... | collective-permute-start | bytes 1769480 | tf_op jit(solution)/shard_map/ppermute | solution.py:519
  4.8 15.7 %copy-start.55 = (bf16[1,128,768]{2,1,0:T(8,128)(2,1)}, bf16[1,128,768]{2,1,0:T(8,128)(2,1)S(1)}, u32[]{:S(2)}) copy-start(bf16[1,128,768]{2,1,0:T(8,128)(2,1)S(1)} %get-tuple-element.152) | copy-start | bytes 589828
  4.9 15.7 %copy-start.58 = (bf16[1,128,768]{2,1,0:T(8,128)(2,1)}, bf16[1,128,768]{2,1,0:T(8,128)(2,1)S(1)}, u32[]{:S(2)}) copy-start(bf16[1,128,768]{2,1,0:T(8,128)(2,1)S(1)} %get-tuple-element.151) | copy-start | bytes 589828
  4.9 7.4 %collective-permute-start.5 = (bf16[1,128,768]{2,1,0:T(8,128)(2,1)S(1)}, bf16[1,128,768]{2,1,0:T(8,128)(2,1)S(1)}, u32[]{:S(2)}, u32[]{:S(2)}) collective-permute-start(bf16[1,128,768]{2,1,0:T(8,128)(2,1)S(1)} %get-tuple-element.151), channel_id=1, source_target_pairs={{0,4},{4,0},{8,12},{12,8},{1,5},{5,1},{9,13},{13,9},{2,6},{6,2},{1... | collective-permute-start | bytes 589832 | tf_op jit(solution)/shard_map/ppermute | solution.py:519
  6.9 29.2 %copy-start.66 = (bf16[768,384]{1,0:T(8,128)(2,1)S(1)}, bf16[768,384]{1,0:T(8,128)(2,1)}, u32[]{:S(2)}) copy-start(bf16[768,384]{1,0:T(8,128)(2,1)} %param.23) | copy-start | bytes 1769476
  6.9 12.7 %collective-permute-start.6 = (bf16[1,128,768]{2,1,0:T(8,128)(2,1)S(1)}, bf16[1,128,768]{2,1,0:T(8,128)(2,1)}, u32[]{:S(2)}, u32[]{:S(2)}) collective-permute-start(bf16[1,128,768]{2,1,0:T(8,128)(2,1)S(1)} %get-tuple-element.152), channel_id=1, source_target_pairs={{0,12},{4,8},{8,4},{12,0},{1,13},{5,9},{9,5},{13,1},{2,14},{6,10},... | collective-permute-start | bytes 589832 | tf_op jit(solution)/shard_map/ppermute | solution.py:519
  10.4 24.2 %collective-permute-start = (bf16[2,128,768]{2,1,0:T(8,128)(2,1)S(1)}, bf16[2,128,768]{2,1,0:T(8,128)(2,1)S(1)}, u32[]{:S(2)}, u32[]{:S(2)}) collective-permute-start(bf16[2,128,768]{2,1,0:T(8,128)(2,1)S(1)} %pad_maximum_fusion.13), channel_id=1, source_target_pairs={{0,8},{4,12},{8,0},{12,4},{1,9},{5,13},{9,1},{13,5},{2,10},{6,14},... | collective-permute-start | bytes 1179656 | tf_op jit(solution)/shard_map/ppermute | solution.py:519
  11.5 48.2 %copy-start.71 = (f32[2,2048]{1,0:T(2,128)}, f32[2,2048]{1,0:T(2,128)S(1)}, u32[]{:S(2)}) copy-start(f32[2,2048]{1,0:T(2,128)S(1)} %convert_element_type.171) | copy-start | bytes 49156
  11.6 25.7 %copy-start.67 = (bf16[384,768]{1,0:T(8,128)(2,1)S(1)}, bf16[384,768]{1,0:T(8,128)(2,1)}, u32[]{:S(2)}) copy-start(bf16[384,768]{1,0:T(8,128)(2,1)} %param.21) | copy-start | bytes 1769476
  13.0 49.8 %collective-permute-start.9 = (bf16[768,384]{1,0:T(8,128)(2,1)}, bf16[768,384]{1,0:T(8,128)(2,1)S(1)}, u32[]{:S(2)}, u32[]{:S(2)}) collective-permute-start(bf16[768,384]{1,0:T(8,128)(2,1)} %pad_maximum_fusion.11), channel_id=1, source_target_pairs={{0,16},{16,0},{1,17},{17,1},{2,18},{18,2},{3,19},{19,3},{4,20},{20... | collective-permute-start | bytes 1769480 | tf_op jit(solution)/shard_map/ppermute | solution.py:519
  20.6 36.6 %collective-permute-start.7 = (bf16[2,128,768]{2,1,0:T(8,128)(2,1)S(1)}, bf16[2,128,768]{2,1,0:T(8,128)(2,1)S(1)}, u32[]{:S(2)}, u32[]{:S(2)}) collective-permute-start(bf16[2,128,768]{2,1,0:T(8,128)(2,1)S(1)} %constant_dynamic-update-slice_fusion.nz), channel_id=1, source_target_pairs={{0,2},{1,3},{2,0},{3,1},{4,6},{5,7},{6,4},{7,5},{8,10},{9,11},{10,... | collective-permute-start | bytes 1179656 | tf_op jit(solution)/shard_map/ppermute | solution.py:519
  34.6 23.6 %collective-permute-start.1 = (bf16[2,128,768]{2,1,0:T(8,128)(2,1)S(1)}, bf16[2,128,768]{2,1,0:T(8,128)(2,1)S(1)}, u32[]{:S(2)}, u32[]{:S(2)}) collective-permute-start(bf16[2,128,768]{2,1,0:T(8,128)(2,1)S(1)} %collective-permute-done.fz), channel_id=1, source_target_pairs={{0,2},{1,3},{2,0},{3,1},{4,6},{5,7},{6,4},{7,5},{8,10},{9,11},{10,... | collective-permute-start | bytes 1179656 | tf_op jit(solution)/shard_map/ppermute | solution.py:519
  58.2 6.5 %collective-permute-start.8 = (bf16[2,2,128,768]{3,2,1,0:T(8,128)(2,1)}, bf16[2,2,128,768]{3,2,1,0:T(8,128)(2,1)}, u32[]{:S(2)}, u32[]{:S(2)}) collective-permute-start(bf16[2,2,128,768]{3,2,1,0:T(8,128)(2,1)} %pad_maximum_fusion.7), channel_id=1, source_target_pairs={{0,1},{1,0},{2,3},{3,2},{4,5},{5,4},{6,7},{7,6},{8,9},{9,8},{10,11... | collective-permute-start | bytes 2359304 | tf_op jit(solution)/shard_map/ppermute | solution.py:519
  59.4 5.3 %collective-permute-start.4 = (bf16[2,2,128,768]{3,2,1,0:T(8,128)(2,1)}, bf16[2,2,128,768]{3,2,1,0:T(8,128)(2,1)}, u32[]{:S(2)}, u32[]{:S(2)}) collective-permute-start(bf16[2,2,128,768]{3,2,1,0:T(8,128)(2,1)} %pad_maximum_fusion.6), channel_id=1, source_target_pairs={{0,1},{1,0},{2,3},{3,2},{4,5},{5,4},{6,7},{7,6},{8,9},{9,8},{10,11... | collective-permute-start | bytes 2359304 | tf_op jit(solution)/shard_map/ppermute | solution.py:519
  62.8 28.3 %collective-permute-start.11 = (bf16[768,768]{1,0:T(8,128)(2,1)}, bf16[768,768]{1,0:T(8,128)(2,1)S(1)}, u32[]{:S(2)}, u32[]{:S(2)}) collective-permute-start(bf16[768,768]{1,0:T(8,128)(2,1)} %get-tuple-element.87), channel_id=1, source_target_pairs={{0,16},{16,0},{1,17},{17,1},{2,18},{18,2},{3,19},{19,3},{4,20},{20... | collective-permute-start | bytes 3538952 | tf_op jit(solution)/shard_map/ppermute | solution.py:519
  64.3 22.1 %collective-permute-start.10 = (bf16[2,256,768]{2,1,0:T(8,128)(2,1)}, bf16[2,256,768]{2,1,0:T(8,128)(2,1)S(1)}, u32[]{:S(2)}, u32[]{:S(2)}) collective-permute-start(bf16[2,256,768]{2,1,0:T(8,128)(2,1)} %get-tuple-element.84), channel_id=1, source_target_pairs={{0,1},{1,0},{2,3},{3,2},{4,5},{5,4},{6,7},{7,6},{8,9},{9,8},{10,11... | collective-permute-start | bytes 2359304 | tf_op jit(solution)/shard_map/ppermute | solution.py:519
  76.7 9.8 %copy-start.34 = (bf16[2,256,768]{2,1,0:T(8,128)(2,1)S(1)}, bf16[2,256,768]{2,1,0:T(8,128)(2,1)}, u32[]{:S(2)}) copy-start(bf16[2,256,768]{2,1,0:T(8,128)(2,1)} %copy-done.33) | copy-start | bytes 2359300
  87.3 14.0 %collective-permute-start.12 = (bf16[2,128,768]{2,1,0:T(8,128)(2,1)S(1)}, bf16[2,128,768]{2,1,0:T(8,128)(2,1)S(1)}, u32[]{:S(2)}, u32[]{:S(2)}) collective-permute-start(bf16[2,128,768]{2,1,0:T(8,128)(2,1)S(1)} %fusion.18), channel_id=1, source_target_pairs={{0,2},{1,3},{2,0},{3,1},{4,6},{5,7},{6,4},{7,5},{8,10},{9,11},{10,... | collective-permute-start | bytes 1179656 | tf_op jit(solution)/shard_map/ppermute | solution.py:519
  91.3 14.6 %collective-permute-start.13 = (bf16[384,768]{1,0:T(8,128)(2,1)S(1)}, bf16[384,768]{1,0:T(8,128)(2,1)S(1)}, u32[]{:S(2)}, u32[]{:S(2)}) collective-permute-start(bf16[384,768]{1,0:T(8,128)(2,1)S(1)} %dynamic-slice_convert_fusion), channel_id=1, source_target_pairs={{0,4},{4,0},{8,12},{12,8},{1,5},{5,1},{9,13},{13,9},{2,6},{6,2},{1... | collective-permute-start | bytes 1769480 | tf_op jit(solution)/shard_map/ppermute | solution.py:519
  106.1 14.6 %collective-permute-start.14 = (bf16[192,768]{1,0:T(8,128)(2,1)S(1)}, bf16[192,768]{1,0:T(8,128)(2,1)S(1)}, u32[]{:S(2)}, u32[]{:S(2)}) collective-permute-start(bf16[192,768]{1,0:T(8,128)(2,1)S(1)} %dynamic-slice_convert_fusion.1), channel_id=1, source_target_pairs={{0,8},{4,12},{8,0},{12,4},{1,9},{5,13},{9,1},{13,5},{2,10},{6,14},... | collective-permute-start | bytes 884744 | tf_op jit(solution)/shard_map/ppermute | solution.py:519
  126.5 17.2 %collective-permute-start.15 = (bf16[2,256,768]{2,1,0:T(8,128)(2,1)}, bf16[2,256,768]{2,1,0:T(8,128)(2,1)}, u32[]{:S(2)}, u32[]{:S(2)}) collective-permute-start(bf16[2,256,768]{2,1,0:T(8,128)(2,1)} %get-tuple-element.98), channel_id=1, source_target_pairs={{0,1},{1,0},{2,3},{3,2},{4,5},{5,4},{6,7},{7,6},{8,9},{9,8},{10,11... | collective-permute-start | bytes 2359304 | tf_op jit(solution)/shard_map/ppermute | solution.py:519
  128.3 88.5 %copy-start.72 = (f32[2,128]{1,0:T(2,128)}, f32[2,128]{1,0:T(2,128)S(1)}, u32[]{:S(2)}) copy-start(f32[2,128]{1,0:T(2,128)S(1)} %broadcast_multiply_fusion.2) | copy-start | bytes 3076
  142.7 9.3 %collective-permute-start.22 = (bf16[2,256,768]{2,1,0:T(8,128)(2,1)S(1)}, bf16[2,256,768]{2,1,0:T(8,128)(2,1)S(1)}, u32[]{:S(2)}, u32[]{:S(2)}) collective-permute-start(bf16[2,256,768]{2,1,0:T(8,128)(2,1)S(1)} %get-tuple-element.120), channel_id=1, source_target_pairs={{0,1},{1,0},{2,3},{3,2},{4,5},{5,4},{6,7},{7,6},{8,9},{9,8},{10,11... | collective-permute-start | bytes 2359304 | tf_op jit(solution)/shard_map/ppermute | solution.py:519
  143.6 73.1 %copy-start.74 = (f32[2,128]{1,0:T(2,128)}, f32[2,128]{1,0:T(2,128)S(1)}, u32[]{:S(2)}) copy-start(f32[2,128]{1,0:T(2,128)S(1)} %add_rsqrt_fusion) | copy-start | bytes 3076
  143.6 16.2 %collective-permute-start.24 = (bf16[192,768]{1,0:T(8,128)(2,1)S(1)}, bf16[192,768]{1,0:T(8,128)(2,1)S(1)}, u32[]{:S(2)}, u32[]{:S(2)}) collective-permute-start(bf16[192,768]{1,0:T(8,128)(2,1)S(1)} %copy-done.61), channel_id=1, source_target_pairs={{0,8},{4,12},{8,0},{12,4},{1,9},{5,13},{9,1},{13,5},{2,10},{6,14},... | collective-permute-start | bytes 884744 | tf_op jit(solution)/shard_map/ppermute | solution.py:519
  151.9 4.0 %collective-permute-start.17 = (bf16[2,256,768]{2,1,0:T(8,128)(2,1)S(1)}, bf16[2,256,768]{2,1,0:T(8,128)(2,1)S(1)}, u32[]{:S(2)}, u32[]{:S(2)}) collective-permute-start(bf16[2,256,768]{2,1,0:T(8,128)(2,1)S(1)} %get-tuple-element.117), channel_id=1, source_target_pairs={{0,1},{1,0},{2,3},{3,2},{4,5},{5,4},{6,7},{7,6},{8,9},{9,8},{10,11... | collective-permute-start | bytes 2359304 | tf_op jit(solution)/shard_map/ppermute | solution.py:519
  152.2 12.0 %collective-permute-start.23 = (bf16[2,128,768]{2,1,0:T(8,128)(2,1)S(1)}, bf16[2,128,768]{2,1,0:T(8,128)(2,1)S(1)}, u32[]{:S(2)}, u32[]{:S(2)}) collective-permute-start(bf16[2,128,768]{2,1,0:T(8,128)(2,1)S(1)} %fusion.21), channel_id=1, source_target_pairs={{0,2},{1,3},{2,0},{3,1},{4,6},{5,7},{6,4},{7,5},{8,10},{9,11},{10,... | collective-permute-start | bytes 1179656 | tf_op jit(solution)/shard_map/ppermute | solution.py:519
  152.8 19.8 %collective-permute-start.16 = (bf16[2,128,768]{2,1,0:T(8,128)(2,1)S(1)}, bf16[2,128,768]{2,1,0:T(8,128)(2,1)S(1)}, u32[]{:S(2)}, u32[]{:S(2)}) collective-permute-start(bf16[2,128,768]{2,1,0:T(8,128)(2,1)S(1)} %fusion.19), channel_id=1, source_target_pairs={{0,2},{1,3},{2,0},{3,1},{4,6},{5,7},{6,4},{7,5},{8,10},{9,11},{10,... | collective-permute-start | bytes 1179656 | tf_op jit(solution)/shard_map/ppermute | solution.py:519
  154.4 20.6 %collective-permute-start.29 = (bf16[832,384]{1,0:T(8,128)(2,1)S(1)}, bf16[832,384]{1,0:T(8,128)(2,1)S(1)}, u32[]{:S(2)}, u32[]{:S(2)}) collective-permute-start(bf16[832,384]{1,0:T(8,128)(2,1)S(1)} %get-tuple-element.125), channel_id=1, source_target_pairs={{0,16},{16,0},{1,17},{17,1},{2,18},{18,2},{3,19},{19,3},{4,20},{20... | collective-permute-start | bytes 1916936 | tf_op jit(solution)/shard_map/ppermute | solution.py:519
  159.9 51.7 %collective-permute-start.37 = (bf16[2,192,768]{2,1,0:T(8,128)(2,1)S(1)}, bf16[2,192,768]{2,1,0:T(8,128)(2,1)S(1)}, u32[]{:S(2)}, u32[]{:S(2)}) collective-permute-start(bf16[2,192,768]{2,1,0:T(8,128)(2,1)S(1)} %pad_maximum_fusion.12), channel_id=1, source_target_pairs={{0,4},{4,0},{8,12},{12,8},{1,5},{5,1},{9,13},{13,9},{2,6},{6,2},{1... | collective-permute-start | bytes 1769480 | tf_op jit(solution)/shard_map/ppermute | solution.py:519
  164.2 27.1 %collective-permute-start.25 = (bf16[2,128,768]{2,1,0:T(8,128)(2,1)S(1)}, bf16[2,128,768]{2,1,0:T(8,128)(2,1)S(1)}, u32[]{:S(2)}, u32[]{:S(2)}) collective-permute-start(bf16[2,128,768]{2,1,0:T(8,128)(2,1)S(1)} %fusion.9), channel_id=1, source_target_pairs={{0,4},{4,0},{8,12},{12,8},{1,5},{5,1},{9,13},{13,9},{2,6},{6,2},{1... | collective-permute-start | bytes 1179656 | tf_op jit(solution)/shard_map/ppermute | solution.py:519
  166.9 24.4 %collective-permute-start.21 = (bf16[2,128,768]{2,1,0:T(8,128)(2,1)S(1)}, bf16[2,128,768]{2,1,0:T(8,128)(2,1)S(1)}, u32[]{:S(2)}, u32[]{:S(2)}) collective-permute-start(bf16[2,128,768]{2,1,0:T(8,128)(2,1)S(1)} %fusion.20), channel_id=1, source_target_pairs={{0,2},{1,3},{2,0},{3,1},{4,6},{5,7},{6,4},{7,5},{8,10},{9,11},{10,... | collective-permute-start | bytes 1179656 | tf_op jit(solution)/shard_map/ppermute | solution.py:519
  172.7 13.6 %collective-permute-start.18 = (bf16[128,768]{1,0:T(8,128)(2,1)S(1)}, bf16[128,768]{1,0:T(8,128)(2,1)S(1)}, u32[]{:S(2)}, u32[]{:S(2)}) collective-permute-start(bf16[128,768]{1,0:T(8,128)(2,1)S(1)} %get-tuple-element.181), channel_id=1, source_target_pairs={{0,8},{4,12},{8,0},{12,4},{1,9},{5,13},{9,1},{13,5},{2,10},{6,14},... | collective-permute-start | bytes 589832 | tf_op jit(solution)/shard_map/ppermute | solution.py:519
  175.3 16.8 %collective-permute-start.30 = (bf16[208,384]{1,0:T(8,128)(2,1)S(1)}, bf16[208,384]{1,0:T(8,128)(2,1)S(1)}, u32[]{:S(2)}, u32[]{:S(2)}) collective-permute-start(bf16[208,384]{1,0:T(8,128)(2,1)S(1)} %get-tuple-element.153), channel_id=1, source_target_pairs={{0,12},{4,8},{8,4},{12,0},{1,13},{5,9},{9,5},{13,1},{2,14},{6,10},... | collective-permute-start | bytes 479240 | tf_op jit(solution)/shard_map/ppermute | solution.py:519
  186.3 15.6 %collective-permute-start.31 = (bf16[208,384]{1,0:T(8,128)(2,1)S(1)}, bf16[208,384]{1,0:T(8,128)(2,1)S(1)}, u32[]{:S(2)}, u32[]{:S(2)}) collective-permute-start(bf16[208,384]{1,0:T(8,128)(2,1)S(1)} %get-tuple-element.155), channel_id=1, source_target_pairs={{0,8},{4,12},{8,0},{12,4},{1,9},{5,13},{9,1},{13,5},{2,10},{6,14},... | collective-permute-start | bytes 479240 | tf_op jit(solution)/shard_map/ppermute | solution.py:519
  191.3 10.6 %collective-permute-start.32 = (bf16[208,384]{1,0:T(8,128)(2,1)S(1)}, bf16[208,384]{1,0:T(8,128)(2,1)S(1)}, u32[]{:S(2)}, u32[]{:S(2)}) collective-permute-start(bf16[208,384]{1,0:T(8,128)(2,1)S(1)} %get-tuple-element.154), channel_id=1, source_target_pairs={{0,4},{4,0},{8,12},{12,8},{1,5},{5,1},{9,13},{13,9},{2,6},{6,2},{1... | collective-permute-start | bytes 479240 | tf_op jit(solution)/shard_map/ppermute | solution.py:519
  191.3 22.1 %collective-permute-start.19 = (bf16[2,128,768]{2,1,0:T(8,128)(2,1)S(1)}, bf16[2,128,768]{2,1,0:T(8,128)(2,1)S(1)}, u32[]{:S(2)}, u32[]{:S(2)}) collective-permute-start(bf16[2,128,768]{2,1,0:T(8,128)(2,1)S(1)} %pad_maximum_fusion.15), channel_id=1, source_target_pairs={{0,2},{1,3},{2,0},{3,1},{4,6},{5,7},{6,4},{7,5},{8,10},{9,11},{10,... | collective-permute-start | bytes 1179656 | tf_op jit(solution)/shard_map/ppermute | solution.py:519
  192.0 17.5 %collective-permute-start.26 = (bf16[128,768]{1,0:T(8,128)(2,1)S(1)}, bf16[128,768]{1,0:T(8,128)(2,1)S(1)}, u32[]{:S(2)}, u32[]{:S(2)}) collective-permute-start(bf16[128,768]{1,0:T(8,128)(2,1)S(1)} %fusion.28), channel_id=1, source_target_pairs={{0,8},{4,12},{8,0},{12,4},{1,9},{5,13},{9,1},{13,5},{2,10},{6,14},... | collective-permute-start | bytes 589832 | tf_op jit(solution)/shard_map/ppermute | solution.py:519
  202.0 11.0 %collective-permute-start.33 = (bf16[208,384]{1,0:T(8,128)(2,1)S(1)}, bf16[208,384]{1,0:T(8,128)(2,1)S(1)}, u32[]{:S(2)}, u32[]{:S(2)}) collective-permute-start(bf16[208,384]{1,0:T(8,128)(2,1)S(1)} %add_convert_fusion), channel_id=1, source_target_pairs={{0,8},{4,12},{8,0},{12,4},{1,9},{5,13},{9,1},{13,5},{2,10},{6,14},... | collective-permute-start | bytes 479240 | tf_op jit(solution)/shard_map/ppermute | solution.py:519
  211.0 21.1 %collective-permute-start.27 = (bf16[2,128,768]{2,1,0:T(8,128)(2,1)}, bf16[2,128,768]{2,1,0:T(8,128)(2,1)S(1)}, u32[]{:S(2)}, u32[]{:S(2)}) collective-permute-start(bf16[2,128,768]{2,1,0:T(8,128)(2,1)} %fusion.7), channel_id=1, source_target_pairs={{0,2},{1,3},{2,0},{3,1},{4,6},{5,7},{6,4},{7,5},{8,10},{9,11},{10,... | collective-permute-start | bytes 1179656 | tf_op jit(solution)/shard_map/ppermute | solution.py:519
  213.0 9.6 %collective-permute-start.34 = (bf16[2,208,384]{2,1,0:T(8,128)(2,1)S(1)}, bf16[2,208,384]{2,1,0:T(8,128)(2,1)S(1)}, u32[]{:S(2)}, u32[]{:S(2)}) collective-permute-start(bf16[2,208,384]{2,1,0:T(8,128)(2,1)S(1)} %pad_maximum_fusion.17), channel_id=1, source_target_pairs={{0,4},{4,0},{8,12},{12,8},{1,5},{5,1},{9,13},{13,9},{2,6},{6,2},{1... | collective-permute-start | bytes 958472 | tf_op jit(solution)/shard_map/ppermute | solution.py:519
  214.4 18.0 %collective-permute-start.20 = (bf16[2,2,128,768]{3,2,1,0:T(8,128)(2,1)}, bf16[2,2,128,768]{3,2,1,0:T(8,128)(2,1)}, u32[]{:S(2)}, u32[]{:S(2)}) collective-permute-start(bf16[2,2,128,768]{3,2,1,0:T(8,128)(2,1)} %pad_maximum_fusion.8), channel_id=1, source_target_pairs={{0,1},{1,0},{2,3},{3,2},{4,5},{5,4},{6,7},{7,6},{8,9},{9,8},{10,11... | collective-permute-start | bytes 2359304 | tf_op jit(solution)/shard_map/ppermute | solution.py:519
  222.8 1.3 collective-permute-start.35
  224.6 6.0 %collective-permute-start.36 = (f32[8,768]{1,0:T(8,128)}, f32[8,768]{1,0:T(8,128)}, u32[]{:S(2)}, u32[]{:S(2)}) collective-permute-start(f32[8,768]{1,0:T(8,128)} %fusion.34), channel_id=1, source_target_pairs={{0,2},{1,3},{2,0},{3,1},{4,6},{5,7},{6,4},{7,5},{8,10},{9,11},{10,... | collective-permute-start | bytes 73736 | tf_op jit(solution)/shard_map/ppermute | solution.py:519
  232.1 4.4 %collective-permute-start.28 = (bf16[2,2,128,768]{3,2,1,0:T(8,128)(2,1)S(1)}, bf16[2,2,128,768]{3,2,1,0:T(8,128)(2,1)S(1)}, u32[]{:S(2)}, u32[]{:S(2)}) collective-permute-start(bf16[2,2,128,768]{3,2,1,0:T(8,128)(2,1)S(1)} %pad_maximum_fusion.10), channel_id=1, source_target_pairs={{0,1},{1,0},{2,3},{3,2},{4,5},{5,4},{6,7},{7,6},{8,9},{9,8},{10,11... | collective-permute-start | bytes 2359304 | tf_op jit(solution)/shard_map/ppermute | solution.py:519
  (73 other events, 249.1 us)

commit v8 on v3

--- a/solution.py
+++ b/solution.py
@@ -51,7 +51,7 @@
 
 
 def norm_own_kernel(at, xa, xb, ga, gb, fz, fx, fc, ta, tb, s1, b1, s2, b2,
-                    n1_ref, n2_ref, xhat_ref, g_ref, trig_ref, x):
+                    n1_ref, n2_ref, g_ref, trig_ref, x):
     i = pl.program_id(0)
     q = xa.shape[1]
 
@@ -79,12 +79,11 @@
     trig_ref[:, :q] = ta[0]
     trig_ref[:, q:] = tb[0]
     xhat, _ = xhat_of(x[...].astype(F32))
-    xhat_ref[...] = xhat.astype(BF16)
     n1_ref[...] = (xhat * row_of(s1) + row_of(b1)).astype(BF16)
     n2_ref[...] = (xhat * row_of(s2) + row_of(b2)).astype(BF16)
 
 
-def norm_other_kernel(at, nz, nx, nc, ta, tb, s1, b1, n1_ref, xhat_ref, trig_ref, x):
+def norm_other_kernel(at, nz, nx, nc, ta, tb, s1, b1, n1_ref, trig_ref, x):
     i = pl.program_id(0)
     q = nz.shape[1]
     b = i // 2
@@ -102,7 +101,6 @@
     trig_ref[:, :q] = ta[0]
     trig_ref[:, q:] = tb[0]
     xhat, _ = xhat_of(x[...].astype(F32))
-    xhat_ref[...] = xhat.astype(BF16)
     n1_ref[...] = (xhat * row_of(s1) + row_of(b1)).astype(BF16)
 
 
@@ -133,10 +131,10 @@
         x, g, received = arrays[0], arrays[1], arrays[2:]
         specs = [piece(0), piece(2), piece(0), piece(2)]
         operands = [x, x, g, g]
-        kernel, count = norm_own_kernel, 4
+        kernel, count = norm_own_kernel, 3
     else:
         received, specs, operands = arrays, [], []
-        kernel, count = norm_other_kernel, 2
+        kernel, count = norm_other_kernel, 1
     specs += [whole(v) for v in received] + [pick(0), pick(2)] + [whole(v) for v in vectors]
     operands += [*received, trig, trig, *vectors]
     return pl.pallas_call(
@@ -328,7 +326,7 @@
     )(after, qt, dot, kt, vt, trig_own, trig_own, trig_other)
 
 
-def forward_kernel(split, at, n2_ref, g_ref, xhat_ref, up_ref, bias_ref, down_ref, s2_ref,
+def forward_kernel(split, at, n2_ref, g_ref, up_ref, bias_ref, down_ref, s2_ref, b2_ref,
                    ff_ref, a_ref, small_ref, first_ref, second_ref, *scratch):
     i = pl.program_id(0)
     up_part, down_part = scratch if split else (first_ref, second_ref)
@@ -352,8 +350,13 @@
     a_ref[...] = (second * row_of(s2_ref)).astype(BF16)
     small_ref[0:1, :] += jnp.sum(up_grad.astype(F32), axis=0, keepdims=True)
     small_ref[1:2, :] += jnp.sum(g.astype(F32), axis=0, keepdims=True)
-    small_ref[2:3, :] += jnp.sum(second * xhat_ref[...].astype(F32), axis=0, keepdims=True)
+    small_ref[2:3, :] += jnp.sum(second * n2.astype(F32), axis=0, keepdims=True)
     small_ref[3:4, :] += jnp.sum(second, axis=0, keepdims=True)
+
+    @pl.when(i == pl.num_programs(0) - 1)
+    def _():
+        rest = small_ref[2:3, :] - row_of(b2_ref) * small_ref[3:4, :]
+        small_ref[2:3, :] = rest / row_of(s2_ref)
 
     if split:
         half = up_part.shape[0] // 2
@@ -367,7 +370,7 @@
                 ref[half:, half:] = down_part[half:, piece].astype(ref.dtype)
 
 
-def feed_forward(split, at, n2, g, xhat, up, bias, down, scale):
+def feed_forward(split, at, n2, g, up, bias, down, scale, offset):
     rows, width = n2.shape
     hidden = up.shape[1]
     row = pl.BlockSpec((STEP, width), lambda i, at: (i, 0))
@@ -385,8 +388,8 @@
         grid_spec=pltpu.PrefetchScalarGridSpec(
             num_scalar_prefetch=1,
             grid=(rows // STEP,),
-            in_specs=[row, row, row, whole(width, hidden), whole(hidden), whole(hidden, width),
-                      whole(width)],
+            in_specs=[row, row, whole(width, hidden), whole(hidden), whole(hidden, width),
+                      whole(width), whole(width)],
             out_specs=[row, row, whole(8, width)] + [whole(*p.shape) for p in parts],
             scratch_shapes=[pltpu.VMEM((width, hidden), F32), pltpu.VMEM((hidden, width), F32)]
             if split
@@ -395,7 +398,7 @@
         out_shape=[low_shape(rows, width)] * 2 + [shape(8, width)] + parts,
         compiler_params=params(40),
         cost_estimate=cost(12 * rows * width * hidden, 16 * MIB, 2 * rows * hidden),
-    )(at, n2, g, xhat, up, bias, down, scale)
+    )(at, n2, g, up, bias, down, scale, offset)
 
 
 def emit(keep_ref, send_ref, v):
@@ -445,9 +448,9 @@
 def back_kernel(own, split, heads, at, *refs):
     count = 3 if own else 2
     grads, refs = refs[: count * heads], refs[count * heads :]
-    n1_ref, xhat_ref, w_ref, s1_ref, *refs = refs
+    n1_ref, w_ref, s1_ref, *refs = refs
     if own:
-        (a2_ref, small_ff, small_other, mix_other, out_part, after,
+        (a2_ref, b1_ref, small_ff, small_other, mix_other, out_part,
          keep_ref, send_ref, first_ref, second_ref, mix, small) = refs
     else:
         keep_ref, send_ref, mix, small = refs
@@ -470,7 +473,7 @@
     a = first * row_of(s1_ref)
     emit(keep_ref, send_ref, a + a2_ref[...].astype(F32) if own else a)
     mix[...] += mm(grad, n1_ref[...])
-    small[0:1, :] += jnp.sum(first * xhat_ref[...].astype(F32), axis=0, keepdims=True)
+    small[0:1, :] += jnp.sum(first * n1_ref[...].astype(F32), axis=0, keepdims=True)
     small[1:2, :] += jnp.sum(first, axis=0, keepdims=True)
     ones = jnp.ones((8, grad.shape[1]), BF16)
     small[6:7, 3 * wide - tall : 3 * wide] += mm(ones, grad, 1, 1)[0:1]
@@ -478,6 +481,8 @@
     if own:
         @pl.when(i == pl.num_programs(0) - 1)
         def _():
+            rest = small[0:1, :] - row_of(b1_ref) * small[1:2, :]
+            small[0:1, :] = rest / row_of(s1_ref)
             small[2:4, :] = small_ff[2:4, :]
             small[4:6, :] = small_ff[0:2, :]
             if split:
@@ -496,7 +501,7 @@
                 second_ref[...] = small[...]
 
 
-def back(own, split, at, grads, n1, xhat, weights, scale, extra):
+def back(own, split, at, grads, n1, weights, scale, extra):
     rows, width = n1.shape
     heads = len(grads[0])
     wide = heads * HEAD
@@ -510,13 +515,13 @@
         return pl.BlockSpec(dims, lambda i, at: (0,) * len(dims))
 
     half = width // 2
-    specs = [col] * (len(grads) * heads) + [row, row, whole(4 * wide, width), whole(width)]
+    specs = [col] * (len(grads) * heads) + [row, whole(4 * wide, width), whole(width)]
     if not own:
         parts = [shape(tall, width), shape(8, width)]
         scratch = []
     else:
-        specs += [row, whole(8, width), whole(8, width), whole(2 * wide, width),
-                  whole(wide, width), pl.BlockSpec(memory_space=pl.ANY)]
+        specs += [row, whole(width), whole(8, width), whole(8, width), whole(2 * wide, width),
+                  whole(wide, width)]
         scratch = [pltpu.VMEM((tall, width), F32), pltpu.VMEM((8, width), F32)]
         if split:
             parts = [shape(4 * wide + 64, half), low_shape(4 * wide + 64, half)]
@@ -534,7 +539,7 @@
         out_shape=[low_shape(2, STEP, width)] * 2 + parts,
         compiler_params=params(32),
         cost_estimate=cost(4 * rows * width * tall, 10 * MIB),
-    )(at, *[v for vs in grads for v in vs], n1, xhat, weights, scale, *extra)
+    )(at, *[v for vs in grads for v in vs], n1, weights, scale, *extra)
 
 
 def swap(v, axis, size, distance):
@@ -572,22 +577,39 @@
     ).astype(F32)
 
 
-def halve(v, distance, bit):
+def halve(v, distance, bit, *earlier):
     rows = v.shape[0] // 2
     keep = lax.dynamic_slice_in_dim(v, bit * rows, rows, 0)
     send = lax.dynamic_slice_in_dim(v, (1 - bit) * rows, rows, 0).astype(BF16)
-    return keep + swap(send, "ctx", 4, distance).astype(F32)
-
-
-def double(v, c):
+    return keep + tie(swap(send, "ctx", 4, distance), *earlier).astype(F32)
+
+
+def quarter_sum(v, c, *earlier):
+    rows = v.shape[0] // 4
+    mine = 2 * (c % 2) + c // 2
+
+    def part(j):
+        return lax.dynamic_slice_in_dim(v, (mine ^ j) * rows, rows, 0)
+
+    total = part(0)
+    for distance, j in ((3, 3), (2, 1), (1, 2)):
+        sent = swap(part(j).astype(BF16), "ctx", 4, distance)
+        total = total + tie(sent, *earlier).astype(F32)
+    return total
+
+
+def pair_up(v, *earlier):
     v = v.astype(BF16)
-    pair = jnp.stack([v, swap(v, "ctx", 4, 2)])
-    others = swap(pair, "ctx", 4, 1)
+    return jnp.stack([v, tie(swap(v, "ctx", 4, 2), *earlier)])
+
+
+def double(pair, c, *earlier):
+    others = tie(swap(pair, "ctx", 4, 1), *earlier)
     return by_xor([pair[0], pair[1], others[0], others[1]], 2 * (c % 2) + c // 2)
 
 
 def sum_over_ctx(v, c):
-    return double(halve(halve(v, 1, c % 2), 2, c // 2), c)
+    return double(pair_up(quarter_sum(v, c)), c)
 
 
 def butterfly(v, axis_name, size):
@@ -637,15 +659,10 @@
     x_mine, x_theirs = my_quarter(inputs, s), my_quarter(inputs, 1 - s)
     g_theirs = my_quarter(cotangent, 1 - s)
     far_z = swap(jnp.concatenate([x_theirs, g_theirs], axis=0), "ctx", 4, 2)
-    cross = swap(x_theirs, "ctx", 4, 3)
+    cross = swap(tie(x_theirs, far_z), "ctx", 4, 3)
     near = swap(x_mine, "ctx", 4, 1)
-
-    def over_tp(v):
-        v_x = swap(v, "tp", 4, 2)
-        return v, v_x, swap(jnp.stack([v, v_x]), "tp", 4, 1)
-
-    far = over_tp(far_z)
-    others = over_tp(jnp.concatenate([near, cross], axis=0))
+    far_x = swap(far_z, "tp", 4, 2)
+    far = (far_z, far_x, swap(jnp.stack([far_z, far_x]), "tp", 4, 1))
 
     wup = gather_halves(up_projection_weight, fsdp, f, 0)
     wdown = gather_halves(down_projection_weight, fsdp, f, 1)
@@ -659,53 +676,59 @@
         [jnp.cos(angles), jnp.sin(angles), jnp.broadcast_to(places, angles.shape)], axis=1
     )
 
-    n1_own, n2, xhat_own, g, trig_own = norms(
+    n1_own, n2, g, trig_own = norms(
         at, True, (inputs, cotangent, *far), trig,
         (first_scale, first_shift, second_scale, second_shift),
     )
+    others_z = jnp.concatenate([tie(near, n2), tie(cross, n2)], axis=0)
+    others_x = swap(others_z, "tp", 4, 2)
     ff, a2, small_ff, ff_first, ff_second = feed_forward(
-        split, at, n2, g, xhat_own, wup, up_projection_bias, wdown, second_scale
+        split, at, n2, g, wup, up_projection_bias, wdown, second_scale, second_shift
     )
     weights = gather_halves(mix_out_shard, fsdp, f, 1, small_ff)
-    n1_other, xhat_other, trig_other = norms(
-        at, False, (others[0], others[1], tie(others[2], small_ff)), trig,
-        (first_scale, first_shift),
-    )
+    others_x = tie(others_x, small_ff)
+    others = (others_z, others_x, swap(jnp.stack([others_z, others_x]), "tp", 4, 1))
+    n1_other, trig_other = norms(at, False, others, trig, (first_scale, first_shift))
     kt, vt, qt, dot = project(
         n1_own, n1_other, trig_own, trig_other, g, weights, query_key_value_bias
     )
-    if split:
-        ff_rest = ff_first + swap(ff_second, "fsdp", 2, 1).astype(F32)
-    else:
-        ff_rest = small_ff
     per_head = []
+    after = small_ff
     for h in range(heads):
-        after = ff_rest if h == heads - 1 else small_ff
+        if split and h == heads - 1:
+            after = tie(swap(ff_second, "fsdp", 2, 1), per_head[h - 1][0])
+            after = ff_first + after.astype(F32)
         per_head.append(attention(h, after, qt, dot, kt, vt, trig_own, trig_other))
     o, dq, dk, dv = zip(*per_head)
+    ff_half = halve(after, 1, c % 2, o[-1]) if split else after
+
+    def over_core(keep, send, *earlier):
+        v = keep.astype(F32) + tie(swap(send, "tp", 4, 1), *earlier).astype(F32)
+        return v.reshape(2, 2, quarter, width)
+
+    def over_x(v, *earlier):
+        return v[:, 0] + tie(swap(v[:, 1].astype(BF16), "tp", 4, 2), *earlier).astype(F32)
+
     keep_b, send_b, out_part = branch(o, g, ff, weights)
+    keep_o, send_o, mix_other, small_other = back(
+        False, split, at, (dk, dv), n1_other, weights, tie(first_scale, keep_b, ff_half), ()
+    )
+    half_b = over_core(keep_b, send_b)
+    keep_w, send_w, late_first, late_second = back(
+        True, split, at, (dq, dk, dv), n1_own, weights, tie(first_scale, half_b),
+        (a2, first_shift, small_ff, small_other, mix_other, out_part),
+    )
+    half_o = over_core(keep_o, send_o)
+    half_w = over_core(keep_w, send_w)
     if split:
-        ff_half = halve(ff_rest, 1, c % 2)
+        ff_pair = pair_up(halve(ff_half, 2, c // 2, keep_w), half_w)
     else:
-        ff_half = small_ff
-    keep_o, send_o, mix_other, small_other = back(
-        False, split, at, (dk, dv), n1_other, xhat_other, weights, first_scale, ()
-    )
-    keep_w, send_w, late_first, late_second = back(
-        True, split, at, (dq, dk, dv), n1_own, xhat_own, weights, first_scale,
-        (a2, small_ff, small_other, mix_other, out_part, ff_half),
-    )
-
-    def scatter_tp(keep, send):
-        v = keep.astype(F32) + swap(send, "tp", 4, 1).astype(F32)
-        v = v.reshape(2, 2, quarter, width)
-        return v[:, 0] + swap(v[:, 1].astype(BF16), "tp", 4, 2).astype(F32)
-
-    def over_ctx(v, distance):
-        return swap(v.astype(BF16), "ctx", 4, distance).astype(F32)
-
-    def gather_tp(mine, theirs):
-        ours = jnp.stack([mine, theirs]).astype(BF16)
+        ff_pair = half_w
+
+    def over_ctx(v, distance, *earlier):
+        return tie(swap(v.astype(BF16), "ctx", 4, distance), *earlier).astype(F32)
+
+    def gather_tp(ours):
         pair = jnp.stack([ours, swap(ours, "tp", 4, 2)])
         core = swap(pair, "tp", 4, 1)
         pieces = by_xor((pair[0], core[0], pair[1], core[1]), t)
@@ -713,35 +736,36 @@
         return jnp.stack([jnp.where(s == 0, pieces[0], pieces[1]),
                           jnp.where(s == 0, pieces[1], pieces[0])]).astype(F32)
 
-    sums_b = scatter_tp(keep_b, send_b)
-    block_out = gather_tp(sums_b[0], over_ctx(sums_b[1], 2))
+    sums_b = over_x(half_b, half_w)
+    branches = jnp.stack([sums_b[0], over_ctx(sums_b[1], 2)]).astype(BF16)
+    block_out = gather_tp(branches)
     block_out = (
         inputs.astype(F32) + block_out + (attention_output_bias + down_projection_bias)
     )
 
-    sums_o = scatter_tp(keep_o, send_o)
-    sums_w = scatter_tp(keep_w, send_w)
-    a = jnp.stack([
-        sums_w[0] + over_ctx(sums_o[0], 1),
-        over_ctx(sums_w[1], 2) + over_ctx(sums_o[1], 3),
-    ])
+    sums_o = over_x(half_o, ff_pair)
+    sums_w = over_x(half_w)
+    sums_w = sums_w + over_ctx(sums_o, 1)
+    a = jnp.stack([sums_w[0], over_ctx(sums_w[1], 2, branches)])
     xhat, inv = xhat_of(jnp.concatenate([x_mine, x_theirs], axis=0).astype(F32))
     norm_grad = inv * (
         a
         - jnp.mean(a, axis=-1, keepdims=True)
         - xhat * jnp.mean(a * xhat, axis=-1, keepdims=True)
     )
-    inputs_grad = cotangent.astype(F32) + gather_tp(norm_grad[0], norm_grad[1])
+    norm_grad = norm_grad.astype(BF16)
+    inputs_grad = cotangent.astype(F32) + gather_tp(norm_grad)
 
     if split:
-        q = double(halve(ff_half, 2, c // 2), c)
+        q = double(ff_pair, c, norm_grad)
         up_total = jnp.concatenate(q[:2], axis=0).astype(F32)
         down_total = jnp.concatenate(q[2:], axis=0).astype(F32)
         down_total = jnp.concatenate(
             [down_total[:, : width // 2], down_total[:, width // 2 :]], axis=0
         )
-        late = late_first + swap(late_second, "fsdp", 2, 1).astype(F32)
-        late = jnp.concatenate(sum_over_ctx(late, c), axis=0).astype(F32)
+        late = late_first + tie(swap(late_second, "fsdp", 2, 1), sums_o).astype(F32)
+        late = double(pair_up(quarter_sum(late, c, sums_w), norm_grad), c)
+        late = jnp.concatenate(late, axis=0).astype(F32)
         small = jnp.concatenate([late[4 * local : 4 * local + 8], late[4 * local + 8 :][:8]], axis=1)
     else:
         q = sum_over_ctx(scatter_any(ff_first, 0), c)

time: 230 us -> 252 us (1.096)
  local copies, waits for them, and re-layouts: 10.7 us -> 24.3 us
  other arithmetic: 28.3 us -> 40.8 us
  waiting for transfers between devices: 85.9 us -> 82.1 us
  starting transfers between devices: 40.6 us -> 37.3 us
  Pallas kernels: 62.4 us -> 65.3 us
    unnamed x100 -> x160, local copies, waits for them, and re-layouts: 4.59 us -> 16.5 us
    add x10, other arithmetic: 3.37 us -> 7.52 us  [the longest x1 2 us: shards(): inputs_grad = cotangent.astype(F32) + gather_tp(norm_grad)]
    ppermute x36, waiting for transfers between devices: 85.9 us -> 82.1 us  [swap(): return lax.ppermute(v, axis, [(i, i ^ distance) for i in range(size)])]
    ppermute x36, starting transfers between devices: 40.6 us -> 37.3 us  [swap(): return lax.ppermute(v, axis, [(i, i ^ distance) for i in range(size)])]
  transfers between devices with their start and end apart: 36 -> 36, of which waited for: 12 -> 11; matrix products, arithmetic and copies ran while one was open for 13% -> 16% of each run, Pallas kernels for 27% -> 22%
where the time goes in v8:
time: 252 us
  waiting for transfers between devices  82.1 us (33%)
  Pallas kernels  65.3 us (26%)
  other arithmetic  40.8 us (16%)
  starting transfers between devices  37.3 us (15%)
  local copies, waits for them, and re-layouts  24.3 us (10%)
    ppermute x36, waiting for transfers between devices, swap(): return lax.ppermute(v, axis, [(i, i ^ distance) for i in range(size)])  82.1 us
    ppermute x36, starting transfers between devices, swap(): return lax.ppermute(v, axis, [(i, i ^ distance) for i in range(size)])  37.3 us
    pallas_call x3, Pallas kernels, attention(): pl.pallas_call(attention_kernel, grid=(rows // lanes,), in_specs=[pl.Bloc...  29 us
    unnamed x160, local copies, waits for them, and re-layouts  16.5 us
    pallas_call x2, Pallas kernels, back(): pl.pallas_call(functools.partial(back_kernel, own, split, heads), grid_sp...  11 us
    pallas_call x1, Pallas kernels, feed_forward(): pl.pallas_call(functools.partial(forward_kernel, split), grid_spec=pltpu....  10.6 us
    pallas_call x2, Pallas kernels, norms(): pl.pallas_call(kernel, grid_spec=pltpu.PrefetchScalarGridSpec(num_scalar_...  6.96 us
  transfers between devices with their start and end apart: 36, of which 11 were waited for; matrix products, arithmetic and copies ran while one was open for 16% of the time, Pallas kernels for 22%

profile of v8, /device:TPU:0, one launch (start us, length us, event | category | flops | bytes accessed | tf_op | source)
XLA Modules:
  0.0 251.6 jit_solution(9060298902767016071)
XLA Ops:
  1.8 1.8 constant_dynamic-slice_fusion
  4.6 4.1 %collective-permute-start = (bf16[2,128,768]{2,1,0:T(8,128)(2,1)S(1)}, bf16[2,128,768]{2,1,0:T(8,128)(2,1)S(1)}, u32[]{:S(2)}, u32[]{:S(2)}) collective-permute-start(bf16[2,128,768]{2,1,0:T(8,128)(2,1)S(1)} %pad_maximum_fusion.13), channel_id=1, source_target_pairs={{0,8},{4,12},{8,0},{12,4},{1,9},{5,13},{9,1},{13,5},{2,10},{6,14},... | collective-permute-start | bytes 1179656 | tf_op jit(solution)/shard_map/ppermute | solution.py:546
  8.7 1.5 collective-permute-start.4
  11.6 1.5 collective-permute-start.9
  13.1 1.6 collective-permute-start.5
  14.7 11.5 %collective-permute-done.fz = bf16[2,128,768]{2,1,0:T(8,128)(2,1)S(1)} collective-permute-done((bf16[2,128,768]{2,1,0:T(8,128)(2,1)S(1)}, bf16[2,128,768]{2,1,0:T(8,128)(2,1)S(1)}, u32[]{:S(2)}, u32[]{:S(2)}) %collective-permute-start) | collective-permute-done | bytes 393248 | tf_op jit(solution)/shard_map/ppermute | solution.py:546
  26.3 1.5 collective-permute-start.1
  28.4 8.1 %collective-permute-done.1.fx = bf16[2,128,768]{2,1,0:T(8,128)(2,1)S(1)} collective-permute-done((bf16[2,128,768]{2,1,0:T(8,128)(2,1)S(1)}, bf16[2,128,768]{2,1,0:T(8,128)(2,1)S(1)}, u32[]{:S(2)}, u32[]{:S(2)}) %collective-permute-start.1) | collective-permute-done | bytes 393248 | tf_op jit(solution)/shard_map/ppermute | solution.py:546
  37.6 4.3 %collective-permute-start.6 = (bf16[1,128,768]{2,1,0:T(8,128)(2,1)}, bf16[1,128,768]{2,1,0:T(8,128)(2,1)S(1)}, u32[]{:S(2)}, u32[]{:S(2)}) collective-permute-start(bf16[1,128,768]{2,1,0:T(8,128)(2,1)} %get-tuple-element.77), channel_id=1, source_target_pairs={{0,12},{4,8},{8,4},{12,0},{1,13},{5,9},{9,5},{13,1},{2,14},{6,10},... | collective-permute-start | bytes 589832 | tf_op jit(solution)/shard_map/ppermute | solution.py:546
  45.3 3.7 %shard_map.254 = (bf16[1024,768]{1,0:T(8,128)(2,1)S(1)}, bf16[1024,768]{1,0:T(8,128)(2,1)S(1)}, bf16[1024,768]{1,0:T(8,128)(2,1)S(1)}, f32[24,1024]{1,0:T(8,128)S(1)}) custom-call(s32[4]{0:T(128)S(1)} %pad_add_fusion.at, bf16[2,512,768]{2,1,0:T(8,128)(2,1)S(1)} %copy-done, bf16[2,512,768]{2,1,0:T(8,128)(2,1)S(1)} %copy-done, ...), custom_call_target="tpu_custom_call" | custom-call | bytes 4718592 | tf_op jit(solution)/shard_map/pallas_call | solution.py:140
  51.9 1.6 collective-permute-start.7
  53.5 10.6 %shard_map.255 = (bf16[1024,768]{1,0:T(8,128)(2,1)S(1)}, bf16[1024,768]{1,0:T(8,128)(2,1)S(1)}, f32[8,768]{1,0:T(8,128)S(1)}, f32[768,768]{1,0:T(8,128)S(1)}, bf16[768,768]{1,0:T(8,128)(2,1)}) custom-call(s32[4]{0:T(128)S(1)} %pad_add_fusion.at, bf16[1024,768]{1,0:T(8,128)(2,1)S(1)} %get-tuple-element.72.n2_ref, ...), custom_call_target="tpu_custom_call" | custom-call | flops 7247757312 | bytes 16777216 | tf_op jit(solution)/shard_map/pallas_call | solution.py:386
  64.1 1.4 copy-done.7
  70.7 1.6 collective-permute-start.10
  72.3 1.5 broadcast_select_fusion.5
  75.1 3.3 %shard_map.256 = (bf16[1024,768]{1,0:T(8,128)(2,1)S(1)}, f32[24,1024]{1,0:T(8,128)S(1)}) custom-call(s32[4]{0:T(128)S(1)} %pad_add_fusion.at, bf16[2,128,768]{2,1,0:T(8,128)(2,1)S(1)} %copy-done.6, bf16[2,128,768]{2,1,0:T(8,128)(2,1)S(1)} %copy-done.23, bf16[2,2,128,768]{3,2,1,0:T(8,128)(2,1)} %collective-permute-done.8.nc, ...), custom_call_target="tpu_custom_call" | custom-call | bytes 4718592 | tf_op jit(solution)/shard_map/pallas_call | solution.py:140
  78.4 4.4 %shard_map.257 = (bf16[192,2048]{1,0:T(8,128)(2,1)S(1)}, bf16[192,2048]{1,0:T(8,128)(2,1)S(1)}, bf16[192,1024]{1,0:T(8,128)(2,1)S(1)}, bf16[192,1024]{1,0:T(8,128)(2,1)S(1)}) custom-call(bf16[1024,768]{1,0:T(8,128)(2,1)S(1)} %copy-done.14, bf16[1024,768]{1,0:T(8,128)(2,1)S(1)} %get-tuple-element.80.n1x.refs_6_, f32[24,1024]{1,0:T(8,128)S(1)} %copy-done.52, ...), custom_call_target="tpu_custom_call" | custom-call | flops 1811939328 | bytes 9437184 | tf_op jit(solution)/shard_map/pallas_call | solution.py:204
  82.8 9.7 %shard_map.259 = (bf16[64,1024]{1,0:T(8,128)(2,1)S(1)}, bf16[64,1024]{1,0:T(8,128)(2,1)S(1)}, bf16[64,2048]{1,0:T(8,128)(2,1)S(1)}, bf16[64,2048]{1,0:T(8,128)(2,1)S(1)}) custom-call(f32[8,768]{1,0:T(8,128)S(1)} %copy-done.45, bf16[192,1024]{1,0:T(8,128)(2,1)S(1)} %get-tuple-element.84.q_ref, bf16[192,1024]{1,0:T(8,128)(2,1)S(1)} %get-tuple-element.85.do_ref, ...), custom_call_target="tpu_custom_call" | custom-call | flops 5368709120 | bytes 2097152 | tf_op jit(solution)/shard_map/pallas_call | solution.py:307
  93.2 6.2 %collective-permute-done.10 = bf16[768,768]{1,0:T(8,128)(2,1)} collective-permute-done((bf16[768,768]{1,0:T(8,128)(2,1)}, bf16[768,768]{1,0:T(8,128)(2,1)}, u32[]{:S(2)}, u32[]{:S(2)}) %collective-permute-start.10) | collective-permute-done | bytes 1179680 | tf_op jit(solution)/shard_map/ppermute | solution.py:546
  99.4 1.6 convert_add_fusion.1.after
  101.1 9.7 %shard_map.260 = (bf16[64,1024]{1,0:T(8,128)(2,1)S(1)}, bf16[64,1024]{1,0:T(8,128)(2,1)S(1)}, bf16[64,2048]{1,0:T(8,128)(2,1)S(1)}, bf16[64,2048]{1,0:T(8,128)(2,1)S(1)}) custom-call(f32[768,768]{1,0:T(8,128)S(1)} %convert_add_fusion.1.after, bf16[192,1024]{1,0:T(8,128)(2,1)S(1)} %get-tuple-element.84.q_ref, bf16[192,1024]{1,0:T(8,128)(2,1)S(1)} %get-tuple-element.85.do_ref, ...), custom_call_target="tpu_custom_call" | custom-call | flops 5368709120 | bytes 2097152 | tf_op jit(solution)/shard_map/pallas_call | solution.py:307
  112.5 9.7 %shard_map.258 = (bf16[64,1024]{1,0:T(8,128)(2,1)S(1)}, bf16[64,1024]{1,0:T(8,128)(2,1)S(1)}, bf16[64,2048]{1,0:T(8,128)(2,1)S(1)}, bf16[64,2048]{1,0:T(8,128)(2,1)S(1)}) custom-call(f32[8,768]{1,0:T(8,128)S(1)} %copy-done.45, bf16[192,1024]{1,0:T(8,128)(2,1)S(1)} %get-tuple-element.84.q_ref, bf16[192,1024]{1,0:T(8,128)(2,1)S(1)} %get-tuple-element.85.do_ref, ...), custom_call_target="tpu_custom_call" | custom-call | flops 5368709120 | bytes 2097152 | tf_op jit(solution)/shard_map/pallas_call | solution.py:307
  122.2 3.3 %shard_map.261 = (bf16[2,256,768]{2,1,0:T(8,128)(2,1)S(1)}, bf16[2,256,768]{2,1,0:T(8,128)(2,1)}, f32[192,768]{1,0:T(8,128)S(1)}) custom-call(bf16[64,1024]{1,0:T(8,128)(2,1)S(1)} %get-tuple-element.88.refs_0_, bf16[64,1024]{1,0:T(8,128)(2,1)S(1)} %get-tuple-element.89.refs_1_, bf16[64,1024]{1,0:T(8,128)(2,1)S(1)} %get-tuple-element.93.refs_2_, ...), custom_call_target="tpu_custom_call" | custom-call | flops 603979776 | bytes 8388608 | tf_op jit(solution)/shard_map/pallas_call | solution.py:436
  127.2 1.8 fusion.8
  131.1 1.7 convert_add_fusion.6
  135.3 4.8 %shard_map.262 = (bf16[2,256,768]{2,1,0:T(8,128)(2,1)S(1)}, bf16[2,256,768]{2,1,0:T(8,128)(2,1)S(1)}, f32[384,768]{1,0:T(8,128)S(1)}, f32[8,768]{1,0:T(8,128)S(1)}) custom-call(s32[4]{0:T(128)S(1)} %pad_add_fusion.at, bf16[64,2048]{1,0:T(8,128)(2,1)S(1)} %copy-done.35, bf16[64,2048]{1,0:T(8,128)(2,1)S(1)} %get-tuple-element.101.refs_1_.refs_4_, ...), custom_call_target="tpu_custom_call" | custom-call | flops 1207959552 | bytes 10485760 | tf_op jit(solution)/shard_map/pallas_call | solution.py:530
  140.5 1.4 convert_add_fusion.4
  142.3 6.1 %shard_map.263 = (bf16[2,256,768]{2,1,0:T(8,128)(2,1)S(1)}, bf16[2,256,768]{2,1,0:T(8,128)(2,1)S(1)}, f32[832,384]{1,0:T(8,128)S(1)}, bf16[832,384]{1,0:T(8,128)(2,1)S(1)}) custom-call(s32[4]{0:T(128)S(1)} %pad_add_fusion.at, bf16[64,1024]{1,0:T(8,128)(2,1)S(1)} %copy-done.41, bf16[64,1024]{1,0:T(8,128)(2,1)S(1)} %get-tuple-element.98.refs_1_, ...), custom_call_target="tpu_custom_call" | custom-call | flops 1811939328 | bytes 10485760 | tf_op jit(solution)/shard_map/pallas_call | solution.py:530
  149.3 1.5 collective-permute-start.27
  150.9 2.1 collective-permute-start.22
  153.2 1.6 collective-permute-start.20
  154.9 11.9 %collective-permute-done.22 = bf16[192,768]{1,0:T(8,128)(2,1)S(1)} collective-permute-done((bf16[192,768]{1,0:T(8,128)(2,1)S(1)}, bf16[192,768]{1,0:T(8,128)(2,1)S(1)}, u32[]{:S(2)}, u32[]{:S(2)}) %collective-permute-start.22) | collective-permute-done | bytes 294944 | tf_op jit(solution)/shard_map/ppermute | solution.py:546
  166.9 1.6 collective-permute-start.18
  168.7 3.5 %collective-permute-start.35 = (bf16[2,192,768]{2,1,0:T(8,128)(2,1)S(1)}, bf16[2,192,768]{2,1,0:T(8,128)(2,1)S(1)}, u32[]{:S(2)}, u32[]{:S(2)}) collective-permute-start(bf16[2,192,768]{2,1,0:T(8,128)(2,1)S(1)} %pad_maximum_fusion.12), channel_id=1, source_target_pairs={{0,4},{4,0},{8,12},{12,8},{1,5},{5,1},{9,13},{13,9},{2,6},{6,2},{1... | collective-permute-start | bytes 1769480 | tf_op jit(solution)/shard_map/ppermute | solution.py:546
  172.6 1.5 collective-permute-start.28
  174.2 6.6 %collective-permute-done.15 = bf16[128,768]{1,0:T(8,128)(2,1)S(1)} collective-permute-done((bf16[128,768]{1,0:T(8,128)(2,1)S(1)}, bf16[128,768]{1,0:T(8,128)(2,1)S(1)}, u32[]{:S(2)}, u32[]{:S(2)}) %collective-permute-start.15) | collective-permute-done | bytes 196640 | tf_op jit(solution)/shard_map/ppermute | solution.py:546
  181.3 23.3 %collective-permute-done.23 = bf16[2,128,768]{2,1,0:T(8,128)(2,1)S(1)} collective-permute-done((bf16[2,128,768]{2,1,0:T(8,128)(2,1)S(1)}, bf16[2,128,768]{2,1,0:T(8,128)(2,1)S(1)}, u32[]{:S(2)}, u32[]{:S(2)}) %collective-permute-start.23) | collective-permute-done | bytes 393248 | tf_op jit(solution)/shard_map/ppermute | solution.py:546
  206.2 1.8 collective-permute-done.30
  209.4 3.8 %collective-permute-done.16 = bf16[2,128,768]{2,1,0:T(8,128)(2,1)S(1)} collective-permute-done((bf16[2,128,768]{2,1,0:T(8,128)(2,1)S(1)}, bf16[2,128,768]{2,1,0:T(8,128)(2,1)S(1)}, u32[]{:S(2)}, u32[]{:S(2)}) %collective-permute-start.16) | collective-permute-done | bytes 393248 | tf_op jit(solution)/shard_map/ppermute | solution.py:546
  214.3 5.4 %collective-permute-done.24 = bf16[128,768]{1,0:T(8,128)(2,1)S(1)} collective-permute-done((bf16[128,768]{1,0:T(8,128)(2,1)S(1)}, bf16[128,768]{1,0:T(8,128)(2,1)S(1)}, u32[]{:S(2)}, u32[]{:S(2)}) %collective-permute-start.24) | collective-permute-done | bytes 196640 | tf_op jit(solution)/shard_map/ppermute | solution.py:546
  219.8 1.5 fusion.16
  221.3 2.1 fusion.7
  226.5 2.0 fusion.15
  228.6 3.4 %collective-permute-done.32 = bf16[2,208,384]{2,1,0:T(8,128)(2,1)S(1)} collective-permute-done((bf16[2,208,384]{2,1,0:T(8,128)(2,1)S(1)}, bf16[2,208,384]{2,1,0:T(8,128)(2,1)S(1)}, u32[]{:S(2)}, u32[]{:S(2)}) %collective-permute-start.32) | collective-permute-done | bytes 319520 | tf_op jit(solution)/shard_map/ppermute | solution.py:546
  237.5 2.2 slice.171
  245.1 2.1 add_add_fusion
  247.3 1.6 broadcast_select_fusion.21
  249.0 2.0 convert_add_fusion
  (273 shorter events, 48.4 us)
Async XLA Ops:
  0.7 10.0 %copy-start.59 = (bf16[384,3,192]{0,2,1:T(8,128)(2,1)S(1)}, bf16[384,3,192]{0,2,1:T(8,128)(2,1)}, u32[]{:S(2)}) copy-start(bf16[384,3,192]{0,2,1:T(8,128)(2,1)} %param.17) | copy-start | bytes 1327108
  0.7 14.0 %copy-start.77 = (s32[2,2048]{1,0:T(2,128)S(1)}, s32[2,2048]{1,0:T(2,128)}, u32[]{:S(2)}) copy-start(s32[2,2048]{1,0:T(2,128)} %param.16) | copy-start | bytes 49156
  4.6 21.7 %collective-permute-start = (bf16[2,128,768]{2,1,0:T(8,128)(2,1)S(1)}, bf16[2,128,768]{2,1,0:T(8,128)(2,1)S(1)}, u32[]{:S(2)}, u32[]{:S(2)}) collective-permute-start(bf16[2,128,768]{2,1,0:T(8,128)(2,1)S(1)} %pad_maximum_fusion.13), channel_id=1, source_target_pairs={{0,8},{4,12},{8,0},{12,4},{1,9},{5,13},{9,1},{13,5},{2,10},{6,14},... | collective-permute-start | bytes 1179656 | tf_op jit(solution)/shard_map/ppermute | solution.py:546
  8.7 28.9 %collective-permute-start.4 = (bf16[768,384]{1,0:T(8,128)(2,1)S(1)}, bf16[768,384]{1,0:T(8,128)(2,1)}, u32[]{:S(2)}, u32[]{:S(2)}) collective-permute-start(bf16[768,384]{1,0:T(8,128)(2,1)S(1)} %copy-done.66), channel_id=1, source_target_pairs={{0,16},{16,0},{1,17},{17,1},{2,18},{18,2},{3,19},{19,3},{4,20},{20... | collective-permute-start | bytes 1769480 | tf_op jit(solution)/shard_map/ppermute | solution.py:546
  10.2 32.9 %collective-permute-start.3 = (bf16[384,768]{1,0:T(8,128)(2,1)S(1)}, bf16[384,768]{1,0:T(8,128)(2,1)S(1)}, u32[]{:S(2)}, u32[]{:S(2)}) collective-permute-start(bf16[384,768]{1,0:T(8,128)(2,1)S(1)} %copy-done.67), channel_id=1, source_target_pairs={{0,16},{16,0},{1,17},{17,1},{2,18},{18,2},{3,19},{19,3},{4,20},{20... | collective-permute-start | bytes 1769480 | tf_op jit(solution)/shard_map/ppermute | solution.py:546
  11.6 60.7 %collective-permute-start.9 = (bf16[768,384]{1,0:T(8,128)(2,1)}, bf16[768,384]{1,0:T(8,128)(2,1)}, u32[]{:S(2)}, u32[]{:S(2)}) collective-permute-start(bf16[768,384]{1,0:T(8,128)(2,1)} %pad_maximum_fusion.11), channel_id=1, source_target_pairs={{0,16},{16,0},{1,17},{17,1},{2,18},{18,2},{3,19},{19,3},{4,20},{20... | collective-permute-start | bytes 1769480 | tf_op jit(solution)/shard_map/ppermute | solution.py:546
  13.1 37.6 %collective-permute-start.5 = (bf16[1,128,768]{2,1,0:T(8,128)(2,1)}, bf16[1,128,768]{2,1,0:T(8,128)(2,1)}, u32[]{:S(2)}, u32[]{:S(2)}) collective-permute-start(bf16[1,128,768]{2,1,0:T(8,128)(2,1)} %get-tuple-element.149), channel_id=1, source_target_pairs={{0,4},{4,0},{8,12},{12,8},{1,5},{5,1},{9,13},{13,9},{2,6},{6,2},{1... | collective-permute-start | bytes 589832 | tf_op jit(solution)/shard_map/ppermute | solution.py:546
  26.3 16.8 %copy-start.9 = (bf16[2,128,768]{2,1,0:T(8,128)(2,1)}, bf16[2,128,768]{2,1,0:T(8,128)(2,1)S(1)}, u32[]{:S(2)}) copy-start(bf16[2,128,768]{2,1,0:T(8,128)(2,1)S(1)} %collective-permute-done.fz) | copy-start | bytes 1179652
  26.3 10.2 %collective-permute-start.1 = (bf16[2,128,768]{2,1,0:T(8,128)(2,1)S(1)}, bf16[2,128,768]{2,1,0:T(8,128)(2,1)S(1)}, u32[]{:S(2)}, u32[]{:S(2)}) collective-permute-start(bf16[2,128,768]{2,1,0:T(8,128)(2,1)S(1)} %collective-permute-done.fz), channel_id=1, source_target_pairs={{0,2},{1,3},{2,0},{3,1},{4,6},{5,7},{6,4},{7,5},{8,10},{9,11},{10,... | collective-permute-start | bytes 1179656 | tf_op jit(solution)/shard_map/ppermute | solution.py:546
  37.5 6.0 %collective-permute-start.2 = (bf16[2,2,128,768]{3,2,1,0:T(8,128)(2,1)}, bf16[2,2,128,768]{3,2,1,0:T(8,128)(2,1)}, u32[]{:S(2)}, u32[]{:S(2)}) collective-permute-start(bf16[2,2,128,768]{3,2,1,0:T(8,128)(2,1)} %pad_maximum_fusion.6), channel_id=1, source_target_pairs={{0,1},{1,0},{2,3},{3,2},{4,5},{5,4},{6,7},{7,6},{8,9},{9,8},{10,11... | collective-permute-start | bytes 2359304 | tf_op jit(solution)/shard_map/ppermute | solution.py:546
  37.6 13.1 %collective-permute-start.6 = (bf16[1,128,768]{2,1,0:T(8,128)(2,1)}, bf16[1,128,768]{2,1,0:T(8,128)(2,1)S(1)}, u32[]{:S(2)}, u32[]{:S(2)}) collective-permute-start(bf16[1,128,768]{2,1,0:T(8,128)(2,1)} %get-tuple-element.77), channel_id=1, source_target_pairs={{0,12},{4,8},{8,4},{12,0},{1,13},{5,9},{9,5},{13,1},{2,14},{6,10},... | collective-permute-start | bytes 589832 | tf_op jit(solution)/shard_map/ppermute | solution.py:546
  50.7 13.4 %copy-start.18 = (bf16[1024,768]{1,0:T(8,128)(2,1)}, bf16[1024,768]{1,0:T(8,128)(2,1)S(1)}, u32[]{:S(2)}) copy-start(bf16[1024,768]{1,0:T(8,128)(2,1)S(1)} %get-tuple-element.73.g_ref.refs_3_) | copy-start | bytes 4718596
  51.9 15.4 %copy-start.5 = (bf16[2,128,768]{2,1,0:T(8,128)(2,1)}, bf16[2,128,768]{2,1,0:T(8,128)(2,1)S(1)}, u32[]{:S(2)}) copy-start(bf16[2,128,768]{2,1,0:T(8,128)(2,1)S(1)} %constant_dynamic-update-slice_fusion.nz) | copy-start | bytes 1179652
  51.9 15.4 %collective-permute-start.7 = (bf16[2,128,768]{2,1,0:T(8,128)(2,1)S(1)}, bf16[2,128,768]{2,1,0:T(8,128)(2,1)S(1)}, u32[]{:S(2)}, u32[]{:S(2)}) collective-permute-start(bf16[2,128,768]{2,1,0:T(8,128)(2,1)S(1)} %constant_dynamic-update-slice_fusion.nz), channel_id=1, source_target_pairs={{0,2},{1,3},{2,0},{3,1},{4,6},{5,7},{6,4},{7,5},{8,10},{9,11},{10,... | collective-permute-start | bytes 1179656 | tf_op jit(solution)/shard_map/ppermute | solution.py:546
  69.5 4.4 %collective-permute-start.8 = (bf16[2,2,128,768]{3,2,1,0:T(8,128)(2,1)}, bf16[2,2,128,768]{3,2,1,0:T(8,128)(2,1)}, u32[]{:S(2)}, u32[]{:S(2)}) collective-permute-start(bf16[2,2,128,768]{3,2,1,0:T(8,128)(2,1)} %pad_maximum_fusion.7), channel_id=1, source_target_pairs={{0,1},{1,0},{2,3},{3,2},{4,5},{5,4},{6,7},{7,6},{8,9},{9,8},{10,11... | collective-permute-start | bytes 2359304 | tf_op jit(solution)/shard_map/ppermute | solution.py:546
  70.7 28.8 %collective-permute-start.10 = (bf16[768,768]{1,0:T(8,128)(2,1)}, bf16[768,768]{1,0:T(8,128)(2,1)}, u32[]{:S(2)}, u32[]{:S(2)}) collective-permute-start(bf16[768,768]{1,0:T(8,128)(2,1)} %get-tuple-element.91), channel_id=1, source_target_pairs={{0,16},{16,0},{1,17},{17,1},{2,18},{18,2},{3,19},{19,3},{4,20},{20... | collective-permute-start | bytes 3538952 | tf_op jit(solution)/shard_map/ppermute | solution.py:546
  73.9 48.3 %copy-start.2 = (bf16[768,768]{1,0:T(8,128)(2,1)}, bf16[768,768]{1,0:T(8,128)(2,1)S(1)}, u32[]{:S(2)}) copy-start(bf16[768,768]{1,0:T(8,128)(2,1)S(1)} %pad_maximum_fusion.4.w_ref.refs_5_.refs_7_.refs_10_) | copy-start | bytes 3538948
  82.8 16.6 %copy-start.8 = (f32[768,768]{1,0:T(8,128)S(1)}, f32[768,768]{1,0:T(8,128)}, u32[]{:S(2)}) copy-start(f32[768,768]{1,0:T(8,128)} %copy-done.7) | copy-start | bytes 7077892
  111.5 10.7 %copy-start.32 = (bf16[64,2048]{1,0:T(8,128)(2,1)}, bf16[64,2048]{1,0:T(8,128)(2,1)S(1)}, u32[]{:S(2)}) copy-start(bf16[64,2048]{1,0:T(8,128)(2,1)S(1)} %get-tuple-element.105.refs_5_.refs_8_) | copy-start | bytes 786436
  111.5 10.7 %copy-start.38 = (bf16[64,1024]{1,0:T(8,128)(2,1)}, bf16[64,1024]{1,0:T(8,128)(2,1)S(1)}, u32[]{:S(2)}) copy-start(bf16[64,1024]{1,0:T(8,128)(2,1)S(1)} %get-tuple-element.99.refs_2_) | copy-start | bytes 393220
  112.5 18.6 %collective-permute-start.13 = (bf16[384,768]{1,0:T(8,128)(2,1)}, bf16[384,768]{1,0:T(8,128)(2,1)}, u32[]{:S(2)}, u32[]{:S(2)}) collective-permute-start(bf16[384,768]{1,0:T(8,128)(2,1)} %dynamic-slice_convert_fusion), channel_id=1, source_target_pairs={{0,4},{4,0},{8,12},{12,8},{1,5},{5,1},{9,13},{13,9},{2,6},{6,2},{1... | collective-permute-start | bytes 1769480 | tf_op jit(solution)/shard_map/ppermute | solution.py:546
  127.2 13.2 %collective-permute-start.11 = (bf16[2,256,768]{2,1,0:T(8,128)(2,1)}, bf16[2,256,768]{2,1,0:T(8,128)(2,1)}, u32[]{:S(2)}, u32[]{:S(2)}) collective-permute-start(bf16[2,256,768]{2,1,0:T(8,128)(2,1)} %get-tuple-element.96), channel_id=1, source_target_pairs={{0,1},{1,0},{2,3},{3,2},{4,5},{5,4},{6,7},{7,6},{8,9},{9,8},{10,11... | collective-permute-start | bytes 2359304 | tf_op jit(solution)/shard_map/ppermute | solution.py:546
  131.0 95.5 %copy-start.70 = (f32[2,128]{1,0:T(2,128)}, f32[2,128]{1,0:T(2,128)S(1)}, u32[]{:S(2)}) copy-start(f32[2,128]{1,0:T(2,128)S(1)} %add_rsqrt_fusion) | copy-start | bytes 3076
  132.9 18.0 %collective-permute-start.21 = (bf16[192,768]{1,0:T(8,128)(2,1)S(1)}, bf16[192,768]{1,0:T(8,128)(2,1)S(1)}, u32[]{:S(2)}, u32[]{:S(2)}) collective-permute-start(bf16[192,768]{1,0:T(8,128)(2,1)S(1)} %dynamic-slice_convert_fusion.1), channel_id=1, source_target_pairs={{0,8},{4,12},{8,0},{12,4},{1,9},{5,13},{9,1},{13,5},{2,10},{6,14},... | collective-permute-start | bytes 884744 | tf_op jit(solution)/shard_map/ppermute | solution.py:546
  140.2 12.8 %collective-permute-start.19 = (bf16[2,256,768]{2,1,0:T(8,128)(2,1)S(1)}, bf16[2,256,768]{2,1,0:T(8,128)(2,1)S(1)}, u32[]{:S(2)}, u32[]{:S(2)}) collective-permute-start(bf16[2,256,768]{2,1,0:T(8,128)(2,1)S(1)} %get-tuple-element.117), channel_id=1, source_target_pairs={{0,1},{1,0},{2,3},{3,2},{4,5},{5,4},{6,7},{7,6},{8,9},{9,8},{10,11... | collective-permute-start | bytes 2359304 | tf_op jit(solution)/shard_map/ppermute | solution.py:546
  148.4 6.4 %collective-permute-start.14 = (bf16[2,256,768]{2,1,0:T(8,128)(2,1)S(1)}, bf16[2,256,768]{2,1,0:T(8,128)(2,1)S(1)}, u32[]{:S(2)}, u32[]{:S(2)}) collective-permute-start(bf16[2,256,768]{2,1,0:T(8,128)(2,1)S(1)} %get-tuple-element.114), channel_id=1, source_target_pairs={{0,1},{1,0},{2,3},{3,2},{4,5},{5,4},{6,7},{7,6},{8,9},{9,8},{10,11... | collective-permute-start | bytes 2359304 | tf_op jit(solution)/shard_map/ppermute | solution.py:546
  148.7 19.7 %collective-permute-start.12 = (bf16[2,128,768]{2,1,0:T(8,128)(2,1)S(1)}, bf16[2,128,768]{2,1,0:T(8,128)(2,1)S(1)}, u32[]{:S(2)}, u32[]{:S(2)}) collective-permute-start(bf16[2,128,768]{2,1,0:T(8,128)(2,1)S(1)} %fusion.17), channel_id=1, source_target_pairs={{0,2},{1,3},{2,0},{3,1},{4,6},{5,7},{6,4},{7,5},{8,10},{9,11},{10,... | collective-permute-start | bytes 1179656 | tf_op jit(solution)/shard_map/ppermute | solution.py:546
  149.3 23.1 %collective-permute-start.27 = (bf16[832,384]{1,0:T(8,128)(2,1)S(1)}, bf16[832,384]{1,0:T(8,128)(2,1)S(1)}, u32[]{:S(2)}, u32[]{:S(2)}) collective-permute-start(bf16[832,384]{1,0:T(8,128)(2,1)S(1)} %get-tuple-element.123), channel_id=1, source_target_pairs={{0,16},{16,0},{1,17},{17,1},{2,18},{18,2},{3,19},{19,3},{4,20},{20... | collective-permute-start | bytes 1916936 | tf_op jit(solution)/shard_map/ppermute | solution.py:546
  150.9 15.9 %collective-permute-start.22 = (bf16[192,768]{1,0:T(8,128)(2,1)S(1)}, bf16[192,768]{1,0:T(8,128)(2,1)S(1)}, u32[]{:S(2)}, u32[]{:S(2)}) collective-permute-start(bf16[192,768]{1,0:T(8,128)(2,1)S(1)} %add_convert_fusion), channel_id=1, source_target_pairs={{0,8},{4,12},{8,0},{12,4},{1,9},{5,13},{9,1},{13,5},{2,10},{6,14},... | collective-permute-start | bytes 884744 | tf_op jit(solution)/shard_map/ppermute | solution.py:546
  153.2 19.0 %collective-permute-start.20 = (bf16[2,128,768]{2,1,0:T(8,128)(2,1)S(1)}, bf16[2,128,768]{2,1,0:T(8,128)(2,1)S(1)}, u32[]{:S(2)}, u32[]{:S(2)}) collective-permute-start(bf16[2,128,768]{2,1,0:T(8,128)(2,1)S(1)} %fusion.19), channel_id=1, source_target_pairs={{0,2},{1,3},{2,0},{3,1},{4,6},{5,7},{6,4},{7,5},{8,10},{9,11},{10,... | collective-permute-start | bytes 1179656 | tf_op jit(solution)/shard_map/ppermute | solution.py:546
  166.9 13.9 %collective-permute-start.18 = (bf16[2,128,768]{2,1,0:T(8,128)(2,1)S(1)}, bf16[2,128,768]{2,1,0:T(8,128)(2,1)S(1)}, u32[]{:S(2)}, u32[]{:S(2)}) collective-permute-start(bf16[2,128,768]{2,1,0:T(8,128)(2,1)S(1)} %fusion.18), channel_id=1, source_target_pairs={{0,2},{1,3},{2,0},{3,1},{4,6},{5,7},{6,4},{7,5},{8,10},{9,11},{10,... | collective-permute-start | bytes 1179656 | tf_op jit(solution)/shard_map/ppermute | solution.py:546
  168.6 44.6 %copy-start.57 = (bf16[1,128,768]{2,1,0:T(8,128)(2,1)}, bf16[1,128,768]{2,1,0:T(8,128)(2,1)S(1)}, u32[]{:S(2)}) copy-start(bf16[1,128,768]{2,1,0:T(8,128)(2,1)S(1)} %get-tuple-element.174) | copy-start | bytes 589828
  168.6 12.2 %collective-permute-start.15 = (bf16[128,768]{1,0:T(8,128)(2,1)S(1)}, bf16[128,768]{1,0:T(8,128)(2,1)S(1)}, u32[]{:S(2)}, u32[]{:S(2)}) collective-permute-start(bf16[128,768]{1,0:T(8,128)(2,1)S(1)} %get-tuple-element.175), channel_id=1, source_target_pairs={{0,8},{4,12},{8,0},{12,4},{1,9},{5,13},{9,1},{13,5},{2,10},{6,14},... | collective-permute-start | bytes 589832 | tf_op jit(solution)/shard_map/ppermute | solution.py:546
  168.7 55.2 %collective-permute-start.35 = (bf16[2,192,768]{2,1,0:T(8,128)(2,1)S(1)}, bf16[2,192,768]{2,1,0:T(8,128)(2,1)S(1)}, u32[]{:S(2)}, u32[]{:S(2)}) collective-permute-start(bf16[2,192,768]{2,1,0:T(8,128)(2,1)S(1)} %pad_maximum_fusion.12), channel_id=1, source_target_pairs={{0,4},{4,0},{8,12},{12,8},{1,5},{5,1},{9,13},{13,9},{2,6},{6,2},{1... | collective-permute-start | bytes 1769480 | tf_op jit(solution)/shard_map/ppermute | solution.py:546
  172.3 32.3 %collective-permute-start.23 = (bf16[2,128,768]{2,1,0:T(8,128)(2,1)S(1)}, bf16[2,128,768]{2,1,0:T(8,128)(2,1)S(1)}, u32[]{:S(2)}, u32[]{:S(2)}) collective-permute-start(bf16[2,128,768]{2,1,0:T(8,128)(2,1)S(1)} %fusion.9), channel_id=1, source_target_pairs={{0,4},{4,0},{8,12},{12,8},{1,5},{5,1},{9,13},{13,9},{2,6},{6,2},{1... | collective-permute-start | bytes 1179656 | tf_op jit(solution)/shard_map/ppermute | solution.py:546
  172.6 32.6 %collective-permute-start.28 = (bf16[208,384]{1,0:T(8,128)(2,1)S(1)}, bf16[208,384]{1,0:T(8,128)(2,1)S(1)}, u32[]{:S(2)}, u32[]{:S(2)}) collective-permute-start(bf16[208,384]{1,0:T(8,128)(2,1)S(1)} %get-tuple-element.151), channel_id=1, source_target_pairs={{0,12},{4,8},{8,4},{12,0},{1,13},{5,9},{9,5},{13,1},{2,14},{6,10},... | collective-permute-start | bytes 479240 | tf_op jit(solution)/shard_map/ppermute | solution.py:546
  180.7 32.5 %copy-start.60 = (bf16[128,768]{1,0:T(8,128)(2,1)}, bf16[128,768]{1,0:T(8,128)(2,1)S(1)}, u32[]{:S(2)}) copy-start(bf16[128,768]{1,0:T(8,128)(2,1)S(1)} %collective-permute-done.15) | copy-start | bytes 589828
  180.7 25.5 %collective-permute-start.29 = (bf16[208,384]{1,0:T(8,128)(2,1)S(1)}, bf16[208,384]{1,0:T(8,128)(2,1)S(1)}, u32[]{:S(2)}, u32[]{:S(2)}) collective-permute-start(bf16[208,384]{1,0:T(8,128)(2,1)S(1)} %get-tuple-element.153), channel_id=1, source_target_pairs={{0,8},{4,12},{8,0},{12,4},{1,9},{5,13},{9,1},{13,5},{2,10},{6,14},... | collective-permute-start | bytes 479240 | tf_op jit(solution)/shard_map/ppermute | solution.py:546
  180.8 27.2 %collective-permute-start.30 = (bf16[208,384]{1,0:T(8,128)(2,1)S(1)}, bf16[208,384]{1,0:T(8,128)(2,1)S(1)}, u32[]{:S(2)}, u32[]{:S(2)}) collective-permute-start(bf16[208,384]{1,0:T(8,128)(2,1)S(1)} %get-tuple-element.152), channel_id=1, source_target_pairs={{0,4},{4,0},{8,12},{12,8},{1,5},{5,1},{9,13},{13,9},{2,6},{6,2},{1... | collective-permute-start | bytes 479240 | tf_op jit(solution)/shard_map/ppermute | solution.py:546
  204.6 8.6 %collective-permute-start.16 = (bf16[2,128,768]{2,1,0:T(8,128)(2,1)S(1)}, bf16[2,128,768]{2,1,0:T(8,128)(2,1)S(1)}, u32[]{:S(2)}, u32[]{:S(2)}) collective-permute-start(bf16[2,128,768]{2,1,0:T(8,128)(2,1)S(1)} %pad_maximum_fusion.15), channel_id=1, source_target_pairs={{0,2},{1,3},{2,0},{3,1},{4,6},{5,7},{6,4},{7,5},{8,10},{9,11},{10,... | collective-permute-start | bytes 1179656 | tf_op jit(solution)/shard_map/ppermute | solution.py:546
  205.3 14.4 %collective-permute-start.24 = (bf16[128,768]{1,0:T(8,128)(2,1)S(1)}, bf16[128,768]{1,0:T(8,128)(2,1)S(1)}, u32[]{:S(2)}, u32[]{:S(2)}) collective-permute-start(bf16[128,768]{1,0:T(8,128)(2,1)S(1)} %fusion.21), channel_id=1, source_target_pairs={{0,8},{4,12},{8,0},{12,4},{1,9},{5,13},{9,1},{13,5},{2,10},{6,14},... | collective-permute-start | bytes 589832 | tf_op jit(solution)/shard_map/ppermute | solution.py:546
  208.1 16.1 %collective-permute-start.31 = (bf16[208,384]{1,0:T(8,128)(2,1)S(1)}, bf16[208,384]{1,0:T(8,128)(2,1)S(1)}, u32[]{:S(2)}, u32[]{:S(2)}) collective-permute-start(bf16[208,384]{1,0:T(8,128)(2,1)S(1)} %add_convert_fusion.1), channel_id=1, source_target_pairs={{0,8},{4,12},{8,0},{12,4},{1,9},{5,13},{9,1},{13,5},{2,10},{6,14},... | collective-permute-start | bytes 479240 | tf_op jit(solution)/shard_map/ppermute | solution.py:546
  214.2 28.8 %collective-permute-start.17 = (bf16[2,2,128,768]{3,2,1,0:T(8,128)(2,1)}, bf16[2,2,128,768]{3,2,1,0:T(8,128)(2,1)}, u32[]{:S(2)}, u32[]{:S(2)}) collective-permute-start(bf16[2,2,128,768]{3,2,1,0:T(8,128)(2,1)} %pad_maximum_fusion.8), channel_id=1, source_target_pairs={{0,1},{1,0},{2,3},{3,2},{4,5},{5,4},{6,7},{7,6},{8,9},{9,8},{10,11... | collective-permute-start | bytes 2359304 | tf_op jit(solution)/shard_map/ppermute | solution.py:546
  223.3 18.4 %collective-permute-start.25 = (bf16[2,128,768]{2,1,0:T(8,128)(2,1)}, bf16[2,128,768]{2,1,0:T(8,128)(2,1)}, u32[]{:S(2)}, u32[]{:S(2)}) collective-permute-start(bf16[2,128,768]{2,1,0:T(8,128)(2,1)} %fusion.7), channel_id=1, source_target_pairs={{0,2},{1,3},{2,0},{3,1},{4,6},{5,7},{6,4},{7,5},{8,10},{9,11},{10,... | collective-permute-start | bytes 1179656 | tf_op jit(solution)/shard_map/ppermute | solution.py:546
  224.3 7.7 %collective-permute-start.32 = (bf16[2,208,384]{2,1,0:T(8,128)(2,1)S(1)}, bf16[2,208,384]{2,1,0:T(8,128)(2,1)S(1)}, u32[]{:S(2)}, u32[]{:S(2)}) collective-permute-start(bf16[2,208,384]{2,1,0:T(8,128)(2,1)S(1)} %pad_maximum_fusion.17), channel_id=1, source_target_pairs={{0,4},{4,0},{8,12},{12,8},{1,5},{5,1},{9,13},{13,9},{2,6},{6,2},{1... | collective-permute-start | bytes 958472 | tf_op jit(solution)/shard_map/ppermute | solution.py:546
  232.1 1.3 collective-permute-start.33
  234.0 6.3 %collective-permute-start.34 = (f32[8,768]{1,0:T(8,128)}, f32[8,768]{1,0:T(8,128)}, u32[]{:S(2)}, u32[]{:S(2)}) collective-permute-start(f32[8,768]{1,0:T(8,128)} %fusion.27), channel_id=1, source_target_pairs={{0,2},{1,3},{2,0},{3,1},{4,6},{5,7},{6,4},{7,5},{8,10},{9,11},{10,... | collective-permute-start | bytes 73736 | tf_op jit(solution)/shard_map/ppermute | solution.py:546
  242.8 4.4 %collective-permute-start.26 = (bf16[2,2,128,768]{3,2,1,0:T(8,128)(2,1)S(1)}, bf16[2,2,128,768]{3,2,1,0:T(8,128)(2,1)S(1)}, u32[]{:S(2)}, u32[]{:S(2)}) collective-permute-start(bf16[2,2,128,768]{3,2,1,0:T(8,128)(2,1)S(1)} %pad_maximum_fusion.10), channel_id=1, source_target_pairs={{0,1},{1,0},{2,3},{3,2},{4,5},{5,4},{6,7},{7,6},{8,9},{9,8},{10,11... | collective-permute-start | bytes 2359304 | tf_op jit(solution)/shard_map/ppermute | solution.py:546
  (67 other events, 246.0 us)

commit v9 on v8

--- a/solution.py
+++ b/solution.py
@@ -450,10 +450,10 @@
     grads, refs = refs[: count * heads], refs[count * heads :]
     n1_ref, w_ref, s1_ref, *refs = refs
     if own:
-        (a2_ref, b1_ref, small_ff, small_other, mix_other, out_part,
+        (half_b, a2_ref, b1_ref, small_ff, small_other, mix_other, out_part,
          keep_ref, send_ref, first_ref, second_ref, mix, small) = refs
     else:
-        keep_ref, send_ref, mix, small = refs
+        keep_b, ff_half, keep_ref, send_ref, mix, small = refs
     i = pl.program_id(0)
     wide = heads * HEAD
     tall = mix.shape[0]
@@ -516,11 +516,13 @@
 
     half = width // 2
     specs = [col] * (len(grads) * heads) + [row, whole(4 * wide, width), whole(width)]
+    earlier = pl.BlockSpec(memory_space=pl.ANY)
     if not own:
+        specs += [earlier, earlier]
         parts = [shape(tall, width), shape(8, width)]
         scratch = []
     else:
-        specs += [row, whole(width), whole(8, width), whole(8, width), whole(2 * wide, width),
+        specs += [earlier, row, whole(width), whole(8, width), whole(8, width), whole(2 * wide, width),
                   whole(wide, width)]
         scratch = [pltpu.VMEM((tall, width), F32), pltpu.VMEM((8, width), F32)]
         if split:
@@ -659,10 +661,15 @@
     x_mine, x_theirs = my_quarter(inputs, s), my_quarter(inputs, 1 - s)
     g_theirs = my_quarter(cotangent, 1 - s)
     far_z = swap(jnp.concatenate([x_theirs, g_theirs], axis=0), "ctx", 4, 2)
-    cross = swap(tie(x_theirs, far_z), "ctx", 4, 3)
+    cross = swap(x_theirs, "ctx", 4, 3)
     near = swap(x_mine, "ctx", 4, 1)
-    far_x = swap(far_z, "tp", 4, 2)
-    far = (far_z, far_x, swap(jnp.stack([far_z, far_x]), "tp", 4, 1))
+
+    def over_tp(v):
+        v_x = swap(v, "tp", 4, 2)
+        return v, v_x, swap(jnp.stack([v, v_x]), "tp", 4, 1)
+
+    far = over_tp(far_z)
+    others = over_tp(jnp.concatenate([near, cross], axis=0))
 
     wup = gather_halves(up_projection_weight, fsdp, f, 0)
     wdown = gather_halves(down_projection_weight, fsdp, f, 1)
@@ -680,15 +687,14 @@
         at, True, (inputs, cotangent, *far), trig,
         (first_scale, first_shift, second_scale, second_shift),
     )
-    others_z = jnp.concatenate([tie(near, n2), tie(cross, n2)], axis=0)
-    others_x = swap(others_z, "tp", 4, 2)
     ff, a2, small_ff, ff_first, ff_second = feed_forward(
         split, at, n2, g, wup, up_projection_bias, wdown, second_scale, second_shift
     )
     weights = gather_halves(mix_out_shard, fsdp, f, 1, small_ff)
-    others_x = tie(others_x, small_ff)
-    others = (others_z, others_x, swap(jnp.stack([others_z, others_x]), "tp", 4, 1))
-    n1_other, trig_other = norms(at, False, others, trig, (first_scale, first_shift))
+    n1_other, trig_other = norms(
+        at, False, (others[0], others[1], tie(others[2], small_ff)), trig,
+        (first_scale, first_shift),
+    )
     kt, vt, qt, dot = project(
         n1_own, n1_other, trig_own, trig_other, g, weights, query_key_value_bias
     )
@@ -696,11 +702,10 @@
     after = small_ff
     for h in range(heads):
         if split and h == heads - 1:
-            after = tie(swap(ff_second, "fsdp", 2, 1), per_head[h - 1][0])
-            after = ff_first + after.astype(F32)
+            after = ff_first + swap(ff_second, "fsdp", 2, 1).astype(F32)
         per_head.append(attention(h, after, qt, dot, kt, vt, trig_own, trig_other))
     o, dq, dk, dv = zip(*per_head)
-    ff_half = halve(after, 1, c % 2, o[-1]) if split else after
+    ff_half = halve(after, 1, c % 2) if split else after
 
     def over_core(keep, send, *earlier):
         v = keep.astype(F32) + tie(swap(send, "tp", 4, 1), *earlier).astype(F32)
@@ -711,19 +716,15 @@
 
     keep_b, send_b, out_part = branch(o, g, ff, weights)
     keep_o, send_o, mix_other, small_other = back(
-        False, split, at, (dk, dv), n1_other, weights, tie(first_scale, keep_b, ff_half), ()
+        False, split, at, (dk, dv), n1_other, weights, first_scale, (keep_b, ff_half)
     )
     half_b = over_core(keep_b, send_b)
     keep_w, send_w, late_first, late_second = back(
-        True, split, at, (dq, dk, dv), n1_own, weights, tie(first_scale, half_b),
-        (a2, first_shift, small_ff, small_other, mix_other, out_part),
+        True, split, at, (dq, dk, dv), n1_own, weights, first_scale,
+        (half_b, a2, first_shift, small_ff, small_other, mix_other, out_part),
     )
     half_o = over_core(keep_o, send_o)
     half_w = over_core(keep_w, send_w)
-    if split:
-        ff_pair = pair_up(halve(ff_half, 2, c // 2, keep_w), half_w)
-    else:
-        ff_pair = half_w
 
     def over_ctx(v, distance, *earlier):
         return tie(swap(v.astype(BF16), "ctx", 4, distance), *earlier).astype(F32)
@@ -743,7 +744,7 @@
         inputs.astype(F32) + block_out + (attention_output_bias + down_projection_bias)
     )
 
-    sums_o = over_x(half_o, ff_pair)
+    sums_o = over_x(half_o, half_w)
     sums_w = over_x(half_w)
     sums_w = sums_w + over_ctx(sums_o, 1)
     a = jnp.stack([sums_w[0], over_ctx(sums_w[1], 2, branches)])
@@ -757,7 +758,7 @@
     inputs_grad = cotangent.astype(F32) + gather_tp(norm_grad)
 
     if split:
-        q = double(ff_pair, c, norm_grad)
+        q = double(pair_up(halve(ff_half, 2, c // 2), sums_o), c, norm_grad)
         up_total = jnp.concatenate(q[:2], axis=0).astype(F32)
         down_total = jnp.concatenate(q[2:], axis=0).astype(F32)
         down_total = jnp.concatenate(

time: 252 us -> 232 us (0.921)
  other arithmetic: 40.8 us -> 31.6 us
  local copies, waits for them, and re-layouts: 24.3 us -> 15.2 us
  Pallas kernels: 65.3 us -> 62.7 us
    unnamed x160 -> x124, local copies, waits for them, and re-layouts: 16.5 us -> 8.16 us
    convert_element_type x2, other arithmetic: 4.09 us -> 0.53 us  [shards(): norm_grad = norm_grad.astype(BF16)]
  transfers between devices with their start and end apart: 36 -> 36, of which waited for: 11 -> 14; matrix products, arithmetic and copies ran while one was open for 16% -> 13% of each run, Pallas kernels for 22% -> 27%
where the time goes in v9:
time: 232 us; the launch traced here: 231 us
  waiting for transfers between devices  84 us (36%)
  Pallas kernels  62.7 us (27%)
  starting transfers between devices  35.9 us (15%)
  other arithmetic  31.6 us (14%)
  local copies, waits for them, and re-layouts  15.2 us (7%)
    ppermute x36, waiting for transfers between devices, swap(): return lax.ppermute(v, axis, [(i, i ^ distance) for i in range(size)])  84 us
    ppermute x36, starting transfers between devices, swap(): return lax.ppermute(v, axis, [(i, i ^ distance) for i in range(size)])  35.9 us
    pallas_call x3, Pallas kernels, attention(): pl.pallas_call(attention_kernel, grid=(rows // lanes,), in_specs=[pl.Bloc...  29 us
    pallas_call x2, Pallas kernels, back(): pl.pallas_call(functools.partial(back_kernel, own, split, heads), grid_sp...  11 us
    pallas_call x1, Pallas kernels, feed_forward(): pl.pallas_call(functools.partial(forward_kernel, split), grid_spec=pltpu....  9.99 us
    unnamed x124, local copies, waits for them, and re-layouts  8.16 us
    pallas_call x2, Pallas kernels, norms(): pl.pallas_call(kernel, grid_spec=pltpu.PrefetchScalarGridSpec(num_scalar_...  4.93 us
  transfers between devices with their start and end apart: 36, of which 14 were waited for; matrix products, arithmetic and copies ran while one was open for 13% of the time, Pallas kernels for 27%

profile of v9, /device:TPU:0, one launch (start us, length us, event | category | flops | bytes accessed | tf_op | source)
XLA Modules:
  0.0 231.0 jit_solution(7041802812702163192)
XLA Ops:
  1.9 5.1 %collective-permute-start.6 = (bf16[1,128,768]{2,1,0:T(8,128)(2,1)S(1)}, bf16[1,128,768]{2,1,0:T(8,128)(2,1)S(1)}, u32[]{:S(2)}, u32[]{:S(2)}) collective-permute-start(bf16[1,128,768]{2,1,0:T(8,128)(2,1)S(1)} %get-tuple-element.134), channel_id=1, source_target_pairs={{0,12},{4,8},{8,4},{12,0},{1,13},{5,9},{9,5},{13,1},{2,14},{6,10},... | collective-permute-start | bytes 589832 | tf_op jit(solution)/shard_map/ppermute | solution.py:548
  8.7 1.5 collective-permute-start.3
  13.0 10.9 %collective-permute-done.5 = bf16[1,128,768]{2,1,0:T(8,128)(2,1)S(1)} collective-permute-done((bf16[1,128,768]{2,1,0:T(8,128)(2,1)S(1)}, bf16[1,128,768]{2,1,0:T(8,128)(2,1)S(1)}, u32[]{:S(2)}, u32[]{:S(2)}) %collective-permute-start.5) | collective-permute-done | bytes 196640 | tf_op jit(solution)/shard_map/ppermute | solution.py:548
  23.8 1.5 collective-permute-start.9
  25.4 1.6 collective-permute-start.7
  27.0 5.1 %collective-permute-done.fz = bf16[2,128,768]{2,1,0:T(8,128)(2,1)S(1)} collective-permute-done((bf16[2,128,768]{2,1,0:T(8,128)(2,1)}, bf16[2,128,768]{2,1,0:T(8,128)(2,1)S(1)}, u32[]{:S(2)}, u32[]{:S(2)}) %collective-permute-start) | collective-permute-done | bytes 393248 | tf_op jit(solution)/shard_map/ppermute | solution.py:548
  32.1 1.5 collective-permute-start.1
  33.7 2.8 %collective-permute-done.7.nx = bf16[2,128,768]{2,1,0:T(8,128)(2,1)S(1)} collective-permute-done((bf16[2,128,768]{2,1,0:T(8,128)(2,1)S(1)}, bf16[2,128,768]{2,1,0:T(8,128)(2,1)S(1)}, u32[]{:S(2)}, u32[]{:S(2)}) %collective-permute-start.7) | collective-permute-done | bytes 393248 | tf_op jit(solution)/shard_map/ppermute | solution.py:548
  36.7 6.9 %collective-permute-done.1.fx = bf16[2,128,768]{2,1,0:T(8,128)(2,1)S(1)} collective-permute-done((bf16[2,128,768]{2,1,0:T(8,128)(2,1)S(1)}, bf16[2,128,768]{2,1,0:T(8,128)(2,1)S(1)}, u32[]{:S(2)}, u32[]{:S(2)}) %collective-permute-start.1) | collective-permute-done | bytes 393248 | tf_op jit(solution)/shard_map/ppermute | solution.py:548
  45.1 1.5 broadcast_select_fusion.7
  46.8 1.2 copy-done
  48.1 2.7 %shard_map.254 = (bf16[1024,768]{1,0:T(8,128)(2,1)S(1)}, bf16[1024,768]{1,0:T(8,128)(2,1)S(1)}, bf16[1024,768]{1,0:T(8,128)(2,1)S(1)}, f32[24,1024]{1,0:T(8,128)S(1)}) custom-call(s32[4]{0:T(128)S(1)} %pad_add_fusion.at, bf16[2,512,768]{2,1,0:T(8,128)(2,1)S(1)} %copy-done, bf16[2,512,768]{2,1,0:T(8,128)(2,1)S(1)} %copy-done, ...), custom_call_target="tpu_custom_call" | custom-call | bytes 4718592 | tf_op jit(solution)/shard_map/pallas_call | solution.py:140
  50.8 10.0 %shard_map.255 = (bf16[1024,768]{1,0:T(8,128)(2,1)S(1)}, bf16[1024,768]{1,0:T(8,128)(2,1)S(1)}, f32[8,768]{1,0:T(8,128)S(1)}, f32[768,768]{1,0:T(8,128)S(1)}, bf16[768,768]{1,0:T(8,128)(2,1)S(1)}) custom-call(s32[4]{0:T(128)S(1)} %pad_add_fusion.at, bf16[1024,768]{1,0:T(8,128)(2,1)S(1)} %get-tuple-element.64.n2_ref, ...), custom_call_target="tpu_custom_call" | custom-call | flops 7247757312 | bytes 16777216 | tf_op jit(solution)/shard_map/pallas_call | solution.py:386
  61.4 1.3 broadcast_select_fusion.5
  62.9 2.2 shard_map.256
  65.1 4.5 %shard_map.257 = (bf16[192,2048]{1,0:T(8,128)(2,1)S(1)}, bf16[192,2048]{1,0:T(8,128)(2,1)S(1)}, bf16[192,1024]{1,0:T(8,128)(2,1)S(1)}, bf16[192,1024]{1,0:T(8,128)(2,1)S(1)}) custom-call(bf16[1024,768]{1,0:T(8,128)(2,1)S(1)} %get-tuple-element.67.n1o.refs_9_, bf16[1024,768]{1,0:T(8,128)(2,1)S(1)} %get-tuple-element.69.n1x.refs_6_, ...), custom_call_target="tpu_custom_call" | custom-call | flops 1811939328 | bytes 9437184 | tf_op jit(solution)/shard_map/pallas_call | solution.py:204
  69.6 9.7 %shard_map.259 = (bf16[64,1024]{1,0:T(8,128)(2,1)S(1)}, bf16[64,1024]{1,0:T(8,128)(2,1)S(1)}, bf16[64,2048]{1,0:T(8,128)(2,1)S(1)}, bf16[64,2048]{1,0:T(8,128)(2,1)S(1)}) custom-call(f32[8,768]{1,0:T(8,128)S(1)} %get-tuple-element.66.after.refs_15_, bf16[192,1024]{1,0:T(8,128)(2,1)S(1)} %get-tuple-element.73.q_ref, ...), custom_call_target="tpu_custom_call" | custom-call | flops 5368709120 | bytes 2097152 | tf_op jit(solution)/shard_map/pallas_call | solution.py:307
  81.4 9.7 %shard_map.258 = (bf16[64,1024]{1,0:T(8,128)(2,1)S(1)}, bf16[64,1024]{1,0:T(8,128)(2,1)S(1)}, bf16[64,2048]{1,0:T(8,128)(2,1)S(1)}, bf16[64,2048]{1,0:T(8,128)(2,1)S(1)}) custom-call(f32[8,768]{1,0:T(8,128)S(1)} %get-tuple-element.66.after.refs_15_, bf16[192,1024]{1,0:T(8,128)(2,1)S(1)} %get-tuple-element.73.q_ref, ...), custom_call_target="tpu_custom_call" | custom-call | flops 5368709120 | bytes 2097152 | tf_op jit(solution)/shard_map/pallas_call | solution.py:307
  92.8 2.6 %collective-permute-start.13 = (bf16[384,768]{1,0:T(8,128)(2,1)}, bf16[384,768]{1,0:T(8,128)(2,1)}, u32[]{:S(2)}, u32[]{:S(2)}) collective-permute-start(bf16[384,768]{1,0:T(8,128)(2,1)} %dynamic-slice_convert_fusion), channel_id=1, source_target_pairs={{0,4},{4,0},{8,12},{12,8},{1,5},{5,1},{9,13},{13,9},{2,6},{6,2},{1... | collective-permute-start | bytes 1769480 | tf_op jit(solution)/shard_map/ppermute | solution.py:548
  95.4 9.7 %shard_map.260 = (bf16[64,1024]{1,0:T(8,128)(2,1)S(1)}, bf16[64,1024]{1,0:T(8,128)(2,1)S(1)}, bf16[64,2048]{1,0:T(8,128)(2,1)S(1)}, bf16[64,2048]{1,0:T(8,128)(2,1)S(1)}) custom-call(f32[768,768]{1,0:T(8,128)S(1)} %convert_add_fusion.1.after, bf16[192,1024]{1,0:T(8,128)(2,1)S(1)} %get-tuple-element.73.q_ref, bf16[192,1024]{1,0:T(8,128)(2,1)S(1)} %get-tuple-element.74.do_ref, ...), custom_call_target="tpu_custom_call" | custom-call | flops 5368709120 | bytes 2097152 | tf_op jit(solution)/shard_map/pallas_call | solution.py:307
  105.1 3.3 %shard_map.261 = (bf16[2,256,768]{2,1,0:T(8,128)(2,1)S(1)}, bf16[2,256,768]{2,1,0:T(8,128)(2,1)}, f32[192,768]{1,0:T(8,128)S(1)}) custom-call(bf16[64,1024]{1,0:T(8,128)(2,1)S(1)} %get-tuple-element.77.refs_0_, bf16[64,1024]{1,0:T(8,128)(2,1)S(1)} %get-tuple-element.78.refs_1_, bf16[64,1024]{1,0:T(8,128)(2,1)S(1)} %get-tuple-element.81.refs_2_, ...), custom_call_target="tpu_custom_call" | custom-call | flops 603979776 | bytes 8388608 | tf_op jit(solution)/shard_map/pallas_call | solution.py:436
  110.2 1.3 add.138
  112.3 1.7 convert_add_fusion.6.refs_10_
  114.6 4.9 %shard_map.262 = (bf16[2,256,768]{2,1,0:T(8,128)(2,1)S(1)}, bf16[2,256,768]{2,1,0:T(8,128)(2,1)S(1)}, f32[384,768]{1,0:T(8,128)S(1)}, f32[8,768]{1,0:T(8,128)S(1)}) custom-call(s32[4]{0:T(128)S(1)} %pad_add_fusion.at, bf16[64,2048]{1,0:T(8,128)(2,1)S(1)} %copy-done.15, bf16[64,2048]{1,0:T(8,128)(2,1)S(1)} %copy-done.11, bf16[64,2048]{1,0:T(8,128)(2,1)S(1)} %copy-done.19, ...), custom_call_target="tpu_custom_call" | custom-call | flops 1207959552 | bytes 10485760 | tf_op jit(solution)/shard_map/pallas_call | solution.py:532
  119.9 1.5 convert_add_fusion.4
  121.6 6.2 %shard_map.263 = (bf16[2,256,768]{2,1,0:T(8,128)(2,1)S(1)}, bf16[2,256,768]{2,1,0:T(8,128)(2,1)S(1)}, f32[832,384]{1,0:T(8,128)S(1)}, bf16[832,384]{1,0:T(8,128)(2,1)S(1)}) custom-call(s32[4]{0:T(128)S(1)} %pad_add_fusion.at, bf16[64,1024]{1,0:T(8,128)(2,1)S(1)} %copy-done.27, bf16[64,1024]{1,0:T(8,128)(2,1)S(1)} %copy-done.25, ...), custom_call_target="tpu_custom_call" | custom-call | flops 1811939328 | bytes 10485760 | tf_op jit(solution)/shard_map/pallas_call | solution.py:532
  128.2 1.6 collective-permute-start.12
  129.7 1.5 collective-permute-start.25
  131.3 2.3 %collective-permute-start.34 = (bf16[192,768]{1,0:T(8,128)(2,1)S(1)}, bf16[192,768]{1,0:T(8,128)(2,1)S(1)}, u32[]{:S(2)}, u32[]{:S(2)}) collective-permute-start(bf16[192,768]{1,0:T(8,128)(2,1)S(1)} %add_convert_fusion), channel_id=1, source_target_pairs={{0,8},{4,12},{8,0},{12,4},{1,9},{5,13},{9,1},{13,5},{2,10},{6,14},... | collective-permute-start | bytes 884744 | tf_op jit(solution)/shard_map/ppermute | solution.py:548
  134.6 5.6 %collective-permute-done.12 = bf16[2,128,768]{2,1,0:T(8,128)(2,1)S(1)} collective-permute-done((bf16[2,128,768]{2,1,0:T(8,128)(2,1)S(1)}, bf16[2,128,768]{2,1,0:T(8,128)(2,1)S(1)}, u32[]{:S(2)}, u32[]{:S(2)}) %collective-permute-start.12) | collective-permute-done | bytes 393248 | tf_op jit(solution)/shard_map/ppermute | solution.py:548
  140.4 2.4 %collective-permute-start.15 = (bf16[128,768]{1,0:T(8,128)(2,1)S(1)}, bf16[128,768]{1,0:T(8,128)(2,1)S(1)}, u32[]{:S(2)}, u32[]{:S(2)}) collective-permute-start(bf16[128,768]{1,0:T(8,128)(2,1)S(1)} %get-tuple-element.159), channel_id=1, source_target_pairs={{0,8},{4,12},{8,0},{12,4},{1,9},{5,13},{9,1},{13,5},{2,10},{6,14},... | collective-permute-start | bytes 589832 | tf_op jit(solution)/shard_map/ppermute | solution.py:548
  142.8 1.5 collective-permute-start.18
  144.3 4.4 %collective-permute-done.20 = bf16[2,128,768]{2,1,0:T(8,128)(2,1)S(1)} collective-permute-done((bf16[2,128,768]{2,1,0:T(8,128)(2,1)S(1)}, bf16[2,128,768]{2,1,0:T(8,128)(2,1)S(1)}, u32[]{:S(2)}, u32[]{:S(2)}) %collective-permute-start.20) | collective-permute-done | bytes 393248 | tf_op jit(solution)/shard_map/ppermute | solution.py:548
  149.2 2.2 collective-permute-done.34
  152.1 3.0 %collective-permute-start.26 = (bf16[208,384]{1,0:T(8,128)(2,1)S(1)}, bf16[208,384]{1,0:T(8,128)(2,1)S(1)}, u32[]{:S(2)}, u32[]{:S(2)}) collective-permute-start(bf16[208,384]{1,0:T(8,128)(2,1)S(1)} %get-tuple-element.135), channel_id=1, source_target_pairs={{0,12},{4,8},{8,4},{12,0},{1,13},{5,9},{9,5},{13,1},{2,14},{6,10},... | collective-permute-start | bytes 479240 | tf_op jit(solution)/shard_map/ppermute | solution.py:548
  156.3 2.8 %collective-permute-start.28 = (bf16[208,384]{1,0:T(8,128)(2,1)S(1)}, bf16[208,384]{1,0:T(8,128)(2,1)S(1)}, u32[]{:S(2)}, u32[]{:S(2)}) collective-permute-start(bf16[208,384]{1,0:T(8,128)(2,1)S(1)} %get-tuple-element.136), channel_id=1, source_target_pairs={{0,4},{4,0},{8,12},{12,8},{1,5},{5,1},{9,13},{13,9},{2,6},{6,2},{1... | collective-permute-start | bytes 479240 | tf_op jit(solution)/shard_map/ppermute | solution.py:548
  159.1 8.3 %collective-permute-done.21 = bf16[2,128,768]{2,1,0:T(8,128)(2,1)S(1)} collective-permute-done((bf16[2,128,768]{2,1,0:T(8,128)(2,1)S(1)}, bf16[2,128,768]{2,1,0:T(8,128)(2,1)S(1)}, u32[]{:S(2)}, u32[]{:S(2)}) %collective-permute-start.21) | collective-permute-done | bytes 393248 | tf_op jit(solution)/shard_map/ppermute | solution.py:548
  168.1 10.6 %collective-permute-done.26 = bf16[208,384]{1,0:T(8,128)(2,1)S(1)} collective-permute-done((bf16[208,384]{1,0:T(8,128)(2,1)S(1)}, bf16[208,384]{1,0:T(8,128)(2,1)S(1)}, u32[]{:S(2)}, u32[]{:S(2)}) %collective-permute-start.26) | collective-permute-done | bytes 159776 | tf_op jit(solution)/shard_map/ppermute | solution.py:548
  178.8 12.3 %collective-permute-done.28 = bf16[208,384]{1,0:T(8,128)(2,1)S(1)} collective-permute-done((bf16[208,384]{1,0:T(8,128)(2,1)S(1)}, bf16[208,384]{1,0:T(8,128)(2,1)S(1)}, u32[]{:S(2)}, u32[]{:S(2)}) %collective-permute-start.28) | collective-permute-done | bytes 159776 | tf_op jit(solution)/shard_map/ppermute | solution.py:548
  194.3 6.7 %collective-permute-done.29 = bf16[208,384]{1,0:T(8,128)(2,1)S(1)} collective-permute-done((bf16[208,384]{1,0:T(8,128)(2,1)S(1)}, bf16[208,384]{1,0:T(8,128)(2,1)S(1)}, u32[]{:S(2)}, u32[]{:S(2)}) %collective-permute-start.29) | collective-permute-done | bytes 159776 | tf_op jit(solution)/shard_map/ppermute | solution.py:548
  203.5 7.0 %collective-permute-done.30 = bf16[2,208,384]{2,1,0:T(8,128)(2,1)S(1)} collective-permute-done((bf16[2,208,384]{2,1,0:T(8,128)(2,1)S(1)}, bf16[2,208,384]{2,1,0:T(8,128)(2,1)S(1)}, u32[]{:S(2)}, u32[]{:S(2)}) %collective-permute-start.30) | collective-permute-done | bytes 319520 | tf_op jit(solution)/shard_map/ppermute | solution.py:548
  215.8 1.4 reshape_squeeze.3
  217.2 2.2 slice.171
  221.4 1.3 broadcast_select_fusion.25
  223.3 1.5 broadcast_select_fusion.21
  225.2 1.2 copy-done.2
  226.4 2.0 convert_add_fusion
  228.4 2.1 add_add_fusion
  (237 shorter events, 34.8 us)
Async XLA Ops:
  0.7 10.7 %copy-start.59 = (s32[2,2048]{1,0:T(2,128)S(1)}, s32[2,2048]{1,0:T(2,128)}, u32[]{:S(2)}) copy-start(s32[2,2048]{1,0:T(2,128)} %param.16) | copy-start | bytes 49156
  0.7 11.4 %copy-start.44 = (bf16[384,3,192]{0,2,1:T(8,128)(2,1)S(1)}, bf16[384,3,192]{0,2,1:T(8,128)(2,1)}, u32[]{:S(2)}) copy-start(bf16[384,3,192]{0,2,1:T(8,128)(2,1)} %param.17) | copy-start | bytes 1327108
  0.7 11.4 %copy-start.48 = (bf16[192,384]{1,0:T(8,128)(2,1)S(1)}, bf16[192,384]{1,0:T(8,128)(2,1)}, u32[]{:S(2)}) copy-start(bf16[192,384]{1,0:T(8,128)(2,1)} %param.19) | copy-start | bytes 442372
  1.9 23.5 %copy-start.38 = (bf16[1,128,768]{2,1,0:T(8,128)(2,1)}, bf16[1,128,768]{2,1,0:T(8,128)(2,1)S(1)}, u32[]{:S(2)}) copy-start(bf16[1,128,768]{2,1,0:T(8,128)(2,1)S(1)} %get-tuple-element.134) | copy-start | bytes 589828
  1.9 23.5 %copy-start.41 = (bf16[1,128,768]{2,1,0:T(8,128)(2,1)}, bf16[1,128,768]{2,1,0:T(8,128)(2,1)S(1)}, u32[]{:S(2)}) copy-start(bf16[1,128,768]{2,1,0:T(8,128)(2,1)S(1)} %get-tuple-element.133) | copy-start | bytes 589828
  1.9 23.5 %collective-permute-start.6 = (bf16[1,128,768]{2,1,0:T(8,128)(2,1)S(1)}, bf16[1,128,768]{2,1,0:T(8,128)(2,1)S(1)}, u32[]{:S(2)}, u32[]{:S(2)}) collective-permute-start(bf16[1,128,768]{2,1,0:T(8,128)(2,1)S(1)} %get-tuple-element.134), channel_id=1, source_target_pairs={{0,12},{4,8},{8,4},{12,0},{1,13},{5,9},{9,5},{13,1},{2,14},{6,10},... | collective-permute-start | bytes 589832 | tf_op jit(solution)/shard_map/ppermute | solution.py:548
  8.7 23.4 %collective-permute-start = (bf16[2,128,768]{2,1,0:T(8,128)(2,1)}, bf16[2,128,768]{2,1,0:T(8,128)(2,1)S(1)}, u32[]{:S(2)}, u32[]{:S(2)}) collective-permute-start(bf16[2,128,768]{2,1,0:T(8,128)(2,1)} %pad_maximum_fusion.13), channel_id=1, source_target_pairs={{0,8},{4,12},{8,0},{12,4},{1,9},{5,13},{9,1},{13,5},{2,10},{6,14},... | collective-permute-start | bytes 1179656 | tf_op jit(solution)/shard_map/ppermute | solution.py:548
  8.7 35.1 %collective-permute-start.3 = (bf16[384,768]{1,0:T(8,128)(2,1)S(1)}, bf16[384,768]{1,0:T(8,128)(2,1)}, u32[]{:S(2)}, u32[]{:S(2)}) collective-permute-start(bf16[384,768]{1,0:T(8,128)(2,1)S(1)} %copy-done.49), channel_id=1, source_target_pairs={{0,16},{16,0},{1,17},{17,1},{2,18},{18,2},{3,19},{19,3},{4,20},{20... | collective-permute-start | bytes 1769480 | tf_op jit(solution)/shard_map/ppermute | solution.py:548
  10.2 34.8 %collective-permute-start.4 = (bf16[768,384]{1,0:T(8,128)(2,1)}, bf16[768,384]{1,0:T(8,128)(2,1)}, u32[]{:S(2)}, u32[]{:S(2)}) collective-permute-start(bf16[768,384]{1,0:T(8,128)(2,1)} %param.23), channel_id=1, source_target_pairs={{0,16},{16,0},{1,17},{17,1},{2,18},{18,2},{3,19},{19,3},{4,20},{20... | collective-permute-start | bytes 1769480 | tf_op jit(solution)/shard_map/ppermute | solution.py:548
  10.7 13.1 %collective-permute-start.5 = (bf16[1,128,768]{2,1,0:T(8,128)(2,1)S(1)}, bf16[1,128,768]{2,1,0:T(8,128)(2,1)S(1)}, u32[]{:S(2)}, u32[]{:S(2)}) collective-permute-start(bf16[1,128,768]{2,1,0:T(8,128)(2,1)S(1)} %get-tuple-element.133), channel_id=1, source_target_pairs={{0,4},{4,0},{8,12},{12,8},{1,5},{5,1},{9,13},{13,9},{2,6},{6,2},{1... | collective-permute-start | bytes 589832 | tf_op jit(solution)/shard_map/ppermute | solution.py:548
  23.8 37.6 %collective-permute-start.9 = (bf16[768,384]{1,0:T(8,128)(2,1)}, bf16[768,384]{1,0:T(8,128)(2,1)}, u32[]{:S(2)}, u32[]{:S(2)}) collective-permute-start(bf16[768,384]{1,0:T(8,128)(2,1)} %pad_maximum_fusion.11), channel_id=1, source_target_pairs={{0,16},{16,0},{1,17},{17,1},{2,18},{18,2},{3,19},{19,3},{4,20},{20... | collective-permute-start | bytes 1769480 | tf_op jit(solution)/shard_map/ppermute | solution.py:548
  25.4 11.1 %collective-permute-start.7 = (bf16[2,128,768]{2,1,0:T(8,128)(2,1)S(1)}, bf16[2,128,768]{2,1,0:T(8,128)(2,1)S(1)}, u32[]{:S(2)}, u32[]{:S(2)}) collective-permute-start(bf16[2,128,768]{2,1,0:T(8,128)(2,1)S(1)} %constant_dynamic-update-slice_fusion.nz), channel_id=1, source_target_pairs={{0,2},{1,3},{2,0},{3,1},{4,6},{5,7},{6,4},{7,5},{8,10},{9,11},{10,... | collective-permute-start | bytes 1179656 | tf_op jit(solution)/shard_map/ppermute | solution.py:548
  32.1 11.6 %collective-permute-start.1 = (bf16[2,128,768]{2,1,0:T(8,128)(2,1)S(1)}, bf16[2,128,768]{2,1,0:T(8,128)(2,1)S(1)}, u32[]{:S(2)}, u32[]{:S(2)}) collective-permute-start(bf16[2,128,768]{2,1,0:T(8,128)(2,1)S(1)} %collective-permute-done.fz), channel_id=1, source_target_pairs={{0,2},{1,3},{2,0},{3,1},{4,6},{5,7},{6,4},{7,5},{8,10},{9,11},{10,... | collective-permute-start | bytes 1179656 | tf_op jit(solution)/shard_map/ppermute | solution.py:548
  36.6 26.2 %collective-permute-start.8 = (bf16[2,2,128,768]{3,2,1,0:T(8,128)(2,1)S(1)}, bf16[2,2,128,768]{3,2,1,0:T(8,128)(2,1)S(1)}, u32[]{:S(2)}, u32[]{:S(2)}) collective-permute-start(bf16[2,2,128,768]{3,2,1,0:T(8,128)(2,1)S(1)} %pad_maximum_fusion.7), channel_id=1, source_target_pairs={{0,1},{1,0},{2,3},{3,2},{4,5},{5,4},{6,7},{7,6},{8,9},{9,8},{10,11... | collective-permute-start | bytes 2359304 | tf_op jit(solution)/shard_map/ppermute | solution.py:548
  43.7 3.0 %collective-permute-start.2 = (bf16[2,2,128,768]{3,2,1,0:T(8,128)(2,1)S(1)}, bf16[2,2,128,768]{3,2,1,0:T(8,128)(2,1)S(1)}, u32[]{:S(2)}, u32[]{:S(2)}) collective-permute-start(bf16[2,2,128,768]{3,2,1,0:T(8,128)(2,1)S(1)} %pad_maximum_fusion.6), channel_id=1, source_target_pairs={{0,1},{1,0},{2,3},{3,2},{4,5},{5,4},{6,7},{7,6},{8,9},{9,8},{10,11... | collective-permute-start | bytes 2359304 | tf_op jit(solution)/shard_map/ppermute | solution.py:548
  50.8 14.3 %copy-start.6 = (bf16[1024,768]{1,0:T(8,128)(2,1)}, bf16[1024,768]{1,0:T(8,128)(2,1)S(1)}, u32[]{:S(2)}) copy-start(bf16[1024,768]{1,0:T(8,128)(2,1)S(1)} %get-tuple-element.67.n1o.refs_9_) | copy-start | bytes 4718596
  50.8 10.6 %copy-start.45 = (bf16[384,3,192]{0,2,1:T(8,128)(2,1)S(1)}, bf16[384,3,192]{0,2,1:T(8,128)(2,1)}, u32[]{:S(2)}) copy-start(bf16[384,3,192]{0,2,1:T(8,128)(2,1)} %param.17) | copy-start | bytes 1327108
  60.9 18.4 %copy-start.32 = (f32[8,768]{1,0:T(8,128)}, f32[8,768]{1,0:T(8,128)S(1)}, u32[]{:S(2)}) copy-start(f32[8,768]{1,0:T(8,128)S(1)} %get-tuple-element.66.after.refs_15_) | copy-start | bytes 73732
  60.9 30.2 %collective-permute-start.10 = (bf16[768,768]{1,0:T(8,128)(2,1)S(1)}, bf16[768,768]{1,0:T(8,128)(2,1)S(1)}, u32[]{:S(2)}, u32[]{:S(2)}) collective-permute-start(bf16[768,768]{1,0:T(8,128)(2,1)S(1)} %get-tuple-element.80), channel_id=1, source_target_pairs={{0,16},{16,0},{1,17},{17,1},{2,18},{18,2},{3,19},{19,3},{4,20},{20... | collective-permute-start | bytes 3538952 | tf_op jit(solution)/shard_map/ppermute | solution.py:548
  91.8 13.2 %copy-start.3 = (f32[768,768]{1,0:T(8,128)}, f32[768,768]{1,0:T(8,128)S(1)}, u32[]{:S(2)}) copy-start(f32[768,768]{1,0:T(8,128)S(1)} %convert_add_fusion.1.after) | copy-start | bytes 7077892
  92.8 19.5 %collective-permute-start.13 = (bf16[384,768]{1,0:T(8,128)(2,1)}, bf16[384,768]{1,0:T(8,128)(2,1)}, u32[]{:S(2)}, u32[]{:S(2)}) collective-permute-start(bf16[384,768]{1,0:T(8,128)(2,1)} %dynamic-slice_convert_fusion), channel_id=1, source_target_pairs={{0,4},{4,0},{8,12},{12,8},{1,5},{5,1},{9,13},{13,9},{2,6},{6,2},{1... | collective-permute-start | bytes 1769480 | tf_op jit(solution)/shard_map/ppermute | solution.py:548
  109.2 10.6 %collective-permute-start.11 = (bf16[2,256,768]{2,1,0:T(8,128)(2,1)}, bf16[2,256,768]{2,1,0:T(8,128)(2,1)}, u32[]{:S(2)}, u32[]{:S(2)}) collective-permute-start(bf16[2,256,768]{2,1,0:T(8,128)(2,1)} %get-tuple-element.84), channel_id=1, source_target_pairs={{0,1},{1,0},{2,3},{3,2},{4,5},{5,4},{6,7},{7,6},{8,9},{9,8},{10,11... | collective-permute-start | bytes 2359304 | tf_op jit(solution)/shard_map/ppermute | solution.py:548
  112.2 91.0 %copy-start.52 = (f32[2,128]{1,0:T(2,128)}, f32[2,128]{1,0:T(2,128)S(1)}, u32[]{:S(2)}) copy-start(f32[2,128]{1,0:T(2,128)S(1)} %add_rsqrt_fusion) | copy-start | bytes 3076
  114.1 17.2 %collective-permute-start.33 = (bf16[192,768]{1,0:T(8,128)(2,1)S(1)}, bf16[192,768]{1,0:T(8,128)(2,1)S(1)}, u32[]{:S(2)}, u32[]{:S(2)}) collective-permute-start(bf16[192,768]{1,0:T(8,128)(2,1)S(1)} %dynamic-slice_convert_fusion.1), channel_id=1, source_target_pairs={{0,8},{4,12},{8,0},{12,4},{1,9},{5,13},{9,1},{13,5},{2,10},{6,14},... | collective-permute-start | bytes 884744 | tf_op jit(solution)/shard_map/ppermute | solution.py:548
  119.5 14.2 %collective-permute-start.19 = (bf16[2,256,768]{2,1,0:T(8,128)(2,1)S(1)}, bf16[2,256,768]{2,1,0:T(8,128)(2,1)S(1)}, u32[]{:S(2)}, u32[]{:S(2)}) collective-permute-start(bf16[2,256,768]{2,1,0:T(8,128)(2,1)S(1)} %get-tuple-element.102), channel_id=1, source_target_pairs={{0,1},{1,0},{2,3},{3,2},{4,5},{5,4},{6,7},{7,6},{8,9},{9,8},{10,11... | collective-permute-start | bytes 2359304 | tf_op jit(solution)/shard_map/ppermute | solution.py:548
  127.7 6.7 %collective-permute-start.14 = (bf16[2,256,768]{2,1,0:T(8,128)(2,1)S(1)}, bf16[2,256,768]{2,1,0:T(8,128)(2,1)S(1)}, u32[]{:S(2)}, u32[]{:S(2)}) collective-permute-start(bf16[2,256,768]{2,1,0:T(8,128)(2,1)S(1)} %get-tuple-element.99), channel_id=1, source_target_pairs={{0,1},{1,0},{2,3},{3,2},{4,5},{5,4},{6,7},{7,6},{8,9},{9,8},{10,11... | collective-permute-start | bytes 2359304 | tf_op jit(solution)/shard_map/ppermute | solution.py:548
  128.2 12.0 %collective-permute-start.12 = (bf16[2,128,768]{2,1,0:T(8,128)(2,1)S(1)}, bf16[2,128,768]{2,1,0:T(8,128)(2,1)S(1)}, u32[]{:S(2)}, u32[]{:S(2)}) collective-permute-start(bf16[2,128,768]{2,1,0:T(8,128)(2,1)S(1)} %fusion.17), channel_id=1, source_target_pairs={{0,2},{1,3},{2,0},{3,1},{4,6},{5,7},{6,4},{7,5},{8,10},{9,11},{10,... | collective-permute-start | bytes 1179656 | tf_op jit(solution)/shard_map/ppermute | solution.py:548
  129.7 22.1 %collective-permute-start.25 = (bf16[832,384]{1,0:T(8,128)(2,1)S(1)}, bf16[832,384]{1,0:T(8,128)(2,1)S(1)}, u32[]{:S(2)}, u32[]{:S(2)}) collective-permute-start(bf16[832,384]{1,0:T(8,128)(2,1)S(1)} %get-tuple-element.106), channel_id=1, source_target_pairs={{0,16},{16,0},{1,17},{17,1},{2,18},{18,2},{3,19},{19,3},{4,20},{20... | collective-permute-start | bytes 1916936 | tf_op jit(solution)/shard_map/ppermute | solution.py:548
  131.3 20.1 %collective-permute-start.34 = (bf16[192,768]{1,0:T(8,128)(2,1)S(1)}, bf16[192,768]{1,0:T(8,128)(2,1)S(1)}, u32[]{:S(2)}, u32[]{:S(2)}) collective-permute-start(bf16[192,768]{1,0:T(8,128)(2,1)S(1)} %add_convert_fusion), channel_id=1, source_target_pairs={{0,8},{4,12},{8,0},{12,4},{1,9},{5,13},{9,1},{13,5},{2,10},{6,14},... | collective-permute-start | bytes 884744 | tf_op jit(solution)/shard_map/ppermute | solution.py:548
  133.8 14.8 %collective-permute-start.20 = (bf16[2,128,768]{2,1,0:T(8,128)(2,1)S(1)}, bf16[2,128,768]{2,1,0:T(8,128)(2,1)S(1)}, u32[]{:S(2)}, u32[]{:S(2)}) collective-permute-start(bf16[2,128,768]{2,1,0:T(8,128)(2,1)S(1)} %fusion.19), channel_id=1, source_target_pairs={{0,2},{1,3},{2,0},{3,1},{4,6},{5,7},{6,4},{7,5},{8,10},{9,11},{10,... | collective-permute-start | bytes 1179656 | tf_op jit(solution)/shard_map/ppermute | solution.py:548
  140.4 15.2 %collective-permute-start.15 = (bf16[128,768]{1,0:T(8,128)(2,1)S(1)}, bf16[128,768]{1,0:T(8,128)(2,1)S(1)}, u32[]{:S(2)}, u32[]{:S(2)}) collective-permute-start(bf16[128,768]{1,0:T(8,128)(2,1)S(1)} %get-tuple-element.159), channel_id=1, source_target_pairs={{0,8},{4,12},{8,0},{12,4},{1,9},{5,13},{9,1},{13,5},{2,10},{6,14},... | collective-permute-start | bytes 589832 | tf_op jit(solution)/shard_map/ppermute | solution.py:548
  142.8 13.5 %collective-permute-start.18 = (bf16[2,128,768]{2,1,0:T(8,128)(2,1)S(1)}, bf16[2,128,768]{2,1,0:T(8,128)(2,1)S(1)}, u32[]{:S(2)}, u32[]{:S(2)}) collective-permute-start(bf16[2,128,768]{2,1,0:T(8,128)(2,1)S(1)} %fusion.18), channel_id=1, source_target_pairs={{0,2},{1,3},{2,0},{3,1},{4,6},{5,7},{6,4},{7,5},{8,10},{9,11},{10,... | collective-permute-start | bytes 1179656 | tf_op jit(solution)/shard_map/ppermute | solution.py:548
  148.7 18.7 %collective-permute-start.21 = (bf16[2,128,768]{2,1,0:T(8,128)(2,1)S(1)}, bf16[2,128,768]{2,1,0:T(8,128)(2,1)S(1)}, u32[]{:S(2)}, u32[]{:S(2)}) collective-permute-start(bf16[2,128,768]{2,1,0:T(8,128)(2,1)S(1)} %fusion.9), channel_id=1, source_target_pairs={{0,4},{4,0},{8,12},{12,8},{1,5},{5,1},{9,13},{13,9},{2,6},{6,2},{1... | collective-permute-start | bytes 1179656 | tf_op jit(solution)/shard_map/ppermute | solution.py:548
  151.5 42.5 %collective-permute-start.35 = (bf16[2,192,768]{2,1,0:T(8,128)(2,1)S(1)}, bf16[2,192,768]{2,1,0:T(8,128)(2,1)S(1)}, u32[]{:S(2)}, u32[]{:S(2)}) collective-permute-start(bf16[2,192,768]{2,1,0:T(8,128)(2,1)S(1)} %pad_maximum_fusion.12), channel_id=1, source_target_pairs={{0,4},{4,0},{8,12},{12,8},{1,5},{5,1},{9,13},{13,9},{2,6},{6,2},{1... | collective-permute-start | bytes 1769480 | tf_op jit(solution)/shard_map/ppermute | solution.py:548
  152.1 26.7 %collective-permute-start.26 = (bf16[208,384]{1,0:T(8,128)(2,1)S(1)}, bf16[208,384]{1,0:T(8,128)(2,1)S(1)}, u32[]{:S(2)}, u32[]{:S(2)}) collective-permute-start(bf16[208,384]{1,0:T(8,128)(2,1)S(1)} %get-tuple-element.135), channel_id=1, source_target_pairs={{0,12},{4,8},{8,4},{12,0},{1,13},{5,9},{9,5},{13,1},{2,14},{6,10},... | collective-permute-start | bytes 479240 | tf_op jit(solution)/shard_map/ppermute | solution.py:548
  155.6 23.2 %collective-permute-start.27 = (bf16[208,384]{1,0:T(8,128)(2,1)S(1)}, bf16[208,384]{1,0:T(8,128)(2,1)S(1)}, u32[]{:S(2)}, u32[]{:S(2)}) collective-permute-start(bf16[208,384]{1,0:T(8,128)(2,1)S(1)} %get-tuple-element.137), channel_id=1, source_target_pairs={{0,8},{4,12},{8,0},{12,4},{1,9},{5,13},{9,1},{13,5},{2,10},{6,14},... | collective-permute-start | bytes 479240 | tf_op jit(solution)/shard_map/ppermute | solution.py:548
  156.3 34.7 %collective-permute-start.28 = (bf16[208,384]{1,0:T(8,128)(2,1)S(1)}, bf16[208,384]{1,0:T(8,128)(2,1)S(1)}, u32[]{:S(2)}, u32[]{:S(2)}) collective-permute-start(bf16[208,384]{1,0:T(8,128)(2,1)S(1)} %get-tuple-element.136), channel_id=1, source_target_pairs={{0,4},{4,0},{8,12},{12,8},{1,5},{5,1},{9,13},{13,9},{2,6},{6,2},{1... | collective-permute-start | bytes 479240 | tf_op jit(solution)/shard_map/ppermute | solution.py:548
  167.4 23.9 %collective-permute-start.16 = (bf16[2,128,768]{2,1,0:T(8,128)(2,1)S(1)}, bf16[2,128,768]{2,1,0:T(8,128)(2,1)S(1)}, u32[]{:S(2)}, u32[]{:S(2)}) collective-permute-start(bf16[2,128,768]{2,1,0:T(8,128)(2,1)S(1)} %pad_maximum_fusion.15), channel_id=1, source_target_pairs={{0,2},{1,3},{2,0},{3,1},{4,6},{5,7},{6,4},{7,5},{8,10},{9,11},{10,... | collective-permute-start | bytes 1179656 | tf_op jit(solution)/shard_map/ppermute | solution.py:548
  178.7 13.6 %collective-permute-start.22 = (bf16[128,768]{1,0:T(8,128)(2,1)S(1)}, bf16[128,768]{1,0:T(8,128)(2,1)S(1)}, u32[]{:S(2)}, u32[]{:S(2)}) collective-permute-start(bf16[128,768]{1,0:T(8,128)(2,1)S(1)} %fusion.21), channel_id=1, source_target_pairs={{0,8},{4,12},{8,0},{12,4},{1,9},{5,13},{9,1},{13,5},{2,10},{6,14},... | collective-permute-start | bytes 589832 | tf_op jit(solution)/shard_map/ppermute | solution.py:548
  191.1 9.8 %collective-permute-start.29 = (bf16[208,384]{1,0:T(8,128)(2,1)S(1)}, bf16[208,384]{1,0:T(8,128)(2,1)S(1)}, u32[]{:S(2)}, u32[]{:S(2)}) collective-permute-start(bf16[208,384]{1,0:T(8,128)(2,1)S(1)} %add_convert_fusion.1), channel_id=1, source_target_pairs={{0,8},{4,12},{8,0},{12,4},{1,9},{5,13},{9,1},{13,5},{2,10},{6,14},... | collective-permute-start | bytes 479240 | tf_op jit(solution)/shard_map/ppermute | solution.py:548
  192.3 29.0 %collective-permute-start.17 = (bf16[2,2,128,768]{3,2,1,0:T(8,128)(2,1)}, bf16[2,2,128,768]{3,2,1,0:T(8,128)(2,1)}, u32[]{:S(2)}, u32[]{:S(2)}) collective-permute-start(bf16[2,2,128,768]{3,2,1,0:T(8,128)(2,1)} %pad_maximum_fusion.8), channel_id=1, source_target_pairs={{0,1},{1,0},{2,3},{3,2},{4,5},{5,4},{6,7},{7,6},{8,9},{9,8},{10,11... | collective-permute-start | bytes 2359304 | tf_op jit(solution)/shard_map/ppermute | solution.py:548
  193.1 10.2 %copy-start.54 = (f32[2,128]{1,0:T(2,128)}, f32[2,128]{1,0:T(2,128)S(1)}, u32[]{:S(2)}) copy-start(f32[2,128]{1,0:T(2,128)S(1)} %broadcast_multiply_fusion) | copy-start | bytes 3076
  193.1 10.2 %copy-start.56 = (f32[2,128]{1,0:T(2,128)}, f32[2,128]{1,0:T(2,128)S(1)}, u32[]{:S(2)}) copy-start(f32[2,128]{1,0:T(2,128)S(1)} %broadcast_multiply_fusion.1) | copy-start | bytes 3076
  193.4 18.5 %collective-permute-start.23 = (bf16[2,128,768]{2,1,0:T(8,128)(2,1)S(1)}, bf16[2,128,768]{2,1,0:T(8,128)(2,1)S(1)}, u32[]{:S(2)}, u32[]{:S(2)}) collective-permute-start(bf16[2,128,768]{2,1,0:T(8,128)(2,1)S(1)} %fusion.7), channel_id=1, source_target_pairs={{0,2},{1,3},{2,0},{3,1},{4,6},{5,7},{6,4},{7,5},{8,10},{9,11},{10,... | collective-permute-start | bytes 1179656 | tf_op jit(solution)/shard_map/ppermute | solution.py:548
  201.0 9.5 %collective-permute-start.30 = (bf16[2,208,384]{2,1,0:T(8,128)(2,1)S(1)}, bf16[2,208,384]{2,1,0:T(8,128)(2,1)S(1)}, u32[]{:S(2)}, u32[]{:S(2)}) collective-permute-start(bf16[2,208,384]{2,1,0:T(8,128)(2,1)S(1)} %pad_maximum_fusion.17), channel_id=1, source_target_pairs={{0,4},{4,0},{8,12},{12,8},{1,5},{5,1},{9,13},{13,9},{2,6},{6,2},{1... | collective-permute-start | bytes 958472 | tf_op jit(solution)/shard_map/ppermute | solution.py:548
  210.7 2.7 %collective-permute-start.31 = (f32[8,768]{1,0:T(8,128)S(1)}, f32[8,768]{1,0:T(8,128)S(1)}, u32[]{:S(2)}, u32[]{:S(2)}) collective-permute-start(f32[8,768]{1,0:T(8,128)S(1)} %pad_maximum_fusion.18), channel_id=1, source_target_pairs={{0,1},{1,0},{2,3},{3,2},{4,5},{5,4},{6,7},{7,6},{8,9},{9,8},{10,11... | collective-permute-start | bytes 73736 | tf_op jit(solution)/shard_map/ppermute | solution.py:548
  212.8 10.0 %collective-permute-start.24 = (bf16[2,2,128,768]{3,2,1,0:T(8,128)(2,1)}, bf16[2,2,128,768]{3,2,1,0:T(8,128)(2,1)}, u32[]{:S(2)}, u32[]{:S(2)}) collective-permute-start(bf16[2,2,128,768]{3,2,1,0:T(8,128)(2,1)} %pad_maximum_fusion.10), channel_id=1, source_target_pairs={{0,1},{1,0},{2,3},{3,2},{4,5},{5,4},{6,7},{7,6},{8,9},{9,8},{10,11... | collective-permute-start | bytes 2359304 | tf_op jit(solution)/shard_map/ppermute | solution.py:548
  213.9 6.0 %collective-permute-start.32 = (f32[8,768]{1,0:T(8,128)}, f32[8,768]{1,0:T(8,128)}, u32[]{:S(2)}, u32[]{:S(2)}) collective-permute-start(f32[8,768]{1,0:T(8,128)} %fusion.27), channel_id=1, source_target_pairs={{0,2},{1,3},{2,0},{3,1},{4,6},{5,7},{6,4},{7,5},{8,10},{9,11},{10,... | collective-permute-start | bytes 73736 | tf_op jit(solution)/shard_map/ppermute | solution.py:548
  (49 other events, 136.1 us)

commit v10 on v9

--- a/solution.py
+++ b/solution.py
@@ -451,7 +451,8 @@
     n1_ref, w_ref, s1_ref, *refs = refs
     if own:
         (half_b, a2_ref, b1_ref, small_ff, small_other, mix_other, out_part,
-         keep_ref, send_ref, first_ref, second_ref, mix, small) = refs
+         keep_ref, send_ref, small, first_ref, *refs) = refs
+        *second, mix = refs
     else:
         keep_b, ff_half, keep_ref, send_ref, mix, small = refs
     i = pl.program_id(0)
@@ -487,18 +488,13 @@
             small[4:6, :] = small_ff[0:2, :]
             if split:
                 half = mix.shape[1] // 2
-                vectors = small[...].astype(BF16)
-                for ref, f in ((first_ref, at[3]), (second_ref, 1 - at[3])):
+                for ref, f in ((first_ref, at[3]), (second[0], 1 - at[3])):
                     piece = pl.ds(pl.multiple_of(f * half, 128), half)
                     ref[: 3 * wide, :] = mix[:, piece].astype(ref.dtype)
-                    ref[3 * wide : 4 * wide, :] = out_part[:, piece].astype(ref.dtype)
-                    both = jnp.concatenate([vectors[:, :half], vectors[:, half:]], axis=0)
-                    ref[4 * wide : 4 * wide + 16, :] = both.astype(ref.dtype)
-                    ref[4 * wide + 16 :, :] = jnp.zeros((48, half), ref.dtype)
+                    ref[3 * wide :, :] = out_part[:, piece].astype(ref.dtype)
             else:
                 first_ref[: 3 * wide, :] = mix[...]
                 first_ref[3 * wide :, :] = out_part[...]
-                second_ref[...] = small[...]
 
 
 def back(own, split, at, grads, n1, weights, scale, extra):
@@ -524,11 +520,12 @@
     else:
         specs += [earlier, row, whole(width), whole(8, width), whole(8, width), whole(2 * wide, width),
                   whole(wide, width)]
-        scratch = [pltpu.VMEM((tall, width), F32), pltpu.VMEM((8, width), F32)]
+        scratch = [pltpu.VMEM((tall, width), F32)]
+        parts = [shape(8, width)]
         if split:
-            parts = [shape(4 * wide + 64, half), low_shape(4 * wide + 64, half)]
+            parts += [shape(4 * wide, half), low_shape(4 * wide, half)]
         else:
-            parts = [shape(4 * wide, width), shape(8, width)]
+            parts += [shape(4 * wide, width)]
     return pl.pallas_call(
         functools.partial(back_kernel, own, split, heads),
         grid_spec=pltpu.PrefetchScalarGridSpec(
@@ -719,7 +716,7 @@
         False, split, at, (dk, dv), n1_other, weights, first_scale, (keep_b, ff_half)
     )
     half_b = over_core(keep_b, send_b)
-    keep_w, send_w, late_first, late_second = back(
+    keep_w, send_w, small, *late_parts = back(
         True, split, at, (dq, dk, dv), n1_own, weights, first_scale,
         (half_b, a2, first_shift, small_ff, small_other, mix_other, out_part),
     )
@@ -729,8 +726,8 @@
     def over_ctx(v, distance, *earlier):
         return tie(swap(v.astype(BF16), "ctx", 4, distance), *earlier).astype(F32)
 
-    def gather_tp(ours):
-        pair = jnp.stack([ours, swap(ours, "tp", 4, 2)])
+    def gather_tp(ours, *earlier):
+        pair = jnp.stack([ours, tie(swap(ours, "tp", 4, 2), *earlier)])
         core = swap(pair, "tp", 4, 1)
         pieces = by_xor((pair[0], core[0], pair[1], core[1]), t)
         pieces = jnp.concatenate(pieces, axis=1)
@@ -739,11 +736,6 @@
 
     sums_b = over_x(half_b, half_w)
     branches = jnp.stack([sums_b[0], over_ctx(sums_b[1], 2)]).astype(BF16)
-    block_out = gather_tp(branches)
-    block_out = (
-        inputs.astype(F32) + block_out + (attention_output_bias + down_projection_bias)
-    )
-
     sums_o = over_x(half_o, half_w)
     sums_w = over_x(half_w)
     sums_w = sums_w + over_ctx(sums_o, 1)
@@ -755,29 +747,31 @@
         - xhat * jnp.mean(a * xhat, axis=-1, keepdims=True)
     )
     norm_grad = norm_grad.astype(BF16)
+    block_out = gather_tp(branches, a)
+    block_out = (
+        inputs.astype(F32) + block_out + (attention_output_bias + down_projection_bias)
+    )
     inputs_grad = cotangent.astype(F32) + gather_tp(norm_grad)
 
     if split:
-        q = double(pair_up(halve(ff_half, 2, c // 2), sums_o), c, norm_grad)
+        q = double(pair_up(halve(ff_half, 2, c // 2), norm_grad), c)
         up_total = jnp.concatenate(q[:2], axis=0).astype(F32)
         down_total = jnp.concatenate(q[2:], axis=0).astype(F32)
         down_total = jnp.concatenate(
             [down_total[:, : width // 2], down_total[:, width // 2 :]], axis=0
         )
-        late = late_first + tie(swap(late_second, "fsdp", 2, 1), sums_o).astype(F32)
-        late = double(pair_up(quarter_sum(late, c, sums_w), norm_grad), c)
-        late = jnp.concatenate(late, axis=0).astype(F32)
-        small = jnp.concatenate([late[4 * local : 4 * local + 8], late[4 * local + 8 :][:8]], axis=1)
+        late = late_parts[0] + tie(swap(late_parts[1], "fsdp", 2, 1), sums_o).astype(F32)
+        late = double(pair_up(quarter_sum(late, c, a), norm_grad), c)
     else:
         q = sum_over_ctx(scatter_any(ff_first, 0), c)
         up_total = jnp.concatenate(q, axis=0).astype(F32)
         q = sum_over_ctx(scatter_any(ff_second, 1), c)
         down_total = jnp.concatenate(q, axis=0).astype(F32)
-        q = sum_over_ctx(scatter_any(late_first, 1), c)
-        late = jnp.concatenate(q, axis=0).astype(F32)
-        small = butterfly(butterfly(late_second, "fsdp", fsdp), "ctx", 4)
-    mix_total = late[: 3 * local].reshape(3, local, -1).transpose(2, 0, 1)
-    out_total = late[3 * local : 4 * local]
+        q = sum_over_ctx(scatter_any(late_parts[0], 1), c)
+        late = q
+    mix_total = jnp.stack(late[:3]).astype(F32).transpose(2, 0, 1)
+    out_total = late[3].astype(F32)
+    small = butterfly(butterfly(tie(small, norm_grad), "fsdp", fsdp), "ctx", 4)
     norm_small = butterfly(small, "tp", 4)
     bias_total = norm_small[5] * 0.25
     return (

time: 232 us -> 238 us (1.026)
  starting transfers between devices: 35.9 us -> 40.7 us
    ppermute x36 -> x39, starting transfers between devices: 35.9 us -> 40.7 us  [swap(): return lax.ppermute(v, axis, [(i, i ^ distance) for i in range(size)])]
    unnamed x124 -> x132, local copies, waits for them, and re-layouts: 8.16 us -> 9.54 us
    ppermute x36 -> x39, waiting for transfers between devices: 84 us -> 84.6 us  [swap(): return lax.ppermute(v, axis, [(i, i ^ distance) for i in range(size)])]
  transfers between devices with their start and end apart: 36 -> 39, of which waited for: 14 -> 16; matrix products, arithmetic and copies ran while one was open for 13% -> 13% of each run, Pallas kernels for 27% -> 26%
where the time goes in v10:
time: 238 us; the launch traced here: 237 us
  waiting for transfers between devices  84.6 us (36%)
  Pallas kernels  62.8 us (26%)
  starting transfers between devices  40.7 us (17%)
  other arithmetic  33 us (14%)
  local copies, waits for them, and re-layouts  14.3 us (6%)
    ppermute x39, waiting for transfers between devices, swap(): return lax.ppermute(v, axis, [(i, i ^ distance) for i in range(size)])  84.6 us
    ppermute x39, starting transfers between devices, swap(): return lax.ppermute(v, axis, [(i, i ^ distance) for i in range(size)])  40.7 us
    pallas_call x3, Pallas kernels, attention(): pl.pallas_call(attention_kernel, grid=(rows // lanes,), in_specs=[pl.Bloc...  29 us
    pallas_call x2, Pallas kernels, back(): pl.pallas_call(functools.partial(back_kernel, own, split, heads), grid_sp...  11.1 us
    pallas_call x1, Pallas kernels, feed_forward(): pl.pallas_call(functools.partial(forward_kernel, split), grid_spec=pltpu....  9.99 us
    unnamed x132, local copies, waits for them, and re-layouts  9.54 us
    pallas_call x2, Pallas kernels, norms(): pl.pallas_call(kernel, grid_spec=pltpu.PrefetchScalarGridSpec(num_scalar_...  4.93 us
  transfers between devices with their start and end apart: 39, of which 16 were waited for; matrix products, arithmetic and copies ran while one was open for 13% of the time, Pallas kernels for 26%

profile of v10, /device:TPU:0, one launch (start us, length us, event | category | flops | bytes accessed | tf_op | source)
XLA Modules:
  0.0 237.0 jit_solution(8374689123876603665)
XLA Ops:
  1.9 5.1 %collective-permute-start.6 = (bf16[1,128,768]{2,1,0:T(8,128)(2,1)S(1)}, bf16[1,128,768]{2,1,0:T(8,128)(2,1)S(1)}, u32[]{:S(2)}, u32[]{:S(2)}) collective-permute-start(bf16[1,128,768]{2,1,0:T(8,128)(2,1)S(1)} %get-tuple-element.138), channel_id=1, source_target_pairs={{0,12},{4,8},{8,4},{12,0},{1,13},{5,9},{9,5},{13,1},{2,14},{6,10},... | collective-permute-start | bytes 589832 | tf_op jit(solution)/shard_map/ppermute | solution.py:545
  8.7 1.5 collective-permute-start.3
  13.0 10.9 %collective-permute-done.5 = bf16[1,128,768]{2,1,0:T(8,128)(2,1)S(1)} collective-permute-done((bf16[1,128,768]{2,1,0:T(8,128)(2,1)S(1)}, bf16[1,128,768]{2,1,0:T(8,128)(2,1)S(1)}, u32[]{:S(2)}, u32[]{:S(2)}) %collective-permute-start.5) | collective-permute-done | bytes 196640 | tf_op jit(solution)/shard_map/ppermute | solution.py:545
  23.8 1.5 collective-permute-start.9
  25.4 1.6 collective-permute-start.7
  27.0 5.1 %collective-permute-done.fz = bf16[2,128,768]{2,1,0:T(8,128)(2,1)S(1)} collective-permute-done((bf16[2,128,768]{2,1,0:T(8,128)(2,1)}, bf16[2,128,768]{2,1,0:T(8,128)(2,1)S(1)}, u32[]{:S(2)}, u32[]{:S(2)}) %collective-permute-start) | collective-permute-done | bytes 393248 | tf_op jit(solution)/shard_map/ppermute | solution.py:545
  32.1 1.5 collective-permute-start.1
  33.7 2.8 %collective-permute-done.7.nx = bf16[2,128,768]{2,1,0:T(8,128)(2,1)S(1)} collective-permute-done((bf16[2,128,768]{2,1,0:T(8,128)(2,1)S(1)}, bf16[2,128,768]{2,1,0:T(8,128)(2,1)S(1)}, u32[]{:S(2)}, u32[]{:S(2)}) %collective-permute-start.7) | collective-permute-done | bytes 393248 | tf_op jit(solution)/shard_map/ppermute | solution.py:545
  36.7 6.9 %collective-permute-done.1.fx = bf16[2,128,768]{2,1,0:T(8,128)(2,1)S(1)} collective-permute-done((bf16[2,128,768]{2,1,0:T(8,128)(2,1)S(1)}, bf16[2,128,768]{2,1,0:T(8,128)(2,1)S(1)}, u32[]{:S(2)}, u32[]{:S(2)}) %collective-permute-start.1) | collective-permute-done | bytes 393248 | tf_op jit(solution)/shard_map/ppermute | solution.py:545
  45.1 1.5 broadcast_select_fusion.7
  46.8 1.2 copy-done
  48.1 2.7 %shard_map.254 = (bf16[1024,768]{1,0:T(8,128)(2,1)S(1)}, bf16[1024,768]{1,0:T(8,128)(2,1)S(1)}, bf16[1024,768]{1,0:T(8,128)(2,1)S(1)}, f32[24,1024]{1,0:T(8,128)S(1)}) custom-call(s32[4]{0:T(128)S(1)} %pad_add_fusion.at, bf16[2,512,768]{2,1,0:T(8,128)(2,1)S(1)} %copy-done, bf16[2,512,768]{2,1,0:T(8,128)(2,1)S(1)} %copy-done, ...), custom_call_target="tpu_custom_call" | custom-call | bytes 4718592 | tf_op jit(solution)/shard_map/pallas_call | solution.py:140
  50.8 10.0 %shard_map.255 = (bf16[1024,768]{1,0:T(8,128)(2,1)S(1)}, bf16[1024,768]{1,0:T(8,128)(2,1)S(1)}, f32[8,768]{1,0:T(8,128)S(1)}, f32[768,768]{1,0:T(8,128)S(1)}, bf16[768,768]{1,0:T(8,128)(2,1)S(1)}) custom-call(s32[4]{0:T(128)S(1)} %pad_add_fusion.at, bf16[1024,768]{1,0:T(8,128)(2,1)S(1)} %get-tuple-element.66.n2_ref, ...), custom_call_target="tpu_custom_call" | custom-call | flops 7247757312 | bytes 16777216 | tf_op jit(solution)/shard_map/pallas_call | solution.py:386
  61.4 1.3 broadcast_select_fusion.5
  62.9 2.2 shard_map.256
  65.1 4.5 %shard_map.257 = (bf16[192,2048]{1,0:T(8,128)(2,1)S(1)}, bf16[192,2048]{1,0:T(8,128)(2,1)S(1)}, bf16[192,1024]{1,0:T(8,128)(2,1)S(1)}, bf16[192,1024]{1,0:T(8,128)(2,1)S(1)}) custom-call(bf16[1024,768]{1,0:T(8,128)(2,1)S(1)} %get-tuple-element.69.n1o.refs_9_, bf16[1024,768]{1,0:T(8,128)(2,1)S(1)} %get-tuple-element.71.n1x.refs_6_, ...), custom_call_target="tpu_custom_call" | custom-call | flops 1811939328 | bytes 9437184 | tf_op jit(solution)/shard_map/pallas_call | solution.py:204
  69.6 9.7 %shard_map.259 = (bf16[64,1024]{1,0:T(8,128)(2,1)S(1)}, bf16[64,1024]{1,0:T(8,128)(2,1)S(1)}, bf16[64,2048]{1,0:T(8,128)(2,1)S(1)}, bf16[64,2048]{1,0:T(8,128)(2,1)S(1)}) custom-call(f32[8,768]{1,0:T(8,128)S(1)} %get-tuple-element.68.after.refs_15_, bf16[192,1024]{1,0:T(8,128)(2,1)S(1)} %get-tuple-element.75.q_ref, ...), custom_call_target="tpu_custom_call" | custom-call | flops 5368709120 | bytes 2097152 | tf_op jit(solution)/shard_map/pallas_call | solution.py:307
  81.3 9.7 %shard_map.258 = (bf16[64,1024]{1,0:T(8,128)(2,1)S(1)}, bf16[64,1024]{1,0:T(8,128)(2,1)S(1)}, bf16[64,2048]{1,0:T(8,128)(2,1)S(1)}, bf16[64,2048]{1,0:T(8,128)(2,1)S(1)}) custom-call(f32[8,768]{1,0:T(8,128)S(1)} %get-tuple-element.68.after.refs_15_, bf16[192,1024]{1,0:T(8,128)(2,1)S(1)} %get-tuple-element.75.q_ref, ...), custom_call_target="tpu_custom_call" | custom-call | flops 5368709120 | bytes 2097152 | tf_op jit(solution)/shard_map/pallas_call | solution.py:307
  92.7 2.6 %collective-permute-start.13 = (bf16[384,768]{1,0:T(8,128)(2,1)}, bf16[384,768]{1,0:T(8,128)(2,1)}, u32[]{:S(2)}, u32[]{:S(2)}) collective-permute-start(bf16[384,768]{1,0:T(8,128)(2,1)} %dynamic-slice_convert_fusion), channel_id=1, source_target_pairs={{0,4},{4,0},{8,12},{12,8},{1,5},{5,1},{9,13},{13,9},{2,6},{6,2},{1... | collective-permute-start | bytes 1769480 | tf_op jit(solution)/shard_map/ppermute | solution.py:545
  95.3 9.7 %shard_map.260 = (bf16[64,1024]{1,0:T(8,128)(2,1)S(1)}, bf16[64,1024]{1,0:T(8,128)(2,1)S(1)}, bf16[64,2048]{1,0:T(8,128)(2,1)S(1)}, bf16[64,2048]{1,0:T(8,128)(2,1)S(1)}) custom-call(f32[768,768]{1,0:T(8,128)S(1)} %convert_add_fusion.1.after, bf16[192,1024]{1,0:T(8,128)(2,1)S(1)} %get-tuple-element.75.q_ref, bf16[192,1024]{1,0:T(8,128)(2,1)S(1)} %get-tuple-element.76.do_ref, ...), custom_call_target="tpu_custom_call" | custom-call | flops 5368709120 | bytes 2097152 | tf_op jit(solution)/shard_map/pallas_call | solution.py:307
  105.0 3.3 %shard_map.261 = (bf16[2,256,768]{2,1,0:T(8,128)(2,1)S(1)}, bf16[2,256,768]{2,1,0:T(8,128)(2,1)}, f32[192,768]{1,0:T(8,128)S(1)}) custom-call(bf16[64,1024]{1,0:T(8,128)(2,1)S(1)} %get-tuple-element.79.refs_0_, bf16[64,1024]{1,0:T(8,128)(2,1)S(1)} %get-tuple-element.80.refs_1_, bf16[64,1024]{1,0:T(8,128)(2,1)S(1)} %get-tuple-element.83.refs_2_, ...), custom_call_target="tpu_custom_call" | custom-call | flops 603979776 | bytes 8388608 | tf_op jit(solution)/shard_map/pallas_call | solution.py:436
  110.2 1.3 add.151
  112.3 1.7 convert_add_fusion.6.refs_10_
  114.6 4.9 %shard_map.262 = (bf16[2,256,768]{2,1,0:T(8,128)(2,1)S(1)}, bf16[2,256,768]{2,1,0:T(8,128)(2,1)S(1)}, f32[384,768]{1,0:T(8,128)S(1)}, f32[8,768]{1,0:T(8,128)S(1)}) custom-call(s32[4]{0:T(128)S(1)} %pad_add_fusion.at, bf16[64,2048]{1,0:T(8,128)(2,1)S(1)} %copy-done.15, bf16[64,2048]{1,0:T(8,128)(2,1)S(1)} %copy-done.11, bf16[64,2048]{1,0:T(8,128)(2,1)S(1)} %copy-done.19, ...), custom_call_target="tpu_custom_call" | custom-call | flops 1207959552 | bytes 10485760 | tf_op jit(solution)/shard_map/pallas_call | solution.py:529
  119.9 1.5 convert_add_fusion.4
  121.6 6.2 %shard_map.263 = (bf16[2,256,768]{2,1,0:T(8,128)(2,1)S(1)}, bf16[2,256,768]{2,1,0:T(8,128)(2,1)S(1)}, f32[8,768]{1,0:T(8,128)S(1)}, f32[768,384]{1,0:T(8,128)S(1)}, bf16[768,384]{1,0:T(8,128)(2,1)S(1)}) custom-call(s32[4]{0:T(128)S(1)} %pad_add_fusion.at, bf16[64,1024]{1,0:T(8,128)(2,1)S(1)} %copy-done.27, bf16[64,1024]{1,0:T(8,128)(2,1)S(1)} %copy-done.25, ...), custom_call_target="tpu_custom_call" | custom-call | flops 1811939328 | bytes 10485760 | tf_op jit(solution)/shard_map/pallas_call | solution.py:529
  128.2 1.6 collective-permute-start.12
  129.8 1.5 collective-permute-start.25
  131.4 2.3 collective-permute-start.37
  134.7 5.5 %collective-permute-done.12 = bf16[2,128,768]{2,1,0:T(8,128)(2,1)S(1)} collective-permute-done((bf16[2,128,768]{2,1,0:T(8,128)(2,1)S(1)}, bf16[2,128,768]{2,1,0:T(8,128)(2,1)S(1)}, u32[]{:S(2)}, u32[]{:S(2)}) %collective-permute-start.12) | collective-permute-done | bytes 393248 | tf_op jit(solution)/shard_map/ppermute | solution.py:545
  140.4 2.5 %collective-permute-start.15 = (bf16[128,768]{1,0:T(8,128)(2,1)S(1)}, bf16[128,768]{1,0:T(8,128)(2,1)S(1)}, u32[]{:S(2)}, u32[]{:S(2)}) collective-permute-start(bf16[128,768]{1,0:T(8,128)(2,1)S(1)} %get-tuple-element.161), channel_id=1, source_target_pairs={{0,8},{4,12},{8,0},{12,4},{1,9},{5,13},{9,1},{13,5},{2,10},{6,14},... | collective-permute-start | bytes 589832 | tf_op jit(solution)/shard_map/ppermute | solution.py:545
  142.9 1.5 collective-permute-start.17
  144.4 4.3 %collective-permute-done.19 = bf16[2,128,768]{2,1,0:T(8,128)(2,1)S(1)} collective-permute-done((bf16[2,128,768]{2,1,0:T(8,128)(2,1)S(1)}, bf16[2,128,768]{2,1,0:T(8,128)(2,1)S(1)}, u32[]{:S(2)}, u32[]{:S(2)}) %collective-permute-start.19) | collective-permute-done | bytes 393248 | tf_op jit(solution)/shard_map/ppermute | solution.py:545
  149.5 3.5 %collective-permute-start.26 = (bf16[192,384]{1,0:T(8,128)(2,1)S(1)}, bf16[192,384]{1,0:T(8,128)(2,1)S(1)}, u32[]{:S(2)}, u32[]{:S(2)}) collective-permute-start(bf16[192,384]{1,0:T(8,128)(2,1)S(1)} %get-tuple-element.145), channel_id=1, source_target_pairs={{0,12},{4,8},{8,4},{12,0},{1,13},{5,9},{9,5},{13,1},{2,14},{6,10},... | collective-permute-start | bytes 442376 | tf_op jit(solution)/shard_map/ppermute | solution.py:545
  152.9 2.8 %collective-permute-done.15 = bf16[128,768]{1,0:T(8,128)(2,1)S(1)} collective-permute-done((bf16[128,768]{1,0:T(8,128)(2,1)S(1)}, bf16[128,768]{1,0:T(8,128)(2,1)S(1)}, u32[]{:S(2)}, u32[]{:S(2)}) %collective-permute-start.15) | collective-permute-done | bytes 196640 | tf_op jit(solution)/shard_map/ppermute | solution.py:545
  156.4 3.2 %collective-permute-start.28 = (bf16[192,384]{1,0:T(8,128)(2,1)S(1)}, bf16[192,384]{1,0:T(8,128)(2,1)S(1)}, u32[]{:S(2)}, u32[]{:S(2)}) collective-permute-start(bf16[192,384]{1,0:T(8,128)(2,1)S(1)} %get-tuple-element.146), channel_id=1, source_target_pairs={{0,4},{4,0},{8,12},{12,8},{1,5},{5,1},{9,13},{13,9},{2,6},{6,2},{1... | collective-permute-start | bytes 442376 | tf_op jit(solution)/shard_map/ppermute | solution.py:545
  159.6 10.8 %collective-permute-done.20 = bf16[2,128,768]{2,1,0:T(8,128)(2,1)S(1)} collective-permute-done((bf16[2,128,768]{2,1,0:T(8,128)(2,1)S(1)}, bf16[2,128,768]{2,1,0:T(8,128)(2,1)S(1)}, u32[]{:S(2)}, u32[]{:S(2)}) %collective-permute-start.20) | collective-permute-done | bytes 393248 | tf_op jit(solution)/shard_map/ppermute | solution.py:545
  170.8 11.1 %collective-permute-done.21 = bf16[128,768]{1,0:T(8,128)(2,1)S(1)} collective-permute-done((bf16[128,768]{1,0:T(8,128)(2,1)S(1)}, bf16[128,768]{1,0:T(8,128)(2,1)S(1)}, u32[]{:S(2)}, u32[]{:S(2)}) %collective-permute-start.21) | collective-permute-done | bytes 196640 | tf_op jit(solution)/shard_map/ppermute | solution.py:545
  183.9 1.5 collective-permute-start.23
  187.2 2.2 collective-permute-start.29
  189.4 4.5 %collective-permute-done.16 = bf16[2,128,768]{2,1,0:T(8,128)(2,1)S(1)} collective-permute-done((bf16[2,128,768]{2,1,0:T(8,128)(2,1)S(1)}, bf16[2,128,768]{2,1,0:T(8,128)(2,1)S(1)}, u32[]{:S(2)}, u32[]{:S(2)}) %collective-permute-start.16) | collective-permute-done | bytes 393248 | tf_op jit(solution)/shard_map/ppermute | solution.py:545
  195.0 9.9 %collective-permute-done.32 = f32[8,768]{1,0:T(8,128)S(1)} collective-permute-done((f32[8,768]{1,0:T(8,128)S(1)}, f32[8,768]{1,0:T(8,128)S(1)}, u32[]{:S(2)}, u32[]{:S(2)}) %collective-permute-start.32) | collective-permute-done | bytes 24608 | tf_op jit(solution)/shard_map/ppermute | solution.py:545
  206.4 3.2 %collective-permute-done.33 = f32[8,768]{1,0:T(8,128)S(1)} collective-permute-done((f32[8,768]{1,0:T(8,128)S(1)}, f32[8,768]{1,0:T(8,128)S(1)}, u32[]{:S(2)}, u32[]{:S(2)}) %collective-permute-start.33) | collective-permute-done | bytes 24608 | tf_op jit(solution)/shard_map/ppermute | solution.py:545
  217.1 4.7 %collective-permute-done.30 = bf16[2,192,384]{2,1,0:T(8,128)(2,1)} collective-permute-done((bf16[2,192,384]{2,1,0:T(8,128)(2,1)}, bf16[2,192,384]{2,1,0:T(8,128)(2,1)}, u32[]{:S(2)}, u32[]{:S(2)}) %collective-permute-start.30) | collective-permute-done | bytes 294944 | tf_op jit(solution)/shard_map/ppermute | solution.py:545
  221.8 1.8 fusion.22
  228.1 1.3 broadcast_select_fusion.25
  232.3 2.0 convert_add_fusion
  234.4 2.1 add_add_fusion
  (250 shorter events, 40.9 us)
Async XLA Ops:
  1.9 23.5 %copy-start.38 = (bf16[1,128,768]{2,1,0:T(8,128)(2,1)}, bf16[1,128,768]{2,1,0:T(8,128)(2,1)S(1)}, u32[]{:S(2)}) copy-start(bf16[1,128,768]{2,1,0:T(8,128)(2,1)S(1)} %get-tuple-element.138) | copy-start | bytes 589828
  1.9 23.5 %copy-start.41 = (bf16[1,128,768]{2,1,0:T(8,128)(2,1)}, bf16[1,128,768]{2,1,0:T(8,128)(2,1)S(1)}, u32[]{:S(2)}) copy-start(bf16[1,128,768]{2,1,0:T(8,128)(2,1)S(1)} %get-tuple-element.137) | copy-start | bytes 589828
  1.9 23.5 %collective-permute-start.6 = (bf16[1,128,768]{2,1,0:T(8,128)(2,1)S(1)}, bf16[1,128,768]{2,1,0:T(8,128)(2,1)S(1)}, u32[]{:S(2)}, u32[]{:S(2)}) collective-permute-start(bf16[1,128,768]{2,1,0:T(8,128)(2,1)S(1)} %get-tuple-element.138), channel_id=1, source_target_pairs={{0,12},{4,8},{8,4},{12,0},{1,13},{5,9},{9,5},{13,1},{2,14},{6,10},... | collective-permute-start | bytes 589832 | tf_op jit(solution)/shard_map/ppermute | solution.py:545
  8.7 23.4 %collective-permute-start = (bf16[2,128,768]{2,1,0:T(8,128)(2,1)}, bf16[2,128,768]{2,1,0:T(8,128)(2,1)S(1)}, u32[]{:S(2)}, u32[]{:S(2)}) collective-permute-start(bf16[2,128,768]{2,1,0:T(8,128)(2,1)} %pad_maximum_fusion.13), channel_id=1, source_target_pairs={{0,8},{4,12},{8,0},{12,4},{1,9},{5,13},{9,1},{13,5},{2,10},{6,14},... | collective-permute-start | bytes 1179656 | tf_op jit(solution)/shard_map/ppermute | solution.py:545
  8.7 35.1 %collective-permute-start.3 = (bf16[384,768]{1,0:T(8,128)(2,1)S(1)}, bf16[384,768]{1,0:T(8,128)(2,1)}, u32[]{:S(2)}, u32[]{:S(2)}) collective-permute-start(bf16[384,768]{1,0:T(8,128)(2,1)S(1)} %copy-done.57), channel_id=1, source_target_pairs={{0,16},{16,0},{1,17},{17,1},{2,18},{18,2},{3,19},{19,3},{4,20},{20... | collective-permute-start | bytes 1769480 | tf_op jit(solution)/shard_map/ppermute | solution.py:545
  10.2 34.8 %collective-permute-start.4 = (bf16[768,384]{1,0:T(8,128)(2,1)}, bf16[768,384]{1,0:T(8,128)(2,1)}, u32[]{:S(2)}, u32[]{:S(2)}) collective-permute-start(bf16[768,384]{1,0:T(8,128)(2,1)} %param.23), channel_id=1, source_target_pairs={{0,16},{16,0},{1,17},{17,1},{2,18},{18,2},{3,19},{19,3},{4,20},{20... | collective-permute-start | bytes 1769480 | tf_op jit(solution)/shard_map/ppermute | solution.py:545
  10.7 13.1 %collective-permute-start.5 = (bf16[1,128,768]{2,1,0:T(8,128)(2,1)S(1)}, bf16[1,128,768]{2,1,0:T(8,128)(2,1)S(1)}, u32[]{:S(2)}, u32[]{:S(2)}) collective-permute-start(bf16[1,128,768]{2,1,0:T(8,128)(2,1)S(1)} %get-tuple-element.137), channel_id=1, source_target_pairs={{0,4},{4,0},{8,12},{12,8},{1,5},{5,1},{9,13},{13,9},{2,6},{6,2},{1... | collective-permute-start | bytes 589832 | tf_op jit(solution)/shard_map/ppermute | solution.py:545
  23.8 37.6 %collective-permute-start.9 = (bf16[768,384]{1,0:T(8,128)(2,1)}, bf16[768,384]{1,0:T(8,128)(2,1)}, u32[]{:S(2)}, u32[]{:S(2)}) collective-permute-start(bf16[768,384]{1,0:T(8,128)(2,1)} %pad_maximum_fusion.11), channel_id=1, source_target_pairs={{0,16},{16,0},{1,17},{17,1},{2,18},{18,2},{3,19},{19,3},{4,20},{20... | collective-permute-start | bytes 1769480 | tf_op jit(solution)/shard_map/ppermute | solution.py:545
  25.4 11.1 %collective-permute-start.7 = (bf16[2,128,768]{2,1,0:T(8,128)(2,1)S(1)}, bf16[2,128,768]{2,1,0:T(8,128)(2,1)S(1)}, u32[]{:S(2)}, u32[]{:S(2)}) collective-permute-start(bf16[2,128,768]{2,1,0:T(8,128)(2,1)S(1)} %constant_dynamic-update-slice_fusion.nz), channel_id=1, source_target_pairs={{0,2},{1,3},{2,0},{3,1},{4,6},{5,7},{6,4},{7,5},{8,10},{9,11},{10,... | collective-permute-start | bytes 1179656 | tf_op jit(solution)/shard_map/ppermute | solution.py:545
  32.1 11.6 %collective-permute-start.1 = (bf16[2,128,768]{2,1,0:T(8,128)(2,1)S(1)}, bf16[2,128,768]{2,1,0:T(8,128)(2,1)S(1)}, u32[]{:S(2)}, u32[]{:S(2)}) collective-permute-start(bf16[2,128,768]{2,1,0:T(8,128)(2,1)S(1)} %collective-permute-done.fz), channel_id=1, source_target_pairs={{0,2},{1,3},{2,0},{3,1},{4,6},{5,7},{6,4},{7,5},{8,10},{9,11},{10,... | collective-permute-start | bytes 1179656 | tf_op jit(solution)/shard_map/ppermute | solution.py:545
  36.6 26.2 %collective-permute-start.8 = (bf16[2,2,128,768]{3,2,1,0:T(8,128)(2,1)S(1)}, bf16[2,2,128,768]{3,2,1,0:T(8,128)(2,1)S(1)}, u32[]{:S(2)}, u32[]{:S(2)}) collective-permute-start(bf16[2,2,128,768]{3,2,1,0:T(8,128)(2,1)S(1)} %pad_maximum_fusion.7), channel_id=1, source_target_pairs={{0,1},{1,0},{2,3},{3,2},{4,5},{5,4},{6,7},{7,6},{8,9},{9,8},{10,11... | collective-permute-start | bytes 2359304 | tf_op jit(solution)/shard_map/ppermute | solution.py:545
  43.7 3.0 %collective-permute-start.2 = (bf16[2,2,128,768]{3,2,1,0:T(8,128)(2,1)S(1)}, bf16[2,2,128,768]{3,2,1,0:T(8,128)(2,1)S(1)}, u32[]{:S(2)}, u32[]{:S(2)}) collective-permute-start(bf16[2,2,128,768]{3,2,1,0:T(8,128)(2,1)S(1)} %pad_maximum_fusion.6), channel_id=1, source_target_pairs={{0,1},{1,0},{2,3},{3,2},{4,5},{5,4},{6,7},{7,6},{8,9},{9,8},{10,11... | collective-permute-start | bytes 2359304 | tf_op jit(solution)/shard_map/ppermute | solution.py:545
  50.8 14.3 %copy-start.6 = (bf16[1024,768]{1,0:T(8,128)(2,1)}, bf16[1024,768]{1,0:T(8,128)(2,1)S(1)}, u32[]{:S(2)}) copy-start(bf16[1024,768]{1,0:T(8,128)(2,1)S(1)} %get-tuple-element.69.n1o.refs_9_) | copy-start | bytes 4718596
  60.9 18.4 %copy-start.32 = (f32[8,768]{1,0:T(8,128)}, f32[8,768]{1,0:T(8,128)S(1)}, u32[]{:S(2)}) copy-start(f32[8,768]{1,0:T(8,128)S(1)} %get-tuple-element.68.after.refs_15_) | copy-start | bytes 73732
  60.9 30.1 %collective-permute-start.10 = (bf16[768,768]{1,0:T(8,128)(2,1)S(1)}, bf16[768,768]{1,0:T(8,128)(2,1)S(1)}, u32[]{:S(2)}, u32[]{:S(2)}) collective-permute-start(bf16[768,768]{1,0:T(8,128)(2,1)S(1)} %get-tuple-element.82), channel_id=1, source_target_pairs={{0,16},{16,0},{1,17},{17,1},{2,18},{18,2},{3,19},{19,3},{4,20},{20... | collective-permute-start | bytes 3538952 | tf_op jit(solution)/shard_map/ppermute | solution.py:545
  91.8 13.2 %copy-start.3 = (f32[768,768]{1,0:T(8,128)}, f32[768,768]{1,0:T(8,128)S(1)}, u32[]{:S(2)}) copy-start(f32[768,768]{1,0:T(8,128)S(1)} %convert_add_fusion.1.after) | copy-start | bytes 7077892
  92.7 19.5 %collective-permute-start.13 = (bf16[384,768]{1,0:T(8,128)(2,1)}, bf16[384,768]{1,0:T(8,128)(2,1)}, u32[]{:S(2)}, u32[]{:S(2)}) collective-permute-start(bf16[384,768]{1,0:T(8,128)(2,1)} %dynamic-slice_convert_fusion), channel_id=1, source_target_pairs={{0,4},{4,0},{8,12},{12,8},{1,5},{5,1},{9,13},{13,9},{2,6},{6,2},{1... | collective-permute-start | bytes 1769480 | tf_op jit(solution)/shard_map/ppermute | solution.py:545
  109.2 10.7 %collective-permute-start.11 = (bf16[2,256,768]{2,1,0:T(8,128)(2,1)}, bf16[2,256,768]{2,1,0:T(8,128)(2,1)}, u32[]{:S(2)}, u32[]{:S(2)}) collective-permute-start(bf16[2,256,768]{2,1,0:T(8,128)(2,1)} %get-tuple-element.86), channel_id=1, source_target_pairs={{0,1},{1,0},{2,3},{3,2},{4,5},{5,4},{6,7},{7,6},{8,9},{9,8},{10,11... | collective-permute-start | bytes 2359304 | tf_op jit(solution)/shard_map/ppermute | solution.py:545
  112.2 93.2 %copy-start.60 = (f32[2,128]{1,0:T(2,128)}, f32[2,128]{1,0:T(2,128)S(1)}, u32[]{:S(2)}) copy-start(f32[2,128]{1,0:T(2,128)S(1)} %add_rsqrt_fusion) | copy-start | bytes 3076
  114.0 17.3 %collective-permute-start.36 = (bf16[192,768]{1,0:T(8,128)(2,1)S(1)}, bf16[192,768]{1,0:T(8,128)(2,1)S(1)}, u32[]{:S(2)}, u32[]{:S(2)}) collective-permute-start(bf16[192,768]{1,0:T(8,128)(2,1)S(1)} %dynamic-slice_convert_fusion.1), channel_id=1, source_target_pairs={{0,8},{4,12},{8,0},{12,4},{1,9},{5,13},{9,1},{13,5},{2,10},{6,14},... | collective-permute-start | bytes 884744 | tf_op jit(solution)/shard_map/ppermute | solution.py:545
  119.5 14.2 %collective-permute-start.18 = (bf16[2,256,768]{2,1,0:T(8,128)(2,1)S(1)}, bf16[2,256,768]{2,1,0:T(8,128)(2,1)S(1)}, u32[]{:S(2)}, u32[]{:S(2)}) collective-permute-start(bf16[2,256,768]{2,1,0:T(8,128)(2,1)S(1)} %get-tuple-element.104), channel_id=1, source_target_pairs={{0,1},{1,0},{2,3},{3,2},{4,5},{5,4},{6,7},{7,6},{8,9},{9,8},{10,11... | collective-permute-start | bytes 2359304 | tf_op jit(solution)/shard_map/ppermute | solution.py:545
  127.8 6.7 %collective-permute-start.14 = (bf16[2,256,768]{2,1,0:T(8,128)(2,1)S(1)}, bf16[2,256,768]{2,1,0:T(8,128)(2,1)S(1)}, u32[]{:S(2)}, u32[]{:S(2)}) collective-permute-start(bf16[2,256,768]{2,1,0:T(8,128)(2,1)S(1)} %get-tuple-element.101), channel_id=1, source_target_pairs={{0,1},{1,0},{2,3},{3,2},{4,5},{5,4},{6,7},{7,6},{8,9},{9,8},{10,11... | collective-permute-start | bytes 2359304 | tf_op jit(solution)/shard_map/ppermute | solution.py:545
  128.2 12.0 %collective-permute-start.12 = (bf16[2,128,768]{2,1,0:T(8,128)(2,1)S(1)}, bf16[2,128,768]{2,1,0:T(8,128)(2,1)S(1)}, u32[]{:S(2)}, u32[]{:S(2)}) collective-permute-start(bf16[2,128,768]{2,1,0:T(8,128)(2,1)S(1)} %fusion.16), channel_id=1, source_target_pairs={{0,2},{1,3},{2,0},{3,1},{4,6},{5,7},{6,4},{7,5},{8,10},{9,11},{10,... | collective-permute-start | bytes 1179656 | tf_op jit(solution)/shard_map/ppermute | solution.py:545
  129.8 19.5 %collective-permute-start.25 = (bf16[768,384]{1,0:T(8,128)(2,1)S(1)}, bf16[768,384]{1,0:T(8,128)(2,1)S(1)}, u32[]{:S(2)}, u32[]{:S(2)}) collective-permute-start(bf16[768,384]{1,0:T(8,128)(2,1)S(1)} %get-tuple-element.109), channel_id=1, source_target_pairs={{0,16},{16,0},{1,17},{17,1},{2,18},{18,2},{3,19},{19,3},{4,20},{20... | collective-permute-start | bytes 1769480 | tf_op jit(solution)/shard_map/ppermute | solution.py:545
  131.4 54.0 %copy-start.44 = (bf16[192,768]{1,0:T(8,128)(2,1)}, bf16[192,768]{1,0:T(8,128)(2,1)S(1)}, u32[]{:S(2)}) copy-start(bf16[192,768]{1,0:T(8,128)(2,1)S(1)} %add_convert_fusion) | copy-start | bytes 884740
  131.4 52.5 %collective-permute-start.37 = (bf16[192,768]{1,0:T(8,128)(2,1)S(1)}, bf16[192,768]{1,0:T(8,128)(2,1)S(1)}, u32[]{:S(2)}, u32[]{:S(2)}) collective-permute-start(bf16[192,768]{1,0:T(8,128)(2,1)S(1)} %add_convert_fusion), channel_id=1, source_target_pairs={{0,8},{4,12},{8,0},{12,4},{1,9},{5,13},{9,1},{13,5},{2,10},{6,14},... | collective-permute-start | bytes 884744 | tf_op jit(solution)/shard_map/ppermute | solution.py:545
  133.9 14.8 %collective-permute-start.19 = (bf16[2,128,768]{2,1,0:T(8,128)(2,1)S(1)}, bf16[2,128,768]{2,1,0:T(8,128)(2,1)S(1)}, u32[]{:S(2)}, u32[]{:S(2)}) collective-permute-start(bf16[2,128,768]{2,1,0:T(8,128)(2,1)S(1)} %fusion.18), channel_id=1, source_target_pairs={{0,2},{1,3},{2,0},{3,1},{4,6},{5,7},{6,4},{7,5},{8,10},{9,11},{10,... | collective-permute-start | bytes 1179656 | tf_op jit(solution)/shard_map/ppermute | solution.py:545
  140.4 15.3 %collective-permute-start.15 = (bf16[128,768]{1,0:T(8,128)(2,1)S(1)}, bf16[128,768]{1,0:T(8,128)(2,1)S(1)}, u32[]{:S(2)}, u32[]{:S(2)}) collective-permute-start(bf16[128,768]{1,0:T(8,128)(2,1)S(1)} %get-tuple-element.161), channel_id=1, source_target_pairs={{0,8},{4,12},{8,0},{12,4},{1,9},{5,13},{9,1},{13,5},{2,10},{6,14},... | collective-permute-start | bytes 589832 | tf_op jit(solution)/shard_map/ppermute | solution.py:545
  142.9 13.5 %collective-permute-start.17 = (bf16[2,128,768]{2,1,0:T(8,128)(2,1)S(1)}, bf16[2,128,768]{2,1,0:T(8,128)(2,1)S(1)}, u32[]{:S(2)}, u32[]{:S(2)}) collective-permute-start(bf16[2,128,768]{2,1,0:T(8,128)(2,1)S(1)} %fusion.17), channel_id=1, source_target_pairs={{0,2},{1,3},{2,0},{3,1},{4,6},{5,7},{6,4},{7,5},{8,10},{9,11},{10,... | collective-permute-start | bytes 1179656 | tf_op jit(solution)/shard_map/ppermute | solution.py:545
  148.7 21.6 %collective-permute-start.20 = (bf16[2,128,768]{2,1,0:T(8,128)(2,1)S(1)}, bf16[2,128,768]{2,1,0:T(8,128)(2,1)S(1)}, u32[]{:S(2)}, u32[]{:S(2)}) collective-permute-start(bf16[2,128,768]{2,1,0:T(8,128)(2,1)S(1)} %fusion.9), channel_id=1, source_target_pairs={{0,4},{4,0},{8,12},{12,8},{1,5},{5,1},{9,13},{13,9},{2,6},{6,2},{1... | collective-permute-start | bytes 1179656 | tf_op jit(solution)/shard_map/ppermute | solution.py:545
  149.5 36.8 %collective-permute-start.26 = (bf16[192,384]{1,0:T(8,128)(2,1)S(1)}, bf16[192,384]{1,0:T(8,128)(2,1)S(1)}, u32[]{:S(2)}, u32[]{:S(2)}) collective-permute-start(bf16[192,384]{1,0:T(8,128)(2,1)S(1)} %get-tuple-element.145), channel_id=1, source_target_pairs={{0,12},{4,8},{8,4},{12,0},{1,13},{5,9},{9,5},{13,1},{2,14},{6,10},... | collective-permute-start | bytes 442376 | tf_op jit(solution)/shard_map/ppermute | solution.py:545
  155.7 38.3 %copy-start.48 = (bf16[128,768]{1,0:T(8,128)(2,1)}, bf16[128,768]{1,0:T(8,128)(2,1)S(1)}, u32[]{:S(2)}) copy-start(bf16[128,768]{1,0:T(8,128)(2,1)S(1)} %collective-permute-done.15) | copy-start | bytes 589828
  155.7 30.6 %collective-permute-start.27 = (bf16[192,384]{1,0:T(8,128)(2,1)S(1)}, bf16[192,384]{1,0:T(8,128)(2,1)S(1)}, u32[]{:S(2)}, u32[]{:S(2)}) collective-permute-start(bf16[192,384]{1,0:T(8,128)(2,1)S(1)} %get-tuple-element.147), channel_id=1, source_target_pairs={{0,8},{4,12},{8,0},{12,4},{1,9},{5,13},{9,1},{13,5},{2,10},{6,14},... | collective-permute-start | bytes 442376 | tf_op jit(solution)/shard_map/ppermute | solution.py:545
  156.4 30.7 %collective-permute-start.28 = (bf16[192,384]{1,0:T(8,128)(2,1)S(1)}, bf16[192,384]{1,0:T(8,128)(2,1)S(1)}, u32[]{:S(2)}, u32[]{:S(2)}) collective-permute-start(bf16[192,384]{1,0:T(8,128)(2,1)S(1)} %get-tuple-element.146), channel_id=1, source_target_pairs={{0,4},{4,0},{8,12},{12,8},{1,5},{5,1},{9,13},{13,9},{2,6},{6,2},{1... | collective-permute-start | bytes 442376 | tf_op jit(solution)/shard_map/ppermute | solution.py:545
  170.6 11.4 %collective-permute-start.21 = (bf16[128,768]{1,0:T(8,128)(2,1)S(1)}, bf16[128,768]{1,0:T(8,128)(2,1)S(1)}, u32[]{:S(2)}, u32[]{:S(2)}) collective-permute-start(bf16[128,768]{1,0:T(8,128)(2,1)S(1)} %fusion.20), channel_id=1, source_target_pairs={{0,8},{4,12},{8,0},{12,4},{1,9},{5,13},{9,1},{13,5},{2,10},{6,14},... | collective-permute-start | bytes 589832 | tf_op jit(solution)/shard_map/ppermute | solution.py:545
  181.9 12.0 %collective-permute-start.16 = (bf16[2,128,768]{2,1,0:T(8,128)(2,1)S(1)}, bf16[2,128,768]{2,1,0:T(8,128)(2,1)S(1)}, u32[]{:S(2)}, u32[]{:S(2)}) collective-permute-start(bf16[2,128,768]{2,1,0:T(8,128)(2,1)S(1)} %pad_maximum_fusion.15), channel_id=1, source_target_pairs={{0,2},{1,3},{2,0},{3,1},{4,6},{5,7},{6,4},{7,5},{8,10},{9,11},{10,... | collective-permute-start | bytes 1179656 | tf_op jit(solution)/shard_map/ppermute | solution.py:545
  183.9 31.4 %collective-permute-start.23 = (bf16[2,128,768]{2,1,0:T(8,128)(2,1)}, bf16[2,128,768]{2,1,0:T(8,128)(2,1)S(1)}, u32[]{:S(2)}, u32[]{:S(2)}) collective-permute-start(bf16[2,128,768]{2,1,0:T(8,128)(2,1)} %fusion.7), channel_id=1, source_target_pairs={{0,2},{1,3},{2,0},{3,1},{4,6},{5,7},{6,4},{7,5},{8,10},{9,11},{10,... | collective-permute-start | bytes 1179656 | tf_op jit(solution)/shard_map/ppermute | solution.py:545
  186.2 38.4 %collective-permute-start.38 = (bf16[2,192,768]{2,1,0:T(8,128)(2,1)}, bf16[2,192,768]{2,1,0:T(8,128)(2,1)}, u32[]{:S(2)}, u32[]{:S(2)}) collective-permute-start(bf16[2,192,768]{2,1,0:T(8,128)(2,1)} %pad_maximum_fusion.12), channel_id=1, source_target_pairs={{0,4},{4,0},{8,12},{12,8},{1,5},{5,1},{9,13},{13,9},{2,6},{6,2},{1... | collective-permute-start | bytes 1769480 | tf_op jit(solution)/shard_map/ppermute | solution.py:545
  186.2 7.7 %collective-permute-start.31 = (f32[8,768]{1,0:T(8,128)S(1)}, f32[8,768]{1,0:T(8,128)S(1)}, u32[]{:S(2)}, u32[]{:S(2)}) collective-permute-start(f32[8,768]{1,0:T(8,128)S(1)} %get-tuple-element.116), channel_id=1, source_target_pairs={{0,16},{16,0},{1,17},{17,1},{2,18},{18,2},{3,19},{19,3},{4,20},{20... | collective-permute-start | bytes 73736 | tf_op jit(solution)/shard_map/ppermute | solution.py:545
  187.2 24.1 %collective-permute-start.29 = (bf16[192,384]{1,0:T(8,128)(2,1)S(1)}, bf16[192,384]{1,0:T(8,128)(2,1)S(1)}, u32[]{:S(2)}, u32[]{:S(2)}) collective-permute-start(bf16[192,384]{1,0:T(8,128)(2,1)S(1)} %add_convert_fusion.1), channel_id=1, source_target_pairs={{0,8},{4,12},{8,0},{12,4},{1,9},{5,13},{9,1},{13,5},{2,10},{6,14},... | collective-permute-start | bytes 442376 | tf_op jit(solution)/shard_map/ppermute | solution.py:545
  193.9 10.9 %collective-permute-start.32 = (f32[8,768]{1,0:T(8,128)S(1)}, f32[8,768]{1,0:T(8,128)S(1)}, u32[]{:S(2)}, u32[]{:S(2)}) collective-permute-start(f32[8,768]{1,0:T(8,128)S(1)} %add.166), channel_id=1, source_target_pairs={{0,4},{4,0},{8,12},{12,8},{1,5},{5,1},{9,13},{13,9},{2,6},{6,2},{1... | collective-permute-start | bytes 73736 | tf_op jit(solution)/shard_map/ppermute | solution.py:545
  194.9 33.2 %collective-permute-start.22 = (bf16[2,2,128,768]{3,2,1,0:T(8,128)(2,1)}, bf16[2,2,128,768]{3,2,1,0:T(8,128)(2,1)}, u32[]{:S(2)}, u32[]{:S(2)}) collective-permute-start(bf16[2,2,128,768]{3,2,1,0:T(8,128)(2,1)} %pad_maximum_fusion.9), channel_id=1, source_target_pairs={{0,1},{1,0},{2,3},{3,2},{4,5},{5,4},{6,7},{7,6},{8,9},{9,8},{10,11... | collective-permute-start | bytes 2359304 | tf_op jit(solution)/shard_map/ppermute | solution.py:545
  204.8 4.7 %collective-permute-start.33 = (f32[8,768]{1,0:T(8,128)S(1)}, f32[8,768]{1,0:T(8,128)S(1)}, u32[]{:S(2)}, u32[]{:S(2)}) collective-permute-start(f32[8,768]{1,0:T(8,128)S(1)} %add.167), channel_id=1, source_target_pairs={{0,8},{4,12},{8,0},{12,4},{1,9},{5,13},{9,1},{13,5},{2,10},{6,14},... | collective-permute-start | bytes 73736 | tf_op jit(solution)/shard_map/ppermute | solution.py:545
  209.5 1.2 collective-permute-start.34
  210.7 3.8 %collective-permute-start.35 = (f32[8,768]{1,0:T(8,128)S(1)}, f32[8,768]{1,0:T(8,128)S(1)}, u32[]{:S(2)}, u32[]{:S(2)}) collective-permute-start(f32[8,768]{1,0:T(8,128)S(1)} %add.169), channel_id=1, source_target_pairs={{0,2},{1,3},{2,0},{3,1},{4,6},{5,7},{6,4},{7,5},{8,10},{9,11},{10,... | collective-permute-start | bytes 73736 | tf_op jit(solution)/shard_map/ppermute | solution.py:545
  212.7 9.1 %collective-permute-start.30 = (bf16[2,192,384]{2,1,0:T(8,128)(2,1)}, bf16[2,192,384]{2,1,0:T(8,128)(2,1)}, u32[]{:S(2)}, u32[]{:S(2)}) collective-permute-start(bf16[2,192,384]{2,1,0:T(8,128)(2,1)} %pad_maximum_fusion.17), channel_id=1, source_target_pairs={{0,4},{4,0},{8,12},{12,8},{1,5},{5,1},{9,13},{13,9},{2,6},{6,2},{1... | collective-permute-start | bytes 884744 | tf_op jit(solution)/shard_map/ppermute | solution.py:545
  215.2 21.2 %copy-start.62 = (f32[768]{0:T(1024)}, f32[768]{0:T(1024)S(1)}, u32[]{:S(2)}) copy-start(f32[768]{0:T(1024)S(1)} %get-tuple-element.191) | copy-start | bytes 9220
  217.1 12.5 %collective-permute-start.24 = (bf16[2,2,128,768]{3,2,1,0:T(8,128)(2,1)S(1)}, bf16[2,2,128,768]{3,2,1,0:T(8,128)(2,1)S(1)}, u32[]{:S(2)}, u32[]{:S(2)}) collective-permute-start(bf16[2,2,128,768]{3,2,1,0:T(8,128)(2,1)S(1)} %pad_maximum_fusion.10), channel_id=1, source_target_pairs={{0,1},{1,0},{2,3},{3,2},{4,5},{5,4},{6,7},{7,6},{8,9},{9,8},{10,11... | collective-permute-start | bytes 2359304 | tf_op jit(solution)/shard_map/ppermute | solution.py:545
  (56 other events, 233.4 us)

commit v11 on v9

--- a/solution.py
+++ b/solution.py
@@ -729,8 +729,8 @@
     def over_ctx(v, distance, *earlier):
         return tie(swap(v.astype(BF16), "ctx", 4, distance), *earlier).astype(F32)
 
-    def gather_tp(ours):
-        pair = jnp.stack([ours, swap(ours, "tp", 4, 2)])
+    def gather_tp(ours, *earlier):
+        pair = jnp.stack([ours, tie(swap(ours, "tp", 4, 2), *earlier)])
         core = swap(pair, "tp", 4, 1)
         pieces = by_xor((pair[0], core[0], pair[1], core[1]), t)
         pieces = jnp.concatenate(pieces, axis=1)
@@ -739,11 +739,6 @@
 
     sums_b = over_x(half_b, half_w)
     branches = jnp.stack([sums_b[0], over_ctx(sums_b[1], 2)]).astype(BF16)
-    block_out = gather_tp(branches)
-    block_out = (
-        inputs.astype(F32) + block_out + (attention_output_bias + down_projection_bias)
-    )
-
     sums_o = over_x(half_o, half_w)
     sums_w = over_x(half_w)
     sums_w = sums_w + over_ctx(sums_o, 1)
@@ -755,6 +750,10 @@
         - xhat * jnp.mean(a * xhat, axis=-1, keepdims=True)
     )
     norm_grad = norm_grad.astype(BF16)
+    block_out = gather_tp(branches, a)
+    block_out = (
+        inputs.astype(F32) + block_out + (attention_output_bias + down_projection_bias)
+    )
     inputs_grad = cotangent.astype(F32) + gather_tp(norm_grad)
 
     if split:
@@ -764,8 +763,8 @@
         down_total = jnp.concatenate(
             [down_total[:, : width // 2], down_total[:, width // 2 :]], axis=0
         )
-        late = late_first + tie(swap(late_second, "fsdp", 2, 1), sums_o).astype(F32)
-        late = double(pair_up(quarter_sum(late, c, sums_w), norm_grad), c)
+        late = late_first + tie(swap(late_second, "fsdp", 2, 1), sums_w).astype(F32)
+        late = double(pair_up(quarter_sum(late, c, a), norm_grad), c)
         late = jnp.concatenate(late, axis=0).astype(F32)
         small = jnp.concatenate([late[4 * local : 4 * local + 8], late[4 * local + 8 :][:8]], axis=1)
     else:

time: 232 us -> 221 us (0.953)
  waiting for transfers between devices: 84 us -> 73.8 us
  other arithmetic: 31.6 us -> 34.1 us
    ppermute x36, waiting for transfers between devices: 84 us -> 73.8 us  [swap(): return lax.ppermute(v, axis, [(i, i ^ distance) for i in range(size)])]
    unnamed x124 -> x106, local copies, waits for them, and re-layouts: 8.16 us -> 6 us
  transfers between devices with their start and end apart: 36 -> 36, of which waited for: 14 -> 17; matrix products, arithmetic and copies ran while one was open for 13% -> 16% of each run, Pallas kernels for 27% -> 28%
where the time goes in v11:
time: 221 us; the launch traced here: 220 us
  waiting for transfers between devices  73.8 us (33%)
  Pallas kernels  62.1 us (28%)
  starting transfers between devices  34.6 us (16%)
  other arithmetic  34.1 us (15%)
  local copies, waits for them, and re-layouts  13.7 us (6%)
    ppermute x36, waiting for transfers between devices, swap(): return lax.ppermute(v, axis, [(i, i ^ distance) for i in range(size)])  73.8 us
    ppermute x36, starting transfers between devices, swap(): return lax.ppermute(v, axis, [(i, i ^ distance) for i in range(size)])  34.6 us
    pallas_call x3, Pallas kernels, attention(): pl.pallas_call(attention_kernel, grid=(rows // lanes,), in_specs=[pl.Bloc...  29 us
    pallas_call x2, Pallas kernels, back(): pl.pallas_call(functools.partial(back_kernel, own, split, heads), grid_sp...  11.1 us
    pallas_call x1, Pallas kernels, feed_forward(): pl.pallas_call(functools.partial(forward_kernel, split), grid_spec=pltpu....  9.97 us
    unnamed x106, local copies, waits for them, and re-layouts  6 us
    pallas_call x2, Pallas kernels, norms(): pl.pallas_call(kernel, grid_spec=pltpu.PrefetchScalarGridSpec(num_scalar_...  4.91 us
    pallas_call x1, Pallas kernels, project(): pl.pallas_call(project_kernel, grid=(8,), in_specs=[pl.BlockSpec((STEP, w...  4.44 us
  transfers between devices with their start and end apart: 36, of which 17 were waited for; matrix products, arithmetic and copies ran while one was open for 16% of the time, Pallas kernels for 28%

profile of v11, /device:TPU:0, one launch (start us, length us, event | category | flops | bytes accessed | tf_op | source)
XLA Modules:
  0.0 220.0 jit_solution(198829391446247236)
XLA Ops:
  0.7 1.2 constant_dynamic-slice_fusion
  1.9 5.1 %collective-permute-start.6 = (bf16[1,128,768]{2,1,0:T(8,128)(2,1)S(1)}, bf16[1,128,768]{2,1,0:T(8,128)(2,1)S(1)}, u32[]{:S(2)}, u32[]{:S(2)}) collective-permute-start(bf16[1,128,768]{2,1,0:T(8,128)(2,1)S(1)} %get-tuple-element.136), channel_id=1, source_target_pairs={{0,12},{4,8},{8,4},{12,0},{1,13},{5,9},{9,5},{13,1},{2,14},{6,10},... | collective-permute-start | bytes 589832 | tf_op jit(solution)/shard_map/ppermute | solution.py:548
  8.8 1.5 collective-permute-start.3
  12.3 11.5 %collective-permute-done.5 = bf16[1,128,768]{2,1,0:T(8,128)(2,1)S(1)} collective-permute-done((bf16[1,128,768]{2,1,0:T(8,128)(2,1)S(1)}, bf16[1,128,768]{2,1,0:T(8,128)(2,1)S(1)}, u32[]{:S(2)}, u32[]{:S(2)}) %collective-permute-start.5) | collective-permute-done | bytes 196640 | tf_op jit(solution)/shard_map/ppermute | solution.py:548
  23.9 1.5 collective-permute-start.9
  25.5 1.6 collective-permute-start.7
  27.6 4.6 %collective-permute-done.fz = bf16[2,128,768]{2,1,0:T(8,128)(2,1)S(1)} collective-permute-done((bf16[2,128,768]{2,1,0:T(8,128)(2,1)}, bf16[2,128,768]{2,1,0:T(8,128)(2,1)S(1)}, u32[]{:S(2)}, u32[]{:S(2)}) %collective-permute-start) | collective-permute-done | bytes 393248 | tf_op jit(solution)/shard_map/ppermute | solution.py:548
  32.2 1.5 collective-permute-start.1
  33.9 2.6 %collective-permute-done.7.nx = bf16[2,128,768]{2,1,0:T(8,128)(2,1)S(1)} collective-permute-done((bf16[2,128,768]{2,1,0:T(8,128)(2,1)S(1)}, bf16[2,128,768]{2,1,0:T(8,128)(2,1)S(1)}, u32[]{:S(2)}, u32[]{:S(2)}) %collective-permute-start.7) | collective-permute-done | bytes 393248 | tf_op jit(solution)/shard_map/ppermute | solution.py:548
  36.7 7.0 %collective-permute-done.1.fx = bf16[2,128,768]{2,1,0:T(8,128)(2,1)S(1)} collective-permute-done((bf16[2,128,768]{2,1,0:T(8,128)(2,1)S(1)}, bf16[2,128,768]{2,1,0:T(8,128)(2,1)S(1)}, u32[]{:S(2)}, u32[]{:S(2)}) %collective-permute-start.1) | collective-permute-done | bytes 393248 | tf_op jit(solution)/shard_map/ppermute | solution.py:548
  46.1 1.3 broadcast_select_fusion.7
  47.7 1.2 copy-done
  49.1 2.7 %shard_map.254 = (bf16[1024,768]{1,0:T(8,128)(2,1)S(1)}, bf16[1024,768]{1,0:T(8,128)(2,1)S(1)}, bf16[1024,768]{1,0:T(8,128)(2,1)S(1)}, f32[24,1024]{1,0:T(8,128)S(1)}) custom-call(s32[4]{0:T(128)S(1)} %pad_add_fusion.at, bf16[2,512,768]{2,1,0:T(8,128)(2,1)S(1)} %copy-done, bf16[2,512,768]{2,1,0:T(8,128)(2,1)S(1)} %copy-done, ...), custom_call_target="tpu_custom_call" | custom-call | bytes 4718592 | tf_op jit(solution)/shard_map/pallas_call | solution.py:140
  51.9 10.0 %shard_map.255 = (bf16[1024,768]{1,0:T(8,128)(2,1)S(1)}, bf16[1024,768]{1,0:T(8,128)(2,1)S(1)}, f32[8,768]{1,0:T(8,128)S(1)}, f32[768,768]{1,0:T(8,128)S(1)}, bf16[768,768]{1,0:T(8,128)(2,1)S(1)}) custom-call(s32[4]{0:T(128)S(1)} %pad_add_fusion.at, bf16[1024,768]{1,0:T(8,128)(2,1)S(1)} %get-tuple-element.65.n2_ref, ...), custom_call_target="tpu_custom_call" | custom-call | flops 7247757312 | bytes 16777216 | tf_op jit(solution)/shard_map/pallas_call | solution.py:386
  62.4 1.3 broadcast_select_fusion.5
  64.7 2.2 shard_map.256
  66.9 4.4 %shard_map.257 = (bf16[192,2048]{1,0:T(8,128)(2,1)S(1)}, bf16[192,2048]{1,0:T(8,128)(2,1)S(1)}, bf16[192,1024]{1,0:T(8,128)(2,1)S(1)}, bf16[192,1024]{1,0:T(8,128)(2,1)S(1)}) custom-call(bf16[1024,768]{1,0:T(8,128)(2,1)S(1)} %get-tuple-element.68.n1o.refs_9_, bf16[1024,768]{1,0:T(8,128)(2,1)S(1)} %get-tuple-element.70.n1x.refs_6_, ...), custom_call_target="tpu_custom_call" | custom-call | flops 1811939328 | bytes 9437184 | tf_op jit(solution)/shard_map/pallas_call | solution.py:204
  71.4 9.7 %shard_map.259 = (bf16[64,1024]{1,0:T(8,128)(2,1)S(1)}, bf16[64,1024]{1,0:T(8,128)(2,1)S(1)}, bf16[64,2048]{1,0:T(8,128)(2,1)S(1)}, bf16[64,2048]{1,0:T(8,128)(2,1)S(1)}) custom-call(f32[8,768]{1,0:T(8,128)S(1)} %get-tuple-element.67.after.refs_15_, bf16[192,1024]{1,0:T(8,128)(2,1)S(1)} %get-tuple-element.74.q_ref, ...), custom_call_target="tpu_custom_call" | custom-call | flops 5368709120 | bytes 2097152 | tf_op jit(solution)/shard_map/pallas_call | solution.py:307
  81.0 9.7 %shard_map.258 = (bf16[64,1024]{1,0:T(8,128)(2,1)S(1)}, bf16[64,1024]{1,0:T(8,128)(2,1)S(1)}, bf16[64,2048]{1,0:T(8,128)(2,1)S(1)}, bf16[64,2048]{1,0:T(8,128)(2,1)S(1)}) custom-call(f32[8,768]{1,0:T(8,128)S(1)} %get-tuple-element.67.after.refs_15_, bf16[192,1024]{1,0:T(8,128)(2,1)S(1)} %get-tuple-element.74.q_ref, ...), custom_call_target="tpu_custom_call" | custom-call | flops 5368709120 | bytes 2097152 | tf_op jit(solution)/shard_map/pallas_call | solution.py:307
  91.0 2.6 %collective-permute-start.13 = (bf16[384,768]{1,0:T(8,128)(2,1)S(1)}, bf16[384,768]{1,0:T(8,128)(2,1)S(1)}, u32[]{:S(2)}, u32[]{:S(2)}) collective-permute-start(bf16[384,768]{1,0:T(8,128)(2,1)S(1)} %dynamic-slice_convert_fusion), channel_id=1, source_target_pairs={{0,4},{4,0},{8,12},{12,8},{1,5},{5,1},{9,13},{13,9},{2,6},{6,2},{1... | collective-permute-start | bytes 1769480 | tf_op jit(solution)/shard_map/ppermute | solution.py:548
  93.7 9.7 %shard_map.260 = (bf16[64,1024]{1,0:T(8,128)(2,1)S(1)}, bf16[64,1024]{1,0:T(8,128)(2,1)S(1)}, bf16[64,2048]{1,0:T(8,128)(2,1)S(1)}, bf16[64,2048]{1,0:T(8,128)(2,1)S(1)}) custom-call(f32[768,768]{1,0:T(8,128)S(1)} %convert_add_fusion.1.after, bf16[192,1024]{1,0:T(8,128)(2,1)S(1)} %get-tuple-element.74.q_ref, bf16[192,1024]{1,0:T(8,128)(2,1)S(1)} %get-tuple-element.75.do_ref, ...), custom_call_target="tpu_custom_call" | custom-call | flops 5368709120 | bytes 2097152 | tf_op jit(solution)/shard_map/pallas_call | solution.py:307
  103.4 2.7 %shard_map.261 = (bf16[2,256,768]{2,1,0:T(8,128)(2,1)S(1)}, bf16[2,256,768]{2,1,0:T(8,128)(2,1)S(1)}, f32[192,768]{1,0:T(8,128)S(1)}) custom-call(bf16[64,1024]{1,0:T(8,128)(2,1)S(1)} %get-tuple-element.78.refs_0_, bf16[64,1024]{1,0:T(8,128)(2,1)S(1)} %get-tuple-element.79.refs_1_, bf16[64,1024]{1,0:T(8,128)(2,1)S(1)} %get-tuple-element.82.refs_2_, ...), custom_call_target="tpu_custom_call" | custom-call | flops 603979776 | bytes 8388608 | tf_op jit(solution)/shard_map/pallas_call | solution.py:436
  108.4 4.8 %shard_map.262 = (bf16[2,256,768]{2,1,0:T(8,128)(2,1)S(1)}, bf16[2,256,768]{2,1,0:T(8,128)(2,1)S(1)}, f32[384,768]{1,0:T(8,128)S(1)}, f32[8,768]{1,0:T(8,128)S(1)}) custom-call(s32[4]{0:T(128)S(1)} %pad_add_fusion.at, bf16[64,2048]{1,0:T(8,128)(2,1)S(1)} %get-tuple-element.89.refs_0_.refs_3_, bf16[64,2048]{1,0:T(8,128)(2,1)S(1)} %get-tuple-element.90.refs_1_.refs_4_, ...), custom_call_target="tpu_custom_call" | custom-call | flops 1207959552 | bytes 10485760 | tf_op jit(solution)/shard_map/pallas_call | solution.py:532
  113.5 6.2 %shard_map.263 = (bf16[2,256,768]{2,1,0:T(8,128)(2,1)S(1)}, bf16[2,256,768]{2,1,0:T(8,128)(2,1)S(1)}, f32[832,384]{1,0:T(8,128)S(1)}, bf16[832,384]{1,0:T(8,128)(2,1)S(1)}) custom-call(s32[4]{0:T(128)S(1)} %pad_add_fusion.at, bf16[64,1024]{1,0:T(8,128)(2,1)S(1)} %get-tuple-element.86.refs_0_, bf16[64,1024]{1,0:T(8,128)(2,1)S(1)} %get-tuple-element.87.refs_1_, ...), custom_call_target="tpu_custom_call" | custom-call | flops 1811939328 | bytes 10485760 | tf_op jit(solution)/shard_map/pallas_call | solution.py:532
  120.4 1.5 collective-permute-start.12
  121.9 1.6 collective-permute-done.33
  126.2 6.3 %collective-permute-done.12 = bf16[2,128,768]{2,1,0:T(8,128)(2,1)S(1)} collective-permute-done((bf16[2,128,768]{2,1,0:T(8,128)(2,1)S(1)}, bf16[2,128,768]{2,1,0:T(8,128)(2,1)S(1)}, u32[]{:S(2)}, u32[]{:S(2)}) %collective-permute-start.12) | collective-permute-done | bytes 393248 | tf_op jit(solution)/shard_map/ppermute | solution.py:548
  133.3 2.1 collective-permute-start.15
  136.2 1.5 collective-permute-start.17
  137.7 3.2 %collective-permute-done.19 = bf16[2,128,768]{2,1,0:T(8,128)(2,1)S(1)} collective-permute-done((bf16[2,128,768]{2,1,0:T(8,128)(2,1)S(1)}, bf16[2,128,768]{2,1,0:T(8,128)(2,1)S(1)}, u32[]{:S(2)}, u32[]{:S(2)}) %collective-permute-start.19) | collective-permute-done | bytes 393248 | tf_op jit(solution)/shard_map/ppermute | solution.py:548
  142.6 1.4 add.142
  144.0 1.5 collective-permute-start.25
  149.1 1.3 collective-permute-start.16
  150.4 6.1 %collective-permute-done.20 = bf16[2,128,768]{2,1,0:T(8,128)(2,1)} collective-permute-done((bf16[2,128,768]{2,1,0:T(8,128)(2,1)}, bf16[2,128,768]{2,1,0:T(8,128)(2,1)}, u32[]{:S(2)}, u32[]{:S(2)}) %collective-permute-start.20) | collective-permute-done | bytes 393248 | tf_op jit(solution)/shard_map/ppermute | solution.py:548
  156.5 1.2 fusion.11
  158.8 2.8 %collective-permute-start.26 = (bf16[208,384]{1,0:T(8,128)(2,1)S(1)}, bf16[208,384]{1,0:T(8,128)(2,1)S(1)}, u32[]{:S(2)}, u32[]{:S(2)}) collective-permute-start(bf16[208,384]{1,0:T(8,128)(2,1)S(1)} %get-tuple-element.137), channel_id=1, source_target_pairs={{0,12},{4,8},{8,4},{12,0},{1,13},{5,9},{9,5},{13,1},{2,14},{6,10},... | collective-permute-start | bytes 479240 | tf_op jit(solution)/shard_map/ppermute | solution.py:548
  162.5 15.1 %collective-permute-done.21 = bf16[128,768]{1,0:T(8,128)(2,1)S(1)} collective-permute-done((bf16[128,768]{1,0:T(8,128)(2,1)S(1)}, bf16[128,768]{1,0:T(8,128)(2,1)S(1)}, u32[]{:S(2)}, u32[]{:S(2)}) %collective-permute-start.21) | collective-permute-done | bytes 196640 | tf_op jit(solution)/shard_map/ppermute | solution.py:548
  178.4 5.1 %collective-permute-done.27 = bf16[208,384]{1,0:T(8,128)(2,1)S(1)} collective-permute-done((bf16[208,384]{1,0:T(8,128)(2,1)S(1)}, bf16[208,384]{1,0:T(8,128)(2,1)S(1)}, u32[]{:S(2)}, u32[]{:S(2)}) %collective-permute-start.27) | collective-permute-done | bytes 159776 | tf_op jit(solution)/shard_map/ppermute | solution.py:548
  183.5 1.6 collective-permute-done.28
  188.2 1.9 pad_maximum_fusion.9
  190.4 2.7 %collective-permute-done.29 = bf16[208,384]{1,0:T(8,128)(2,1)S(1)} collective-permute-done((bf16[208,384]{1,0:T(8,128)(2,1)S(1)}, bf16[208,384]{1,0:T(8,128)(2,1)S(1)}, u32[]{:S(2)}, u32[]{:S(2)}) %collective-permute-start.29) | collective-permute-done | bytes 159776 | tf_op jit(solution)/shard_map/ppermute | solution.py:548
  196.4 4.8 %collective-permute-done.30 = bf16[2,208,384]{2,1,0:T(8,128)(2,1)S(1)} collective-permute-done((bf16[2,208,384]{2,1,0:T(8,128)(2,1)S(1)}, bf16[2,208,384]{2,1,0:T(8,128)(2,1)S(1)}, u32[]{:S(2)}, u32[]{:S(2)}) %collective-permute-start.30) | collective-permute-done | bytes 319520 | tf_op jit(solution)/shard_map/ppermute | solution.py:548
  205.3 1.4 reshape_squeeze.3
  206.7 2.2 slice.171
  210.9 1.3 broadcast_select_fusion.25
  213.5 1.5 broadcast_select_fusion.21
  215.3 2.0 convert_add_fusion
  217.3 2.1 add_add_fusion
  (219 shorter events, 39.7 us)
Async XLA Ops:
  0.7 10.8 %copy-start.49 = (s32[2,2048]{1,0:T(2,128)S(1)}, s32[2,2048]{1,0:T(2,128)}, u32[]{:S(2)}) copy-start(s32[2,2048]{1,0:T(2,128)} %param.16) | copy-start | bytes 49156
  0.7 10.8 %copy-start.29 = (bf16[384,3,192]{0,2,1:T(8,128)(2,1)S(1)}, bf16[384,3,192]{0,2,1:T(8,128)(2,1)}, u32[]{:S(2)}) copy-start(bf16[384,3,192]{0,2,1:T(8,128)(2,1)} %param.17) | copy-start | bytes 1327108
  0.7 10.8 %copy-start.35 = (bf16[192,384]{1,0:T(8,128)(2,1)S(1)}, bf16[192,384]{1,0:T(8,128)(2,1)}, u32[]{:S(2)}) copy-start(bf16[192,384]{1,0:T(8,128)(2,1)} %param.19) | copy-start | bytes 442372
  1.9 31.8 %copy-start.17 = (bf16[1,128,768]{2,1,0:T(8,128)(2,1)}, bf16[1,128,768]{2,1,0:T(8,128)(2,1)S(1)}, u32[]{:S(2)}) copy-start(bf16[1,128,768]{2,1,0:T(8,128)(2,1)S(1)} %get-tuple-element.136) | copy-start | bytes 589828
  1.9 31.8 %copy-start.19 = (bf16[1,128,768]{2,1,0:T(8,128)(2,1)}, bf16[1,128,768]{2,1,0:T(8,128)(2,1)S(1)}, u32[]{:S(2)}) copy-start(bf16[1,128,768]{2,1,0:T(8,128)(2,1)S(1)} %get-tuple-element.135) | copy-start | bytes 589828
  1.9 23.5 %collective-permute-start.6 = (bf16[1,128,768]{2,1,0:T(8,128)(2,1)S(1)}, bf16[1,128,768]{2,1,0:T(8,128)(2,1)S(1)}, u32[]{:S(2)}, u32[]{:S(2)}) collective-permute-start(bf16[1,128,768]{2,1,0:T(8,128)(2,1)S(1)} %get-tuple-element.136), channel_id=1, source_target_pairs={{0,12},{4,8},{8,4},{12,0},{1,13},{5,9},{9,5},{13,1},{2,14},{6,10},... | collective-permute-start | bytes 589832 | tf_op jit(solution)/shard_map/ppermute | solution.py:548
  8.8 23.4 %collective-permute-start = (bf16[2,128,768]{2,1,0:T(8,128)(2,1)}, bf16[2,128,768]{2,1,0:T(8,128)(2,1)S(1)}, u32[]{:S(2)}, u32[]{:S(2)}) collective-permute-start(bf16[2,128,768]{2,1,0:T(8,128)(2,1)} %pad_maximum_fusion.13), channel_id=1, source_target_pairs={{0,8},{4,12},{8,0},{12,4},{1,9},{5,13},{9,1},{13,5},{2,10},{6,14},... | collective-permute-start | bytes 1179656 | tf_op jit(solution)/shard_map/ppermute | solution.py:548
  8.8 35.1 %collective-permute-start.3 = (bf16[384,768]{1,0:T(8,128)(2,1)S(1)}, bf16[384,768]{1,0:T(8,128)(2,1)}, u32[]{:S(2)}, u32[]{:S(2)}) collective-permute-start(bf16[384,768]{1,0:T(8,128)(2,1)S(1)} %copy-done.37), channel_id=1, source_target_pairs={{0,16},{16,0},{1,17},{17,1},{2,18},{18,2},{3,19},{19,3},{4,20},{20... | collective-permute-start | bytes 1769480 | tf_op jit(solution)/shard_map/ppermute | solution.py:548
  10.3 34.9 %collective-permute-start.4 = (bf16[768,384]{1,0:T(8,128)(2,1)S(1)}, bf16[768,384]{1,0:T(8,128)(2,1)}, u32[]{:S(2)}, u32[]{:S(2)}) collective-permute-start(bf16[768,384]{1,0:T(8,128)(2,1)S(1)} %copy-done.38), channel_id=1, source_target_pairs={{0,16},{16,0},{1,17},{17,1},{2,18},{18,2},{3,19},{19,3},{4,20},{20... | collective-permute-start | bytes 1769480 | tf_op jit(solution)/shard_map/ppermute | solution.py:548
  10.8 13.1 %collective-permute-start.5 = (bf16[1,128,768]{2,1,0:T(8,128)(2,1)S(1)}, bf16[1,128,768]{2,1,0:T(8,128)(2,1)S(1)}, u32[]{:S(2)}, u32[]{:S(2)}) collective-permute-start(bf16[1,128,768]{2,1,0:T(8,128)(2,1)S(1)} %get-tuple-element.135), channel_id=1, source_target_pairs={{0,4},{4,0},{8,12},{12,8},{1,5},{5,1},{9,13},{13,9},{2,6},{6,2},{1... | collective-permute-start | bytes 589832 | tf_op jit(solution)/shard_map/ppermute | solution.py:548
  23.9 38.5 %collective-permute-start.9 = (bf16[768,384]{1,0:T(8,128)(2,1)}, bf16[768,384]{1,0:T(8,128)(2,1)}, u32[]{:S(2)}, u32[]{:S(2)}) collective-permute-start(bf16[768,384]{1,0:T(8,128)(2,1)} %pad_maximum_fusion.11), channel_id=1, source_target_pairs={{0,16},{16,0},{1,17},{17,1},{2,18},{18,2},{3,19},{19,3},{4,20},{20... | collective-permute-start | bytes 1769480 | tf_op jit(solution)/shard_map/ppermute | solution.py:548
  25.5 11.1 %collective-permute-start.7 = (bf16[2,128,768]{2,1,0:T(8,128)(2,1)S(1)}, bf16[2,128,768]{2,1,0:T(8,128)(2,1)S(1)}, u32[]{:S(2)}, u32[]{:S(2)}) collective-permute-start(bf16[2,128,768]{2,1,0:T(8,128)(2,1)S(1)} %constant_dynamic-update-slice_fusion.nz), channel_id=1, source_target_pairs={{0,2},{1,3},{2,0},{3,1},{4,6},{5,7},{6,4},{7,5},{8,10},{9,11},{10,... | collective-permute-start | bytes 1179656 | tf_op jit(solution)/shard_map/ppermute | solution.py:548
  32.2 11.6 %copy-start.2 = (bf16[2,128,768]{2,1,0:T(8,128)(2,1)}, bf16[2,128,768]{2,1,0:T(8,128)(2,1)S(1)}, u32[]{:S(2)}) copy-start(bf16[2,128,768]{2,1,0:T(8,128)(2,1)S(1)} %collective-permute-done.fz) | copy-start | bytes 1179652
  32.2 11.5 %collective-permute-start.1 = (bf16[2,128,768]{2,1,0:T(8,128)(2,1)S(1)}, bf16[2,128,768]{2,1,0:T(8,128)(2,1)S(1)}, u32[]{:S(2)}, u32[]{:S(2)}) collective-permute-start(bf16[2,128,768]{2,1,0:T(8,128)(2,1)S(1)} %collective-permute-done.fz), channel_id=1, source_target_pairs={{0,2},{1,3},{2,0},{3,1},{4,6},{5,7},{6,4},{7,5},{8,10},{9,11},{10,... | collective-permute-start | bytes 1179656 | tf_op jit(solution)/shard_map/ppermute | solution.py:548
  36.7 27.2 %collective-permute-start.8 = (bf16[2,2,128,768]{3,2,1,0:T(8,128)(2,1)S(1)}, bf16[2,2,128,768]{3,2,1,0:T(8,128)(2,1)S(1)}, u32[]{:S(2)}, u32[]{:S(2)}) collective-permute-start(bf16[2,2,128,768]{3,2,1,0:T(8,128)(2,1)S(1)} %pad_maximum_fusion.7), channel_id=1, source_target_pairs={{0,1},{1,0},{2,3},{3,2},{4,5},{5,4},{6,7},{7,6},{8,9},{9,8},{10,11... | collective-permute-start | bytes 2359304 | tf_op jit(solution)/shard_map/ppermute | solution.py:548
  43.8 3.8 %collective-permute-start.2 = (bf16[2,2,128,768]{3,2,1,0:T(8,128)(2,1)S(1)}, bf16[2,2,128,768]{3,2,1,0:T(8,128)(2,1)S(1)}, u32[]{:S(2)}, u32[]{:S(2)}) collective-permute-start(bf16[2,2,128,768]{3,2,1,0:T(8,128)(2,1)S(1)} %pad_maximum_fusion.6), channel_id=1, source_target_pairs={{0,1},{1,0},{2,3},{3,2},{4,5},{5,4},{6,7},{7,6},{8,9},{9,8},{10,11... | collective-permute-start | bytes 2359304 | tf_op jit(solution)/shard_map/ppermute | solution.py:548
  51.8 10.6 %copy-start.30 = (bf16[384,3,192]{0,2,1:T(8,128)(2,1)S(1)}, bf16[384,3,192]{0,2,1:T(8,128)(2,1)}, u32[]{:S(2)}) copy-start(bf16[384,3,192]{0,2,1:T(8,128)(2,1)} %param.17) | copy-start | bytes 1327108
  61.8 28.9 %collective-permute-start.10 = (bf16[768,768]{1,0:T(8,128)(2,1)S(1)}, bf16[768,768]{1,0:T(8,128)(2,1)S(1)}, u32[]{:S(2)}, u32[]{:S(2)}) collective-permute-start(bf16[768,768]{1,0:T(8,128)(2,1)S(1)} %get-tuple-element.81), channel_id=1, source_target_pairs={{0,16},{16,0},{1,17},{17,1},{2,18},{18,2},{3,19},{19,3},{4,20},{20... | collective-permute-start | bytes 3538952 | tf_op jit(solution)/shard_map/ppermute | solution.py:548
  91.0 16.3 %collective-permute-start.13 = (bf16[384,768]{1,0:T(8,128)(2,1)S(1)}, bf16[384,768]{1,0:T(8,128)(2,1)S(1)}, u32[]{:S(2)}, u32[]{:S(2)}) collective-permute-start(bf16[384,768]{1,0:T(8,128)(2,1)S(1)} %dynamic-slice_convert_fusion), channel_id=1, source_target_pairs={{0,4},{4,0},{8,12},{12,8},{1,5},{5,1},{9,13},{13,9},{2,6},{6,2},{1... | collective-permute-start | bytes 1769480 | tf_op jit(solution)/shard_map/ppermute | solution.py:548
  106.1 7.3 %collective-permute-start.11 = (bf16[2,256,768]{2,1,0:T(8,128)(2,1)S(1)}, bf16[2,256,768]{2,1,0:T(8,128)(2,1)S(1)}, u32[]{:S(2)}, u32[]{:S(2)}) collective-permute-start(bf16[2,256,768]{2,1,0:T(8,128)(2,1)S(1)} %get-tuple-element.85), channel_id=1, source_target_pairs={{0,1},{1,0},{2,3},{3,2},{4,5},{5,4},{6,7},{7,6},{8,9},{9,8},{10,11... | collective-permute-start | bytes 2359304 | tf_op jit(solution)/shard_map/ppermute | solution.py:548
  107.5 15.9 %collective-permute-start.33 = (bf16[192,768]{1,0:T(8,128)(2,1)S(1)}, bf16[192,768]{1,0:T(8,128)(2,1)S(1)}, u32[]{:S(2)}, u32[]{:S(2)}) collective-permute-start(bf16[192,768]{1,0:T(8,128)(2,1)S(1)} %dynamic-slice_convert_fusion.1), channel_id=1, source_target_pairs={{0,8},{4,12},{8,0},{12,4},{1,9},{5,13},{9,1},{13,5},{2,10},{6,14},... | collective-permute-start | bytes 884744 | tf_op jit(solution)/shard_map/ppermute | solution.py:548
  113.3 11.5 %collective-permute-start.18 = (bf16[2,256,768]{2,1,0:T(8,128)(2,1)S(1)}, bf16[2,256,768]{2,1,0:T(8,128)(2,1)S(1)}, u32[]{:S(2)}, u32[]{:S(2)}) collective-permute-start(bf16[2,256,768]{2,1,0:T(8,128)(2,1)S(1)} %get-tuple-element.103), channel_id=1, source_target_pairs={{0,1},{1,0},{2,3},{3,2},{4,5},{5,4},{6,7},{7,6},{8,9},{9,8},{10,11... | collective-permute-start | bytes 2359304 | tf_op jit(solution)/shard_map/ppermute | solution.py:548
  119.8 6.2 %collective-permute-start.14 = (bf16[2,256,768]{2,1,0:T(8,128)(2,1)S(1)}, bf16[2,256,768]{2,1,0:T(8,128)(2,1)S(1)}, u32[]{:S(2)}, u32[]{:S(2)}) collective-permute-start(bf16[2,256,768]{2,1,0:T(8,128)(2,1)S(1)} %get-tuple-element.100), channel_id=1, source_target_pairs={{0,1},{1,0},{2,3},{3,2},{4,5},{5,4},{6,7},{7,6},{8,9},{9,8},{10,11... | collective-permute-start | bytes 2359304 | tf_op jit(solution)/shard_map/ppermute | solution.py:548
  120.4 12.0 %collective-permute-start.12 = (bf16[2,128,768]{2,1,0:T(8,128)(2,1)S(1)}, bf16[2,128,768]{2,1,0:T(8,128)(2,1)S(1)}, u32[]{:S(2)}, u32[]{:S(2)}) collective-permute-start(bf16[2,128,768]{2,1,0:T(8,128)(2,1)S(1)} %fusion.16), channel_id=1, source_target_pairs={{0,2},{1,3},{2,0},{3,1},{4,6},{5,7},{6,4},{7,5},{8,10},{9,11},{10,... | collective-permute-start | bytes 1179656 | tf_op jit(solution)/shard_map/ppermute | solution.py:548
  124.2 21.4 %collective-permute-start.34 = (bf16[192,768]{1,0:T(8,128)(2,1)}, bf16[192,768]{1,0:T(8,128)(2,1)}, u32[]{:S(2)}, u32[]{:S(2)}) collective-permute-start(bf16[192,768]{1,0:T(8,128)(2,1)} %add_convert_fusion), channel_id=1, source_target_pairs={{0,8},{4,12},{8,0},{12,4},{1,9},{5,13},{9,1},{13,5},{2,10},{6,14},... | collective-permute-start | bytes 884744 | tf_op jit(solution)/shard_map/ppermute | solution.py:548
  125.0 15.8 %collective-permute-start.19 = (bf16[2,128,768]{2,1,0:T(8,128)(2,1)S(1)}, bf16[2,128,768]{2,1,0:T(8,128)(2,1)S(1)}, u32[]{:S(2)}, u32[]{:S(2)}) collective-permute-start(bf16[2,128,768]{2,1,0:T(8,128)(2,1)S(1)} %fusion.18), channel_id=1, source_target_pairs={{0,2},{1,3},{2,0},{3,1},{4,6},{5,7},{6,4},{7,5},{8,10},{9,11},{10,... | collective-permute-start | bytes 1179656 | tf_op jit(solution)/shard_map/ppermute | solution.py:548
  133.3 14.7 %collective-permute-start.15 = (bf16[128,768]{1,0:T(8,128)(2,1)}, bf16[128,768]{1,0:T(8,128)(2,1)}, u32[]{:S(2)}, u32[]{:S(2)}) collective-permute-start(bf16[128,768]{1,0:T(8,128)(2,1)} %get-tuple-element.161), channel_id=1, source_target_pairs={{0,8},{4,12},{8,0},{12,4},{1,9},{5,13},{9,1},{13,5},{2,10},{6,14},... | collective-permute-start | bytes 589832 | tf_op jit(solution)/shard_map/ppermute | solution.py:548
  136.2 14.2 %collective-permute-start.17 = (bf16[2,128,768]{2,1,0:T(8,128)(2,1)}, bf16[2,128,768]{2,1,0:T(8,128)(2,1)}, u32[]{:S(2)}, u32[]{:S(2)}) collective-permute-start(bf16[2,128,768]{2,1,0:T(8,128)(2,1)} %fusion.17), channel_id=1, source_target_pairs={{0,2},{1,3},{2,0},{3,1},{4,6},{5,7},{6,4},{7,5},{8,10},{9,11},{10,... | collective-permute-start | bytes 1179656 | tf_op jit(solution)/shard_map/ppermute | solution.py:548
  141.7 14.8 %collective-permute-start.20 = (bf16[2,128,768]{2,1,0:T(8,128)(2,1)}, bf16[2,128,768]{2,1,0:T(8,128)(2,1)}, u32[]{:S(2)}, u32[]{:S(2)}) collective-permute-start(bf16[2,128,768]{2,1,0:T(8,128)(2,1)} %fusion.9), channel_id=1, source_target_pairs={{0,4},{4,0},{8,12},{12,8},{1,5},{5,1},{9,13},{13,9},{2,6},{6,2},{1... | collective-permute-start | bytes 1179656 | tf_op jit(solution)/shard_map/ppermute | solution.py:548
  142.6 47.5 %copy-start.42 = (f32[2,128]{1,0:T(2,128)}, f32[2,128]{1,0:T(2,128)S(1)}, u32[]{:S(2)}) copy-start(f32[2,128]{1,0:T(2,128)S(1)} %add_rsqrt_fusion) | copy-start | bytes 3076
  142.6 13.9 %copy-start.26 = (f32[2,256,768]{2,1,0:T(8,128)S(1)}, f32[2,256,768]{2,1,0:T(8,128)}, u32[]{:S(2)}) copy-start(f32[2,256,768]{2,1,0:T(8,128)} %copy-done.25) | copy-start | bytes 4718596
  144.0 14.6 %collective-permute-start.25 = (bf16[832,384]{1,0:T(8,128)(2,1)}, bf16[832,384]{1,0:T(8,128)(2,1)S(1)}, u32[]{:S(2)}, u32[]{:S(2)}) collective-permute-start(bf16[832,384]{1,0:T(8,128)(2,1)} %copy-done.14), channel_id=1, source_target_pairs={{0,16},{16,0},{1,17},{17,1},{2,18},{18,2},{3,19},{19,3},{4,20},{20... | collective-permute-start | bytes 1916936 | tf_op jit(solution)/shard_map/ppermute | solution.py:548
  146.7 31.7 %collective-permute-start.35 = (bf16[2,192,768]{2,1,0:T(8,128)(2,1)S(1)}, bf16[2,192,768]{2,1,0:T(8,128)(2,1)S(1)}, u32[]{:S(2)}, u32[]{:S(2)}) collective-permute-start(bf16[2,192,768]{2,1,0:T(8,128)(2,1)S(1)} %pad_maximum_fusion.12), channel_id=1, source_target_pairs={{0,4},{4,0},{8,12},{12,8},{1,5},{5,1},{9,13},{13,9},{2,6},{6,2},{1... | collective-permute-start | bytes 1769480 | tf_op jit(solution)/shard_map/ppermute | solution.py:548
  149.1 38.2 %collective-permute-start.16 = (bf16[2,128,768]{2,1,0:T(8,128)(2,1)S(1)}, bf16[2,128,768]{2,1,0:T(8,128)(2,1)S(1)}, u32[]{:S(2)}, u32[]{:S(2)}) collective-permute-start(bf16[2,128,768]{2,1,0:T(8,128)(2,1)S(1)} %pad_maximum_fusion.15), channel_id=1, source_target_pairs={{0,2},{1,3},{2,0},{3,1},{4,6},{5,7},{6,4},{7,5},{8,10},{9,11},{10,... | collective-permute-start | bytes 1179656 | tf_op jit(solution)/shard_map/ppermute | solution.py:548
  157.7 19.8 %collective-permute-start.21 = (bf16[128,768]{1,0:T(8,128)(2,1)S(1)}, bf16[128,768]{1,0:T(8,128)(2,1)S(1)}, u32[]{:S(2)}, u32[]{:S(2)}) collective-permute-start(bf16[128,768]{1,0:T(8,128)(2,1)S(1)} %fusion.20), channel_id=1, source_target_pairs={{0,8},{4,12},{8,0},{12,4},{1,9},{5,13},{9,1},{13,5},{2,10},{6,14},... | collective-permute-start | bytes 589832 | tf_op jit(solution)/shard_map/ppermute | solution.py:548
  158.8 19.6 %collective-permute-start.26 = (bf16[208,384]{1,0:T(8,128)(2,1)S(1)}, bf16[208,384]{1,0:T(8,128)(2,1)S(1)}, u32[]{:S(2)}, u32[]{:S(2)}) collective-permute-start(bf16[208,384]{1,0:T(8,128)(2,1)S(1)} %get-tuple-element.137), channel_id=1, source_target_pairs={{0,12},{4,8},{8,4},{12,0},{1,13},{5,9},{9,5},{13,1},{2,14},{6,10},... | collective-permute-start | bytes 479240 | tf_op jit(solution)/shard_map/ppermute | solution.py:548
  161.5 22.0 %collective-permute-start.27 = (bf16[208,384]{1,0:T(8,128)(2,1)S(1)}, bf16[208,384]{1,0:T(8,128)(2,1)S(1)}, u32[]{:S(2)}, u32[]{:S(2)}) collective-permute-start(bf16[208,384]{1,0:T(8,128)(2,1)S(1)} %get-tuple-element.139), channel_id=1, source_target_pairs={{0,8},{4,12},{8,0},{12,4},{1,9},{5,13},{9,1},{13,5},{2,10},{6,14},... | collective-permute-start | bytes 479240 | tf_op jit(solution)/shard_map/ppermute | solution.py:548
  162.5 15.8 %copy-start.21 = (f32[1,128,768]{2,1,0:T(8,128)}, f32[1,128,768]{2,1,0:T(8,128)S(1)}, u32[]{:S(2)}) copy-start(f32[1,128,768]{2,1,0:T(8,128)S(1)} %get-tuple-element.153) | copy-start | bytes 1179652
  177.6 7.6 %collective-permute-start.28 = (bf16[208,384]{1,0:T(8,128)(2,1)S(1)}, bf16[208,384]{1,0:T(8,128)(2,1)S(1)}, u32[]{:S(2)}, u32[]{:S(2)}) collective-permute-start(bf16[208,384]{1,0:T(8,128)(2,1)S(1)} %get-tuple-element.138), channel_id=1, source_target_pairs={{0,4},{4,0},{8,12},{12,8},{1,5},{5,1},{9,13},{13,9},{2,6},{6,2},{1... | collective-permute-start | bytes 479240 | tf_op jit(solution)/shard_map/ppermute | solution.py:548
  178.0 12.1 %copy-start.44 = (f32[2,128]{1,0:T(2,128)}, f32[2,128]{1,0:T(2,128)S(1)}, u32[]{:S(2)}) copy-start(f32[2,128]{1,0:T(2,128)S(1)} %broadcast_multiply_fusion) | copy-start | bytes 3076
  178.0 12.1 %copy-start.46 = (f32[2,128]{1,0:T(2,128)}, f32[2,128]{1,0:T(2,128)S(1)}, u32[]{:S(2)}) copy-start(f32[2,128]{1,0:T(2,128)S(1)} %broadcast_multiply_fusion.1) | copy-start | bytes 3076
  178.3 17.0 %collective-permute-start.23 = (bf16[2,128,768]{2,1,0:T(8,128)(2,1)S(1)}, bf16[2,128,768]{2,1,0:T(8,128)(2,1)S(1)}, u32[]{:S(2)}, u32[]{:S(2)}) collective-permute-start(bf16[2,128,768]{2,1,0:T(8,128)(2,1)S(1)} %fusion.7), channel_id=1, source_target_pairs={{0,2},{1,3},{2,0},{3,1},{4,6},{5,7},{6,4},{7,5},{8,10},{9,11},{10,... | collective-permute-start | bytes 1179656 | tf_op jit(solution)/shard_map/ppermute | solution.py:548
  185.2 7.8 %collective-permute-start.29 = (bf16[208,384]{1,0:T(8,128)(2,1)S(1)}, bf16[208,384]{1,0:T(8,128)(2,1)S(1)}, u32[]{:S(2)}, u32[]{:S(2)}) collective-permute-start(bf16[208,384]{1,0:T(8,128)(2,1)S(1)} %add_convert_fusion.1), channel_id=1, source_target_pairs={{0,8},{4,12},{8,0},{12,4},{1,9},{5,13},{9,1},{13,5},{2,10},{6,14},... | collective-permute-start | bytes 479240 | tf_op jit(solution)/shard_map/ppermute | solution.py:548
  190.1 20.8 %collective-permute-start.22 = (bf16[2,2,128,768]{3,2,1,0:T(8,128)(2,1)}, bf16[2,2,128,768]{3,2,1,0:T(8,128)(2,1)}, u32[]{:S(2)}, u32[]{:S(2)}) collective-permute-start(bf16[2,2,128,768]{3,2,1,0:T(8,128)(2,1)} %pad_maximum_fusion.9), channel_id=1, source_target_pairs={{0,1},{1,0},{2,3},{3,2},{4,5},{5,4},{6,7},{7,6},{8,9},{9,8},{10,11... | collective-permute-start | bytes 2359304 | tf_op jit(solution)/shard_map/ppermute | solution.py:548
  193.1 8.1 %collective-permute-start.30 = (bf16[2,208,384]{2,1,0:T(8,128)(2,1)S(1)}, bf16[2,208,384]{2,1,0:T(8,128)(2,1)S(1)}, u32[]{:S(2)}, u32[]{:S(2)}) collective-permute-start(bf16[2,208,384]{2,1,0:T(8,128)(2,1)S(1)} %pad_maximum_fusion.17), channel_id=1, source_target_pairs={{0,4},{4,0},{8,12},{12,8},{1,5},{5,1},{9,13},{13,9},{2,6},{6,2},{1... | collective-permute-start | bytes 958472 | tf_op jit(solution)/shard_map/ppermute | solution.py:548
  196.4 16.0 %collective-permute-start.24 = (bf16[2,2,128,768]{3,2,1,0:T(8,128)(2,1)}, bf16[2,2,128,768]{3,2,1,0:T(8,128)(2,1)}, u32[]{:S(2)}, u32[]{:S(2)}) collective-permute-start(bf16[2,2,128,768]{3,2,1,0:T(8,128)(2,1)} %pad_maximum_fusion.10), channel_id=1, source_target_pairs={{0,1},{1,0},{2,3},{3,2},{4,5},{5,4},{6,7},{7,6},{8,9},{9,8},{10,11... | collective-permute-start | bytes 2359304 | tf_op jit(solution)/shard_map/ppermute | solution.py:548
  201.3 1.3 collective-permute-start.31
  203.2 6.3 %collective-permute-start.32 = (f32[8,768]{1,0:T(8,128)}, f32[8,768]{1,0:T(8,128)}, u32[]{:S(2)}, u32[]{:S(2)}) collective-permute-start(f32[8,768]{1,0:T(8,128)} %fusion.26), channel_id=1, source_target_pairs={{0,2},{1,3},{2,0},{3,1},{4,6},{5,7},{6,4},{7,5},{8,10},{9,11},{10,... | collective-permute-start | bytes 73736 | tf_op jit(solution)/shard_map/ppermute | solution.py:548
  (40 other events, 153.4 us)

commit v12 on v11

--- a/solution.py
+++ b/solution.py
@@ -763,8 +763,8 @@
         down_total = jnp.concatenate(
             [down_total[:, : width // 2], down_total[:, width // 2 :]], axis=0
         )
-        late = late_first + tie(swap(late_second, "fsdp", 2, 1), sums_w).astype(F32)
-        late = double(pair_up(quarter_sum(late, c, a), norm_grad), c)
+        late = late_first + tie(swap(late_second, "fsdp", 2, 1), a).astype(F32)
+        late = double(pair_up(quarter_sum(late, c, norm_grad)), c, block_out)
         late = jnp.concatenate(late, axis=0).astype(F32)
         small = jnp.concatenate([late[4 * local : 4 * local + 8], late[4 * local + 8 :][:8]], axis=1)
     else:

time: 221 us -> 215 us (0.973)
  other arithmetic: 34.1 us -> 26.5 us
  waiting for transfers between devices: 73.8 us -> 79.1 us
  local copies, waits for them, and re-layouts: 13.7 us -> 9.7 us
    ppermute x36, waiting for transfers between devices: 73.8 us -> 79.1 us  [swap(): return lax.ppermute(v, axis, [(i, i ^ distance) for i in range(size)])]
    unnamed x106 -> x70, local copies, waits for them, and re-layouts: 6 us -> 3.93 us
  transfers between devices with their start and end apart: 36 -> 36, of which waited for: 17 -> 17; matrix products, arithmetic and copies ran while one was open for 16% -> 14% of each run, Pallas kernels for 28% -> 29%
where the time goes in v12:
time: 215 us
  waiting for transfers between devices  79.1 us (37%)
  Pallas kernels  62.1 us (29%)
  starting transfers between devices  35.6 us (17%)
  other arithmetic  26.5 us (12%)
  local copies, waits for them, and re-layouts  9.7 us (5%)
    ppermute x36, waiting for transfers between devices, swap(): return lax.ppermute(v, axis, [(i, i ^ distance) for i in range(size)])  79.1 us
    ppermute x36, starting transfers between devices, swap(): return lax.ppermute(v, axis, [(i, i ^ distance) for i in range(size)])  35.6 us
    pallas_call x3, Pallas kernels, attention(): pl.pallas_call(attention_kernel, grid=(rows // lanes,), in_specs=[pl.Bloc...  29 us
    pallas_call x2, Pallas kernels, back(): pl.pallas_call(functools.partial(back_kernel, own, split, heads), grid_sp...  11.1 us
    pallas_call x1, Pallas kernels, feed_forward(): pl.pallas_call(functools.partial(forward_kernel, split), grid_spec=pltpu....  9.97 us
    pallas_call x2, Pallas kernels, norms(): pl.pallas_call(kernel, grid_spec=pltpu.PrefetchScalarGridSpec(num_scalar_...  4.91 us
    pallas_call x1, Pallas kernels, project(): pl.pallas_call(project_kernel, grid=(8,), in_specs=[pl.BlockSpec((STEP, w...  4.43 us
  transfers between devices with their start and end apart: 36, of which 17 were waited for; matrix products, arithmetic and copies ran while one was open for 14% of the time, Pallas kernels for 29%

profile of v12, /device:TPU:0, one launch (start us, length us, event | category | flops | bytes accessed | tf_op | source)
XLA Modules:
  0.0 214.6 jit_solution(7123919589832988968)
XLA Ops:
  0.7 1.2 constant_dynamic-slice_fusion
  1.9 5.1 %collective-permute-start.6 = (bf16[1,128,768]{2,1,0:T(8,128)(2,1)S(1)}, bf16[1,128,768]{2,1,0:T(8,128)(2,1)S(1)}, u32[]{:S(2)}, u32[]{:S(2)}) collective-permute-start(bf16[1,128,768]{2,1,0:T(8,128)(2,1)S(1)} %get-tuple-element.136), channel_id=1, source_target_pairs={{0,12},{4,8},{8,4},{12,0},{1,13},{5,9},{9,5},{13,1},{2,14},{6,10},... | collective-permute-start | bytes 589832 | tf_op jit(solution)/shard_map/ppermute | solution.py:548
  8.8 1.5 collective-permute-start.3
  12.3 11.5 %collective-permute-done.5 = bf16[1,128,768]{2,1,0:T(8,128)(2,1)S(1)} collective-permute-done((bf16[1,128,768]{2,1,0:T(8,128)(2,1)S(1)}, bf16[1,128,768]{2,1,0:T(8,128)(2,1)S(1)}, u32[]{:S(2)}, u32[]{:S(2)}) %collective-permute-start.5) | collective-permute-done | bytes 196640 | tf_op jit(solution)/shard_map/ppermute | solution.py:548
  23.9 1.5 collective-permute-start.9
  25.5 1.6 collective-permute-start.7
  27.6 4.6 %collective-permute-done.fz = bf16[2,128,768]{2,1,0:T(8,128)(2,1)S(1)} collective-permute-done((bf16[2,128,768]{2,1,0:T(8,128)(2,1)}, bf16[2,128,768]{2,1,0:T(8,128)(2,1)S(1)}, u32[]{:S(2)}, u32[]{:S(2)}) %collective-permute-start) | collective-permute-done | bytes 393248 | tf_op jit(solution)/shard_map/ppermute | solution.py:548
  32.2 1.5 collective-permute-start.1
  33.9 2.6 %collective-permute-done.7.nx = bf16[2,128,768]{2,1,0:T(8,128)(2,1)S(1)} collective-permute-done((bf16[2,128,768]{2,1,0:T(8,128)(2,1)S(1)}, bf16[2,128,768]{2,1,0:T(8,128)(2,1)S(1)}, u32[]{:S(2)}, u32[]{:S(2)}) %collective-permute-start.7) | collective-permute-done | bytes 393248 | tf_op jit(solution)/shard_map/ppermute | solution.py:548
  36.7 7.0 %collective-permute-done.1.fx = bf16[2,128,768]{2,1,0:T(8,128)(2,1)S(1)} collective-permute-done((bf16[2,128,768]{2,1,0:T(8,128)(2,1)S(1)}, bf16[2,128,768]{2,1,0:T(8,128)(2,1)S(1)}, u32[]{:S(2)}, u32[]{:S(2)}) %collective-permute-start.1) | collective-permute-done | bytes 393248 | tf_op jit(solution)/shard_map/ppermute | solution.py:548
  43.9 1.1 broadcast_select_fusion.9
  45.2 1.3 broadcast_select_fusion.7
  46.7 1.2 copy-done
  48.1 2.7 %shard_map.254 = (bf16[1024,768]{1,0:T(8,128)(2,1)S(1)}, bf16[1024,768]{1,0:T(8,128)(2,1)S(1)}, bf16[1024,768]{1,0:T(8,128)(2,1)S(1)}, f32[24,1024]{1,0:T(8,128)S(1)}) custom-call(s32[4]{0:T(128)S(1)} %pad_add_fusion.at, bf16[2,512,768]{2,1,0:T(8,128)(2,1)S(1)} %copy-done, bf16[2,512,768]{2,1,0:T(8,128)(2,1)S(1)} %copy-done, ...), custom_call_target="tpu_custom_call" | custom-call | bytes 4718592 | tf_op jit(solution)/shard_map/pallas_call | solution.py:140
  50.9 10.0 %shard_map.255 = (bf16[1024,768]{1,0:T(8,128)(2,1)S(1)}, bf16[1024,768]{1,0:T(8,128)(2,1)S(1)}, f32[8,768]{1,0:T(8,128)S(1)}, f32[768,768]{1,0:T(8,128)S(1)}, bf16[768,768]{1,0:T(8,128)(2,1)S(1)}) custom-call(s32[4]{0:T(128)S(1)} %pad_add_fusion.at, bf16[1024,768]{1,0:T(8,128)(2,1)S(1)} %get-tuple-element.65.n2_ref, ...), custom_call_target="tpu_custom_call" | custom-call | flops 7247757312 | bytes 16777216 | tf_op jit(solution)/shard_map/pallas_call | solution.py:386
  61.5 1.3 broadcast_select_fusion.5
  63.8 2.2 %shard_map.256 = (bf16[1024,768]{1,0:T(8,128)(2,1)S(1)}, f32[24,1024]{1,0:T(8,128)S(1)}) custom-call(s32[4]{0:T(128)S(1)} %pad_add_fusion.at, bf16[2,128,768]{2,1,0:T(8,128)(2,1)S(1)} %constant_dynamic-update-slice_fusion.nz, bf16[2,128,768]{2,1,0:T(8,128)(2,1)S(1)} %copy-done.7, bf16[2,2,128,768]{3,2,1,0:T(8,128)(2,1)S(1)} %collective-permute-done.8.nc, ...), custom_call_target="tpu_custom_call" | custom-call | bytes 4718592 | tf_op jit(solution)/shard_map/pallas_call | solution.py:140
  66.0 4.4 %shard_map.257 = (bf16[192,2048]{1,0:T(8,128)(2,1)S(1)}, bf16[192,2048]{1,0:T(8,128)(2,1)S(1)}, bf16[192,1024]{1,0:T(8,128)(2,1)S(1)}, bf16[192,1024]{1,0:T(8,128)(2,1)S(1)}) custom-call(bf16[1024,768]{1,0:T(8,128)(2,1)S(1)} %get-tuple-element.68.n1o.refs_9_, bf16[1024,768]{1,0:T(8,128)(2,1)S(1)} %get-tuple-element.70.n1x.refs_6_, ...), custom_call_target="tpu_custom_call" | custom-call | flops 1811939328 | bytes 9437184 | tf_op jit(solution)/shard_map/pallas_call | solution.py:204
  70.4 9.7 %shard_map.259 = (bf16[64,1024]{1,0:T(8,128)(2,1)S(1)}, bf16[64,1024]{1,0:T(8,128)(2,1)S(1)}, bf16[64,2048]{1,0:T(8,128)(2,1)S(1)}, bf16[64,2048]{1,0:T(8,128)(2,1)S(1)}) custom-call(f32[8,768]{1,0:T(8,128)S(1)} %get-tuple-element.67.after.refs_15_, bf16[192,1024]{1,0:T(8,128)(2,1)S(1)} %get-tuple-element.74.q_ref, ...), custom_call_target="tpu_custom_call" | custom-call | flops 5368709120 | bytes 2097152 | tf_op jit(solution)/shard_map/pallas_call | solution.py:307
  80.1 9.7 %shard_map.258 = (bf16[64,1024]{1,0:T(8,128)(2,1)S(1)}, bf16[64,1024]{1,0:T(8,128)(2,1)S(1)}, bf16[64,2048]{1,0:T(8,128)(2,1)S(1)}, bf16[64,2048]{1,0:T(8,128)(2,1)S(1)}) custom-call(f32[8,768]{1,0:T(8,128)S(1)} %get-tuple-element.67.after.refs_15_, bf16[192,1024]{1,0:T(8,128)(2,1)S(1)} %get-tuple-element.74.q_ref, ...), custom_call_target="tpu_custom_call" | custom-call | flops 5368709120 | bytes 2097152 | tf_op jit(solution)/shard_map/pallas_call | solution.py:307
  90.1 2.6 %collective-permute-start.13 = (bf16[384,768]{1,0:T(8,128)(2,1)S(1)}, bf16[384,768]{1,0:T(8,128)(2,1)S(1)}, u32[]{:S(2)}, u32[]{:S(2)}) collective-permute-start(bf16[384,768]{1,0:T(8,128)(2,1)S(1)} %dynamic-slice_convert_fusion), channel_id=1, source_target_pairs={{0,4},{4,0},{8,12},{12,8},{1,5},{5,1},{9,13},{13,9},{2,6},{6,2},{1... | collective-permute-start | bytes 1769480 | tf_op jit(solution)/shard_map/ppermute | solution.py:548
  92.7 9.7 %shard_map.260 = (bf16[64,1024]{1,0:T(8,128)(2,1)S(1)}, bf16[64,1024]{1,0:T(8,128)(2,1)S(1)}, bf16[64,2048]{1,0:T(8,128)(2,1)S(1)}, bf16[64,2048]{1,0:T(8,128)(2,1)S(1)}) custom-call(f32[768,768]{1,0:T(8,128)S(1)} %convert_add_fusion.1.after, bf16[192,1024]{1,0:T(8,128)(2,1)S(1)} %get-tuple-element.74.q_ref, bf16[192,1024]{1,0:T(8,128)(2,1)S(1)} %get-tuple-element.75.do_ref, ...), custom_call_target="tpu_custom_call" | custom-call | flops 5368709120 | bytes 2097152 | tf_op jit(solution)/shard_map/pallas_call | solution.py:307
  102.4 2.7 %shard_map.261 = (bf16[2,256,768]{2,1,0:T(8,128)(2,1)S(1)}, bf16[2,256,768]{2,1,0:T(8,128)(2,1)S(1)}, f32[192,768]{1,0:T(8,128)S(1)}) custom-call(bf16[64,1024]{1,0:T(8,128)(2,1)S(1)} %get-tuple-element.78.refs_0_, bf16[64,1024]{1,0:T(8,128)(2,1)S(1)} %get-tuple-element.79.refs_1_, bf16[64,1024]{1,0:T(8,128)(2,1)S(1)} %get-tuple-element.82.refs_2_, ...), custom_call_target="tpu_custom_call" | custom-call | flops 603979776 | bytes 8388608 | tf_op jit(solution)/shard_map/pallas_call | solution.py:436
  107.5 4.8 %shard_map.262 = (bf16[2,256,768]{2,1,0:T(8,128)(2,1)S(1)}, bf16[2,256,768]{2,1,0:T(8,128)(2,1)S(1)}, f32[384,768]{1,0:T(8,128)S(1)}, f32[8,768]{1,0:T(8,128)S(1)}) custom-call(s32[4]{0:T(128)S(1)} %pad_add_fusion.at, bf16[64,2048]{1,0:T(8,128)(2,1)S(1)} %get-tuple-element.89.refs_0_.refs_3_, bf16[64,2048]{1,0:T(8,128)(2,1)S(1)} %get-tuple-element.90.refs_1_.refs_4_, ...), custom_call_target="tpu_custom_call" | custom-call | flops 1207959552 | bytes 10485760 | tf_op jit(solution)/shard_map/pallas_call | solution.py:532
  112.6 6.2 %shard_map.263 = (bf16[2,256,768]{2,1,0:T(8,128)(2,1)S(1)}, bf16[2,256,768]{2,1,0:T(8,128)(2,1)S(1)}, f32[832,384]{1,0:T(8,128)S(1)}, bf16[832,384]{1,0:T(8,128)(2,1)S(1)}) custom-call(s32[4]{0:T(128)S(1)} %pad_add_fusion.at, bf16[64,1024]{1,0:T(8,128)(2,1)S(1)} %get-tuple-element.86.refs_0_, bf16[64,1024]{1,0:T(8,128)(2,1)S(1)} %get-tuple-element.87.refs_1_, ...), custom_call_target="tpu_custom_call" | custom-call | flops 1811939328 | bytes 10485760 | tf_op jit(solution)/shard_map/pallas_call | solution.py:532
  119.4 1.5 collective-permute-start.12
  120.9 1.6 collective-permute-done.33
  125.2 6.2 %collective-permute-done.12 = bf16[2,128,768]{2,1,0:T(8,128)(2,1)S(1)} collective-permute-done((bf16[2,128,768]{2,1,0:T(8,128)(2,1)S(1)}, bf16[2,128,768]{2,1,0:T(8,128)(2,1)S(1)}, u32[]{:S(2)}, u32[]{:S(2)}) %collective-permute-start.12) | collective-permute-done | bytes 393248 | tf_op jit(solution)/shard_map/ppermute | solution.py:548
  132.4 2.1 collective-permute-start.15
  135.2 1.5 collective-permute-start.17
  136.7 3.2 %collective-permute-done.19 = bf16[2,128,768]{2,1,0:T(8,128)(2,1)S(1)} collective-permute-done((bf16[2,128,768]{2,1,0:T(8,128)(2,1)S(1)}, bf16[2,128,768]{2,1,0:T(8,128)(2,1)S(1)}, u32[]{:S(2)}, u32[]{:S(2)}) %collective-permute-start.19) | collective-permute-done | bytes 393248 | tf_op jit(solution)/shard_map/ppermute | solution.py:548
  141.7 1.6 collective-permute-start.25
  143.3 1.1 pad_maximum_fusion.12
  144.4 1.1 collective-permute-start.35
  145.5 1.6 collective-permute-done.15
  149.2 6.3 %collective-permute-done.20 = bf16[2,128,768]{2,1,0:T(8,128)(2,1)} collective-permute-done((bf16[2,128,768]{2,1,0:T(8,128)(2,1)}, bf16[2,128,768]{2,1,0:T(8,128)(2,1)}, u32[]{:S(2)}, u32[]{:S(2)}) %collective-permute-start.20) | collective-permute-done | bytes 393248 | tf_op jit(solution)/shard_map/ppermute | solution.py:548
  155.5 1.2 fusion.11
  157.3 9.4 %collective-permute-done.21 = bf16[128,768]{1,0:T(8,128)(2,1)S(1)} collective-permute-done((bf16[128,768]{1,0:T(8,128)(2,1)S(1)}, bf16[128,768]{1,0:T(8,128)(2,1)S(1)}, u32[]{:S(2)}, u32[]{:S(2)}) %collective-permute-start.21) | collective-permute-done | bytes 196640 | tf_op jit(solution)/shard_map/ppermute | solution.py:548
  168.4 3.8 %collective-permute-done.35 = bf16[2,192,768]{2,1,0:T(8,128)(2,1)S(1)} collective-permute-done((bf16[2,192,768]{2,1,0:T(8,128)(2,1)S(1)}, bf16[2,192,768]{2,1,0:T(8,128)(2,1)S(1)}, u32[]{:S(2)}, u32[]{:S(2)}) %collective-permute-start.35) | collective-permute-done | bytes 589856 | tf_op jit(solution)/shard_map/ppermute | solution.py:548
  172.4 2.4 %collective-permute-start.26 = (bf16[208,384]{1,0:T(8,128)(2,1)S(1)}, bf16[208,384]{1,0:T(8,128)(2,1)S(1)}, u32[]{:S(2)}, u32[]{:S(2)}) collective-permute-start(bf16[208,384]{1,0:T(8,128)(2,1)S(1)} %get-tuple-element.137), channel_id=1, source_target_pairs={{0,12},{4,8},{8,4},{12,0},{1,13},{5,9},{9,5},{13,1},{2,14},{6,10},... | collective-permute-start | bytes 479240 | tf_op jit(solution)/shard_map/ppermute | solution.py:548
  174.8 2.0 collective-permute-start.28
  176.8 1.1 bitcast_select_fusion.2
  181.4 6.4 %collective-permute-done.27 = bf16[208,384]{1,0:T(8,128)(2,1)S(1)} collective-permute-done((bf16[208,384]{1,0:T(8,128)(2,1)S(1)}, bf16[208,384]{1,0:T(8,128)(2,1)S(1)}, u32[]{:S(2)}, u32[]{:S(2)}) %collective-permute-start.27) | collective-permute-done | bytes 159776 | tf_op jit(solution)/shard_map/ppermute | solution.py:548
  189.2 1.1 maximum_convert_fusion.1
  190.3 7.3 %collective-permute-done.29 = bf16[208,384]{1,0:T(8,128)(2,1)S(1)} collective-permute-done((bf16[208,384]{1,0:T(8,128)(2,1)S(1)}, bf16[208,384]{1,0:T(8,128)(2,1)S(1)}, u32[]{:S(2)}, u32[]{:S(2)}) %collective-permute-start.29) | collective-permute-done | bytes 159776 | tf_op jit(solution)/shard_map/ppermute | solution.py:548
  199.7 2.1 add_add_fusion
  201.8 5.4 %collective-permute-done.30 = bf16[2,208,384]{2,1,0:T(8,128)(2,1)S(1)} collective-permute-done((bf16[2,208,384]{2,1,0:T(8,128)(2,1)S(1)}, bf16[2,208,384]{2,1,0:T(8,128)(2,1)S(1)}, u32[]{:S(2)}, u32[]{:S(2)}) %collective-permute-start.30) | collective-permute-done | bytes 319520 | tf_op jit(solution)/shard_map/ppermute | solution.py:548
  207.4 2.0 convert_add_fusion
  (183 shorter events, 33.2 us)
Async XLA Ops:
  0.7 10.8 %copy-start.31 = (s32[2,2048]{1,0:T(2,128)S(1)}, s32[2,2048]{1,0:T(2,128)}, u32[]{:S(2)}) copy-start(s32[2,2048]{1,0:T(2,128)} %param.16) | copy-start | bytes 49156
  0.7 10.8 %copy-start.24 = (bf16[384,3,192]{0,2,1:T(8,128)(2,1)S(1)}, bf16[384,3,192]{0,2,1:T(8,128)(2,1)}, u32[]{:S(2)}) copy-start(bf16[384,3,192]{0,2,1:T(8,128)(2,1)} %param.17) | copy-start | bytes 1327108
  0.7 10.8 %copy-start.26 = (bf16[192,384]{1,0:T(8,128)(2,1)S(1)}, bf16[192,384]{1,0:T(8,128)(2,1)}, u32[]{:S(2)}) copy-start(bf16[192,384]{1,0:T(8,128)(2,1)} %param.19) | copy-start | bytes 442372
  1.9 31.8 %copy-start.17 = (bf16[1,128,768]{2,1,0:T(8,128)(2,1)}, bf16[1,128,768]{2,1,0:T(8,128)(2,1)S(1)}, u32[]{:S(2)}) copy-start(bf16[1,128,768]{2,1,0:T(8,128)(2,1)S(1)} %get-tuple-element.136) | copy-start | bytes 589828
  1.9 31.8 %copy-start.19 = (bf16[1,128,768]{2,1,0:T(8,128)(2,1)}, bf16[1,128,768]{2,1,0:T(8,128)(2,1)S(1)}, u32[]{:S(2)}) copy-start(bf16[1,128,768]{2,1,0:T(8,128)(2,1)S(1)} %get-tuple-element.135) | copy-start | bytes 589828
  1.9 23.5 %collective-permute-start.6 = (bf16[1,128,768]{2,1,0:T(8,128)(2,1)S(1)}, bf16[1,128,768]{2,1,0:T(8,128)(2,1)S(1)}, u32[]{:S(2)}, u32[]{:S(2)}) collective-permute-start(bf16[1,128,768]{2,1,0:T(8,128)(2,1)S(1)} %get-tuple-element.136), channel_id=1, source_target_pairs={{0,12},{4,8},{8,4},{12,0},{1,13},{5,9},{9,5},{13,1},{2,14},{6,10},... | collective-permute-start | bytes 589832 | tf_op jit(solution)/shard_map/ppermute | solution.py:548
  8.8 23.4 %collective-permute-start = (bf16[2,128,768]{2,1,0:T(8,128)(2,1)}, bf16[2,128,768]{2,1,0:T(8,128)(2,1)S(1)}, u32[]{:S(2)}, u32[]{:S(2)}) collective-permute-start(bf16[2,128,768]{2,1,0:T(8,128)(2,1)} %pad_maximum_fusion.13), channel_id=1, source_target_pairs={{0,8},{4,12},{8,0},{12,4},{1,9},{5,13},{9,1},{13,5},{2,10},{6,14},... | collective-permute-start | bytes 1179656 | tf_op jit(solution)/shard_map/ppermute | solution.py:548
  8.8 35.1 %collective-permute-start.3 = (bf16[384,768]{1,0:T(8,128)(2,1)S(1)}, bf16[384,768]{1,0:T(8,128)(2,1)}, u32[]{:S(2)}, u32[]{:S(2)}) collective-permute-start(bf16[384,768]{1,0:T(8,128)(2,1)S(1)} %copy-done.28), channel_id=1, source_target_pairs={{0,16},{16,0},{1,17},{17,1},{2,18},{18,2},{3,19},{19,3},{4,20},{20... | collective-permute-start | bytes 1769480 | tf_op jit(solution)/shard_map/ppermute | solution.py:548
  10.3 34.8 %collective-permute-start.4 = (bf16[768,384]{1,0:T(8,128)(2,1)S(1)}, bf16[768,384]{1,0:T(8,128)(2,1)}, u32[]{:S(2)}, u32[]{:S(2)}) collective-permute-start(bf16[768,384]{1,0:T(8,128)(2,1)S(1)} %copy-done.29), channel_id=1, source_target_pairs={{0,16},{16,0},{1,17},{17,1},{2,18},{18,2},{3,19},{19,3},{4,20},{20... | collective-permute-start | bytes 1769480 | tf_op jit(solution)/shard_map/ppermute | solution.py:548
  10.8 13.1 %collective-permute-start.5 = (bf16[1,128,768]{2,1,0:T(8,128)(2,1)S(1)}, bf16[1,128,768]{2,1,0:T(8,128)(2,1)S(1)}, u32[]{:S(2)}, u32[]{:S(2)}) collective-permute-start(bf16[1,128,768]{2,1,0:T(8,128)(2,1)S(1)} %get-tuple-element.135), channel_id=1, source_target_pairs={{0,4},{4,0},{8,12},{12,8},{1,5},{5,1},{9,13},{13,9},{2,6},{6,2},{1... | collective-permute-start | bytes 589832 | tf_op jit(solution)/shard_map/ppermute | solution.py:548
  23.9 37.6 %collective-permute-start.9 = (bf16[768,384]{1,0:T(8,128)(2,1)}, bf16[768,384]{1,0:T(8,128)(2,1)}, u32[]{:S(2)}, u32[]{:S(2)}) collective-permute-start(bf16[768,384]{1,0:T(8,128)(2,1)} %pad_maximum_fusion.11), channel_id=1, source_target_pairs={{0,16},{16,0},{1,17},{17,1},{2,18},{18,2},{3,19},{19,3},{4,20},{20... | collective-permute-start | bytes 1769480 | tf_op jit(solution)/shard_map/ppermute | solution.py:548
  25.5 11.1 %collective-permute-start.7 = (bf16[2,128,768]{2,1,0:T(8,128)(2,1)S(1)}, bf16[2,128,768]{2,1,0:T(8,128)(2,1)S(1)}, u32[]{:S(2)}, u32[]{:S(2)}) collective-permute-start(bf16[2,128,768]{2,1,0:T(8,128)(2,1)S(1)} %constant_dynamic-update-slice_fusion.nz), channel_id=1, source_target_pairs={{0,2},{1,3},{2,0},{3,1},{4,6},{5,7},{6,4},{7,5},{8,10},{9,11},{10,... | collective-permute-start | bytes 1179656 | tf_op jit(solution)/shard_map/ppermute | solution.py:548
  32.2 11.6 %copy-start.2 = (bf16[2,128,768]{2,1,0:T(8,128)(2,1)}, bf16[2,128,768]{2,1,0:T(8,128)(2,1)S(1)}, u32[]{:S(2)}) copy-start(bf16[2,128,768]{2,1,0:T(8,128)(2,1)S(1)} %collective-permute-done.fz) | copy-start | bytes 1179652
  32.2 11.5 %collective-permute-start.1 = (bf16[2,128,768]{2,1,0:T(8,128)(2,1)S(1)}, bf16[2,128,768]{2,1,0:T(8,128)(2,1)S(1)}, u32[]{:S(2)}, u32[]{:S(2)}) collective-permute-start(bf16[2,128,768]{2,1,0:T(8,128)(2,1)S(1)} %collective-permute-done.fz), channel_id=1, source_target_pairs={{0,2},{1,3},{2,0},{3,1},{4,6},{5,7},{6,4},{7,5},{8,10},{9,11},{10,... | collective-permute-start | bytes 1179656 | tf_op jit(solution)/shard_map/ppermute | solution.py:548
  36.7 26.2 %collective-permute-start.8 = (bf16[2,2,128,768]{3,2,1,0:T(8,128)(2,1)S(1)}, bf16[2,2,128,768]{3,2,1,0:T(8,128)(2,1)S(1)}, u32[]{:S(2)}, u32[]{:S(2)}) collective-permute-start(bf16[2,2,128,768]{3,2,1,0:T(8,128)(2,1)S(1)} %pad_maximum_fusion.7), channel_id=1, source_target_pairs={{0,1},{1,0},{2,3},{3,2},{4,5},{5,4},{6,7},{7,6},{8,9},{9,8},{10,11... | collective-permute-start | bytes 2359304 | tf_op jit(solution)/shard_map/ppermute | solution.py:548
  43.8 2.9 %collective-permute-start.2 = (bf16[2,2,128,768]{3,2,1,0:T(8,128)(2,1)S(1)}, bf16[2,2,128,768]{3,2,1,0:T(8,128)(2,1)S(1)}, u32[]{:S(2)}, u32[]{:S(2)}) collective-permute-start(bf16[2,2,128,768]{3,2,1,0:T(8,128)(2,1)S(1)} %pad_maximum_fusion.6), channel_id=1, source_target_pairs={{0,1},{1,0},{2,3},{3,2},{4,5},{5,4},{6,7},{7,6},{8,9},{9,8},{10,11... | collective-permute-start | bytes 2359304 | tf_op jit(solution)/shard_map/ppermute | solution.py:548
  50.9 10.6 %copy-start.25 = (bf16[384,3,192]{0,2,1:T(8,128)(2,1)S(1)}, bf16[384,3,192]{0,2,1:T(8,128)(2,1)}, u32[]{:S(2)}) copy-start(bf16[384,3,192]{0,2,1:T(8,128)(2,1)} %param.17) | copy-start | bytes 1327108
  50.9 10.6 %copy-start.27 = (bf16[192,384]{1,0:T(8,128)(2,1)S(1)}, bf16[192,384]{1,0:T(8,128)(2,1)}, u32[]{:S(2)}) copy-start(bf16[192,384]{1,0:T(8,128)(2,1)} %param.19) | copy-start | bytes 442372
  60.9 28.9 %collective-permute-start.10 = (bf16[768,768]{1,0:T(8,128)(2,1)S(1)}, bf16[768,768]{1,0:T(8,128)(2,1)S(1)}, u32[]{:S(2)}, u32[]{:S(2)}) collective-permute-start(bf16[768,768]{1,0:T(8,128)(2,1)S(1)} %get-tuple-element.81), channel_id=1, source_target_pairs={{0,16},{16,0},{1,17},{17,1},{2,18},{18,2},{3,19},{19,3},{4,20},{20... | collective-permute-start | bytes 3538952 | tf_op jit(solution)/shard_map/ppermute | solution.py:548
  90.1 16.3 %collective-permute-start.13 = (bf16[384,768]{1,0:T(8,128)(2,1)S(1)}, bf16[384,768]{1,0:T(8,128)(2,1)S(1)}, u32[]{:S(2)}, u32[]{:S(2)}) collective-permute-start(bf16[384,768]{1,0:T(8,128)(2,1)S(1)} %dynamic-slice_convert_fusion), channel_id=1, source_target_pairs={{0,4},{4,0},{8,12},{12,8},{1,5},{5,1},{9,13},{13,9},{2,6},{6,2},{1... | collective-permute-start | bytes 1769480 | tf_op jit(solution)/shard_map/ppermute | solution.py:548
  105.1 7.3 %collective-permute-start.11 = (bf16[2,256,768]{2,1,0:T(8,128)(2,1)S(1)}, bf16[2,256,768]{2,1,0:T(8,128)(2,1)S(1)}, u32[]{:S(2)}, u32[]{:S(2)}) collective-permute-start(bf16[2,256,768]{2,1,0:T(8,128)(2,1)S(1)} %get-tuple-element.85), channel_id=1, source_target_pairs={{0,1},{1,0},{2,3},{3,2},{4,5},{5,4},{6,7},{7,6},{8,9},{9,8},{10,11... | collective-permute-start | bytes 2359304 | tf_op jit(solution)/shard_map/ppermute | solution.py:548
  106.6 15.9 %collective-permute-start.33 = (bf16[192,768]{1,0:T(8,128)(2,1)S(1)}, bf16[192,768]{1,0:T(8,128)(2,1)S(1)}, u32[]{:S(2)}, u32[]{:S(2)}) collective-permute-start(bf16[192,768]{1,0:T(8,128)(2,1)S(1)} %dynamic-slice_convert_fusion.1), channel_id=1, source_target_pairs={{0,8},{4,12},{8,0},{12,4},{1,9},{5,13},{9,1},{13,5},{2,10},{6,14},... | collective-permute-start | bytes 884744 | tf_op jit(solution)/shard_map/ppermute | solution.py:548
  112.3 11.5 %collective-permute-start.18 = (bf16[2,256,768]{2,1,0:T(8,128)(2,1)S(1)}, bf16[2,256,768]{2,1,0:T(8,128)(2,1)S(1)}, u32[]{:S(2)}, u32[]{:S(2)}) collective-permute-start(bf16[2,256,768]{2,1,0:T(8,128)(2,1)S(1)} %get-tuple-element.103), channel_id=1, source_target_pairs={{0,1},{1,0},{2,3},{3,2},{4,5},{5,4},{6,7},{7,6},{8,9},{9,8},{10,11... | collective-permute-start | bytes 2359304 | tf_op jit(solution)/shard_map/ppermute | solution.py:548
  118.8 6.2 %collective-permute-start.14 = (bf16[2,256,768]{2,1,0:T(8,128)(2,1)S(1)}, bf16[2,256,768]{2,1,0:T(8,128)(2,1)S(1)}, u32[]{:S(2)}, u32[]{:S(2)}) collective-permute-start(bf16[2,256,768]{2,1,0:T(8,128)(2,1)S(1)} %get-tuple-element.100), channel_id=1, source_target_pairs={{0,1},{1,0},{2,3},{3,2},{4,5},{5,4},{6,7},{7,6},{8,9},{9,8},{10,11... | collective-permute-start | bytes 2359304 | tf_op jit(solution)/shard_map/ppermute | solution.py:548
  119.4 12.0 %collective-permute-start.12 = (bf16[2,128,768]{2,1,0:T(8,128)(2,1)S(1)}, bf16[2,128,768]{2,1,0:T(8,128)(2,1)S(1)}, u32[]{:S(2)}, u32[]{:S(2)}) collective-permute-start(bf16[2,128,768]{2,1,0:T(8,128)(2,1)S(1)} %fusion.16), channel_id=1, source_target_pairs={{0,2},{1,3},{2,0},{3,1},{4,6},{5,7},{6,4},{7,5},{8,10},{9,11},{10,... | collective-permute-start | bytes 1179656 | tf_op jit(solution)/shard_map/ppermute | solution.py:548
  123.3 20.0 %collective-permute-start.34 = (bf16[192,768]{1,0:T(8,128)(2,1)}, bf16[192,768]{1,0:T(8,128)(2,1)}, u32[]{:S(2)}, u32[]{:S(2)}) collective-permute-start(bf16[192,768]{1,0:T(8,128)(2,1)} %add_convert_fusion), channel_id=1, source_target_pairs={{0,8},{4,12},{8,0},{12,4},{1,9},{5,13},{9,1},{13,5},{2,10},{6,14},... | collective-permute-start | bytes 884744 | tf_op jit(solution)/shard_map/ppermute | solution.py:548
  124.1 15.8 %collective-permute-start.19 = (bf16[2,128,768]{2,1,0:T(8,128)(2,1)S(1)}, bf16[2,128,768]{2,1,0:T(8,128)(2,1)S(1)}, u32[]{:S(2)}, u32[]{:S(2)}) collective-permute-start(bf16[2,128,768]{2,1,0:T(8,128)(2,1)S(1)} %fusion.18), channel_id=1, source_target_pairs={{0,2},{1,3},{2,0},{3,1},{4,6},{5,7},{6,4},{7,5},{8,10},{9,11},{10,... | collective-permute-start | bytes 1179656 | tf_op jit(solution)/shard_map/ppermute | solution.py:548
  125.2 10.0 %copy-start.21 = (f32[2,256,768]{2,1,0:T(8,128)}, f32[2,256,768]{2,1,0:T(8,128)S(1)}, u32[]{:S(2)}) copy-start(f32[2,256,768]{2,1,0:T(8,128)S(1)} %convert_add_fusion.3) | copy-start | bytes 4718596
  131.6 10.1 %copy-start.32 = (f32[768]{0:T(1024)S(1)}, f32[768]{0:T(1024)}, u32[]{:S(2)}) copy-start(f32[768]{0:T(1024)} %param.20) | copy-start | bytes 9220
  131.6 10.1 %copy-start.33 = (f32[768]{0:T(1024)S(1)}, f32[768]{0:T(1024)}, u32[]{:S(2)}) copy-start(f32[768]{0:T(1024)} %param.24) | copy-start | bytes 9220
  132.4 14.8 %collective-permute-start.15 = (bf16[128,768]{1,0:T(8,128)(2,1)}, bf16[128,768]{1,0:T(8,128)(2,1)}, u32[]{:S(2)}, u32[]{:S(2)}) collective-permute-start(bf16[128,768]{1,0:T(8,128)(2,1)} %get-tuple-element.161), channel_id=1, source_target_pairs={{0,8},{4,12},{8,0},{12,4},{1,9},{5,13},{9,1},{13,5},{2,10},{6,14},... | collective-permute-start | bytes 589832 | tf_op jit(solution)/shard_map/ppermute | solution.py:548
  135.2 14.0 %collective-permute-start.17 = (bf16[2,128,768]{2,1,0:T(8,128)(2,1)}, bf16[2,128,768]{2,1,0:T(8,128)(2,1)}, u32[]{:S(2)}, u32[]{:S(2)}) collective-permute-start(bf16[2,128,768]{2,1,0:T(8,128)(2,1)} %fusion.17), channel_id=1, source_target_pairs={{0,2},{1,3},{2,0},{3,1},{4,6},{5,7},{6,4},{7,5},{8,10},{9,11},{10,... | collective-permute-start | bytes 1179656 | tf_op jit(solution)/shard_map/ppermute | solution.py:548
  140.7 14.8 %collective-permute-start.20 = (bf16[2,128,768]{2,1,0:T(8,128)(2,1)}, bf16[2,128,768]{2,1,0:T(8,128)(2,1)}, u32[]{:S(2)}, u32[]{:S(2)}) collective-permute-start(bf16[2,128,768]{2,1,0:T(8,128)(2,1)} %fusion.9), channel_id=1, source_target_pairs={{0,4},{4,0},{8,12},{12,8},{1,5},{5,1},{9,13},{13,9},{2,6},{6,2},{1... | collective-permute-start | bytes 1179656 | tf_op jit(solution)/shard_map/ppermute | solution.py:548
  141.7 13.9 %copy-start.22 = (f32[2,256,768]{2,1,0:T(8,128)S(1)}, f32[2,256,768]{2,1,0:T(8,128)}, u32[]{:S(2)}) copy-start(f32[2,256,768]{2,1,0:T(8,128)} %copy-done.21) | copy-start | bytes 4718596
  141.7 30.5 %collective-permute-start.25 = (bf16[832,384]{1,0:T(8,128)(2,1)}, bf16[832,384]{1,0:T(8,128)(2,1)S(1)}, u32[]{:S(2)}, u32[]{:S(2)}) collective-permute-start(bf16[832,384]{1,0:T(8,128)(2,1)} %copy-done.14), channel_id=1, source_target_pairs={{0,16},{16,0},{1,17},{17,1},{2,18},{18,2},{3,19},{19,3},{4,20},{20... | collective-permute-start | bytes 1916936 | tf_op jit(solution)/shard_map/ppermute | solution.py:548
  144.4 27.8 %collective-permute-start.35 = (bf16[2,192,768]{2,1,0:T(8,128)(2,1)S(1)}, bf16[2,192,768]{2,1,0:T(8,128)(2,1)S(1)}, u32[]{:S(2)}, u32[]{:S(2)}) collective-permute-start(bf16[2,192,768]{2,1,0:T(8,128)(2,1)S(1)} %pad_maximum_fusion.12), channel_id=1, source_target_pairs={{0,4},{4,0},{8,12},{12,8},{1,5},{5,1},{9,13},{13,9},{2,6},{6,2},{1... | collective-permute-start | bytes 1769480 | tf_op jit(solution)/shard_map/ppermute | solution.py:548
  148.2 30.0 %collective-permute-start.16 = (bf16[2,128,768]{2,1,0:T(8,128)(2,1)S(1)}, bf16[2,128,768]{2,1,0:T(8,128)(2,1)S(1)}, u32[]{:S(2)}, u32[]{:S(2)}) collective-permute-start(bf16[2,128,768]{2,1,0:T(8,128)(2,1)S(1)} %pad_maximum_fusion.15), channel_id=1, source_target_pairs={{0,2},{1,3},{2,0},{3,1},{4,6},{5,7},{6,4},{7,5},{8,10},{9,11},{10,... | collective-permute-start | bytes 1179656 | tf_op jit(solution)/shard_map/ppermute | solution.py:548
  156.8 9.9 %collective-permute-start.21 = (bf16[128,768]{1,0:T(8,128)(2,1)S(1)}, bf16[128,768]{1,0:T(8,128)(2,1)S(1)}, u32[]{:S(2)}, u32[]{:S(2)}) collective-permute-start(bf16[128,768]{1,0:T(8,128)(2,1)S(1)} %fusion.20), channel_id=1, source_target_pairs={{0,8},{4,12},{8,0},{12,4},{1,9},{5,13},{9,1},{13,5},{2,10},{6,14},... | collective-permute-start | bytes 589832 | tf_op jit(solution)/shard_map/ppermute | solution.py:548
  167.4 20.5 %collective-permute-start.23 = (bf16[2,128,768]{2,1,0:T(8,128)(2,1)S(1)}, bf16[2,128,768]{2,1,0:T(8,128)(2,1)S(1)}, u32[]{:S(2)}, u32[]{:S(2)}) collective-permute-start(bf16[2,128,768]{2,1,0:T(8,128)(2,1)S(1)} %fusion.7), channel_id=1, source_target_pairs={{0,2},{1,3},{2,0},{3,1},{4,6},{5,7},{6,4},{7,5},{8,10},{9,11},{10,... | collective-permute-start | bytes 1179656 | tf_op jit(solution)/shard_map/ppermute | solution.py:548
  172.4 9.0 %collective-permute-start.26 = (bf16[208,384]{1,0:T(8,128)(2,1)S(1)}, bf16[208,384]{1,0:T(8,128)(2,1)S(1)}, u32[]{:S(2)}, u32[]{:S(2)}) collective-permute-start(bf16[208,384]{1,0:T(8,128)(2,1)S(1)} %get-tuple-element.137), channel_id=1, source_target_pairs={{0,12},{4,8},{8,4},{12,0},{1,13},{5,9},{9,5},{13,1},{2,14},{6,10},... | collective-permute-start | bytes 479240 | tf_op jit(solution)/shard_map/ppermute | solution.py:548
  174.8 12.9 %collective-permute-start.27 = (bf16[208,384]{1,0:T(8,128)(2,1)S(1)}, bf16[208,384]{1,0:T(8,128)(2,1)S(1)}, u32[]{:S(2)}, u32[]{:S(2)}) collective-permute-start(bf16[208,384]{1,0:T(8,128)(2,1)S(1)} %get-tuple-element.139), channel_id=1, source_target_pairs={{0,8},{4,12},{8,0},{12,4},{1,9},{5,13},{9,1},{13,5},{2,10},{6,14},... | collective-permute-start | bytes 479240 | tf_op jit(solution)/shard_map/ppermute | solution.py:548
  174.8 12.9 %collective-permute-start.28 = (bf16[208,384]{1,0:T(8,128)(2,1)S(1)}, bf16[208,384]{1,0:T(8,128)(2,1)S(1)}, u32[]{:S(2)}, u32[]{:S(2)}) collective-permute-start(bf16[208,384]{1,0:T(8,128)(2,1)S(1)} %get-tuple-element.138), channel_id=1, source_target_pairs={{0,4},{4,0},{8,12},{12,8},{1,5},{5,1},{9,13},{13,9},{2,6},{6,2},{1... | collective-permute-start | bytes 479240 | tf_op jit(solution)/shard_map/ppermute | solution.py:548
  180.0 17.7 %collective-permute-start.22 = (bf16[2,2,128,768]{3,2,1,0:T(8,128)(2,1)S(1)}, bf16[2,2,128,768]{3,2,1,0:T(8,128)(2,1)S(1)}, u32[]{:S(2)}, u32[]{:S(2)}) collective-permute-start(bf16[2,2,128,768]{3,2,1,0:T(8,128)(2,1)S(1)} %pad_maximum_fusion.9), channel_id=1, source_target_pairs={{0,1},{1,0},{2,3},{3,2},{4,5},{5,4},{6,7},{7,6},{8,9},{9,8},{10,11... | collective-permute-start | bytes 2359304 | tf_op jit(solution)/shard_map/ppermute | solution.py:548
  187.8 9.8 %collective-permute-start.29 = (bf16[208,384]{1,0:T(8,128)(2,1)S(1)}, bf16[208,384]{1,0:T(8,128)(2,1)S(1)}, u32[]{:S(2)}, u32[]{:S(2)}) collective-permute-start(bf16[208,384]{1,0:T(8,128)(2,1)S(1)} %add_convert_fusion.1), channel_id=1, source_target_pairs={{0,8},{4,12},{8,0},{12,4},{1,9},{5,13},{9,1},{13,5},{2,10},{6,14},... | collective-permute-start | bytes 479240 | tf_op jit(solution)/shard_map/ppermute | solution.py:548
  188.0 10.9 %collective-permute-start.24 = (bf16[2,2,128,768]{3,2,1,0:T(8,128)(2,1)S(1)}, bf16[2,2,128,768]{3,2,1,0:T(8,128)(2,1)S(1)}, u32[]{:S(2)}, u32[]{:S(2)}) collective-permute-start(bf16[2,2,128,768]{3,2,1,0:T(8,128)(2,1)S(1)} %pad_maximum_fusion.10), channel_id=1, source_target_pairs={{0,1},{1,0},{2,3},{3,2},{4,5},{5,4},{6,7},{7,6},{8,9},{9,8},{10,11... | collective-permute-start | bytes 2359304 | tf_op jit(solution)/shard_map/ppermute | solution.py:548
  197.7 9.5 %collective-permute-start.30 = (bf16[2,208,384]{2,1,0:T(8,128)(2,1)S(1)}, bf16[2,208,384]{2,1,0:T(8,128)(2,1)S(1)}, u32[]{:S(2)}, u32[]{:S(2)}) collective-permute-start(bf16[2,208,384]{2,1,0:T(8,128)(2,1)S(1)} %pad_maximum_fusion.17), channel_id=1, source_target_pairs={{0,4},{4,0},{8,12},{12,8},{1,5},{5,1},{9,13},{13,9},{2,6},{6,2},{1... | collective-permute-start | bytes 958472 | tf_op jit(solution)/shard_map/ppermute | solution.py:548
  207.3 2.1 collective-permute-start.31
  209.5 3.9 %collective-permute-start.32 = (f32[8,768]{1,0:T(8,128)S(1)}, f32[8,768]{1,0:T(8,128)S(1)}, u32[]{:S(2)}, u32[]{:S(2)}) collective-permute-start(f32[8,768]{1,0:T(8,128)S(1)} %fusion.26), channel_id=1, source_target_pairs={{0,2},{1,3},{2,0},{3,1},{4,6},{5,7},{6,4},{7,5},{8,10},{9,11},{10,... | collective-permute-start | bytes 73736 | tf_op jit(solution)/shard_map/ppermute | solution.py:548
  (22 other events, 70.1 us)
